TPU v7x, 32 devices: a whole 2x2x4 slice. The times are simulated.
32 devices in a mesh: lat: 8 (over z, x), chan: 4 (over y, core).
Axes of the slice: x: 2, y: 2, z: 4, core: 2. Of those that a mesh axis runs over, the one named last changes fastest.
Arguments:
- coarse_state: float32 [4, 96, 180, 641], P('chan', 'lat'), may hold values from -6 to 6
- fine_state: float32 [4, 184, 360, 641], P('chan', 'lat'), may hold values from -6 to 6
- coarse_noise: int32 [4, 96, 180, 8], P('chan', 'lat'), may hold values from 0 to 262143
- fine_noise: int32 [4, 184, 360, 8], P('chan', 'lat'), may hold values from 0 to 262143
- coarse_rows: int32 [96], replicated, may hold values from -1 to 89, as said below
- fine_rows: int32 [184], replicated, may hold values from -1 to 179, as said below
- pair_slots: int32 [96], replicated, may hold values from -1 to 89, as said below
- first_gain: float32 [641], replicated, may hold values from 0.5 to 1.5
- first_bias: float32 [641], replicated, may hold values from -3 to 3
- mix_weight: bfloat16 [192, 2, 649, 641], P('lat'), may hold values from -0.15625 to 0.15625
- second_gain: float32 [641], replicated, may hold values from 0.5 to 1.5
- second_bias: float32 [641], replicated, may hold values from -3 to 3
- up_weight: bfloat16 [641, 1282], replicated, may hold values from -0.25 to 0.25
- up_bias: float32 [1282], replicated, may hold values from -3 to 3
- down_weight: bfloat16 [1282, 641], replicated, may hold values from -0.15625 to 0.15625
- down_bias: float32 [641], replicated, may hold values from -3 to 3
- coarse_cotangent: float32 [4, 96, 180, 641], P('chan', 'lat'), may hold values from -6 to 6
- fine_cotangent: float32 [4, 184, 360, 641], P('chan', 'lat'), may hold values from -6 to 6
Outputs:
- coarse_out: float32 [4, 96, 180, 641], P('chan', 'lat')
- fine_out: float32 [4, 184, 360, 641], P('chan', 'lat')
- coarse_grad: float32 [4, 96, 180, 641], P('chan', 'lat')
- fine_grad: float32 [4, 184, 360, 641], P('chan', 'lat')
- first_gain_grad: float32 [641], replicated
- first_bias_grad: float32 [641], replicated
- mix_grad: float32 [192, 2, 649, 641], P(('lat', 'chan'))
- second_gain_grad: float32 [641], replicated
- second_bias_grad: float32 [641], replicated
- up_weight_grad: float32 [641, 1282], replicated
- up_bias_grad: float32 [1282], replicated
- down_weight_grad: float32 [1282, 641], replicated
- down_bias_grad: float32 [641], replicated
Inputs may be any that keep to these rules, and one draw needn't show every extreme that they name: `coarse_rows`: each latitude row 0 to 89 stands in exactly one slot; the other slots hold -1. `fine_rows`: each latitude row 0 to 179 stands in exactly one slot; the other slots hold -1. `pair_slots`: each pair 0 to 89 stands in exactly one slot; the other slots hold -1.
All inputs are finite; a program needn't handle non-finite values.
Results may differ from a plain program's by a relative error of at most 0.02.
Values may be sent and summed in bfloat16 or wider, within the bound.
No kernel may reach another device: no remote copies, remote signals or barrier semaphores. Data moves between devices by JAX's collectives and lax.ppermute only.
A program may use at most 832 MiB of HBM per device.

v0:
```python
import math

import jax
import jax.numpy as jnp
from jax import lax
from jax.sharding import PartitionSpec as P

C = 641
NOISE = 8
LA = 90
LB = 180


epsilon = 1e-05
noise_scale = 1.0 / 262144.0


def noise_value(noise_ints):
    return ((noise_ints.astype(jnp.float32) + 0.5) * noise_scale - 0.5) * math.sqrt(12.0)


def layer_norm(values, gain_vector, bias_vector):
    centered = values - jnp.mean(values, axis=-1, keepdims=True)
    variance = jnp.mean(centered * centered, axis=-1, keepdims=True)
    return centered * lax.rsqrt(variance + epsilon) * gain_vector + bias_vector


def activate(values):
    return jax.nn.gelu(values, approximate=False)


def legendre(orders, cosines, sines, degree_total):
    order_real = orders.astype(cosines.dtype)[:, None]
    log_start = 0.5 * jnp.log((2.0 * order_real + 1.0) / (4.0 * math.pi))
    log_start = log_start + 0.5 * (
        lax.lgamma(2.0 * order_real + 1.0)
        - 2.0 * order_real * math.log(2.0)
        - 2.0 * lax.lgamma(order_real + 1.0)
    )
    diagonal = jnp.exp(log_start + order_real * jnp.log(sines)[None, :])

    def recur_step(carry, degree):
        previous, earlier = carry
        degree_real = degree.astype(cosines.dtype)
        grow_factor = jnp.sqrt(
            (4.0 * degree_real * degree_real - 1.0)
            / jnp.maximum(degree_real * degree_real - order_real * order_real, 1.0)
        )
        damp_factor = jnp.sqrt(
            jnp.maximum((degree_real - 1.0) ** 2 - order_real * order_real, 0.0)
            / jnp.maximum(4.0 * (degree_real - 1.0) ** 2 - 1.0, 1.0)
        )
        recurred = grow_factor * (cosines[None, :] * previous - damp_factor * earlier)
        current = jnp.where(
            degree == orders[:, None],
            diagonal,
            jnp.where(degree > orders[:, None], recurred, jnp.zeros_like(recurred)),
        )
        return ((current, previous), current)

    zero_state = jnp.zeros((orders.shape[0], cosines.shape[0]), cosines.dtype)
    unused, stacked = lax.scan(
        recur_step, (zero_state, zero_state), jnp.arange(degree_total, dtype=jnp.int32)
    )
    return stacked


def sphere_tables(orders, row_table, degree_total, dtype):
    occupied = (row_table >= 0).astype(dtype)
    colatitude = math.pi * (jnp.maximum(row_table, 0).astype(dtype) + 0.5) / degree_total
    sines = jnp.sin(colatitude)
    plain_table = legendre(orders, jnp.cos(colatitude), sines, degree_total) * occupied
    quad_table = plain_table * (sines * occupied * (2.0 * math.pi * math.pi / degree_total))
    return (quad_table, plain_table)


def fourier_rows(orders, order_live, lon_count):
    points = jnp.arange(lon_count, dtype=jnp.int32)[None, :]
    phase_angle = (orders[:, None] * points % lon_count).astype(jnp.float32) * (
        2.0 * math.pi / lon_count
    )
    retained = order_live.astype(jnp.float32)[:, None]
    return jnp.stack(
        [jnp.cos(phase_angle) * retained / lon_count, -jnp.sin(phase_angle) * retained / lon_count]
    ).astype(jnp.bfloat16)


def inverse_rows(orders, order_live, lon_count):
    points = jnp.arange(lon_count, dtype=jnp.int32)[None, :]
    phase_angle = (orders[:, None] * points % lon_count).astype(jnp.float32) * (
        2.0 * math.pi / lon_count
    )
    doubling = (
        jnp.where(orders[:, None] == 0, 1.0, 2.0).astype(jnp.float32)
        * order_live.astype(jnp.float32)[:, None]
    )
    return jnp.stack(
        [jnp.cos(phase_angle) * doubling, -jnp.sin(phase_angle) * doubling], axis=1
    ).astype(jnp.bfloat16)


def pick_entries(table, degrees, columns, keeping):
    flat = table.reshape(table.shape[0] * table.shape[1], table.shape[2])
    return (
        jnp.take(flat, degrees * table.shape[1] + columns, axis=0)
        * keeping.astype(jnp.float32)[..., None]
    )


def pair_tables(fine_table, coarse_table, pair_slots, local_pairs):
    pair_dev = local_pairs.shape[0]
    order_pair = local_pairs[None, :]
    degree_pair = pair_slots[:, None]
    both_live = (order_pair >= 0) & (degree_pair >= 0)
    lower_side = order_pair < degree_pair
    degree_safe = jnp.maximum(degree_pair, 0)
    order_safe = jnp.maximum(order_pair, 0)
    column_low = 2 * jnp.arange(pair_dev, dtype=jnp.int32)[None, :]
    first_entry = pick_entries(
        fine_table, jnp.where(lower_side, degree_safe, LB - 1 - degree_safe), column_low, both_live
    )
    second_entry = pick_entries(
        fine_table, LB - 1 - degree_safe, column_low + jnp.where(lower_side, 0, 1), both_live
    )
    lower_real = lower_side.astype(jnp.float32)[..., None]
    zero_entry = jnp.zeros_like(first_entry)
    joined = jnp.stack(
        [
            jnp.stack([first_entry, zero_entry], axis=2),
            jnp.stack([second_entry * lower_real, second_entry * (1.0 - lower_real)], axis=2),
        ],
        axis=2,
    )
    diagonal = pick_entries(fine_table, order_safe, column_low, order_pair >= 0)[0]
    coarse_part = pick_entries(
        coarse_table,
        degree_safe,
        jnp.arange(pair_dev, dtype=jnp.int32)[None, :],
        both_live & (order_pair <= degree_pair),
    )
    return (
        joined.astype(jnp.bfloat16),
        diagonal.astype(jnp.bfloat16),
        coarse_part.astype(jnp.bfloat16),
    )


def sort_positions(pair_slots, local_pairs):
    pair_dev = local_pairs.shape[0]
    degree_pair = local_pairs[:, None]
    order_pair = pair_slots[None, :]
    both_live = (order_pair >= 0) & (degree_pair >= 0)
    lower_side = order_pair < degree_pair
    order_safe = jnp.maximum(order_pair, 0)
    degree_safe = jnp.maximum(degree_pair, 0)
    dump_index = 2 * LB
    coarse_pos = jnp.where(both_live & (order_pair <= degree_pair), order_safe, dump_index)
    first_pos = jnp.where(
        both_live, jnp.where(lower_side, LA + order_safe, LB + order_safe), dump_index
    )
    second_pos = jnp.where(
        both_live, LB + jnp.where(lower_side, order_safe, LB - 1 - order_safe), dump_index
    )
    diagonal_pos = jnp.where(degree_pair >= 0, LA + degree_safe, dump_index)
    fine_pos = jnp.stack([first_pos, second_pos], axis=2).reshape(pair_dev, -1)
    return jnp.concatenate([coarse_pos, fine_pos, diagonal_pos], axis=1)


def inverse_positions(positions):
    pair_dev, source_count = positions.shape
    row_index = jnp.arange(pair_dev, dtype=jnp.int32)[:, None]
    sources = jnp.broadcast_to(jnp.arange(source_count, dtype=jnp.int32)[None, :], positions.shape)
    filled = (
        jnp.full((pair_dev, 2 * LB + 1), source_count, jnp.int32)
        .at[row_index, positions]
        .set(sources)
    )
    return filled[:, : 2 * LB]


def gather_rows(values, index):
    return jax.vmap(
        lambda block, picks: jnp.take(block, picks, axis=1), in_axes=(1, 0), out_axes=1
    )(values, index)


def to_members(coarse_in, fine_in, diagonal_in, inverse):
    sample_count, pair_dev = (coarse_in.shape[0], coarse_in.shape[1])
    width = coarse_in.shape[-1]
    stacked = jnp.concatenate(
        [
            coarse_in,
            fine_in.reshape(sample_count, pair_dev, -1, width),
            diagonal_in[:, :, None, :],
            jnp.zeros((sample_count, pair_dev, 1, width), jnp.bfloat16),
        ],
        axis=2,
    )
    return gather_rows(stacked, inverse).reshape(sample_count, 2 * pair_dev, LB, width)


def from_members(members, positions):
    sample_count, member_count, unused_len, width = members.shape
    pair_dev = member_count // 2
    pair_total = (positions.shape[1] - 1) // 3
    padded = jnp.concatenate(
        [
            members.reshape(sample_count, pair_dev, 2 * LB, width),
            jnp.zeros((sample_count, pair_dev, 1, width), jnp.bfloat16),
        ],
        axis=2,
    )
    picked = gather_rows(padded, positions)
    coarse_part = picked[:, :, :pair_total]
    fine_part = picked[:, :, pair_total : 3 * pair_total].reshape(
        sample_count, pair_dev, pair_total, 2, width
    )
    return (coarse_part, fine_part, picked[:, :, 3 * pair_total])


def to_degrees(joined, diagonal, coarse_part, coarse_in, fine_in):
    sample_count, row_count, order_count, width = fine_in.shape
    fine_split = fine_in.reshape(sample_count, row_count, order_count // 2, 2, width)
    fine_out = jnp.einsum(
        "tiamr,srimc->stiac", joined, fine_split, preferred_element_type=jnp.float32
    ).astype(jnp.bfloat16)
    diagonal_out = jnp.einsum(
        "ir,sric->sic", diagonal, fine_split[:, :, :, 0, :], preferred_element_type=jnp.float32
    ).astype(jnp.bfloat16)
    coarse_out = jnp.einsum(
        "tir,sric->stic", coarse_part, coarse_in, preferred_element_type=jnp.float32
    ).astype(jnp.bfloat16)
    return (coarse_out, fine_out, diagonal_out)


def to_orders(joined, diagonal, coarse_part, coarse_back, fine_back, diagonal_back):
    fine_split = jnp.einsum(
        "tiamr,stiac->srimc", joined, fine_back, preferred_element_type=jnp.float32
    )
    diagonal_term = jnp.einsum(
        "ir,sic->sric", diagonal, diagonal_back, preferred_element_type=jnp.float32
    )
    fine_split = fine_split + jnp.stack([diagonal_term, jnp.zeros_like(diagonal_term)], axis=3)
    sample_count, row_count, pair_dev, unused_two, width = fine_split.shape
    fine_out = fine_split.reshape(sample_count, row_count, 2 * pair_dev, width).astype(jnp.bfloat16)
    coarse_out = jnp.einsum(
        "tir,stic->sric", coarse_part, coarse_back, preferred_element_type=jnp.float32
    ).astype(jnp.bfloat16)
    return (coarse_out, fine_out)


def mix_matrix(weight_slots):
    real_part = weight_slots[:, 0]
    imag_part = weight_slots[:, 1]
    upper_rows = jnp.concatenate([real_part, imag_part], axis=2)
    lower_rows = jnp.concatenate([-imag_part, real_part], axis=2)
    return jnp.concatenate([upper_rows, lower_rows], axis=1)


def mix_apply(spectra, matrix):
    return jnp.einsum("sjui,jio->sjuo", spectra, matrix, preferred_element_type=jnp.float32).astype(
        jnp.bfloat16
    )


def mix_backward(spectra, gradient, matrix):
    spectra_grad = jnp.einsum(
        "sjuo,jio->sjui", gradient, matrix, preferred_element_type=jnp.float32
    ).astype(jnp.bfloat16)
    matrix_grad = jnp.einsum(
        "sjui,sjuo->jio", spectra, gradient, preferred_element_type=jnp.float32
    )
    return (spectra_grad, matrix_grad)


def weight_gradient(matrix_grad, wide_count, channels):
    upper_rows = matrix_grad[:, :wide_count]
    lower_rows = matrix_grad[:, wide_count:]
    real_part = upper_rows[:, :, :channels] + lower_rows[:, :, channels:]
    imag_part = upper_rows[:, :, channels:] - lower_rows[:, :, :channels]
    return jnp.stack([real_part, imag_part], axis=1)


def shards(
    coarse_state,
    fine_state,
    coarse_noise,
    fine_noise,
    coarse_rows,
    fine_rows,
    pair_slots,
    first_gain,
    first_bias,
    mix_weight,
    second_gain,
    second_bias,
    up_weight,
    up_bias,
    down_weight,
    down_bias,
    coarse_cotangent,
    fine_cotangent,
):
    lat_rank = lax.axis_index("lat")
    wide_count = C + NOISE
    member_count = mix_weight.shape[0]
    pair_dev = member_count // 2
    pair_live = pair_slots >= 0
    pair_safe = jnp.maximum(pair_slots, 0)
    local_pairs = lax.dynamic_slice_in_dim(pair_slots, lat_rank * pair_dev, pair_dev)
    local_safe = jnp.maximum(local_pairs, 0)
    fine_orders = jnp.stack([pair_safe, LB - 1 - pair_safe], axis=1).reshape(-1)
    fine_live = jnp.stack([pair_live, pair_live], axis=1).reshape(-1)
    grids = (
        (coarse_state, coarse_noise, coarse_cotangent, pair_safe, pair_live),
        (fine_state, fine_noise, fine_cotangent, fine_orders, fine_live),
    )
    first_pulls = []
    dft_tables = []
    idft_tables = []
    fourier_parts = []
    for grid_state, noise_ints, unused_cot, orders, order_live in grids:
        sample_count, row_dev, lon_count, channels = grid_state.shape
        normed, norm_pull = jax.vjp(layer_norm, grid_state, first_gain, first_bias)
        spread_in = jnp.concatenate([normed, noise_value(noise_ints)], axis=-1).astype(jnp.bfloat16)
        forward_dft = fourier_rows(orders, order_live, lon_count)
        spectrum = jnp.einsum(
            "tmk,srkc->srmtc", forward_dft, spread_in, preferred_element_type=jnp.float32
        )
        fourier_parts.append(
            spectrum.reshape(sample_count, row_dev, orders.shape[0], 2 * wide_count).astype(
                jnp.bfloat16
            )
        )
        first_pulls.append(norm_pull)
        dft_tables.append(forward_dft)
        idft_tables.append(inverse_rows(orders, order_live, lon_count))
    local_fine_orders = jnp.stack([local_safe, LB - 1 - local_safe], axis=1).reshape(-1)
    fine_quad, fine_plain = sphere_tables(local_fine_orders, fine_rows, LB, jnp.float32)
    coarse_quad, coarse_plain = sphere_tables(local_safe, coarse_rows, LA, jnp.float32)
    quad_parts = pair_tables(fine_quad, coarse_quad, pair_slots, local_pairs)
    plain_parts = pair_tables(fine_plain, coarse_plain, pair_slots, local_pairs)
    positions = sort_positions(pair_slots, local_pairs)
    inverse = inverse_positions(positions)
    coarse_four, fine_four = (
        lax.all_to_all(fourier_parts[0], "lat", split_axis=2, concat_axis=1, tiled=True),
        lax.all_to_all(fourier_parts[1], "lat", split_axis=2, concat_axis=1, tiled=True),
    )
    coarse_send, fine_send, diagonal_local = to_degrees(
        quad_parts[0], quad_parts[1], quad_parts[2], coarse_four, fine_four
    )
    coarse_coef, fine_coef = (
        lax.all_to_all(coarse_send, "lat", split_axis=1, concat_axis=2, tiled=True),
        lax.all_to_all(fine_send, "lat", split_axis=1, concat_axis=2, tiled=True),
    )
    members = to_members(coarse_coef, fine_coef, diagonal_local, inverse)
    matrix = mix_matrix(mix_weight)
    mixed_members = mix_apply(members, matrix)
    coarse_mixed, fine_mixed, diagonal_mixed = from_members(mixed_members, positions)
    coarse_back, fine_back = (
        lax.all_to_all(coarse_mixed, "lat", split_axis=2, concat_axis=1, tiled=True),
        lax.all_to_all(fine_mixed, "lat", split_axis=2, concat_axis=1, tiled=True),
    )
    coarse_out_part, fine_out_part = to_orders(
        plain_parts[0], plain_parts[1], plain_parts[2], coarse_back, fine_back, diagonal_mixed
    )
    coarse_synth, fine_synth = (
        lax.all_to_all(coarse_out_part, "lat", split_axis=1, concat_axis=2, tiled=True),
        lax.all_to_all(fine_out_part, "lat", split_axis=1, concat_axis=2, tiled=True),
    )
    outputs = []
    middle_grads = []
    synth_grads = []
    dense_terms = []
    for index_pos, synth_rows in enumerate((coarse_synth, fine_synth)):
        grid_state = grids[index_pos][0]
        cotangent = grids[index_pos][2]
        sample_count, row_dev, lon_count, channels = grid_state.shape
        order_count = synth_rows.shape[2]
        synthesized = jnp.einsum(
            "mtk,srmtc->srkc",
            idft_tables[index_pos],
            synth_rows.reshape(sample_count, row_dev, order_count, 2, channels),
            preferred_element_type=jnp.float32,
        )
        middle = grid_state + synthesized
        normed_two, second_pull = jax.vjp(layer_norm, middle, second_gain, second_bias)
        normed_low = normed_two.astype(jnp.bfloat16)
        pre_act = (
            jnp.einsum("srkc,ch->srkh", normed_low, up_weight, preferred_element_type=jnp.float32)
            + up_bias
        )
        hidden, act_pull = jax.vjp(activate, pre_act)
        hidden_low = hidden.astype(jnp.bfloat16)
        outputs.append(
            middle
            + jnp.einsum(
                "srkh,hc->srkc", hidden_low, down_weight, preferred_element_type=jnp.float32
            )
            + down_bias
        )
        down_bias_part = jnp.sum(cotangent, axis=(0, 1, 2))
        cot_low = cotangent.astype(jnp.bfloat16)
        down_weight_part = jnp.einsum(
            "srkh,srkc->hc", hidden_low, cot_low, preferred_element_type=jnp.float32
        )
        hidden_grad = jnp.einsum(
            "srkc,hc->srkh", cot_low, down_weight, preferred_element_type=jnp.float32
        )
        pre_grad = act_pull(hidden_grad)[0]
        up_bias_part = jnp.sum(pre_grad, axis=(0, 1, 2))
        pre_low = pre_grad.astype(jnp.bfloat16)
        up_weight_part = jnp.einsum(
            "srkc,srkh->ch", normed_low, pre_low, preferred_element_type=jnp.float32
        )
        normed_grad = jnp.einsum(
            "srkh,ch->srkc", pre_low, up_weight, preferred_element_type=jnp.float32
        )
        middle_part, gain_part, bias_part = second_pull(normed_grad)
        middle_grad = cotangent + middle_part
        middle_grads.append(middle_grad)
        dense_terms.append(
            (gain_part, bias_part, up_weight_part, up_bias_part, down_weight_part, down_bias_part)
        )
        field_low = middle_grad.astype(jnp.bfloat16)
        synth_grad = jnp.einsum(
            "mtk,srkc->srmtc", idft_tables[index_pos], field_low, preferred_element_type=jnp.float32
        )
        synth_grads.append(
            synth_grad.reshape(sample_count, row_dev, order_count, 2 * channels).astype(
                jnp.bfloat16
            )
        )
    coarse_sgrad, fine_sgrad = (
        lax.all_to_all(synth_grads[0], "lat", split_axis=2, concat_axis=1, tiled=True),
        lax.all_to_all(synth_grads[1], "lat", split_axis=2, concat_axis=1, tiled=True),
    )
    coarse_dgrad, fine_dgrad, diagonal_dgrad = to_degrees(
        plain_parts[0], plain_parts[1], plain_parts[2], coarse_sgrad, fine_sgrad
    )
    coarse_mgrad, fine_mgrad = (
        lax.all_to_all(coarse_dgrad, "lat", split_axis=1, concat_axis=2, tiled=True),
        lax.all_to_all(fine_dgrad, "lat", split_axis=1, concat_axis=2, tiled=True),
    )
    grad_members = to_members(coarse_mgrad, fine_mgrad, diagonal_dgrad, inverse)
    coef_members, matrix_grad = mix_backward(members, grad_members, matrix)
    mix_grad = lax.psum_scatter(
        weight_gradient(matrix_grad, wide_count, C).astype(jnp.bfloat16),
        "chan",
        scatter_dimension=0,
        tiled=True,
    ).astype(jnp.float32)
    coarse_cgrad, fine_cgrad, diagonal_cgrad = from_members(coef_members, positions)
    coarse_back_grad, fine_back_grad = (
        lax.all_to_all(coarse_cgrad, "lat", split_axis=2, concat_axis=1, tiled=True),
        lax.all_to_all(fine_cgrad, "lat", split_axis=2, concat_axis=1, tiled=True),
    )
    coarse_spec_grad, fine_spec_grad = to_orders(
        quad_parts[0],
        quad_parts[1],
        quad_parts[2],
        coarse_back_grad,
        fine_back_grad,
        diagonal_cgrad,
    )
    coarse_fgrad, fine_fgrad = (
        lax.all_to_all(coarse_spec_grad, "lat", split_axis=1, concat_axis=2, tiled=True),
        lax.all_to_all(fine_spec_grad, "lat", split_axis=1, concat_axis=2, tiled=True),
    )
    state_grads = []
    first_terms = []
    for index_pos, arrived in enumerate((coarse_fgrad, fine_fgrad)):
        sample_count, row_dev, order_count, doubled = arrived.shape
        spread_grad = jnp.einsum(
            "tmk,srmtc->srkc",
            dft_tables[index_pos],
            arrived.reshape(sample_count, row_dev, order_count, 2, wide_count),
            preferred_element_type=jnp.float32,
        )
        state_part, gain_part, bias_part = first_pulls[index_pos](spread_grad[..., :C])
        state_grads.append(middle_grads[index_pos] + state_part)
        first_terms.append((gain_part, bias_part))
    summed = lax.psum(
        (
            first_terms[0][0] + first_terms[1][0],
            first_terms[0][1] + first_terms[1][1],
            dense_terms[0][0] + dense_terms[1][0],
            dense_terms[0][1] + dense_terms[1][1],
            dense_terms[0][2] + dense_terms[1][2],
            dense_terms[0][3] + dense_terms[1][3],
            dense_terms[0][4] + dense_terms[1][4],
            dense_terms[0][5] + dense_terms[1][5],
        ),
        ("lat", "chan"),
    )
    return (
        outputs[0],
        outputs[1],
        state_grads[0],
        state_grads[1],
        summed[0],
        summed[1],
        mix_grad,
        summed[2],
        summed[3],
        summed[4],
        summed[5],
        summed[6],
        summed[7],
    )


def solution(mesh):
    return jax.shard_map(
        shards,
        mesh=mesh,
        in_specs=(
            P("chan", "lat", None, None),
            P("chan", "lat", None, None),
            P("chan", "lat", None, None),
            P("chan", "lat", None, None),
            P(),
            P(),
            P(),
            P(),
            P(),
            P("lat", None, None, None),
            P(),
            P(),
            P(),
            P(),
            P(),
            P(),
            P("chan", "lat", None, None),
            P("chan", "lat", None, None),
        ),
        out_specs=(
            P("chan", "lat", None, None),
            P("chan", "lat", None, None),
            P("chan", "lat", None, None),
            P("chan", "lat", None, None),
            P(),
            P(),
            P(("lat", "chan"), None, None, None),
            P(),
            P(),
            P(),
            P(),
            P(),
            P(),
        ),
        check_vma=False,
    )
```

profile of v0, /device:TPU:0, one launch (start us, length us, event | category | flops | bytes accessed | tf_op | source)
XLA Modules:
  0.0 5188.6 jit_solution(8646144583255692045)
XLA Ops:
  9.2 18.0 reduce_sum.245
  61.2 20.2 reduce_sum.247
  81.8 15.8 multiply_reduce_fusion.3
  128.3 19.9 copy.580
  148.3 23.7 reshape.2913
  178.3 235.0 %while.36 = (s32[]{:T(128)}, f32[12,96]{1,0:T(8,128)S(1)}, f32[12,96]{1,0:T(8,128)S(1)}, f32[90,12,96]{2,1,0:T(8,128)}, s32[90]{0:T(128)S(1)}, /*index=5*/s32[12...) while((s32[]{:T(128)}, f32[12,96]{1,0:T(8,128)S(1)}, ...), condition=%wide.region_4.5_spmd.clone, body=%wide.region_3.4_spmd.clone.sunk | while | flops 10477 | bytes 28143 | solution.py:62
  440.5 18.7 all-to-all-done.2
  472.0 506.6 %while.37 = (s32[]{:T(128)}, f32[24,184]{1,0:T(8,128)S(1)}, f32[24,184]{1,0:T(8,128)S(1)}, f32[180,24,184]{2,1,0:T(8,128)}, s32[180]{0:T(256)S(1)}, /*index=5*/s...) while((s32[]{:T(128)}, f32[24,184]{1,0:T(8,128)S(1)}, ...), condition=%wide.region_8.10_spmd.clone, body=%wide.region_7.9_spmd.clone.sunk | while | flops 39949 | bytes 97983 | solution.py:62
  1042.6 16.9 copy.478
  1059.5 19.5 reshape.2886
  1100.1 89.1 %fusion.255 = (bf16[24,1,649,641]{2,1,3,0:T(2,128)(2,1)}, bf16[24,1,649,641]{2,1,3,0:T(2,128)(2,1)}) fusion(bf16[24,2,649,641]{2,1,3,0:T(2,128)(2,1)} %param.37), kind=kLoop, calls=%fused_computation.538 | loop fusion | bytes 79873728 | tf_op jit(solution)/shard_map/slice | solution.py:254
  1197.4 17.0 scatter_custom_fusion
  1214.8 30.1 copy.745
  1246.3 31.8 fusion.254
  1291.9 19.5 reshape.2682
  1343.0 117.3 %gather_fusion = bf16[4320,1298]{1,0:T(8,128)(2,1)} fusion(bf16[12,290,1298]{2,1,0:T(8,128)(2,1)} %maximum_bitcast_fusion.2, s32[4320]{0:T(1024)S(1)} %reshape.2783), kind=kCustom, calls=%fused_computation.8 | custom fusion | bytes 22464000 | tf_op jit(solution)/shard_map/vmap(jit(_take))/gather | solution.py:183
  1474.3 56.9 %fusion.63 = bf16[1,24,180,1282]{3,2,1,0:T(8,128)(2,1)} fusion(bf16[24,180,1298]{2,1,0:T(8,128)(2,1)} %gather.34, pred[24,180]{1,0:T(8,128)(4,1)S(1)} %broadcast_in_dim.365, bf16[24,649,641]{1,2,0:T(8,128)(2,1)} %bitcast.569, bf16[24,649,641]{1,2,0:T(8,128)(2,1)} %get-tuple-element.618, bf16[24,649,641]{1,2,0:T(8,128)(2,1)} %get-tuple-element.619), kind=kOutput, calls=%fused_computation.147 | convolution fusion | flops 14707911680 | bytes 82200816 | tf_op jit(solution)/shard_map/sjui,jio->sjuo/dot_general | solution.py:261
  1556.5 93.2 %gather_fusion.1 = bf16[3468,1282]{1,0:T(8,128)(2,1)} fusion(bf16[12,361,1282]{2,1,0:T(8,128)(2,1)} %pad_bitcast_fusion.1, s32[3468]{0:T(1024)S(1)} %copy-done.4), kind=kCustom, calls=%fused_computation.9 | custom fusion | bytes 17811648 | tf_op jit(solution)/shard_map/vmap(jit(_take))/gather | solution.py:183
  1716.8 71.0 %all-to-all-done.4 = bf16[1,12,96,1282]{3,1,0,2:T(8,128)(2,1)} async-done(((bf16[1,12,96,1282]{3,1,0,2:T(8,128)(2,1)}), bf16[1,12,96,1282]{3,1,0,2:T(8,128)(2,1)}, u32[]{:S(2)}, u32[]{:S(2)}) %all-to-all-start.4) | async-done | bytes 2953760 | tf_op jit(solution)/shard_map/all_to_all | solution.py:361
  1821.4 113.1 %all-to-all-done.6 = bf16[1,12,96,2,1282]{4,3,1,0,2:T(2,128)(2,1)} async-done(((bf16[1,12,96,2,1282]{4,3,1,0,2:T(2,128)(2,1)}), bf16[1,12,96,2,1282]{4,3,1,0,2:T(2,128)(2,1)}, u32[]{:S(2)}, u32[]{:S(2)}) %all-to-all-start.6) | async-done | bytes 5907488 | tf_op jit(solution)/shard_map/all_to_all | solution.py:362
  1951.7 37.5 fusion.256
  2007.5 27.0 all-to-all-done.5
  2063.2 15.8 copy.512
  2101.0 29.8 multiply_convert_fusion.1
  2130.8 17.5 fusion.260
  2187.4 165.5 %all-to-all-done.7 = bf16[1,184,24,1282]{3,2,0,1:T(8,128)(2,1)} async-done(((bf16[1,184,24,1282]{3,2,0,1:T(8,128)(2,1)}), bf16[1,184,24,1282]{3,2,0,1:T(8,128)(2,1)}, u32[]{:S(2)}, u32[]{:S(2)}) %all-to-all-start.7) | async-done | bytes 11322656 | tf_op jit(solution)/shard_map/all_to_all | solution.py:369
  2367.9 24.6 reshape.2693
  2392.5 26.1 fusion.259
  2429.0 46.9 convert_reduce_fusion.1
  2476.0 108.2 %multiply_convert_fusion = (bf16[23,360,1282]{1,2,0:T(8,128)(2,1)}, f32[23,360,1282]{1,2,0:T(8,128)}) fusion(f32[23,360,1282]{1,2,0:T(8,128)} %get-tuple-element.712, f32[1282]{0:T(1024)S(1)} %copy-done.84, u32[360,1282]{0,1:T(8,128)} %get-tuple-element.539, u32[360,1282]{0,1:T(8,128)} %get-tuple-element.538), kind=kLoop, calls=%fused_computation.45 | loop fusion | flops 732432896 | bytes 109846888 | tf_op jit(solution)/shard_map/convert_element_type | solution.py:394
  2584.2 53.2 %fusion.261 = (f32[1282]{0:T(1024)}, bf16[23,360,1282]{1,2,0:T(8,128)(2,1)}) fusion(f32[23,360,1282]{1,2,0:T(8,128)} %get-tuple-element.611, bf16[1282,641]{0,1:T(8,128)(2,1)S(1)} %copy-done.115, bf16[1,23,360,641]{2,0,3,1:T(2,128)(2,1)} %get-tuple-element.637, f32[23,360,1282]{1,2,0:T(8,128)} %get-tuple-element.712, f32[1282]{0:T(1024)S(1)} %copy-done.84), kind=kOutput, calls=%fused_computation.544 | convolution fusion | flops 13778213888 | bytes 118418336 | tf_op jit(solution)/shard_map/srkc,hc->srkh/dot_general | solution.py:407
  2637.4 33.6 fusion.17
  2671.0 23.9 fusion.251
  2695.0 21.2 convert_bitcast_fusion
  2716.2 19.9 copy.588
  2736.1 23.7 reshape.2916
  2786.2 260.4 %all-to-all-done.10 = bf16[1,23,192,1282]{3,1,0,2:T(8,128)(2,1)} async-done(((bf16[1,23,192,1282]{3,1,0,2:T(8,128)(2,1)}), bf16[1,23,192,1282]{3,1,0,2:T(8,128)(2,1)}, u32[]{:S(2)}, u32[]{:S(2)}) %all-to-all-start.10) | async-done | bytes 11322656 | tf_op jit(solution)/shard_map/all_to_all | solution.py:436
  3059.5 16.9 copy.528
  3076.4 19.6 reshape.2900
  3111.3 35.4 all-to-all-done.9
  3165.8 19.5 reshape.2702
  3189.2 104.2 %all-to-all-done.11 = bf16[1,96,12,2,1282]{4,3,2,0,1:T(2,128)(2,1)} async-done(((bf16[1,96,12,2,1282]{4,3,2,0,1:T(2,128)(2,1)}), bf16[1,96,12,2,1282]{4,3,2,0,1:T(2,128)(2,1)}, u32[]{:S(2)}, u32[]{:S(2)}) %all-to-all-start.11) | async-done | bytes 5907488 | tf_op jit(solution)/shard_map/all_to_all | solution.py:443
  3321.2 117.6 %gather_fusion.2 = bf16[4320,1282]{1,0:T(8,128)(2,1)} fusion(bf16[12,290,1282]{2,1,0:T(8,128)(2,1)} %maximum_bitcast_fusion.3, s32[4320]{0:T(1024)S(1)} %copy-done.3), kind=kCustom, calls=%fused_computation.10 | custom fusion | bytes 22187520 | tf_op jit(solution)/shard_map/vmap(jit(_take))/gather | solution.py:183
  3452.6 55.9 %fusion.60 = bf16[1,24,180,1298]{3,2,1,0:T(8,128)(2,1)} fusion(bf16[24,180,1282]{2,1,0:T(8,128)(2,1)} %gather.38, pred[24,180]{1,0:T(8,128)(4,1)S(1)} %copy-done.32, bf16[24,649,641]{1,2,0:T(8,128)(2,1)} %bitcast.570, bf16[24,649,641]{1,2,0:T(8,128)(2,1)} %get-tuple-element.618, bf16[24,649,641]{1,2,0:T(8,128)(2,1)} %get-tuple-element.619), kind=kOutput, calls=%fused_computation.146 | convolution fusion | flops 14707911680 | bytes 82200816 | tf_op jit(solution)/shard_map/sjuo,jio->sjui/dot_general | solution.py:267
  3533.8 85.3 %gather_fusion.3 = bf16[3468,1298]{1,0:T(8,128)(2,1)} fusion(bf16[12,361,1298]{2,1,0:T(8,128)(2,1)} %pad_bitcast_fusion, s32[3468]{0:T(1024)S(1)} %copy-done.5), kind=kCustom, calls=%fused_computation.11 | custom fusion | bytes 18033600 | tf_op jit(solution)/shard_map/vmap(jit(_take))/gather | solution.py:183
  3647.3 20.4 all-to-all-start.12
  3698.6 65.4 %all-to-all-done.12 = bf16[1,12,96,1298]{3,1,0,2:T(8,128)(2,1)} async-done(((bf16[1,12,96,1298]{3,1,0,2:T(8,128)(2,1)}), bf16[1,12,96,1298]{3,1,0,2:T(8,128)(2,1)}, u32[]{:S(2)}, u32[]{:S(2)}) %all-to-all-start.12) | async-done | bytes 2990624 | tf_op jit(solution)/shard_map/all_to_all | solution.py:455
  3769.2 67.6 %fusion.59 = f32[24,1298,1282]{1,2,0:T(8,128)} fusion(bf16[24,180,1298]{2,1,0:T(8,128)(2,1)} %gather.34, pred[24,180]{1,0:T(8,128)(4,1)S(1)} %copy-done.32, bf16[24,180,1282]{2,1,0:T(8,128)(2,1)} %gather.38), kind=kOutput, calls=%fused_computation.145 | convolution fusion | flops 14388416512 | bytes 182042976 | tf_op jit(solution)/shard_map/sjui,sjuo->jio/dot_general | solution.py:270
  3836.9 76.1 %fusion.15 = (bf16[24,1,649,641]{2,3,0,1:T(8,128)(2,1)}, bf16[24,1,649,641]{2,3,0,1:T(8,128)(2,1)}) fusion(f32[24,1298,1282]{1,2,0:T(8,128)} %fusion.59), kind=kLoop, calls=%fused_computation.64 | loop fusion | flops 39936864 | bytes 199684320 | tf_op jit(solution)/shard_map/stack | solution.py:281
  3939.6 32.4 pad_maximum_fusion.2
  3972.0 190.6 %copy.550 = bf16[24,2,649,641]{2,1,3,0:T(2,128)(2,1)} copy(bf16[24,2,649,641]{2,3,0,1:T(8,128)(2,1)} %pad_maximum_fusion.2) | data formatting | bytes 79873728 | tf_op jit(solution)/shard_map/stack | solution.py:281
  4221.4 16.0 copy.547
  4244.1 31.8 fusion.19
  4276.0 45.8 copy.552
  4323.6 25.8 fusion.49
  4359.3 26.6 fusion.55
  4443.7 500.3 %all-reduce.12.cloned.1.call-done = bf16[24,2,649,641]{2,1,3,0:T(2,128)(2,1)} async-done(((bf16[24,2,649,641]{2,1,3,0:T(2,128)(2,1)}), bf16[24,2,649,641]{2,1,3,0:T(2,128)(2,1)}) %all-reduce.12.cloned.1.call-update) | async-done | bytes 39936880
  4967.5 24.7 reshape.2710
  4992.3 16.4 fusion.68
  5008.7 18.0 multiply_reduce_fusion.1
  5030.0 16.8 multiply_reduce_fusion
  5046.8 40.2 add_add_fusion.2
  5087.1 45.9 copy.554
  5133.0 40.2 all-reduce.7
  (1986 shorter events, 1505.9 us)
Async XLA Ops:
  7.2 2084.3 %copy-start = (bf16[641,1282]{1,0:T(8,128)(2,1)S(1)}, bf16[641,1282]{1,0:T(8,128)(2,1)}, u32[]{:S(2)}) copy-start(bf16[641,1282]{1,0:T(8,128)(2,1)} %param.40) | copy-start | bytes 4930576
  9.2 1186.1 %copy-start.85 = (s32[96]{0:T(128)}, s32[96]{0:T(128)S(1)}, u32[]{:S(2)}) copy-start(s32[96]{0:T(128)S(1)} %get-tuple-element.691) | copy-start | bytes 1156
  53.3 118.9 %all-to-all-start = ((bf16[1,12,96,1298]{3,1,0,2:T(8,128)(2,1)}), bf16[1,12,96,1298]{3,1,0,2:T(8,128)(2,1)}, u32[]{:S(2)}, u32[]{:S(2)}) async-start(bf16[1,12,96,1298]{3,1,0,2:T(8,128)(2,1)} %reshape.2912), calls=%async_computation | async-start | bytes 8650752 | tf_op jit(solution)/shard_map/all_to_all | solution.py:346
  81.5 33.6 copy-start.23
  81.7 33.3 copy-start.90
  172.2 286.9 %all-to-all-start.2 = ((bf16[1,23,192,1298]{3,1,0,2:T(8,128)(2,1)}), bf16[1,23,192,1298]{3,1,0,2:T(8,128)(2,1)}, u32[]{:S(2)}, u32[]{:S(2)}) async-start(bf16[1,23,192,1298]{3,1,0,2:T(8,128)(2,1)} %reshape.2913), calls=%async_computation.2 | async-start | bytes 25952256 | tf_op jit(solution)/shard_map/all_to_all | solution.py:347
  178.2 241.7 %copy-start.105 = (s32[184]{0:T(256)S(1)}, s32[184]{0:T(256)}, u32[]{:S(2)}) copy-start(s32[184]{0:T(256)} %param.33) | copy-start | bytes 2212
  459.2 635.2 %all-to-all-start.1 = ((bf16[1,96,12,1298]{3,2,0,1:T(8,128)(2,1)}), bf16[1,96,12,1298]{3,2,0,1:T(8,128)(2,1)}, u32[]{:S(2)}, u32[]{:S(2)}) async-start(bf16[1,96,12,1298]{3,2,0,1:T(8,128)(2,1)} %copy.469), calls=%async_computation.1 | async-start | bytes 8650752 | tf_op jit(solution)/shard_map/all_to_all | solution.py:353
  1034.0 44.9 copy-start.15
  1094.3 220.9 %all-to-all-start.3 = ((bf16[1,96,12,2,1298]{4,3,2,0,1:T(2,128)(2,1)}), bf16[1,96,12,2,1298]{4,3,2,0,1:T(2,128)(2,1)}, u32[]{:S(2)}, u32[]{:S(2)}) async-start(bf16[1,96,12,2,1298]{4,3,2,0,1:T(2,128)(2,1)} %copy.488), calls=%async_computation.3 | async-start | bytes 12976128 | tf_op jit(solution)/shard_map/all_to_all | solution.py:354
  1100.1 95.2 %copy-start.108 = (s32[96]{0:T(128)S(1)}, s32[96]{0:T(128)}, u32[]{:S(2)}) copy-start(s32[96]{0:T(128)} %get-tuple-element.684) | copy-start | bytes 1156
  1100.1 95.3 %copy-start.109 = (s32[96]{0:T(128)S(1)}, s32[96]{0:T(128)}, u32[]{:S(2)}) copy-start(s32[96]{0:T(128)} %get-tuple-element.685) | copy-start | bytes 1156
  1100.1 96.6 %copy-start.111 = (s32[2]{0:T(128)S(1)}, s32[2]{0:T(128)}, u32[]{:S(2)}) copy-start(s32[2]{0:T(128)} %constant.527) | copy-start | bytes 28
  1100.1 96.9 %copy-start.110 = (s32[2]{0:T(128)S(1)}, s32[2]{0:T(128)}, u32[]{:S(2)}) copy-start(s32[2]{0:T(128)} %constant.524) | copy-start | bytes 28
  1214.6 259.7 %copy-start.31 = (pred[24,180]{1,0:T(8,128)(4,1)}, pred[24,180]{1,0:T(8,128)(4,1)S(1)}, u32[]{:S(2)}) copy-start(pred[24,180]{1,0:T(8,128)(4,1)S(1)} %broadcast_in_dim.365) | copy-start | bytes 12964
  1214.8 128.2 %copy-start.2 = (s32[4320]{0:T(1024)}, s32[4320]{0:T(1024)S(1)}, u32[]{:S(2)}) copy-start(s32[4320]{0:T(1024)S(1)} %reshape.2783) | copy-start | bytes 51844
  1214.8 30.8 copy-start.113
  1244.9 88.5 %copy-start.98 = (bf16[290]{0:T(512)(128)(2,1)}, bf16[290]{0:T(512)(128)(2,1)S(1)}, u32[]{:S(2)}) copy-start(bf16[290]{0:T(512)(128)(2,1)S(1)} %pad.25.clone) | copy-start | bytes 1744
  1678.2 109.6 %all-to-all-start.4 = ((bf16[1,12,96,1282]{3,1,0,2:T(8,128)(2,1)}), bf16[1,12,96,1282]{3,1,0,2:T(8,128)(2,1)}, u32[]{:S(2)}, u32[]{:S(2)}) async-start(bf16[1,12,96,1282]{3,1,0,2:T(8,128)(2,1)} %copy.492), calls=%async_computation.4 | async-start | bytes 8650752 | tf_op jit(solution)/shard_map/all_to_all | solution.py:361
  1709.8 83.1 %copy-start.17 = (f32[90,12,96]{2,1,0:T(8,128)S(1)}, f32[90,12,96]{2,1,0:T(8,128)}, u32[]{:S(2)}) copy-start(f32[90,12,96]{2,1,0:T(8,128)} %get-tuple-element.621) | copy-start | bytes 1244164
  1709.8 83.2 %copy-start.22 = (s32[2048]{0:T(1024)S(1)}, s32[2048]{0:T(1024)}, u32[]{:S(2)}) copy-start(s32[2048]{0:T(1024)} %copy-done.21) | copy-start | bytes 24580
  1716.8 81.3 %copy-start.82 = (s32[96]{0:T(128)S(1)}, s32[96]{0:T(128)}, u32[]{:S(2)}) copy-start(s32[96]{0:T(128)} %param.34) | copy-start | bytes 1156
  1716.8 81.3 %copy-start.91 = (s32[192]{0:T(256)S(1)}, s32[192]{0:T(256)}, u32[]{:S(2)}) copy-start(s32[192]{0:T(256)} %copy-done.90) | copy-start | bytes 2308
  1716.8 81.3 %copy-start.107 = (pred[192]{0:T(512)(128)(4,1)S(1)}, pred[192]{0:T(512)(128)(4,1)}, u32[]{:S(2)}) copy-start(pred[192]{0:T(512)(128)(4,1)} %copy-done.106) | copy-start | bytes 580
  1716.8 81.3 %copy-start.86 = (s32[96]{0:T(128)S(1)}, s32[96]{0:T(128)}, u32[]{:S(2)}) copy-start(s32[96]{0:T(128)} %copy-done.85) | copy-start | bytes 1156
  1787.8 146.7 %all-to-all-start.6 = ((bf16[1,12,96,2,1282]{4,3,1,0,2:T(2,128)(2,1)}), bf16[1,12,96,2,1282]{4,3,1,0,2:T(2,128)(2,1)}, u32[]{:S(2)}, u32[]{:S(2)}) async-start(bf16[1,12,96,2,1282]{4,3,1,0,2:T(2,128)(2,1)} %copy.503), calls=%async_computation.6 | async-start | bytes 12976128 | tf_op jit(solution)/shard_map/all_to_all | solution.py:362
  1814.5 124.7 %copy-start.18 = (bf16[96,12,1,184]{0,3,1,2:T(8,128)(2,1)S(1)}, bf16[96,12,1,184]{0,3,1,2:T(8,128)(2,1)}, u32[]{:S(2)}) copy-start(bf16[96,12,1,184]{0,3,1,2:T(8,128)(2,1)} %get-tuple-element.652) | copy-start | bytes 1271812
  1818.2 121.0 %copy-start.19 = (bf16[96,12,1,184]{0,3,1,2:T(8,128)(2,1)S(1)}, bf16[96,12,1,184]{0,3,1,2:T(8,128)(2,1)}, u32[]{:S(2)}) copy-start(bf16[96,12,1,184]{0,3,1,2:T(8,128)(2,1)} %get-tuple-element.653) | copy-start | bytes 1271812
  1934.4 100.0 %all-to-all-start.5 = ((bf16[1,96,12,1282]{3,2,0,1:T(8,128)(2,1)}), bf16[1,96,12,1282]{3,2,0,1:T(8,128)(2,1)}, u32[]{:S(2)}, u32[]{:S(2)}) async-start(bf16[1,96,12,1282]{3,2,0,1:T(8,128)(2,1)} %copy.498), calls=%async_computation.5 | async-start | bytes 8650752 | tf_op jit(solution)/shard_map/all_to_all | solution.py:368
  1951.7 38.5 copy-start.72
  2079.0 273.9 %all-to-all-start.7 = ((bf16[1,184,24,1282]{3,2,0,1:T(8,128)(2,1)}), bf16[1,184,24,1282]{3,2,0,1:T(8,128)(2,1)}, u32[]{:S(2)}, u32[]{:S(2)}) async-start(bf16[1,184,24,1282]{3,2,0,1:T(8,128)(2,1)} %copy.512), calls=%async_computation.7 | async-start | bytes 24870912 | tf_op jit(solution)/shard_map/all_to_all | solution.py:369
  2090.4 71.3 %copy-start.68 = (f32[12,180]{1,0:T(8,128)}, f32[12,180]{1,0:T(8,128)S(1)}, u32[]{:S(2)}) copy-start(f32[12,180]{1,0:T(8,128)S(1)} %broadcast_multiply_fusion.6) | copy-start | bytes 25924
  2091.5 70.2 %copy-start.73 = (f32[12,180]{1,0:T(8,128)}, f32[12,180]{1,0:T(8,128)S(1)}, u32[]{:S(2)}) copy-start(f32[12,180]{1,0:T(8,128)S(1)} %fusion.183) | copy-start | bytes 25924
  2101.0 29.8 copy-start.10
  2101.0 29.8 copy-start.114
  2352.9 406.9 %all-to-all-start.8 = ((bf16[1,12,96,1282]{3,1,0,2:T(8,128)(2,1)}), bf16[1,12,96,1282]{3,1,0,2:T(8,128)(2,1)}, u32[]{:S(2)}, u32[]{:S(2)}) async-start(bf16[1,12,96,1282]{3,1,0,2:T(8,128)(2,1)} %reshape.2915), calls=%async_computation.8 | async-start | bytes 8650752 | tf_op jit(solution)/shard_map/all_to_all | solution.py:435
  2418.7 252.3 %copy-start.43 = (f32[23,360]{1,0:T(8,128)}, f32[23,360]{1,0:T(8,128)S(1)}, u32[]{:S(2)}) copy-start(f32[23,360]{1,0:T(8,128)S(1)} %broadcast_multiply_fusion.4) | copy-start | bytes 99364
  2429.0 242.0 %copy-start.58 = (f32[23,360]{1,0:T(8,128)}, f32[23,360]{1,0:T(8,128)S(1)}, u32[]{:S(2)}) copy-start(f32[23,360]{1,0:T(8,128)S(1)} %fusion.177) | copy-start | bytes 99364
  2476.0 108.2 %copy-start.115 = (bf16[1282,641]{0,1:T(8,128)(2,1)S(1)}, bf16[1282,641]{0,1:T(8,128)(2,1)}, u32[]{:S(2)}) copy-start(bf16[1282,641]{0,1:T(8,128)(2,1)} %param.42) | copy-start | bytes 4930576
  2637.4 33.6 copy-start.48
  2759.8 286.7 %all-to-all-start.10 = ((bf16[1,23,192,1282]{3,1,0,2:T(8,128)(2,1)}), bf16[1,23,192,1282]{3,1,0,2:T(8,128)(2,1)}, u32[]{:S(2)}, u32[]{:S(2)}) async-start(bf16[1,23,192,1282]{3,1,0,2:T(8,128)(2,1)} %reshape.2916), calls=%async_computation.10 | async-start | bytes 25952256 | tf_op jit(solution)/shard_map/all_to_all | solution.py:436
  3046.5 100.2 %all-to-all-start.9 = ((bf16[1,96,12,1282]{3,2,0,1:T(8,128)(2,1)}), bf16[1,96,12,1282]{3,2,0,1:T(8,128)(2,1)}, u32[]{:S(2)}, u32[]{:S(2)}) async-start(bf16[1,96,12,1282]{3,2,0,1:T(8,128)(2,1)} %copy.521), calls=%async_computation.9 | async-start | bytes 8650752 | tf_op jit(solution)/shard_map/all_to_all | solution.py:442
  3146.7 146.7 %all-to-all-start.11 = ((bf16[1,96,12,2,1282]{4,3,2,0,1:T(2,128)(2,1)}), bf16[1,96,12,2,1282]{4,3,2,0,1:T(2,128)(2,1)}, u32[]{:S(2)}, u32[]{:S(2)}) async-start(bf16[1,96,12,2,1282]{4,3,2,0,1:T(2,128)(2,1)} %copy.530), calls=%async_computation.11 | async-start | bytes 12976128 | tf_op jit(solution)/shard_map/all_to_all | solution.py:443
  3641.9 27.1 copy-start.88
  3641.9 27.1 copy-start.97
  3641.9 27.7 copy-start.16
  3641.9 27.7 copy-start.20
  3647.3 116.7 %all-to-all-start.12 = ((bf16[1,12,96,1298]{3,1,0,2:T(8,128)(2,1)}), bf16[1,12,96,1298]{3,1,0,2:T(8,128)(2,1)}, u32[]{:S(2)}, u32[]{:S(2)}) async-start(bf16[1,12,96,1298]{3,1,0,2:T(8,128)(2,1)} %copy.534), calls=%async_computation.12 | async-start | bytes 8650752 | tf_op jit(solution)/shard_map/all_to_all | solution.py:455
  3764.0 169.5 %all-to-all-start.14 = ((bf16[1,12,96,2,1298]{4,3,1,0,2:T(2,128)(2,1)}), bf16[1,12,96,2,1298]{4,3,1,0,2:T(2,128)(2,1)}, u32[]{:S(2)}, u32[]{:S(2)}) async-start(bf16[1,12,96,2,1298]{4,3,1,0,2:T(2,128)(2,1)} %copy.542), calls=%async_computation.14 | async-start | bytes 12976128 | tf_op jit(solution)/shard_map/all_to_all | solution.py:456
  3933.6 303.8 %all-to-all-start.13 = ((bf16[1,96,12,1298]{3,2,0,1:T(8,128)(2,1)}), bf16[1,96,12,1298]{3,2,0,1:T(8,128)(2,1)}, u32[]{:S(2)}, u32[]{:S(2)}) async-start(bf16[1,96,12,1298]{3,2,0,1:T(8,128)(2,1)} %copy.538), calls=%async_computation.13 | async-start | bytes 8650752 | tf_op jit(solution)/shard_map/all_to_all | solution.py:467
  3939.5 1004.4 %all-reduce.12.cloned.1.call-start = ((), (), s32[]{:S(2)}) async-start(), calls=%async_computation.16 | async-start | bytes 94519296
  4237.4 719.0 %all-to-all-start.15 = ((bf16[1,184,24,1298]{3,2,0,1:T(8,128)(2,1)}), bf16[1,184,24,1298]{3,2,0,1:T(8,128)(2,1)}, u32[]{:S(2)}, u32[]{:S(2)}) async-start(bf16[1,184,24,1298]{3,2,0,1:T(8,128)(2,1)} %copy.547), calls=%async_computation.15 | async-start | bytes 24870912 | tf_op jit(solution)/shard_map/all_to_all | solution.py:468
  4244.1 929.1 %all-reduce.14.cloned.1.call-start = ((), (), s32[]{:S(2)}) async-start(), calls=%async_computation.17 | async-start | bytes 14598144 | tf_op jit(solution)/shard_map/psum | solution.py:483
  4275.9 45.9 copy-start.100
  4275.9 45.9 copy-start.101
  4275.9 46.5 copy-start.103
  4276.0 46.5 copy-start.104
  4276.0 47.1 copy-start.89
  4276.0 73.5 %slice-start.8 = ((s8[6635520]{0:T(1024)(128)(4,1)}), s8[4194304]{0:T(1024)(128)(4,1)S(1)}, s32[]{:S(2)}) async-start(s8[6635520]{0:T(1024)(128)(4,1)} %bitcast.580), calls=%async_computation.26 | async-start | bytes 8388608
  5087.0 45.9 copy-start.83
  5087.0 45.9 copy-start.92
  5087.0 45.9 copy-start.93
  5087.0 45.9 copy-start.94
  5087.1 94.3 %copy-start.1 = (bf16[641,1282]{1,0:T(8,128)(2,1)S(1)}, bf16[641,1282]{1,0:T(8,128)(2,1)}, u32[]{:S(2)}) copy-start(bf16[641,1282]{1,0:T(8,128)(2,1)} %param.40) | copy-start | bytes 4930576
  (85 other events, 1192.7 us)
Sparse Core Ops, SparseCore 0:
  4162.7 781.1 all-reduce.11
  4951.3 167.0 all-reduce.13
where the time goes:
time: 5230 us; the launch traced here: 5190 us
  local copies, waits for them, and re-layouts  1840 us (35%)
  waiting for transfers between devices  1360 us (26%)
  other arithmetic  1010 us (19%)
  matrix products  622 us (12%)
  loops' own time  183 us (3%)
  starting transfers between devices  122 us (2%)
    unnamed x3, waiting for transfers between devices  500 us
    gather x9, local copies, waits for them, and re-layouts, gather_rows(): jnp.take(block, picks, axis=1)  469 us
    all_to_all x1, waiting for transfers between devices, shards(): lax.all_to_all(synth_grads[1], 'lat', split_axis=2, concat_axis=1, tiled=...  260 us
    another operation x1, local copies, waits for them, and re-layouts, weight_gradient(): return jnp.stack([real_part, imag_part], axis=1)  191 us
    dynamic_update_slice x270, other arithmetic, legendre(): lax.scan(recur_step, (zero_state, zero_state), jnp.arange(degree_total, d...  189 us
    another operation x2, loops' own time, legendre(): lax.scan(recur_step, (zero_state, zero_state), jnp.arange(degree_total, d...  183 us
    eq x270, other arithmetic, recur_step(): degree == orders[:, None]  176 us
    unnamed x278, local copies, waits for them, and re-layouts  176 us
  transfers between devices with their start and end apart: 18, of which 10 were waited for; matrix products, arithmetic and copies ran while one was open for 51% of the time, Pallas kernels for 0%

commit v1 on v0

v1 whole, which is shorter than its diff:
```python
import functools
import math

import jax
import jax.numpy as jnp
from jax import lax
from jax.experimental import pallas as pl
from jax.experimental.pallas import tpu as pltpu
from jax.sharding import PartitionSpec as P

C = 641
NOISE = 8
WIDE = C + NOISE
LA = 90
LB = 180

TILE = 128
MAIN = C // TILE * TILE
HALF = TILE // 2
LANES = 2 * MAIN + TILE
PADDED = MAIN + TILE

epsilon = 1e-05
noise_scale = 1.0 / 262144.0
bf16 = jnp.bfloat16
f32 = jnp.float32
VMEM_LIMIT = 60 * 2**20


def call(body, name, flops, moved, **options):
    scratch = options.pop("scratch_shapes", [])
    return pl.pallas_call(
        body,
        scratch_shapes=scratch,
        compiler_params=pltpu.CompilerParams(vmem_limit_bytes=VMEM_LIMIT),
        cost_estimate=pl.CostEstimate(flops=int(flops), bytes_accessed=int(moved), transcendentals=0),
        name=name,
        **options,
    )


def dot(left, right, left_dim, right_dim):
    return lax.dot_general(
        left, right, (((left_dim,), (right_dim,)), ((), ())), preferred_element_type=f32
    )


def join_parts(real, imag, count):
    tail = real[:, MAIN:] + pltpu.roll(imag[:, MAIN:], HALF, 1)
    return jnp.concatenate([real[:, :MAIN], imag[:, :MAIN], tail], axis=1)


def join_narrow(real, imag):
    lane = lax.broadcasted_iota(jnp.int32, (real.shape[0], TILE), 1)
    tail = jnp.where(
        lane == 0, real[:, MAIN:C], jnp.where(lane == HALF, imag[:, MAIN:C], 0.0)
    )
    return jnp.concatenate([real[:, :MAIN], imag[:, :MAIN], tail], axis=1)


def split_parts(joined, count):
    tail = joined[:, 2 * MAIN :]
    real = jnp.concatenate([joined[:, :MAIN], tail], axis=1)[:, :count]
    imag = jnp.concatenate(
        [joined[:, MAIN : 2 * MAIN], pltpu.roll(tail, HALF, 1)], axis=1
    )[:, :count]
    return real, imag


def flat(block):
    return block.astype(f32).reshape(-1, block.shape[-1])


def norm_stats(values):
    centered = values - jnp.mean(values, axis=0, keepdims=True)
    variance = jnp.mean(centered * centered, axis=0, keepdims=True)
    scale = lax.rsqrt(variance + epsilon)
    return centered * scale, scale


def spread_body(state, noise, gain, bias, table, out, held):
    @pl.when(pl.program_id(0) == 0)
    def _():
        held[...] = jnp.zeros_like(held)

    xhat, unused = norm_stats(state[0][:, 0, :])
    held[:C] = xhat * gain[...] + bias[...]
    held[C:WIDE] = ((noise[0].astype(f32) + 0.5) * noise_scale - 0.5) * math.sqrt(12.0)
    result = dot(table[...], held[...].astype(bf16), 1, 1)
    rows = result.shape[0] // 2
    joined = join_parts(result[:rows], result[rows:], WIDE)
    out[:, 0] = joined.reshape(out.shape[0], out.shape[2], LANES).astype(bf16)


def spread(state, noise, gain, bias, table, n_lat, first, count):
    points = state.shape[3]
    subs = table.shape[0] // (2 * n_lat)
    const = lambda r: (0, 0)
    return call(
        spread_body,
        "norm_and_dft",
        2 * count * table.shape[0] * points * PADDED,
        count * (C * points * 4 + n_lat * subs * LANES * 2),
        grid=(count,),
        in_specs=[
            pl.BlockSpec((1, C, 1, points), lambda r: (r + first, 0, 0, 0)),
            pl.BlockSpec((1, NOISE, points), lambda r: (r + first, 0, 0)),
            pl.BlockSpec((C, 1), const),
            pl.BlockSpec((C, 1), const),
            pl.BlockSpec(table.shape, const),
        ],
        out_specs=pl.BlockSpec((n_lat, 1, subs, LANES), lambda r: (0, r, 0, 0)),
        out_shape=jax.ShapeDtypeStruct((n_lat, count, subs, LANES), bf16),
        scratch_shapes=[pltpu.VMEM((PADDED, points), f32)],
    )(state, noise, gain, bias, table)


def legendre_body(total, pairs, order_a, order_b, diag_a, diag_b, cosine, classes, *refs):
    two = order_b is not None
    outs, (held_a, held_b) = refs[: 3 if two else 1], (refs[3:] if two else (refs[1], None))

    def advance(degree, order, diagonal, previous, earlier):
        real = degree.astype(f32)
        grow = jnp.sqrt(
            (4.0 * real * real - 1.0) / jnp.maximum(real * real - order * order, 1.0)
        )
        damp = jnp.sqrt(
            jnp.maximum((real - 1.0) * (real - 1.0) - order * order, 0.0)
            / jnp.maximum(4.0 * (real - 1.0) * (real - 1.0) - 1.0, 1.0)
        )
        grown = grow * (cosine[...] * previous - damp * earlier)
        return jnp.where(real == order, diagonal, jnp.where(real > order, grown, 0.0))

    def step(degree, carry):
        now_a = advance(degree, order_a[...], diag_a[...], carry[0], carry[1])
        held_a[degree] = now_a
        if not two:
            return (now_a, carry[0])
        now_b = advance(degree, order_b[...], diag_b[...], carry[2], carry[3])
        held_b[degree] = now_b
        return (now_a, carry[0], now_b, carry[2])

    zero = diag_a[...] * 0.0
    lax.fori_loop(0, total, step, (zero,) * (4 if two else 2))

    def pick(slot, unused):
        pair = pairs[slot]
        safe = jnp.maximum(pair, 0)
        live = jnp.where(pair >= 0, 1.0, 0.0)
        low = classes[...] <= pair
        near = held_a[safe] * live
        if two:
            far = held_a[LB - 1 - safe] * live
            outs[0][slot] = jnp.where(low, near, far)
            outs[1][slot] = jnp.where(low, far, 0.0)
            outs[2][slot] = jnp.where(low, 0.0, held_b[LB - 1 - safe] * live)
        else:
            outs[0][slot] = jnp.where(low, near, 0.0)
        return unused

    lax.fori_loop(0, pairs.shape[0], pick, 0)


def diagonal_values(orders, live, sines):
    order_real = orders.astype(f32)[:, None]
    log_start = 0.5 * jnp.log((2.0 * order_real + 1.0) / (4.0 * math.pi))
    log_start = log_start + 0.5 * (
        lax.lgamma(2.0 * order_real + 1.0)
        - 2.0 * order_real * math.log(2.0)
        - 2.0 * lax.lgamma(order_real + 1.0)
    )
    diagonal = jnp.exp(log_start + order_real * jnp.log(sines)[None, :])
    return jnp.where(live[:, None], diagonal, 0.0)


def legendre_tables(row_table, pair_slots, classes, total, two):
    slots, rows, wide = pair_slots.shape[0], row_table.shape[0], classes.shape[0]
    occupied = (row_table >= 0).astype(f32)
    colatitude = math.pi * (jnp.maximum(row_table, 0).astype(f32) + 0.5) / total
    sines = jnp.sin(colatitude)
    cosine = jnp.broadcast_to(jnp.cos(colatitude)[None, :], (wide, rows))
    spread_out = lambda v: jnp.broadcast_to(v.astype(f32)[:, None], (wide, rows))
    top = LB // 2 if two else LA - 1
    order_a = jnp.where(classes <= top, classes, 0)
    diag_a = diagonal_values(order_a, classes <= top, sines)
    live_b = (classes >= 1) & (classes <= LB // 2 - 1)
    order_b = jnp.where(live_b, LB - classes, 0)
    diag_b = diagonal_values(order_b, live_b, sines)
    class_wide = jnp.broadcast_to(classes[:, None], (wide, rows))
    if two:
        arrays = [spread_out(order_a), spread_out(order_b), diag_a, diag_b, cosine, class_wide]
        body = functools.partial(legendre_body, total)
    else:
        arrays = [spread_out(order_a), diag_a, cosine, class_wide]

        def body(pairs, order, diagonal, cosines, class_ref, *refs):
            legendre_body(total, pairs, order, None, diagonal, None, cosines, class_ref, *refs)

    shape = jax.ShapeDtypeStruct((slots, wide, rows), f32)
    count = 3 if two else 1
    tables = call(
        body,
        "legendre_tables",
        total * wide * rows * 40,
        count * slots * wide * rows * 4,
        in_specs=[pl.BlockSpec(memory_space=pltpu.SMEM)]
        + [pl.BlockSpec(memory_space=pltpu.VMEM)] * len(arrays),
        out_specs=[pl.BlockSpec(memory_space=pltpu.VMEM)] * count,
        out_shape=[shape] * count,
        scratch_shapes=[pltpu.VMEM((total, wide, rows), f32)] * (2 if two else 1),
    )(pair_slots, *arrays)
    plain = [table * occupied for table in tables]
    weight = sines * occupied * (2.0 * math.pi * math.pi / total)
    return plain, [table * weight for table in plain]


def by_class(table, n_lat, pair_dev):
    split = table.reshape(n_lat, pair_dev // 2, 2, table.shape[1], table.shape[2])
    moved = split.transpose(3, 2, 0, 1, 4)[:pair_dev]
    return moved.reshape(pair_dev, n_lat * pair_dev, table.shape[2]).astype(bf16)


def to_degrees_fine_body(pair_dev, n_chunks, *refs):
    chunks, (table_a, table_b, out) = refs[:n_chunks], refs[n_chunks : n_chunks + 3]
    held, result = refs[n_chunks + 3 : -1], refs[-1]
    n_lat, unused, subs, lanes = out.shape
    half = n_lat * pair_dev // 2
    for chunk, keep in zip(chunks, held):
        keep[...] = flat(chunk[...])
    if subs != 2 * pair_dev:
        result[...] = jnp.zeros_like(result)

    def order_rows(sub):
        parts = [
            keep[pl.ds(sub, keep.shape[0] // subs, stride=subs), :] for keep in held
        ]
        return (parts[0] if len(parts) == 1 else jnp.concatenate(parts, axis=0)).astype(bf16)

    for index in range(pair_dev):
        from_a = dot(table_a[index], order_rows(2 * index), 1, 0)
        from_b = dot(table_b[index], order_rows(2 * index + 1), 1, 0)
        first, second = from_a[: 2 * half], from_a[2 * half :] + from_b
        for odd in range(2):
            rows = slice(odd * half, (odd + 1) * half)
            start = odd * subs + index
            result[pl.ds(start + (1 - odd) * pair_dev, half, stride=2 * subs), :] = first[rows]
            result[pl.ds(start + odd * pair_dev, half, stride=2 * subs), :] = second[rows]
    out[...] = result[...].reshape(out.shape).astype(bf16)


def to_degrees_coarse_body(pair_dev, chunk, table, out, held, result):
    n_lat, unused, subs, lanes = out.shape
    half = n_lat * pair_dev // 2
    held[...] = flat(chunk[...])
    if subs != 2 * pair_dev:
        result[...] = jnp.zeros_like(result)
    rows = held.shape[0] // subs
    for index in range(pair_dev):
        taken = jnp.concatenate(
            [held[pl.ds(odd * pair_dev + index, rows, stride=subs), :] for odd in range(2)], axis=0
        ).astype(bf16)
        made = dot(table[index], taken, 1, 0)
        for odd in range(2):
            result[pl.ds(odd * pair_dev + index, half, stride=subs), :] = made[
                odd * half : (odd + 1) * half
            ]
    out[...] = result[...].reshape(out.shape).astype(bf16)


def to_orders_fine_body(pair_dev, n_chunks, chunk, table_a, table_b, *refs):
    outs, (held, *results) = refs[:n_chunks], refs[n_chunks:]
    n_lat, unused, subs, lanes = chunk.shape
    half = n_lat * pair_dev // 2
    held[...] = flat(chunk[...])
    if subs != 2 * pair_dev:
        for result in results:
            result[...] = jnp.zeros_like(result)
    for index in range(pair_dev):
        first, second = [], []
        for odd in range(2):
            start = odd * subs + index
            first.append(held[pl.ds(start + (1 - odd) * pair_dev, half, stride=2 * subs), :])
            second.append(held[pl.ds(start + odd * pair_dev, half, stride=2 * subs), :])
        second = jnp.concatenate(second, axis=0)
        both = jnp.concatenate(first + [second], axis=0).astype(bf16)
        made = (dot(table_a[index], both, 1, 0), dot(table_b[index], second.astype(bf16), 1, 0))
        for member in range(2):
            begin = 0
            for result in results:
                rows = result.shape[0] // subs
                result[pl.ds(2 * index + member, rows, stride=subs), :] = made[member][
                    begin : begin + rows
                ]
                begin += rows
    for out, result in zip(outs, results):
        out[...] = result[...].reshape(out.shape).astype(bf16)


def to_orders_coarse_body(pair_dev, chunk, table, out, held, result):
    n_lat, unused, subs, lanes = chunk.shape
    half = n_lat * pair_dev // 2
    held[...] = flat(chunk[...])
    if subs != 2 * pair_dev:
        result[...] = jnp.zeros_like(result)
    rows = result.shape[0] // subs
    for index in range(pair_dev):
        taken = jnp.concatenate(
            [held[pl.ds(odd * pair_dev + index, half, stride=subs), :] for odd in range(2)], axis=0
        ).astype(bf16)
        made = dot(table[index], taken, 1, 0)
        for odd in range(2):
            result[pl.ds(odd * pair_dev + index, rows, stride=subs), :] = made[
                odd * rows : (odd + 1) * rows
            ]
    out[...] = result[...].reshape(out.shape).astype(bf16)


def lane_call(body, name, inputs, tables, outs):
    tiled = lambda shape: pl.BlockSpec(tuple(shape[:3]) + (TILE,), lambda t: (0, 0, 0, t))
    whole = lambda shape: pl.BlockSpec(shape, lambda t: (0, 0, 0))
    held = lambda shape: pltpu.VMEM((shape[0] * shape[1] * shape[2], TILE), f32)
    moved = sum(2 * math.prod(s) for s in [a.shape for a in inputs] + outs)
    flops = sum(2 * math.prod(t.shape) for t in tables) * LANES
    made = call(
        body,
        name,
        flops,
        moved,
        grid=(LANES // TILE,),
        in_specs=[tiled(a.shape) for a in inputs] + [whole(t.shape) for t in tables],
        out_specs=[tiled(shape) for shape in outs],
        out_shape=[jax.ShapeDtypeStruct(tuple(shape), bf16) for shape in outs],
        scratch_shapes=[held(a.shape) for a in inputs] + [held(shape) for shape in outs],
    )(*inputs, *tables)
    return made


def mix_body(pair_dev, backward, pairs, fine, coarse, weight, fine_out, coarse_out, members):
    n_lat, unused, subs, lanes = fine.shape
    rows = n_lat * subs
    row = lax.broadcasted_iota(jnp.int32, (rows, 1), 0)
    sub = row % subs
    group = sub // pair_dev
    order_class = row // subs * pair_dev + sub % pair_dev
    coarse_rows = flat(coarse[:, 0])
    count = C if backward else WIDE

    def apply(values, slot):
        real, imag = split_parts(values, count)
        stacked = jnp.concatenate([real, imag], axis=0).astype(bf16)
        by_real = dot(stacked, weight[slot, 0], 1, 0 if backward else 1)
        by_imag = dot(stacked, weight[slot, 1], 1, 0 if backward else 1)
        if backward:
            out_real = by_real[:rows] + by_imag[rows:]
            out_imag = by_real[rows:] - by_imag[:rows]
        else:
            out_real = by_real[:rows] - by_imag[rows:]
            out_imag = by_imag[:rows] + by_real[rows:]
        return join_narrow(out_real[:, :C], out_imag[:, :C])

    coarse_made = jnp.zeros((rows, lanes), f32)
    for odd in range(2):
        pair = pairs[2 * pl.program_id(0) + odd]
        own = group == odd
        low = order_class <= pair
        fine_rows = flat(fine[:, odd])
        lower = jnp.where(own, coarse_rows, jnp.where(low, fine_rows, 0.0))
        upper = jnp.where(own | ~low, fine_rows, 0.0)
        members[2 * odd] = lower.reshape(n_lat, subs, lanes).astype(bf16)
        members[2 * odd + 1] = upper.reshape(n_lat, subs, lanes).astype(bf16)
        from_lower = apply(lower, 2 * odd)
        from_upper = apply(upper, 2 * odd + 1)
        made = jnp.where(own, from_upper, from_lower + from_upper)
        fine_out[:, odd] = made.reshape(n_lat, subs, lanes).astype(bf16)
        coarse_made = jnp.where(own, from_lower, coarse_made)
    coarse_out[:, 0] = coarse_made.reshape(n_lat, subs, lanes).astype(bf16)


def mix(fine, coarse, weight, local_pairs, backward):
    n_lat, pair_dev, subs, lanes = fine.shape
    fine_spec = pl.BlockSpec((n_lat, 2, subs, lanes), lambda k, pairs: (0, k, 0, 0))
    coarse_spec = pl.BlockSpec((n_lat, 1, subs, lanes), lambda k, pairs: (0, k, 0, 0))
    return call(
        functools.partial(mix_body, pair_dev, backward),
        "mix_back" if backward else "mix",
        2 * pair_dev * n_lat * subs * 8 * PADDED * PADDED,
        2 * weight.size + 12 * fine.size,
        grid_spec=pltpu.PrefetchScalarGridSpec(
            num_scalar_prefetch=1,
            grid=(pair_dev // 2,),
            in_specs=[
                fine_spec,
                coarse_spec,
                pl.BlockSpec((4,) + weight.shape[1:], lambda k, pairs: (k, 0, 0, 0)),
            ],
            out_specs=[
                fine_spec,
                coarse_spec,
                pl.BlockSpec((4, n_lat, subs, lanes), lambda k, pairs: (k, 0, 0, 0)),
            ],
        ),
        out_shape=[
            jax.ShapeDtypeStruct(fine.shape, bf16),
            jax.ShapeDtypeStruct(coarse.shape, bf16),
            jax.ShapeDtypeStruct((2 * pair_dev, n_lat, subs, lanes), bf16),
        ],
    )(local_pairs, fine, coarse, weight)


def mix_grad_body(n_parts, *refs):
    values, grads, out = refs[:n_parts], refs[n_parts : 2 * n_parts], refs[2 * n_parts]
    gather = lambda parts: jnp.concatenate([flat(part[0]) for part in parts], axis=0)
    value_real, value_imag = [v.astype(bf16) for v in split_parts(gather(values), WIDE)]
    grad_real, grad_imag = [v.astype(bf16) for v in split_parts(gather(grads), C)]
    out[0, 0] = dot(grad_real, value_real, 0, 0) + dot(grad_imag, value_imag, 0, 0)
    out[0, 1] = dot(grad_imag, value_real, 0, 0) - dot(grad_real, value_imag, 0, 0)


def mix_gradient(values, grads):
    slots = values[0].shape[0]
    shape = values[0].shape[1:]
    spec = pl.BlockSpec((1,) + shape, lambda k: (k, 0, 0, 0))
    rows = len(values) * math.prod(shape[:2])
    return call(
        functools.partial(mix_grad_body, len(values)),
        "mix_gradient",
        8 * slots * rows * C * WIDE,
        slots * (4 * rows * LANES + 8 * C * WIDE),
        grid=(slots,),
        in_specs=[spec] * (2 * len(values)),
        out_specs=pl.BlockSpec((1, 2, C, WIDE), lambda k: (k, 0, 0, 0)),
        out_shape=jax.ShapeDtypeStruct((slots, 2, C, WIDE), f32),
    )(*values, *grads)


def pixel_body(
    synth, state, cotangent, table, gain, bias, up, up_turned, up_bias, down, down_turned,
    down_bias, out, middle_grad, synth_grad, up_grad, down_grad, wide_sums, narrow_sums, held,
    wide_held, narrow_held,
):
    step = pl.program_id(0)

    @pl.when(step == 0)
    def _():
        held[...] = jnp.zeros_like(held)
        up_grad[...] = jnp.zeros_like(up_grad)
        down_grad[...] = jnp.zeros_like(down_grad)
        wide_held[...] = jnp.zeros_like(wide_held)
        narrow_held[...] = jnp.zeros_like(narrow_held)

    real, imag = split_parts(flat(synth[:, 0]), C)
    stacked = jnp.concatenate([real, imag], axis=0).astype(bf16)
    middle = state[0][:, 0, :] + dot(stacked, table[...], 0, 0)
    xhat, scale = norm_stats(middle)
    normed_low = (xhat * gain[...] + bias[...]).astype(bf16)
    pre_act = dot(up_turned[...], normed_low, 1, 0) + up_bias[...]
    share = 0.5 * (1.0 + lax.erf(pre_act * math.sqrt(0.5)))
    density = jnp.exp(-0.5 * pre_act * pre_act) * (1.0 / math.sqrt(2.0 * math.pi))
    hidden_low = (pre_act * share).astype(bf16)
    slope = share + pre_act * density
    out[0] = (middle + dot(down_turned[...], hidden_low, 1, 0) + down_bias[...])[:, None, :]
    grad = cotangent[0][:, 0, :]
    grad_low = grad.astype(bf16)
    pre_grad = dot(down[...], grad_low, 1, 0) * slope
    pre_low = pre_grad.astype(bf16)
    wide_held[...] += pre_grad
    down_grad[...] += dot(grad_low, hidden_low, 1, 1)
    up_grad[...] += dot(normed_low, pre_low, 1, 1)
    normed_grad = dot(up[...], pre_low, 1, 0)
    narrow_held[0] += normed_grad * xhat
    narrow_held[1] += normed_grad
    narrow_held[2] += grad
    scaled = normed_grad * gain[...]
    total = grad + scale * (
        scaled
        - jnp.mean(scaled, axis=0, keepdims=True)
        - xhat * jnp.mean(scaled * xhat, axis=0, keepdims=True)
    )
    middle_grad[0] = total
    held[:C] = total
    result = dot(table[...], held[...].astype(bf16), 1, 1)
    rows = result.shape[0] // 2
    joined = join_parts(result[:rows], result[rows:], C)
    synth_grad[:, 0] = joined.reshape(synth_grad.shape[0], synth_grad.shape[2], LANES).astype(bf16)

    @pl.when(step == pl.num_programs(0) - 1)
    def _():
        wide_sums[...] = jnp.sum(wide_held[...], axis=1, keepdims=True)
        narrow_sums[...] = jnp.sum(narrow_held[...], axis=2, keepdims=True)


def pixels(synth, state, cotangent, table, params, first):
    n_lat, count, subs, lanes = synth.shape
    points = state.shape[3]
    hidden = params[2].shape[1]
    row_spec = pl.BlockSpec((1, C, 1, points), lambda r: (r + first, 0, 0, 0))
    const = lambda array: pl.BlockSpec(array.shape, lambda r: (0,) * array.ndim)
    row_out = lambda shape: pl.BlockSpec((1,) + shape, lambda r: (r,) + (0,) * len(shape))
    wave = pl.BlockSpec((n_lat, 1, subs, lanes), lambda r: (0, r, 0, 0))
    whole = lambda shape: pl.BlockSpec(shape, lambda r: (0,) * len(shape))
    shaped = lambda shape, kind=f32: jax.ShapeDtypeStruct(shape, kind)
    return call(
        pixel_body,
        "feed_forward",
        2 * count * points * (6 * C * hidden + 2 * table.shape[0] * PADDED),
        count * (4 * C * points * 4 + 4 * n_lat * subs * lanes),
        grid=(count,),
        in_specs=[wave, row_spec, row_spec, const(table)] + [const(p) for p in params],
        out_specs=[
            row_out((C, 1, points)),
            row_out((C, points)),
            wave,
            whole((C, hidden)),
            whole((C, hidden)),
            whole((hidden, 1)),
            whole((3, C, 1)),
        ],
        out_shape=[
            shaped((count, C, 1, points)),
            shaped((count, C, points)),
            shaped(synth.shape, bf16),
            shaped((C, hidden)),
            shaped((C, hidden)),
            shaped((hidden, 1)),
            shaped((3, C, 1)),
        ],
        scratch_shapes=[
            pltpu.VMEM((PADDED, points), f32),
            pltpu.VMEM((hidden, points), f32),
            pltpu.VMEM((3, C, points), f32),
        ],
    )(synth, state, cotangent, table, *params)


def final_body(wave, state, middle_grad, table, gain, out, sums, held):
    step = pl.program_id(0)

    @pl.when(step == 0)
    def _():
        held[...] = jnp.zeros_like(held)

    real, imag = split_parts(flat(wave[:, 0]), C)
    stacked = jnp.concatenate([real, imag], axis=0).astype(bf16)
    spread_grad = dot(stacked, table[...], 0, 0)
    xhat, scale = norm_stats(state[0][:, 0, :])
    held[0] += spread_grad * xhat
    held[1] += spread_grad
    scaled = spread_grad * gain[...]
    out[0] = (
        middle_grad[0]
        + scale
        * (
            scaled
            - jnp.mean(scaled, axis=0, keepdims=True)
            - xhat * jnp.mean(scaled * xhat, axis=0, keepdims=True)
        )
    )[:, None, :]

    @pl.when(step == pl.num_programs(0) - 1)
    def _():
        sums[...] = jnp.sum(held[...], axis=2, keepdims=True)


def finish(wave, state, middle_grad, table, gain, first):
    n_lat, count, subs, lanes = wave.shape
    points = state.shape[3]
    return call(
        final_body,
        "first_norm_back",
        2 * count * points * table.shape[0] * PADDED,
        count * (3 * C * points * 4 + 2 * n_lat * subs * lanes),
        grid=(count,),
        in_specs=[
            pl.BlockSpec((n_lat, 1, subs, lanes), lambda r: (0, r, 0, 0)),
            pl.BlockSpec((1, C, 1, points), lambda r: (r + first, 0, 0, 0)),
            pl.BlockSpec((1, C, points), lambda r: (r, 0, 0)),
            pl.BlockSpec(table.shape, lambda r: (0, 0)),
            pl.BlockSpec((C, 1), lambda r: (0, 0)),
        ],
        out_specs=[
            pl.BlockSpec((1, C, 1, points), lambda r: (r, 0, 0, 0)),
            pl.BlockSpec((2, C, 1), lambda r: (0, 0, 0)),
        ],
        out_shape=[
            jax.ShapeDtypeStruct((count, C, 1, points), f32),
            jax.ShapeDtypeStruct((2, C, 1), f32),
        ],
        scratch_shapes=[pltpu.VMEM((2, C, points), f32)],
    )(wave, state, middle_grad, table, gain)


def fourier_tables(orders, live, points, lon_count):
    phase = (orders * points % lon_count).astype(f32) * (2.0 * math.pi / lon_count)
    kept = live.astype(f32)
    cosine, sine = jnp.cos(phase) * kept, -jnp.sin(phase) * kept
    doubling = jnp.where(orders == 0, 1.0, 2.0).astype(f32)
    forward = jnp.concatenate([cosine / lon_count, sine / lon_count], axis=0)
    inverse = jnp.concatenate([cosine * doubling, sine * doubling], axis=0)
    return forward.astype(bf16), inverse.astype(bf16)


def order_rows(n_lat, pair_dev, subs):
    index = jnp.arange(n_lat * subs, dtype=jnp.int32)[:, None]
    return index // subs, index % subs


def fine_fourier(n_lat, pair_dev, subs, lon_count):
    device, sub = order_rows(n_lat, pair_dev, subs)
    kind = device * pair_dev + sub // 2
    member = sub % 2
    live = (sub < 2 * pair_dev) & jnp.where(
        member == 0, kind <= LB // 2, (kind >= 1) & (kind <= LB // 2 - 1)
    )
    orders = jnp.where(live, jnp.where(member == 0, kind, LB - kind), 0)
    points = jnp.arange(lon_count, dtype=jnp.int32)[None, :]
    return fourier_tables(orders, live, points, lon_count)


def coarse_fourier(n_lat, pair_dev, subs, lon_count):
    device, sub = order_rows(n_lat, pair_dev, subs)
    order = device * pair_dev + sub % pair_dev
    points = jnp.arange(2 * lon_count, dtype=jnp.int32)[None, :]
    live = (sub < 2 * pair_dev) & (order < LA) & (sub // pair_dev == points // lon_count)
    orders = jnp.where((sub < 2 * pair_dev) & (order < LA), order, 0)
    return fourier_tables(orders, live, points % lon_count, lon_count)


def swap(values):
    return lax.all_to_all(values, "lat", split_axis=0, concat_axis=0, tiled=True)


def share_slots(members, n_chan):
    share = members.shape[0] // n_chan
    rank = lax.axis_index("chan")
    parts = []
    for step in range(n_chan):
        partner = jnp.bitwise_xor(rank, step) if n_chan & (n_chan - 1) == 0 else (rank + step) % n_chan
        block = lax.dynamic_slice_in_dim(members, partner * share, share)
        if step:
            if n_chan & (n_chan - 1) == 0:
                route = [(k, k ^ step) for k in range(n_chan)]
            else:
                route = [(k, (k + step) % n_chan) for k in range(n_chan)]
            block = lax.ppermute(block, "chan", route)
        parts.append(block)
    return parts


def shards(
    n_lat, n_chan, coarse_state, fine_state, coarse_noise, fine_noise, coarse_rows, fine_rows,
    pair_slots, first_gain, first_bias, mix_weight, second_gain, second_bias, up_weight, up_bias,
    down_weight, down_bias, coarse_cotangent, fine_cotangent,
):
    pair_dev = mix_weight.shape[0] // 2
    subs = -(-2 * pair_dev // 8) * 8
    lat_rank = lax.axis_index("lat")
    fine_dev, fine_points = fine_state.shape[1], fine_state.shape[2]
    coarse_dev, coarse_points = coarse_state.shape[1], coarse_state.shape[2]
    coarse_two = coarse_dev // 2
    column = lambda vector: vector[:, None]

    def fine_in(values):
        return values.transpose(1, 3, 0, 2)

    def coarse_in(values):
        paired = values[0].reshape(coarse_two, 2 * coarse_points, values.shape[3])
        return paired.transpose(0, 2, 1)[:, :, None, :]

    def fine_back(values):
        return values.transpose(2, 0, 3, 1)

    def coarse_back(values):
        turned = values[:, :, 0, :].transpose(0, 2, 1)
        return turned.reshape(1, coarse_dev, coarse_points, C)

    coarse_x, fine_x = coarse_in(coarse_state), fine_in(fine_state)
    coarse_g, fine_g = coarse_in(coarse_cotangent), fine_in(fine_cotangent)
    coarse_forward, coarse_inverse = coarse_fourier(n_lat, pair_dev, subs, coarse_points)
    fine_forward, fine_inverse = fine_fourier(n_lat, pair_dev, subs, fine_points)
    gain_one, bias_one = column(first_gain), column(first_bias)

    coarse_four = swap(
        spread(coarse_x, coarse_in(coarse_noise)[:, :, 0, :], gain_one, bias_one, coarse_forward,
               n_lat, 0, coarse_two)
    )
    fine_four = swap(
        spread(fine_x, fine_in(fine_noise)[:, :, 0, :], gain_one, bias_one, fine_forward,
               n_lat, 0, fine_dev)
    )

    wide = -(-pair_dev // 8) * 8
    classes = lat_rank * pair_dev + jnp.arange(wide, dtype=jnp.int32)
    classes = jnp.where(jnp.arange(wide) < pair_dev, classes, LB).astype(jnp.int32)
    coarse_order = coarse_rows.reshape(-1, 2).T.reshape(-1)
    fine_plain, fine_quad = legendre_tables(fine_rows, pair_slots, classes, LB, True)
    coarse_plain, coarse_quad = legendre_tables(coarse_order, pair_slots, classes, LA, False)
    turn = lambda table: by_class(table, n_lat, pair_dev)

    def fine_tables(parts):
        first, near, far = [turn(part) for part in parts]
        table_a = jnp.concatenate([first, near], axis=1)
        return (table_a, far), (table_a.transpose(0, 2, 1), far.transpose(0, 2, 1))

    fine_quad_in, fine_quad_out = fine_tables(fine_quad)
    fine_plain_in, fine_plain_out = fine_tables(fine_plain)
    coarse_quad_in = turn(coarse_quad[0])
    coarse_plain_in = turn(coarse_plain[0])
    coarse_quad_out = coarse_quad_in.transpose(0, 2, 1)
    coarse_plain_out = coarse_plain_in.transpose(0, 2, 1)
    local_pairs = lax.dynamic_slice_in_dim(pair_slots, lat_rank * pair_dev, pair_dev)
    weight = mix_weight.transpose(0, 1, 3, 2)

    fine_degrees = [n_lat, pair_dev, subs, LANES]
    coarse_degrees = [n_lat, pair_dev // 2, subs, LANES]
    fine_waves = [n_lat, fine_dev, subs, LANES]
    coarse_waves = [n_lat, coarse_two, subs, LANES]

    def to_degrees(coarse_chunk, fine_chunks, coarse_table, fine_pair):
        coarse_made = lane_call(
            functools.partial(to_degrees_coarse_body, pair_dev), "rows_to_degrees",
            [coarse_chunk], [coarse_table], [coarse_degrees],
        )[0]
        fine_made = lane_call(
            functools.partial(to_degrees_fine_body, pair_dev, len(fine_chunks)), "rows_to_degrees",
            fine_chunks, list(fine_pair), [fine_degrees],
        )[0]
        return swap(coarse_made), swap(fine_made)

    def to_orders(coarse_chunk, fine_chunk, coarse_table, fine_pair):
        coarse_made = lane_call(
            functools.partial(to_orders_coarse_body, pair_dev), "degrees_to_rows",
            [coarse_chunk], [coarse_table], [coarse_waves],
        )[0]
        fine_made = lane_call(
            functools.partial(to_orders_fine_body, pair_dev, 1), "degrees_to_rows",
            [fine_chunk], list(fine_pair), [fine_waves],
        )[0]
        return swap(coarse_made), swap(fine_made)

    coarse_coef, fine_coef = to_degrees(coarse_four, [fine_four], coarse_quad_in, fine_quad_in)
    fine_mixed, coarse_mixed, members = mix(fine_coef, coarse_coef, weight, local_pairs, False)
    values = share_slots(members, n_chan)
    coarse_synth, fine_synth = to_orders(
        swap(coarse_mixed), swap(fine_mixed), coarse_plain_out, fine_plain_out
    )

    params = [
        column(second_gain), column(second_bias), up_weight, up_weight.T, column(up_bias),
        down_weight, down_weight.T, column(down_bias),
    ]
    coarse_made = pixels(coarse_synth, coarse_x, coarse_g, coarse_inverse, params, 0)
    fine_made = pixels(fine_synth, fine_x, fine_g, fine_inverse, params, 0)
    coarse_sgrad, fine_sgrad = swap(coarse_made[2]), swap(fine_made[2])
    dense = lax.psum(
        tuple(a + b for a, b in zip(coarse_made[3:], fine_made[3:])), ("lat", "chan")
    )

    coarse_dgrad, fine_dgrad = to_degrees(
        coarse_sgrad, [fine_sgrad], coarse_plain_in, fine_plain_in
    )
    fine_cgrad, coarse_cgrad, grad_members = mix(
        fine_dgrad, coarse_dgrad, weight, local_pairs, True
    )
    grads = share_slots(grad_members, n_chan)
    mix_grad = mix_gradient(values, grads).transpose(0, 1, 3, 2)
    coarse_fgrad, fine_fgrad = to_orders(
        swap(coarse_cgrad), swap(fine_cgrad), coarse_quad_out, fine_quad_out
    )
    coarse_end, coarse_sums = finish(
        coarse_fgrad, coarse_x, coarse_made[1], coarse_forward, gain_one, 0
    )
    fine_end, fine_sums = finish(fine_fgrad, fine_x, fine_made[1], fine_forward, gain_one, 0)
    first_sums = lax.psum(coarse_sums + fine_sums, ("lat", "chan"))[:, :, 0]
    up_grad, down_grad, wide_sums, narrow_sums = dense
    return (
        coarse_back(coarse_made[0]),
        fine_back(fine_made[0]),
        coarse_back(coarse_end),
        fine_back(fine_end),
        first_sums[0],
        first_sums[1],
        mix_grad,
        narrow_sums[0, :, 0],
        narrow_sums[1, :, 0],
        up_grad,
        wide_sums[:, 0],
        down_grad.T,
        narrow_sums[2, :, 0],
    )


def solution(mesh):
    pixel = P("chan", "lat", None, None)
    slots = P("lat", None, None, None)
    return jax.shard_map(
        functools.partial(shards, mesh.shape["lat"], mesh.shape["chan"]),
        mesh=mesh,
        in_specs=(pixel,) * 4 + (P(),) * 5 + (slots,) + (P(),) * 6 + (pixel,) * 2,
        out_specs=(pixel,) * 4 + (P(),) * 2 + (P(("lat", "chan"), None, None, None),) + (P(),) * 6,
        check_vma=False,
    )
```

time: 5230 us -> 2890 us (0.55)
  local copies, waits for them, and re-layouts: 1840 us -> 256 us
  other arithmetic: 1010 us -> 65.8 us
  matrix products: 622 us -> 0 us
  Pallas kernels: 0 us -> 617 us
  blocking collectives: 40.2 us -> 360 us
  loops' own time: 183 us -> 0 us
  waiting for transfers between devices: 1360 us -> 1500 us
  starting transfers between devices: 122 us -> 69.3 us
    dot_general x33 -> x0, matrix products: 622 us -> none  [the longest x2 70.6 us: shards(): jnp.einsum('srkc,hc->srkh', cot_low, down_weight, preferred_element_type=...]
    pallas_call x0 -> x19, Pallas kernels: none -> 617 us  [the longest x2 301 us: pixels(): call(pixel_body, 'feed_forward', 2 * count * points * (6 * C * hidden + 2...]
    gather x27 -> x0, local copies, waits for them, and re-layouts: 524 us -> none  [the longest x9 469 us: gather_rows(): jnp.take(block, picks, axis=1)]
    unnamed x3 -> x1, waiting for transfers between devices: 500 us -> 0.02 us
    all_to_all x16 -> x13, waiting for transfers between devices: 861 us -> 1240 us  [swap(): lax.all_to_all(values, 'lat', split_axis=0, concat_axis=0, tiled=True)]
    all_to_all x0 -> x3, blocking collectives: none -> 301 us  [swap(): lax.all_to_all(values, 'lat', split_axis=0, concat_axis=0, tiled=True)]
    another operation x17 -> x6, local copies, waits for them, and re-layouts: 330 us -> 30.1 us  [coarse_in(): paired = values[0].reshape(coarse_two, 2 * coarse_points, values.shape[3])]
    ppermute x0 -> x6, waiting for transfers between devices: none -> 257 us  [share_slots(): block = lax.ppermute(block, 'chan', route)]
  transfers between devices with their start and end apart: 18 -> 20, of which waited for: 10 -> 15; matrix products, arithmetic and copies ran while one was open for 51% -> 9% of each run, Pallas kernels for 0% -> 19%
where the time goes in v1:
time: 2890 us; the launch traced here: 2880 us
  waiting for transfers between devices  1500 us (52%)
  Pallas kernels  617 us (21%)
  blocking collectives  360 us (12%)
  local copies, waits for them, and re-layouts  256 us (9%)
  starting transfers between devices  69.3 us (2%)
  other arithmetic  65.8 us (2%)
    all_to_all x13, waiting for transfers between devices, swap(): lax.all_to_all(values, 'lat', split_axis=0, concat_axis=0, tiled=True)  1240 us
    all_to_all x3, blocking collectives, swap(): lax.all_to_all(values, 'lat', split_axis=0, concat_axis=0, tiled=True)  301 us
    pallas_call x2, Pallas kernels, pixels(): call(pixel_body, 'feed_forward', 2 * count * points * (6 * C * hidden + 2...  301 us
    ppermute x6, waiting for transfers between devices, share_slots(): block = lax.ppermute(block, 'chan', route)  257 us
    unnamed x82, local copies, waits for them, and re-layouts  107 us
    pallas_call x8, Pallas kernels, lane_call(): call(body, name, flops, moved, grid=(LANES // TILE,), in_specs=[tiled(a.s...  102 us
    pallas_call x2, Pallas kernels, mix(): call(functools.partial(mix_body, pair_dev, backward), 'mix_back' if backw...  68.5 us
    all_to_all x13, starting transfers between devices, swap(): lax.all_to_all(values, 'lat', split_axis=0, concat_axis=0, tiled=True)  65.6 us
  transfers between devices with their start and end apart: 20, of which 15 were waited for; matrix products, arithmetic and copies ran while one was open for 9% of the time, Pallas kernels for 19%

profile of v1, /device:TPU:0, one launch (start us, length us, event | category | flops | bytes accessed | tf_op | source)
XLA Modules:
  0.0 2880.6 jit_solution(10727643225742022014)
XLA Ops:
  10.5 20.7 reduce
  31.1 7.2 reshape_squeeze.9
  38.3 7.5 copy.62
  45.8 8.2 broadcast_in_dim.150.state
  57.8 9.8 norm_and_dft.3
  67.6 7.3 all-to-all-start.2
  77.8 31.5 %norm_and_dft.2 = bf16[8,23,24,1408]{3,2,1,0:T(8,128)(2,1)} custom-call(f32[23,641,1,360]{3,2,1,0:T(1,128)} %bitcast.73, s32[23,8,360]{2,1,0:T(8,128)} %bitcast.111, f32[641,1]{1,0:T(8,128)} %broadcast_in_dim.163.gain, f32[641,1]{1,0:T(8,128)} %broadcast_in_dim.164.bias, bf16[384,360]{1,0:T(8,128)(2,1)} %pad_maximum_fusion.1.table), custom_call_target="tpu_custom_call" | custom-call | flops 4883742720 | bytes 33665376 | tf_op jit(solution)/shard_map/norm_and_dft/pallas_call | solution.py:99
  109.3 38.3 %all-to-all-done.2.chunk = bf16[8,6,24,1408]{3,2,1,0:T(8,128)(2,1)S(1)} async-done(((bf16[8,6,24,1408]{3,2,1,0:T(8,128)(2,1)}), bf16[8,6,24,1408]{3,2,1,0:T(8,128)(2,1)S(1)}, u32[]{:S(2)}, u32[]{:S(2)}) %all-to-all-start.2) | async-done | bytes 3244064 | tf_op jit(solution)/shard_map/all_to_all | solution.py:629
  149.3 5.4 all-to-all-start
  158.8 4.9 legendre_tables.3
  166.8 9.1 rows_to_degrees.5
  176.0 247.7 %all-to-all-done.refs_0_ = bf16[8,23,24,1408]{3,2,1,0:T(8,128)(2,1)} async-done(((bf16[8,23,24,1408]{3,2,1,0:T(8,128)(2,1)}), bf16[8,23,24,1408]{3,2,1,0:T(8,128)(2,1)}, u32[]{:S(2)}, u32[]{:S(2)}) %all-to-all-start) | async-done | bytes 12435488 | tf_op jit(solution)/shard_map/all_to_all | solution.py:629
  423.7 4.7 all-to-all-start.3
  431.8 13.2 legendre_tables.2
  465.7 16.4 rows_to_degrees.4
  482.0 18.6 all-to-all-done.3.coarse
  500.6 4.8 all-to-all-start.1
  506.0 32.5 %copy.117 = bf16[24,2,649,641]{2,3,1,0:T(8,128)(2,1)} copy(bf16[24,2,649,641]{2,1,3,0:T(2,128)(2,1)} %param.27) | data formatting | bytes 79873728 | tf_op args[9]
  538.5 108.4 %all-to-all-done.1.fine = bf16[8,12,24,1408]{3,2,1,0:T(8,128)(2,1)} async-done(((bf16[8,12,24,1408]{3,2,1,0:T(8,128)(2,1)}), bf16[8,12,24,1408]{3,2,1,0:T(8,128)(2,1)}, u32[]{:S(2)}, u32[]{:S(2)}) %all-to-all-start.1) | async-done | bytes 6488096 | tf_op jit(solution)/shard_map/all_to_all | solution.py:629
  646.9 34.2 %mix.1 = (bf16[8,12,24,1408]{3,2,1,0:T(8,128)(2,1)}, bf16[8,6,24,1408]{3,2,1,0:T(8,128)(2,1)}, bf16[24,8,24,1408]{3,2,1,0:T(8,128)(2,1)}) custom-call(s32[12]{0:T(128)} %dynamic_slice.27.pairs, bf16[8,12,24,1408]{3,2,1,0:T(8,128)(2,1)} %all-to-all-done.1.fine, bf16[8,6,24,1408]{3,2,1,0:T(8,128)(2,1)} %all-to-all-done.3.coarse, bf16[24,2,641,649]{3,2,1,0:T(8,128)(2,1)} %bitcast.76), custom_call_target="tpu_custom_call" | custom-call | flops 21743271936 | bytes 78865248 | tf_op jit(solution)/shard_map/mix/pallas_call | solution.py:383
  681.1 77.4 %all_to_all.80.chunk = bf16[8,6,24,1408]{3,2,1,0:T(8,128)(2,1)} all-to-all(bf16[8,6,24,1408]{3,2,1,0:T(8,128)(2,1)} %get-tuple-element.43), channel_id=1, replica_groups=mesh['lat'=8,'chan'=4] {'lat'}, dimensions={0} | all-to-all | bytes 6488064 | tf_op jit(solution)/shard_map/all_to_all | solution.py:629
  758.5 5.4 all-to-all-start.6
  765.2 9.1 degrees_to_rows.4
  774.3 130.7 %all-to-all-done.6.chunk = bf16[8,12,24,1408]{3,2,1,0:T(8,128)(2,1)} async-done(((bf16[8,12,24,1408]{3,2,1,0:T(8,128)(2,1)}), bf16[8,12,24,1408]{3,2,1,0:T(8,128)(2,1)}, u32[]{:S(2)}, u32[]{:S(2)}) %all-to-all-start.6) | async-done | bytes 6488096 | tf_op jit(solution)/shard_map/all_to_all | solution.py:629
  914.8 16.3 degrees_to_rows.5
  931.1 50.6 %all-to-all-done.5.synth = bf16[8,6,24,1408]{3,2,1,0:T(8,128)(2,1)} async-done(((bf16[8,6,24,1408]{3,2,1,0:T(8,128)(2,1)}), bf16[8,6,24,1408]{3,2,1,0:T(8,128)(2,1)}, u32[]{:S(2)}, u32[]{:S(2)}) %all-to-all-start.5) | async-done | bytes 3244064 | tf_op jit(solution)/shard_map/all_to_all | solution.py:629
  981.7 5.5 all-to-all-start.7
  997.3 20.7 reduce.1
  1018.0 7.2 reshape_squeeze.11
  1025.1 7.5 copy.75
  1032.7 8.2 broadcast_in_dim.156.cotangent
  1042.4 68.3 %feed_forward.2 = (f32[6,641,1,360]{3,2,1,0:T(1,128)}, f32[6,641,360]{2,1,0:T(8,128)}, bf16[8,6,24,1408]{3,2,1,0:T(8,128)(2,1)}, f32[641,1282]{1,0:T(8,128)}, f3...) custom-call(bf16[8,6,24,1408]{3,2,1,0:T(8,128)(2,1)} %all-to-all-done.5.synth, ...), custom_call_target="tpu_custom_call" | custom-call | flops 23848110080 | bytes 28641024 | tf_op jit(solution)/shard_map/feed_forward/pallas_call | solution.py:502
  1110.7 144.8 %all-to-all-done.7.synth = bf16[8,23,24,1408]{3,2,1,0:T(8,128)(2,1)} async-done(((bf16[8,23,24,1408]{3,2,1,0:T(8,128)(2,1)}), bf16[8,23,24,1408]{3,2,1,0:T(8,128)(2,1)}, u32[]{:S(2)}, u32[]{:S(2)}) %all-to-all-start.7) | async-done | bytes 12435488 | tf_op jit(solution)/shard_map/all_to_all | solution.py:629
  1255.6 4.6 all-to-all-start.10
  1260.2 232.9 %feed_forward.3 = (f32[23,641,1,360]{3,2,1,0:T(1,128)}, f32[23,641,360]{2,1,0:T(8,128)}, bf16[8,23,24,1408]{3,2,1,0:T(8,128)(2,1)}, f32[641,1282]{1,0:T(8,128)},...) custom-call(bf16[8,23,24,1408]{3,2,1,0:T(8,128)(2,1)} %all-to-all-done.7.synth, ...), custom_call_target="tpu_custom_call" | custom-call | flops 91417755648 | bytes 109790592 | tf_op jit(solution)/shard_map/feed_forward/pallas_call | solution.py:502
  1494.7 6.0 all-to-all-start.8
  1500.7 9.2 rows_to_degrees.7
  1509.9 260.3 %all-to-all-done.8.refs_0_ = bf16[8,23,24,1408]{3,2,1,0:T(8,128)(2,1)} async-done(((bf16[8,23,24,1408]{3,2,1,0:T(8,128)(2,1)}), bf16[8,23,24,1408]{3,2,1,0:T(8,128)(2,1)}, u32[]{:S(2)}, u32[]{:S(2)}) %all-to-all-start.8) | async-done | bytes 12435488 | tf_op jit(solution)/shard_map/all_to_all | solution.py:629
  1773.9 16.4 rows_to_degrees.6
  1790.3 56.6 %all-to-all-done.11.coarse = bf16[8,6,24,1408]{3,2,1,0:T(8,128)(2,1)S(1)} async-done(((bf16[8,6,24,1408]{3,2,1,0:T(8,128)(2,1)}), bf16[8,6,24,1408]{3,2,1,0:T(8,128)(2,1)S(1)}, u32[]{:S(2)}, u32[]{:S(2)}) %all-to-all-start.11) | async-done | bytes 3244064 | tf_op jit(solution)/shard_map/all_to_all | solution.py:629
  1846.9 147.8 %all_to_all.81.fine = bf16[8,12,24,1408]{3,2,1,0:T(8,128)(2,1)} all-to-all(bf16[8,12,24,1408]{3,2,1,0:T(8,128)(2,1)} %rows_to_degrees.6), channel_id=1, replica_groups=mesh['lat'=8,'chan'=4] {'lat'}, dimensions={0} | all-to-all | bytes 12976128 | tf_op jit(solution)/shard_map/all_to_all | solution.py:629
  1994.7 34.2 %mix_back.1 = (bf16[8,12,24,1408]{3,2,1,0:T(8,128)(2,1)}, bf16[8,6,24,1408]{3,2,1,0:T(8,128)(2,1)}, bf16[24,8,24,1408]{3,2,1,0:T(8,128)(2,1)}) custom-call(s32[12]{0:T(128)} %dynamic_slice.27.pairs, bf16[8,12,24,1408]{3,2,1,0:T(8,128)(2,1)} %all_to_all.81.fine, bf16[8,6,24,1408]{3,2,1,0:T(8,128)(2,1)} %copy-done.10, bf16[24,2,641,649]{3,2,1,0:T(8,128)(2,1)} %bitcast.77), custom_call_target="tpu_custom_call" | custom-call | flops 21743271936 | bytes 78865248 | tf_op jit(solution)/shard_map/mix_back/pallas_call | solution.py:383
  2028.9 76.3 %all_to_all.82.chunk = bf16[8,6,24,1408]{3,2,1,0:T(8,128)(2,1)} all-to-all(bf16[8,6,24,1408]{3,2,1,0:T(8,128)(2,1)} %get-tuple-element.49), channel_id=1, replica_groups=mesh['lat'=8,'chan'=4] {'lat'}, dimensions={0} | all-to-all | bytes 6488064 | tf_op jit(solution)/shard_map/all_to_all | solution.py:629
  2105.3 4.9 all-to-all-start.14
  2111.1 9.1 degrees_to_rows.6
  2120.2 130.5 %all-to-all-done.14.chunk = bf16[8,12,24,1408]{3,2,1,0:T(8,128)(2,1)} async-done(((bf16[8,12,24,1408]{3,2,1,0:T(8,128)(2,1)}), bf16[8,12,24,1408]{3,2,1,0:T(8,128)(2,1)}, u32[]{:S(2)}, u32[]{:S(2)}) %all-to-all-start.14) | async-done | bytes 6488096 | tf_op jit(solution)/shard_map/all_to_all | solution.py:629
  2256.5 16.4 degrees_to_rows.7
  2272.9 54.5 %all-to-all-done.13.wave = bf16[8,6,24,1408]{3,2,1,0:T(8,128)(2,1)S(1)} async-done(((bf16[8,6,24,1408]{3,2,1,0:T(8,128)(2,1)}), bf16[8,6,24,1408]{3,2,1,0:T(8,128)(2,1)S(1)}, u32[]{:S(2)}, u32[]{:S(2)}) %all-to-all-start.13) | async-done | bytes 3244064 | tf_op jit(solution)/shard_map/all_to_all | solution.py:629
  2329.0 5.3 all-to-all-start.15
  2334.5 9.3 constant_dynamic-slice_fusion.4
  2346.4 6.5 constant_dynamic-slice_fusion
  2362.4 13.2 copy.105
  2375.6 10.5 reshape.1153
  2387.8 39.3 %collective-permute-done.1.refs_2_ = bf16[6,8,24,1408]{3,2,1,0:T(8,128)(2,1)} collective-permute-done((bf16[6,8,24,1408]{3,2,1,0:T(8,128)(2,1)}, bf16[6,8,24,1408]{3,2,1,0:T(8,128)(2,1)}, u32[]{:S(2)}, u32[]{:S(2)}) %collective-permute-start.1) | collective-permute-done | bytes 3244064 | tf_op jit(solution)/shard_map/ppermute | solution.py:644
  2427.0 73.5 %collective-permute-done.2.refs_3_ = bf16[6,8,24,1408]{3,2,1,0:T(8,128)(2,1)} collective-permute-done((bf16[6,8,24,1408]{3,2,1,0:T(8,128)(2,1)}, bf16[6,8,24,1408]{3,2,1,0:T(8,128)(2,1)}, u32[]{:S(2)}, u32[]{:S(2)}) %collective-permute-start.2) | collective-permute-done | bytes 3244064 | tf_op jit(solution)/shard_map/ppermute | solution.py:644
  2500.6 70.4 %collective-permute-done.4.refs_6_ = bf16[6,8,24,1408]{3,2,1,0:T(8,128)(2,1)} collective-permute-done((bf16[6,8,24,1408]{3,2,1,0:T(8,128)(2,1)}, bf16[6,8,24,1408]{3,2,1,0:T(8,128)(2,1)}, u32[]{:S(2)}, u32[]{:S(2)}) %collective-permute-start.4) | collective-permute-done | bytes 3244064 | tf_op jit(solution)/shard_map/ppermute | solution.py:644
  2571.0 73.5 %collective-permute-done.5.refs_7_ = bf16[6,8,24,1408]{3,2,1,0:T(8,128)(2,1)} collective-permute-done((bf16[6,8,24,1408]{3,2,1,0:T(8,128)(2,1)}, bf16[6,8,24,1408]{3,2,1,0:T(8,128)(2,1)}, u32[]{:S(2)}, u32[]{:S(2)}) %collective-permute-start.5) | collective-permute-done | bytes 3244064 | tf_op jit(solution)/shard_map/ppermute | solution.py:644
  2644.5 24.8 mix_gradient.1
  2669.3 52.0 %copy.100 = f32[6,2,649,641]{2,1,3,0:T(2,128)} copy(f32[6,2,649,641]{2,3,1,0:T(8,128)} %bitcast.80) | data formatting | bytes 39936864
  2721.3 14.4 first_norm_back.2
  2735.8 13.1 copy.106
  2748.8 10.5 reshape.1154
  2759.4 46.2 %first_norm_back.3 = (f32[23,641,1,360]{3,2,1,0:T(1,128)}, f32[2,641,1]{2,1,0:T(8,128)}) custom-call(bf16[8,23,24,1408]{3,2,1,0:T(8,128)(2,1)} %all-to-all-done.15.wave, f32[23,641,1,360]{3,2,1,0:T(1,128)} %bitcast.75, f32[23,641,360]{2,1,0:T(8,128)} %get-tuple-element.53.middle_grad, bf16[384,360]{1,0:T(8,128)(2,1)} %pad_maximum_fusion.1.table, ...), custom_call_target="tpu_custom_call" | custom-call | flops 4883742720 | bytes 76125216 | tf_op jit(solution)/shard_map/first_norm_back/pallas_call | solution.py:567
  2806.7 58.9 %all-reduce = (f32[2,641,1]{2,1,0:T(8,128)S(1)}, f32[3,641,1]{2,1,0:T(8,128)S(1)}, f32[1282]{0:T(1024)}) all-reduce(f32[2,641,1]{2,1,0:T(8,128)S(1)} %add.500, f32[3,641,1]{2,1,0:T(8,128)S(1)} %add.505, f32[1282]{0:T(1024)S(1)} %add_reduce_fusion), channel_id=1, replica_groups=mesh['lat'=8,'chan'=4] {'lat','chan'}, use_global_device_ids=true, to_apply=%region_0.1 | all-reduce | flops 4487 | bytes 35896 | tf_op jit(solution)/shard_map/psum | solution.py:773
  (191 shorter events, 102.7 us)
Async XLA Ops:
  45.8 8.2 copy-start.24
  67.6 80.1 %all-to-all-start.2 = ((bf16[8,6,24,1408]{3,2,1,0:T(8,128)(2,1)}), bf16[8,6,24,1408]{3,2,1,0:T(8,128)(2,1)S(1)}, u32[]{:S(2)}, u32[]{:S(2)}) async-start(bf16[8,6,24,1408]{3,2,1,0:T(8,128)(2,1)} %norm_and_dft.3), calls=%async_computation.2 | async-start | bytes 6488064 | tf_op jit(solution)/shard_map/all_to_all | solution.py:629
  109.3 45.5 %copy-start.31 = (s32[96]{0:T(128)S(1)}, s32[96]{0:T(128)}, u32[]{:S(2)}) copy-start(s32[96]{0:T(128)} %param.22) | copy-start | bytes 1156
  147.6 1.7 copy-start
  149.3 274.3 %all-to-all-start = ((bf16[8,23,24,1408]{3,2,1,0:T(8,128)(2,1)}), bf16[8,23,24,1408]{3,2,1,0:T(8,128)(2,1)}, u32[]{:S(2)}, u32[]{:S(2)}) async-start(bf16[8,23,24,1408]{3,2,1,0:T(8,128)(2,1)} %norm_and_dft.2), calls=%async_computation | async-start | bytes 24870912 | tf_op jit(solution)/shard_map/all_to_all | solution.py:629
  176.0 252.5 %copy-start.29 = (s32[184]{0:T(256)S(1)}, s32[184]{0:T(256)}, u32[]{:S(2)}) copy-start(s32[184]{0:T(256)} %param.23) | copy-start | bytes 2212
  423.7 76.9 %all-to-all-start.3 = ((bf16[8,6,24,1408]{3,2,1,0:T(8,128)(2,1)}), bf16[8,6,24,1408]{3,2,1,0:T(8,128)(2,1)}, u32[]{:S(2)}, u32[]{:S(2)}) async-start(bf16[8,6,24,1408]{3,2,1,0:T(8,128)(2,1)} %rows_to_degrees.5), calls=%async_computation.3 | async-start | bytes 6488064 | tf_op jit(solution)/shard_map/all_to_all | solution.py:629
  482.0 23.4 copy-start.30
  500.6 146.2 %all-to-all-start.1 = ((bf16[8,12,24,1408]{3,2,1,0:T(8,128)(2,1)}), bf16[8,12,24,1408]{3,2,1,0:T(8,128)(2,1)}, u32[]{:S(2)}, u32[]{:S(2)}) async-start(bf16[8,12,24,1408]{3,2,1,0:T(8,128)(2,1)} %rows_to_degrees.4), calls=%async_computation.1 | async-start | bytes 12976128 | tf_op jit(solution)/shard_map/all_to_all | solution.py:629
  758.5 5.4 copy-start.14
  758.5 146.5 %all-to-all-start.6 = ((bf16[8,12,24,1408]{3,2,1,0:T(8,128)(2,1)}), bf16[8,12,24,1408]{3,2,1,0:T(8,128)(2,1)}, u32[]{:S(2)}, u32[]{:S(2)}) async-start(bf16[8,12,24,1408]{3,2,1,0:T(8,128)(2,1)} %get-tuple-element.45), calls=%async_computation.6 | async-start | bytes 12976128 | tf_op jit(solution)/shard_map/all_to_all | solution.py:629
  764.3 10.0 copy-start.12
  905.0 76.7 %all-to-all-start.5 = ((bf16[8,6,24,1408]{3,2,1,0:T(8,128)(2,1)}), bf16[8,6,24,1408]{3,2,1,0:T(8,128)(2,1)}, u32[]{:S(2)}, u32[]{:S(2)}) async-start(bf16[8,6,24,1408]{3,2,1,0:T(8,128)(2,1)} %degrees_to_rows.4), calls=%async_computation.5 | async-start | bytes 6488064 | tf_op jit(solution)/shard_map/all_to_all | solution.py:629
  911.4 2.4 copy-start.3
  913.8 17.4 copy-start.4
  981.7 5.5 copy-start.13
  981.7 273.8 %all-to-all-start.7 = ((bf16[8,23,24,1408]{3,2,1,0:T(8,128)(2,1)}), bf16[8,23,24,1408]{3,2,1,0:T(8,128)(2,1)}, u32[]{:S(2)}, u32[]{:S(2)}) async-start(bf16[8,23,24,1408]{3,2,1,0:T(8,128)(2,1)} %degrees_to_rows.5), calls=%async_computation.7 | async-start | bytes 24870912 | tf_op jit(solution)/shard_map/all_to_all | solution.py:629
  987.2 6.3 copy-start.25
  987.2 7.4 copy-start.26
  989.8 5.7 copy-start.27
  989.8 6.6 copy-start.28
  1032.6 8.2 copy-start.22
  1032.6 8.2 copy-start.23
  1032.6 9.0 copy-start.20
  1032.6 9.0 copy-start.21
  1255.6 237.4 %all-to-all-start.10 = ((bf16[8,6,24,1408]{3,2,1,0:T(8,128)(2,1)}), bf16[8,6,24,1408]{3,2,1,0:T(8,128)(2,1)S(1)}, u32[]{:S(2)}, u32[]{:S(2)}) async-start(bf16[8,6,24,1408]{3,2,1,0:T(8,128)(2,1)} %get-tuple-element.48), calls=%async_computation.10 | async-start | bytes 6488064 | tf_op jit(solution)/shard_map/all_to_all | solution.py:629
  1493.0 1.7 copy-start.1
  1494.7 275.5 %all-to-all-start.8 = ((bf16[8,23,24,1408]{3,2,1,0:T(8,128)(2,1)}), bf16[8,23,24,1408]{3,2,1,0:T(8,128)(2,1)}, u32[]{:S(2)}, u32[]{:S(2)}) async-start(bf16[8,23,24,1408]{3,2,1,0:T(8,128)(2,1)} %get-tuple-element.47), calls=%async_computation.8 | async-start | bytes 24870912 | tf_op jit(solution)/shard_map/all_to_all | solution.py:629
  1770.2 76.6 %all-to-all-start.11 = ((bf16[8,6,24,1408]{3,2,1,0:T(8,128)(2,1)}), bf16[8,6,24,1408]{3,2,1,0:T(8,128)(2,1)S(1)}, u32[]{:S(2)}, u32[]{:S(2)}) async-start(bf16[8,6,24,1408]{3,2,1,0:T(8,128)(2,1)} %rows_to_degrees.7), calls=%async_computation.11 | async-start | bytes 6488064 | tf_op jit(solution)/shard_map/all_to_all | solution.py:629
  1846.9 147.8 %copy-start.10 = (bf16[8,6,24,1408]{3,2,1,0:T(8,128)(2,1)}, bf16[8,6,24,1408]{3,2,1,0:T(8,128)(2,1)S(1)}, u32[]{:S(2)}) copy-start(bf16[8,6,24,1408]{3,2,1,0:T(8,128)(2,1)S(1)} %all-to-all-done.11.coarse) | copy-start | bytes 9732100
  2105.3 4.9 copy-start.11
  2105.3 145.4 %all-to-all-start.14 = ((bf16[8,12,24,1408]{3,2,1,0:T(8,128)(2,1)}), bf16[8,12,24,1408]{3,2,1,0:T(8,128)(2,1)}, u32[]{:S(2)}, u32[]{:S(2)}) async-start(bf16[8,12,24,1408]{3,2,1,0:T(8,128)(2,1)} %get-tuple-element.52), calls=%async_computation.14 | async-start | bytes 12976128 | tf_op jit(solution)/shard_map/all_to_all | solution.py:629
  2250.7 76.6 %all-to-all-start.13 = ((bf16[8,6,24,1408]{3,2,1,0:T(8,128)(2,1)}), bf16[8,6,24,1408]{3,2,1,0:T(8,128)(2,1)S(1)}, u32[]{:S(2)}, u32[]{:S(2)}) async-start(bf16[8,6,24,1408]{3,2,1,0:T(8,128)(2,1)} %degrees_to_rows.6), calls=%async_computation.13 | async-start | bytes 6488064 | tf_op jit(solution)/shard_map/all_to_all | solution.py:629
  2327.3 1.7 copy-start.2
  2329.0 430.4 %all-to-all-start.15 = ((bf16[8,23,24,1408]{3,2,1,0:T(8,128)(2,1)}), bf16[8,23,24,1408]{3,2,1,0:T(8,128)(2,1)}, u32[]{:S(2)}, u32[]{:S(2)}) async-start(bf16[8,23,24,1408]{3,2,1,0:T(8,128)(2,1)} %degrees_to_rows.7), calls=%async_computation.15 | async-start | bytes 24870912 | tf_op jit(solution)/shard_map/all_to_all | solution.py:629
  2334.4 533.1 %all-reduce.4.cloned.1.call-start = ((), (), s32[]{:S(2)}) async-start(), calls=%async_computation.16 | async-start | bytes 14598144 | tf_op jit(solution)/shard_map/psum | solution.py:754
  2334.4 11.2 slice-start
  2334.5 11.2 slice-start.1
  2334.5 11.9 slice-start.2
  2334.5 11.9 slice-start.3
  2343.8 10.7 collective-permute-start
  2343.8 83.3 %collective-permute-start.1 = (bf16[6,8,24,1408]{3,2,1,0:T(8,128)(2,1)}, bf16[6,8,24,1408]{3,2,1,0:T(8,128)(2,1)}, u32[]{:S(2)}, u32[]{:S(2)}) collective-permute-start(bf16[6,8,24,1408]{3,2,1,0:T(8,128)(2,1)} %get-tuple-element.108), channel_id=1, source_target_pairs={{0,2},{1,3},{2,0},{3,1},{4,6},{5,7},{6,4},{7,5},{8,10},{9,11},{10,... | collective-permute-start | bytes 9732104 | tf_op jit(solution)/shard_map/ppermute | solution.py:644
  2345.4 155.2 %collective-permute-start.2 = (bf16[6,8,24,1408]{3,2,1,0:T(8,128)(2,1)}, bf16[6,8,24,1408]{3,2,1,0:T(8,128)(2,1)}, u32[]{:S(2)}, u32[]{:S(2)}) collective-permute-start(bf16[6,8,24,1408]{3,2,1,0:T(8,128)(2,1)} %get-tuple-element.107), channel_id=1, source_target_pairs={{0,3},{1,2},{2,1},{3,0},{4,7},{5,6},{6,5},{7,4},{8,11},{9,10},{10,... | collective-permute-start | bytes 9732104 | tf_op jit(solution)/shard_map/ppermute | solution.py:644
  2346.4 8.4 copy-start.6
  2346.4 8.4 copy-start.8
  2352.9 147.6 %collective-permute-start.3 = (bf16[6,8,24,1408]{3,2,1,0:T(8,128)(2,1)}, bf16[6,8,24,1408]{3,2,1,0:T(8,128)(2,1)}, u32[]{:S(2)}, u32[]{:S(2)}) collective-permute-start(bf16[6,8,24,1408]{3,2,1,0:T(8,128)(2,1)} %get-tuple-element.105), channel_id=1, source_target_pairs={{0,1},{1,0},{2,3},{3,2},{4,5},{5,4},{6,7},{7,6},{8,9},{9,8},{10,11... | collective-permute-start | bytes 9732104 | tf_op jit(solution)/shard_map/ppermute | solution.py:644
  2352.9 218.1 %collective-permute-start.4 = (bf16[6,8,24,1408]{3,2,1,0:T(8,128)(2,1)}, bf16[6,8,24,1408]{3,2,1,0:T(8,128)(2,1)}, u32[]{:S(2)}, u32[]{:S(2)}) collective-permute-start(bf16[6,8,24,1408]{3,2,1,0:T(8,128)(2,1)} %get-tuple-element.104), channel_id=1, source_target_pairs={{0,2},{1,3},{2,0},{3,1},{4,6},{5,7},{6,4},{7,5},{8,10},{9,11},{10,... | collective-permute-start | bytes 9732104 | tf_op jit(solution)/shard_map/ppermute | solution.py:644
  2354.4 3.3 copy-start.32
  2354.5 290.1 %collective-permute-start.5 = (bf16[6,8,24,1408]{3,2,1,0:T(8,128)(2,1)}, bf16[6,8,24,1408]{3,2,1,0:T(8,128)(2,1)}, u32[]{:S(2)}, u32[]{:S(2)}) collective-permute-start(bf16[6,8,24,1408]{3,2,1,0:T(8,128)(2,1)} %get-tuple-element.103), channel_id=1, source_target_pairs={{0,3},{1,2},{2,1},{3,0},{4,7},{5,6},{6,5},{7,4},{8,11},{9,10},{10,... | collective-permute-start | bytes 9732104 | tf_op jit(solution)/shard_map/ppermute | solution.py:644
  2354.8 4.2 copy-start.5
  2354.8 5.3 copy-start.7
  2375.6 10.5 copy-start.15
  2375.6 10.5 copy-start.16
  2386.1 1.1 copy-start.18
  2386.1 1.3 copy-start.19
  2759.4 46.2 %copy-start.17 = (f32[2,641,1]{2,1,0:T(8,128)S(1)}, f32[2,641,1]{2,1,0:T(8,128)}, u32[]{:S(2)}) copy-start(f32[2,641,1]{2,1,0:T(8,128)} %get-tuple-element.55) | copy-start | bytes 15388
  2867.4 4.3 copy-start.9
Sparse Core Ops, SparseCore 0:
  2362.6 386.6 all-reduce.3

commit v2 on v1

--- a/solution.py
+++ b/solution.py
@@ -39,6 +39,16 @@
     )
 
 
+def filled(body, into, position, output=0):
+    if into is None:
+        return body, [], {}
+
+    def skipping(*refs):
+        body(*refs[:position], *refs[position + 1 :])
+
+    return skipping, [pl.BlockSpec(memory_space=pl.ANY)], {position: output}
+
+
 def dot(left, right, left_dim, right_dim):
     return lax.dot_general(
         left, right, (((left_dim,), (right_dim,)), ((), ())), preferred_element_type=f32
@@ -69,6 +79,10 @@
 
 def flat(block):
     return block.astype(f32).reshape(-1, block.shape[-1])
+
+
+def joined_rows(parts):
+    return parts[0] if len(parts) == 1 else jnp.concatenate(parts, axis=0)
 
 
 def norm_stats(values):
@@ -214,50 +228,53 @@
     return plain, [table * weight for table in plain]
 
 
-def by_class(table, n_lat, pair_dev):
-    split = table.reshape(n_lat, pair_dev // 2, 2, table.shape[1], table.shape[2])
-    moved = split.transpose(3, 2, 0, 1, 4)[:pair_dev]
+def by_class(table, n_lat, pair_dev, n_chunks):
+    split = table.reshape(n_lat, n_chunks, pair_dev // (2 * n_chunks), 2, *table.shape[1:])
+    moved = split.transpose(4, 3, 1, 0, 2, 5)[:pair_dev]
     return moved.reshape(pair_dev, n_lat * pair_dev, table.shape[2]).astype(bf16)
 
 
-def to_degrees_fine_body(pair_dev, n_chunks, *refs):
-    chunks, (table_a, table_b, out) = refs[:n_chunks], refs[n_chunks : n_chunks + 3]
-    held, result = refs[n_chunks + 3 : -1], refs[-1]
-    n_lat, unused, subs, lanes = out.shape
+def to_degrees_fine_body(pair_dev, n_in, n_out, *refs):
+    chunks, (table_a, table_b), rest = refs[:n_in], refs[n_in : n_in + 2], refs[n_in + 2 :]
+    outs, held, results = rest[:n_out], rest[n_out : n_out + n_in], rest[n_out + n_in :]
+    n_lat, unused, subs, lanes = outs[0].shape
     half = n_lat * pair_dev // 2
     for chunk, keep in zip(chunks, held):
         keep[...] = flat(chunk[...])
     if subs != 2 * pair_dev:
-        result[...] = jnp.zeros_like(result)
+        for result in results:
+            result[...] = jnp.zeros_like(result)
 
     def order_rows(sub):
-        parts = [
-            keep[pl.ds(sub, keep.shape[0] // subs, stride=subs), :] for keep in held
-        ]
-        return (parts[0] if len(parts) == 1 else jnp.concatenate(parts, axis=0)).astype(bf16)
+        parts = [keep[pl.ds(sub, keep.shape[0] // subs, stride=subs), :] for keep in held]
+        return joined_rows(parts).astype(bf16)
 
     for index in range(pair_dev):
         from_a = dot(table_a[index], order_rows(2 * index), 1, 0)
         from_b = dot(table_b[index], order_rows(2 * index + 1), 1, 0)
         first, second = from_a[: 2 * half], from_a[2 * half :] + from_b
+        begin = 0
         for odd in range(2):
-            rows = slice(odd * half, (odd + 1) * half)
             start = odd * subs + index
-            result[pl.ds(start + (1 - odd) * pair_dev, half, stride=2 * subs), :] = first[rows]
-            result[pl.ds(start + odd * pair_dev, half, stride=2 * subs), :] = second[rows]
-    out[...] = result[...].reshape(out.shape).astype(bf16)
-
-
-def to_degrees_coarse_body(pair_dev, chunk, table, out, held, result):
+            for result in results:
+                count = result.shape[0] // (2 * subs)
+                rows = slice(begin, begin + count)
+                begin += count
+                result[pl.ds(start + (1 - odd) * pair_dev, count, stride=2 * subs), :] = first[rows]
+                result[pl.ds(start + odd * pair_dev, count, stride=2 * subs), :] = second[rows]
+    for out, result in zip(outs, results):
+        out[...] = result[...].reshape(out.shape).astype(bf16)
+
+
+def to_degrees_coarse_body(pair_dev, n_in, n_out, chunk, table, out, held, result):
     n_lat, unused, subs, lanes = out.shape
-    half = n_lat * pair_dev // 2
     held[...] = flat(chunk[...])
     if subs != 2 * pair_dev:
         result[...] = jnp.zeros_like(result)
-    rows = held.shape[0] // subs
+    rows, half = held.shape[0] // subs, result.shape[0] // subs
     for index in range(pair_dev):
-        taken = jnp.concatenate(
-            [held[pl.ds(odd * pair_dev + index, rows, stride=subs), :] for odd in range(2)], axis=0
+        taken = joined_rows(
+            [held[pl.ds(odd * pair_dev + index, rows, stride=subs), :] for odd in range(2)]
         ).astype(bf16)
         made = dot(table[index], taken, 1, 0)
         for odd in range(2):
@@ -267,11 +284,12 @@
     out[...] = result[...].reshape(out.shape).astype(bf16)
 
 
-def to_orders_fine_body(pair_dev, n_chunks, chunk, table_a, table_b, *refs):
-    outs, (held, *results) = refs[:n_chunks], refs[n_chunks:]
-    n_lat, unused, subs, lanes = chunk.shape
-    half = n_lat * pair_dev // 2
-    held[...] = flat(chunk[...])
+def to_orders_fine_body(pair_dev, n_in, n_out, *refs):
+    chunks, (table_a, table_b), rest = refs[:n_in], refs[n_in : n_in + 2], refs[n_in + 2 :]
+    outs, held, results = rest[:n_out], rest[n_out : n_out + n_in], rest[n_out + n_in :]
+    n_lat, unused, subs, lanes = chunks[0].shape
+    for chunk, keep in zip(chunks, held):
+        keep[...] = flat(chunk[...])
     if subs != 2 * pair_dev:
         for result in results:
             result[...] = jnp.zeros_like(result)
@@ -279,10 +297,12 @@
         first, second = [], []
         for odd in range(2):
             start = odd * subs + index
-            first.append(held[pl.ds(start + (1 - odd) * pair_dev, half, stride=2 * subs), :])
-            second.append(held[pl.ds(start + odd * pair_dev, half, stride=2 * subs), :])
-        second = jnp.concatenate(second, axis=0)
-        both = jnp.concatenate(first + [second], axis=0).astype(bf16)
+            for keep in held:
+                count = keep.shape[0] // (2 * subs)
+                first.append(keep[pl.ds(start + (1 - odd) * pair_dev, count, stride=2 * subs), :])
+                second.append(keep[pl.ds(start + odd * pair_dev, count, stride=2 * subs), :])
+        second = joined_rows(second)
+        both = joined_rows(first + [second]).astype(bf16)
         made = (dot(table_a[index], both, 1, 0), dot(table_b[index], second.astype(bf16), 1, 0))
         for member in range(2):
             begin = 0
@@ -296,16 +316,15 @@
         out[...] = result[...].reshape(out.shape).astype(bf16)
 
 
-def to_orders_coarse_body(pair_dev, chunk, table, out, held, result):
-    n_lat, unused, subs, lanes = chunk.shape
-    half = n_lat * pair_dev // 2
+def to_orders_coarse_body(pair_dev, n_in, n_out, chunk, table, out, held, result):
+    n_lat, unused, subs, lanes = out.shape
     held[...] = flat(chunk[...])
     if subs != 2 * pair_dev:
         result[...] = jnp.zeros_like(result)
-    rows = result.shape[0] // subs
+    rows, half = result.shape[0] // subs, held.shape[0] // subs
     for index in range(pair_dev):
-        taken = jnp.concatenate(
-            [held[pl.ds(odd * pair_dev + index, half, stride=subs), :] for odd in range(2)], axis=0
+        taken = joined_rows(
+            [held[pl.ds(odd * pair_dev + index, half, stride=subs), :] for odd in range(2)]
         ).astype(bf16)
         made = dot(table[index], taken, 1, 0)
         for odd in range(2):
@@ -322,7 +341,7 @@
     moved = sum(2 * math.prod(s) for s in [a.shape for a in inputs] + outs)
     flops = sum(2 * math.prod(t.shape) for t in tables) * LANES
     made = call(
-        body,
+        functools.partial(body, len(inputs), len(outs)),
         name,
         flops,
         moved,
@@ -335,7 +354,7 @@
     return made
 
 
-def mix_body(pair_dev, backward, pairs, fine, coarse, weight, fine_out, coarse_out, members):
+def mix_body(pair_dev, first, backward, pairs, fine, coarse, weight, fine_out, coarse_out, members):
     n_lat, unused, subs, lanes = fine.shape
     rows = n_lat * subs
     row = lax.broadcasted_iota(jnp.int32, (rows, 1), 0)
@@ -360,7 +379,7 @@
 
     coarse_made = jnp.zeros((rows, lanes), f32)
     for odd in range(2):
-        pair = pairs[2 * pl.program_id(0) + odd]
+        pair = pairs[2 * (pl.program_id(0) + first) + odd]
         own = group == odd
         low = order_class <= pair
         fine_rows = flat(fine[:, odd])
@@ -376,23 +395,28 @@
     coarse_out[:, 0] = coarse_made.reshape(n_lat, subs, lanes).astype(bf16)
 
 
-def mix(fine, coarse, weight, local_pairs, backward):
-    n_lat, pair_dev, subs, lanes = fine.shape
+def mix(fine, coarse, weight, local_pairs, first, backward, into):
+    n_lat, count, subs, lanes = fine.shape
+    pair_dev = weight.shape[0] // 2
     fine_spec = pl.BlockSpec((n_lat, 2, subs, lanes), lambda k, pairs: (0, k, 0, 0))
-    coarse_spec = pl.BlockSpec((n_lat, 1, subs, lanes), lambda k, pairs: (0, k, 0, 0))
+    coarse_spec = pl.BlockSpec((n_lat, 1, subs, lanes), lambda k, pairs: (0, k + first, 0, 0))
+    body, extra, alias = filled(
+        functools.partial(mix_body, pair_dev, first, backward), into, 4, 1
+    )
     return call(
-        functools.partial(mix_body, pair_dev, backward),
+        body,
         "mix_back" if backward else "mix",
-        2 * pair_dev * n_lat * subs * 8 * PADDED * PADDED,
-        2 * weight.size + 12 * fine.size,
+        2 * count * n_lat * subs * 8 * PADDED * PADDED,
+        2 * weight.size * count // pair_dev + 12 * fine.size,
         grid_spec=pltpu.PrefetchScalarGridSpec(
             num_scalar_prefetch=1,
-            grid=(pair_dev // 2,),
+            grid=(count // 2,),
             in_specs=[
                 fine_spec,
                 coarse_spec,
-                pl.BlockSpec((4,) + weight.shape[1:], lambda k, pairs: (k, 0, 0, 0)),
-            ],
+                pl.BlockSpec((4,) + weight.shape[1:], lambda k, pairs: (k + first, 0, 0, 0)),
+            ]
+            + extra,
             out_specs=[
                 fine_spec,
                 coarse_spec,
@@ -402,9 +426,10 @@
         out_shape=[
             jax.ShapeDtypeStruct(fine.shape, bf16),
             jax.ShapeDtypeStruct(coarse.shape, bf16),
-            jax.ShapeDtypeStruct((2 * pair_dev, n_lat, subs, lanes), bf16),
+            jax.ShapeDtypeStruct((2 * count, n_lat, subs, lanes), bf16),
         ],
-    )(local_pairs, fine, coarse, weight)
+        input_output_aliases=alias,
+    )(local_pairs, fine, coarse, weight, *([] if into is None else [into]))
 
 
 def mix_grad_body(n_parts, *refs):
@@ -412,8 +437,8 @@
     gather = lambda parts: jnp.concatenate([flat(part[0]) for part in parts], axis=0)
     value_real, value_imag = [v.astype(bf16) for v in split_parts(gather(values), WIDE)]
     grad_real, grad_imag = [v.astype(bf16) for v in split_parts(gather(grads), C)]
-    out[0, 0] = dot(grad_real, value_real, 0, 0) + dot(grad_imag, value_imag, 0, 0)
-    out[0, 1] = dot(grad_imag, value_real, 0, 0) - dot(grad_real, value_imag, 0, 0)
+    out[0, :, 0, :] = dot(grad_real, value_real, 0, 0) + dot(grad_imag, value_imag, 0, 0)
+    out[0, :, 1, :] = dot(grad_imag, value_real, 0, 0) - dot(grad_real, value_imag, 0, 0)
 
 
 def mix_gradient(values, grads):
@@ -428,8 +453,8 @@
         slots * (4 * rows * LANES + 8 * C * WIDE),
         grid=(slots,),
         in_specs=[spec] * (2 * len(values)),
-        out_specs=pl.BlockSpec((1, 2, C, WIDE), lambda k: (k, 0, 0, 0)),
-        out_shape=jax.ShapeDtypeStruct((slots, 2, C, WIDE), f32),
+        out_specs=pl.BlockSpec((1, C, 2, WIDE), lambda k: (k, 0, 0, 0)),
+        out_shape=jax.ShapeDtypeStruct((slots, C, 2, WIDE), f32),
     )(*values, *grads)
 
 
@@ -489,7 +514,7 @@
         narrow_sums[...] = jnp.sum(narrow_held[...], axis=2, keepdims=True)
 
 
-def pixels(synth, state, cotangent, table, params, first):
+def pixels(synth, state, cotangent, table, params, first, into):
     n_lat, count, subs, lanes = synth.shape
     points = state.shape[3]
     hidden = params[2].shape[1]
@@ -499,15 +524,17 @@
     wave = pl.BlockSpec((n_lat, 1, subs, lanes), lambda r: (0, r, 0, 0))
     whole = lambda shape: pl.BlockSpec(shape, lambda r: (0,) * len(shape))
     shaped = lambda shape, kind=f32: jax.ShapeDtypeStruct(shape, kind)
+    body, extra, alias = filled(pixel_body, into, 4 + len(params))
     return call(
-        pixel_body,
+        body,
         "feed_forward",
         2 * count * points * (6 * C * hidden + 2 * table.shape[0] * PADDED),
         count * (4 * C * points * 4 + 4 * n_lat * subs * lanes),
         grid=(count,),
-        in_specs=[wave, row_spec, row_spec, const(table)] + [const(p) for p in params],
+        in_specs=[wave, row_spec, row_spec, const(table)] + [const(p) for p in params] + extra,
+        input_output_aliases=alias,
         out_specs=[
-            row_out((C, 1, points)),
+            row_spec,
             row_out((C, points)),
             wave,
             whole((C, hidden)),
@@ -516,7 +543,7 @@
             whole((3, C, 1)),
         ],
         out_shape=[
-            shaped((count, C, 1, points)),
+            shaped(state.shape),
             shaped((count, C, points)),
             shaped(synth.shape, bf16),
             shaped((C, hidden)),
@@ -529,7 +556,7 @@
             pltpu.VMEM((hidden, points), f32),
             pltpu.VMEM((3, C, points), f32),
         ],
-    )(synth, state, cotangent, table, *params)
+    )(synth, state, cotangent, table, *params, *([] if into is None else [into]))
 
 
 def final_body(wave, state, middle_grad, table, gain, out, sums, held):
@@ -561,11 +588,12 @@
         sums[...] = jnp.sum(held[...], axis=2, keepdims=True)
 
 
-def finish(wave, state, middle_grad, table, gain, first):
+def finish(wave, state, middle_grad, table, gain, first, into):
     n_lat, count, subs, lanes = wave.shape
     points = state.shape[3]
+    body, extra, alias = filled(final_body, into, 5)
     return call(
-        final_body,
+        body,
         "first_norm_back",
         2 * count * points * table.shape[0] * PADDED,
         count * (3 * C * points * 4 + 2 * n_lat * subs * lanes),
@@ -576,17 +604,40 @@
             pl.BlockSpec((1, C, points), lambda r: (r, 0, 0)),
             pl.BlockSpec(table.shape, lambda r: (0, 0)),
             pl.BlockSpec((C, 1), lambda r: (0, 0)),
-        ],
+        ]
+        + extra,
+        input_output_aliases=alias,
         out_specs=[
-            pl.BlockSpec((1, C, 1, points), lambda r: (r, 0, 0, 0)),
+            pl.BlockSpec((1, C, 1, points), lambda r: (r + first, 0, 0, 0)),
             pl.BlockSpec((2, C, 1), lambda r: (0, 0, 0)),
         ],
         out_shape=[
-            jax.ShapeDtypeStruct((count, C, 1, points), f32),
+            jax.ShapeDtypeStruct(state.shape, f32),
             jax.ShapeDtypeStruct((2, C, 1), f32),
         ],
         scratch_shapes=[pltpu.VMEM((2, C, points), f32)],
-    )(wave, state, middle_grad, table, gain)
+    )(wave, state, middle_grad, table, gain, *([] if into is None else [into]))
+
+
+def part_rows_body(paired, out):
+    turned = paired[0][:, 0, :].T
+    count = turned.shape[0] // 2
+    for half in range(2):
+        out[half] = turned[half * count : (half + 1) * count][:, None, :]
+
+
+def part_rows(paired):
+    pairs, points = paired.shape[0], paired.shape[3] // 2
+    return call(
+        part_rows_body,
+        "part_rows",
+        0,
+        8 * paired.size,
+        grid=(pairs,),
+        in_specs=[pl.BlockSpec((1, C, 1, 2 * points), lambda r: (r, 0, 0, 0))],
+        out_specs=pl.BlockSpec((2, points, 1, C), lambda r: (r, 0, 0, 0)),
+        out_shape=jax.ShapeDtypeStruct((2 * pairs, points, 1, C), f32),
+    )(paired)
 
 
 def fourier_tables(orders, live, points, lon_count):
@@ -625,25 +676,98 @@
     return fourier_tables(orders, live, points % lon_count, lon_count)
 
 
-def swap(values):
-    return lax.all_to_all(values, "lat", split_axis=0, concat_axis=0, tiled=True)
-
-
-def share_slots(members, n_chan):
+class Line:
+    def __init__(self):
+        self.before = self.last = None
+        self.work, self.later = [], []
+        self.aside = None
+
+    def swap(self, values):
+        waits = self.work + ([] if self.last is None else [self.last])
+        if waits:
+            values = lax.optimization_barrier((values, waits))[0]
+        self.before = self.last
+        self.last = lax.all_to_all(values, "lat", split_axis=0, concat_axis=0, tiled=True)
+        self.work, self.later = self.later, []
+        self.step_aside()
+        return self.last
+
+    def step_aside(self):
+        if self.aside is not None:
+            next(self.aside, None)
+
+    def hold(self, values):
+        if self.before is None:
+            return values
+        return lax.optimization_barrier((values, self.before))[0]
+
+    def keep(self, values):
+        self.work.append(values)
+        return values
+
+    def keep_later(self, values):
+        self.later.append(values)
+        return values
+
+
+def partners(count, step):
+    if count & (count - 1) == 0:
+        return [(k, k ^ step) for k in range(count)], lambda rank: jnp.bitwise_xor(rank, step)
+    return [(k, (k + step) % count) for k in range(count)], lambda rank: (rank + step) % count
+
+
+def share_slots(members, n_chan, step):
     share = members.shape[0] // n_chan
-    rank = lax.axis_index("chan")
-    parts = []
-    for step in range(n_chan):
-        partner = jnp.bitwise_xor(rank, step) if n_chan & (n_chan - 1) == 0 else (rank + step) % n_chan
-        block = lax.dynamic_slice_in_dim(members, partner * share, share)
-        if step:
-            if n_chan & (n_chan - 1) == 0:
-                route = [(k, k ^ step) for k in range(n_chan)]
-            else:
-                route = [(k, (k + step) % n_chan) for k in range(n_chan)]
-            block = lax.ppermute(block, "chan", route)
-        parts.append(block)
-    return parts
+    route, find = partners(n_chan, step)
+    block = lax.dynamic_slice_in_dim(members, find(lax.axis_index("chan")) * share, share)
+    return lax.ppermute(block, "chan", route) if step else block
+
+
+def sum_over(values, sizes):
+    for axis, size in sizes:
+        if size & (size - 1):
+            values = lax.psum(values, axis)
+            continue
+        step = 1
+        while step < size:
+            values = values + lax.ppermute(values, axis, partners(size, step)[0])
+            step *= 2
+    return values
+
+
+def add_dense(arrays, axes, line, result):
+    columns = max(array.shape[1] for array in arrays)
+    heights = [array.shape[0] for array in arrays]
+    steps = [
+        (axis, 2**k) for axis, size in axes for k in range(size.bit_length() - 1)
+    ]
+    rows = -(-sum(heights) // (8 * 2 ** len(steps))) * 8 * 2 ** len(steps)
+    wide = [jnp.pad(a, ((0, 0), (0, columns - a.shape[1]))) for a in arrays]
+    held = jnp.pad(jnp.concatenate(wide, axis=0), ((0, rows - sum(heights)), (0, 0)))
+    sizes = dict(axes)
+    odd = lambda axis, step: (lax.axis_index(axis) // step) % 2 == 1
+    for axis, step in steps:
+        low, high = jnp.split(line.hold(held), 2, axis=0)
+        upper = odd(axis, step)
+        other = lax.ppermute(jnp.where(upper, low, high), axis, partners(sizes[axis], step)[0])
+        held = line.keep_later(jnp.where(upper, high, low) + other)
+        yield
+    held = held.astype(bf16)
+    for axis, step in reversed(steps):
+        if (axis, step) == steps[1]:
+            yield
+        held = line.hold(held)
+        upper = odd(axis, step)
+        other = lax.ppermute(held, axis, partners(sizes[axis], step)[0])
+        held = jnp.concatenate(
+            [jnp.where(upper, other, held), jnp.where(upper, held, other)], axis=0
+        )
+        line.keep_later(held)
+        yield
+    begin = 0
+    for array, height in zip(arrays, heights):
+        result.append(held[begin : begin + height, : array.shape[1]].astype(f32))
+        begin += height
 
 
 def shards(
@@ -670,122 +794,220 @@
         return values.transpose(2, 0, 3, 1)
 
     def coarse_back(values):
-        turned = values[:, :, 0, :].transpose(0, 2, 1)
-        return turned.reshape(1, coarse_dev, coarse_points, C)
-
-    coarse_x, fine_x = coarse_in(coarse_state), fine_in(fine_state)
-    coarse_g, fine_g = coarse_in(coarse_cotangent), fine_in(fine_cotangent)
-    coarse_forward, coarse_inverse = coarse_fourier(n_lat, pair_dev, subs, coarse_points)
+        return part_rows(values).transpose(2, 0, 1, 3)
+
+    line = Line()
+    row_cuts = [(fine_dev + 1) // 2, fine_dev // 2] if fine_dev >= 8 else [fine_dev]
+    row_starts = [sum(row_cuts[:k]) for k in range(len(row_cuts))]
+    n_chunks = 2 if pair_dev % 4 == 0 else 1
+    chunk_pairs = pair_dev // n_chunks
+    chunk_range = range(n_chunks)
+
+    fine_x = fine_in(fine_state)
+    fine_noise_in = fine_noise[0].transpose(0, 2, 1)
     fine_forward, fine_inverse = fine_fourier(n_lat, pair_dev, subs, fine_points)
     gain_one, bias_one = column(first_gain), column(first_bias)
-
-    coarse_four = swap(
-        spread(coarse_x, coarse_in(coarse_noise)[:, :, 0, :], gain_one, bias_one, coarse_forward,
-               n_lat, 0, coarse_two)
-    )
-    fine_four = swap(
-        spread(fine_x, fine_in(fine_noise)[:, :, 0, :], gain_one, bias_one, fine_forward,
-               n_lat, 0, fine_dev)
+    fine_four = []
+    for start, count in zip(row_starts, row_cuts):
+        made = spread(fine_x, fine_noise_in, gain_one, bias_one, fine_forward, n_lat, start, count)
+        fine_four.append(line.swap(line.keep(made)))
+    coarse_x = coarse_in(coarse_state)
+    coarse_forward, coarse_inverse = coarse_fourier(n_lat, pair_dev, subs, coarse_points)
+    coarse_noise_in = coarse_in(coarse_noise)[:, :, 0, :]
+    coarse_four = line.swap(
+        spread(coarse_x, coarse_noise_in, gain_one, bias_one, coarse_forward, n_lat, 0, coarse_two)
     )
 
     wide = -(-pair_dev // 8) * 8
     classes = lat_rank * pair_dev + jnp.arange(wide, dtype=jnp.int32)
     classes = jnp.where(jnp.arange(wide) < pair_dev, classes, LB).astype(jnp.int32)
     coarse_order = coarse_rows.reshape(-1, 2).T.reshape(-1)
-    fine_plain, fine_quad = legendre_tables(fine_rows, pair_slots, classes, LB, True)
+    by_device = fine_rows.reshape(n_lat, fine_dev)
+    fine_order = jnp.concatenate(
+        [by_device[:, a : a + c].reshape(-1) for a, c in zip(row_starts, row_cuts)]
+    )
+    fine_plain, fine_quad = legendre_tables(fine_order, pair_slots, classes, LB, True)
     coarse_plain, coarse_quad = legendre_tables(coarse_order, pair_slots, classes, LA, False)
-    turn = lambda table: by_class(table, n_lat, pair_dev)
+    turn = lambda table, chunks=n_chunks: by_class(table, n_lat, pair_dev, chunks)
 
     def fine_tables(parts):
         first, near, far = [turn(part) for part in parts]
         table_a = jnp.concatenate([first, near], axis=1)
-        return (table_a, far), (table_a.transpose(0, 2, 1), far.transpose(0, 2, 1))
+        return [table_a, far], [table_a.transpose(0, 2, 1), far.transpose(0, 2, 1)]
 
     fine_quad_in, fine_quad_out = fine_tables(fine_quad)
     fine_plain_in, fine_plain_out = fine_tables(fine_plain)
-    coarse_quad_in = turn(coarse_quad[0])
-    coarse_plain_in = turn(coarse_plain[0])
+    coarse_quad_in = turn(coarse_quad[0], 1)
+    coarse_plain_in = turn(coarse_plain[0], 1)
     coarse_quad_out = coarse_quad_in.transpose(0, 2, 1)
     coarse_plain_out = coarse_plain_in.transpose(0, 2, 1)
     local_pairs = lax.dynamic_slice_in_dim(pair_slots, lat_rank * pair_dev, pair_dev)
     weight = mix_weight.transpose(0, 1, 3, 2)
 
-    fine_degrees = [n_lat, pair_dev, subs, LANES]
-    coarse_degrees = [n_lat, pair_dev // 2, subs, LANES]
-    fine_waves = [n_lat, fine_dev, subs, LANES]
-    coarse_waves = [n_lat, coarse_two, subs, LANES]
-
-    def to_degrees(coarse_chunk, fine_chunks, coarse_table, fine_pair):
+    fine_degrees = [[n_lat, chunk_pairs, subs, LANES]] * n_chunks
+    coarse_degrees = [[n_lat, pair_dev // 2, subs, LANES]]
+    fine_waves = [[n_lat, count, subs, LANES] for count in row_cuts]
+    coarse_waves = [[n_lat, coarse_two, subs, LANES]]
+
+    def spectral(coarse_chunk, fine_chunks, in_tables, out_tables, backward, aside):
+        fine_made = lane_call(
+            functools.partial(to_degrees_fine_body, pair_dev), "rows_to_degrees",
+            line.hold(fine_chunks), in_tables[1], fine_degrees,
+        )
+        line.keep(fine_made)
+        arrived, mixed, shared = [], [], []
+
+        def mix_chunk(k):
+            fine, coarse = line.hold((arrived[k], arrived_coarse))
+            made = mix(
+                fine, coarse, weight, local_pairs, k * chunk_pairs // 2, backward,
+                mixed[-1][1] if mixed else None,
+            )
+            mixed.append(line.keep(made))
+
+        def share_next(count=1):
+            members = joined_rows([made[2] for made in mixed])
+            for step in range(len(shared), min(len(shared) + count, n_chan)):
+                shared.append(line.keep(share_slots(line.hold(members), n_chan, step)))
+
+        arrived.append(line.swap(fine_made[0]))
         coarse_made = lane_call(
             functools.partial(to_degrees_coarse_body, pair_dev), "rows_to_degrees",
-            [coarse_chunk], [coarse_table], [coarse_degrees],
+            [line.hold(coarse_chunk)], [in_tables[0]], coarse_degrees,
         )[0]
-        fine_made = lane_call(
-            functools.partial(to_degrees_fine_body, pair_dev, len(fine_chunks)), "rows_to_degrees",
-            fine_chunks, list(fine_pair), [fine_degrees],
-        )[0]
-        return swap(coarse_made), swap(fine_made)
-
-    def to_orders(coarse_chunk, fine_chunk, coarse_table, fine_pair):
+        arrived_coarse = line.swap(line.keep(coarse_made))
+        for k in range(1, n_chunks):
+            arrived.append(line.swap(fine_made[k]))
+            mix_chunk(k - 1)
+        if n_chunks == 1:
+            mix_chunk(0)
+        fine_back = []
+        for k in range(n_chunks - 1):
+            fine_back.append(line.swap(mixed[k][0]))
+            mix_chunk(k + 1)
+        arrived_coarse = line.swap(mixed[-1][1])
+        share_next(2)
+        fine_back.append(line.swap(mixed[-1][0]))
+        share_next()
         coarse_made = lane_call(
             functools.partial(to_orders_coarse_body, pair_dev), "degrees_to_rows",
-            [coarse_chunk], [coarse_table], [coarse_waves],
+            [line.hold(arrived_coarse)], [out_tables[0]], coarse_waves,
         )[0]
+        coarse_end = line.swap(line.keep(coarse_made))
+        share_next(n_chan)
         fine_made = lane_call(
-            functools.partial(to_orders_fine_body, pair_dev, 1), "degrees_to_rows",
-            [fine_chunk], list(fine_pair), [fine_waves],
-        )[0]
-        return swap(coarse_made), swap(fine_made)
-
-    coarse_coef, fine_coef = to_degrees(coarse_four, [fine_four], coarse_quad_in, fine_quad_in)
-    fine_mixed, coarse_mixed, members = mix(fine_coef, coarse_coef, weight, local_pairs, False)
-    values = share_slots(members, n_chan)
-    coarse_synth, fine_synth = to_orders(
-        swap(coarse_mixed), swap(fine_mixed), coarse_plain_out, fine_plain_out
-    )
+            functools.partial(to_orders_fine_body, pair_dev), "degrees_to_rows",
+            line.hold(fine_back), out_tables[1], fine_waves,
+        )
+        line.keep(fine_made)
+        fine_end = []
+        for k, made in enumerate(fine_made):
+            fine_end.append(line.swap(made))
+            aside(k, coarse_end, fine_end, shared)
+        return fine_end, shared
 
     params = [
         column(second_gain), column(second_bias), up_weight, up_weight.T, column(up_bias),
         down_weight, down_weight.T, column(down_bias),
     ]
-    coarse_made = pixels(coarse_synth, coarse_x, coarse_g, coarse_inverse, params, 0)
-    fine_made = pixels(fine_synth, fine_x, fine_g, fine_inverse, params, 0)
-    coarse_sgrad, fine_sgrad = swap(coarse_made[2]), swap(fine_made[2])
-    dense = lax.psum(
-        tuple(a + b for a, b in zip(coarse_made[3:], fine_made[3:])), ("lat", "chan")
-    )
-
-    coarse_dgrad, fine_dgrad = to_degrees(
-        coarse_sgrad, [fine_sgrad], coarse_plain_in, fine_plain_in
-    )
-    fine_cgrad, coarse_cgrad, grad_members = mix(
-        fine_dgrad, coarse_dgrad, weight, local_pairs, True
-    )
-    grads = share_slots(grad_members, n_chan)
-    mix_grad = mix_gradient(values, grads).transpose(0, 1, 3, 2)
-    coarse_fgrad, fine_fgrad = to_orders(
-        swap(coarse_cgrad), swap(fine_cgrad), coarse_quad_out, fine_quad_out
-    )
-    coarse_end, coarse_sums = finish(
-        coarse_fgrad, coarse_x, coarse_made[1], coarse_forward, gain_one, 0
-    )
-    fine_end, fine_sums = finish(fine_fgrad, fine_x, fine_made[1], fine_forward, gain_one, 0)
-    first_sums = lax.psum(coarse_sums + fine_sums, ("lat", "chan"))[:, :, 0]
-    up_grad, down_grad, wide_sums, narrow_sums = dense
+    coarse_g, fine_g = coarse_in(coarse_cotangent), fine_in(fine_cotangent)
+    coarse_made, fine_made = [], []
+
+    def fine_pixels(k, synth):
+        into = fine_made[-1][0] if fine_made else None
+        made = pixels(
+            line.hold(synth), fine_x, fine_g, fine_inverse, params, row_starts[k], into
+        )
+        fine_made.append(line.keep(made))
+
+    def forward_aside(k, coarse_end, fine_end, shared):
+        if k == 0:
+            made = pixels(
+                line.hold(coarse_end), coarse_x, coarse_g, coarse_inverse, params, 0, None
+            )
+            coarse_made.extend(line.keep(made))
+        else:
+            if k == 1:
+                coarse_made[0] = line.keep(coarse_back(line.hold(coarse_made[0])))
+            fine_pixels(k - 1, fine_end[k - 1])
+
+    fine_synth, values = spectral(
+        coarse_four, fine_four, (coarse_quad_in, fine_quad_in), (coarse_plain_out, fine_plain_out),
+        False, forward_aside,
+    )
+    if len(row_cuts) == 1:
+        fine_pixels(0, fine_synth[0])
+    fine_sgrad = []
+    for k in range(len(row_cuts)):
+        fine_sgrad.append(line.swap(fine_made[k][2]))
+        if k + 1 < len(row_cuts):
+            fine_pixels(k + 1, fine_synth[k + 1])
+    axes = (("chan", n_chan), ("lat", n_lat))
+    hidden = up_bias.shape[0]
+    total = coarse_made[3:]
+    for made in fine_made:
+        total = [x + y for x, y in zip(total, made[3:])]
+    narrow = jnp.concatenate([total[2][:, 0], total[3].reshape(-1)])
+    narrow = jnp.pad(narrow, (0, -narrow.shape[0] % hidden)).reshape(-1, hidden)
+    dense = []
+    line.aside = add_dense([line.hold(total[0]), total[1], narrow], axes, line, dense)
+    line.step_aside()
+    coarse_sgrad = line.swap(coarse_made[2])
+    if len(row_cuts) == 1:
+        coarse_made[0] = coarse_back(coarse_made[0])
+    ends, mix_grads = [], []
+
+    def backward_aside(k, coarse_end, fine_end, shared):
+        if k == 0:
+            mix_grads.append(line.keep(mix_gradient(values, line.hold(shared))))
+            made = finish(
+                line.hold(coarse_end), coarse_x, coarse_made[1], coarse_forward, gain_one, 0, None
+            )
+        else:
+            if k == 1:
+                ends[0][0] = line.keep(coarse_back(line.hold(ends[0][0])))
+            into = ends[-1][0] if k > 1 else None
+            made = finish(
+                line.hold(fine_end[k - 1]), fine_x, fine_made[k - 1][1], fine_forward, gain_one,
+                row_starts[k - 1], into,
+            )
+        ends.append(list(line.keep(made)))
+
+    fine_fgrad, grads = spectral(
+        coarse_sgrad, fine_sgrad, (coarse_plain_in, fine_plain_in), (coarse_quad_out, fine_quad_out),
+        True, backward_aside,
+    )
+    for unused in line.aside:
+        pass
+    up_grad, down_grad, narrow = dense
+    narrow = narrow.reshape(-1)
+    narrow_sums = narrow[hidden : hidden + 3 * C].reshape(3, C)
+    if len(row_cuts) == 1:
+        ends[0][0] = coarse_back(ends[0][0])
+    into = ends[-1][0] if len(row_cuts) > 1 else None
+    last_wave = lax.optimization_barrier((fine_fgrad[-1], line.work + line.later))[0]
+    ends.append(
+        finish(
+            last_wave, fine_x, fine_made[-1][1], fine_forward, gain_one, row_starts[-1], into
+        )
+    )
+    mix_grad = mix_grads[0].transpose(0, 2, 3, 1)
+    sums = sum(end[1] for end in ends)
+    first_sums = sum_over(sums[:, :, 0], axes)
     return (
-        coarse_back(coarse_made[0]),
-        fine_back(fine_made[0]),
-        coarse_back(coarse_end),
-        fine_back(fine_end),
+        coarse_made[0],
+        fine_back(fine_made[-1][0]),
+        ends[0][0],
+        fine_back(ends[-1][0]),
         first_sums[0],
         first_sums[1],
         mix_grad,
-        narrow_sums[0, :, 0],
-        narrow_sums[1, :, 0],
+        narrow_sums[0],
+        narrow_sums[1],
         up_grad,
-        wide_sums[:, 0],
+        narrow[:hidden],
         down_grad.T,
-        narrow_sums[2, :, 0],
+        narrow_sums[2],
     )
 
 

time: 2890 us -> 2530 us (0.88)
  blocking collectives: 360 us -> 77.4 us
  waiting for transfers between devices: 1500 us -> 1290 us
  starting transfers between devices: 69.3 us -> 135 us
  other arithmetic: 65.8 us -> 111 us
  Pallas kernels: 617 us -> 662 us
    all_to_all x13 -> x23, waiting for transfers between devices: 1240 us -> 724 us  [swap(): lax.all_to_all(values, 'lat', split_axis=0, concat_axis=0, tiled=True)]
    ppermute x6 -> x21, waiting for transfers between devices: 257 us -> 563 us  [the longest x5 247 us: add_dense(): lax.ppermute(jnp.where(upper, low, high), axis, partners(sizes[axis], ste...]
    all_to_all x3 -> x1, blocking collectives: 301 us -> 77.4 us  [swap(): lax.all_to_all(values, 'lat', split_axis=0, concat_axis=0, tiled=True)]
    psum x1 -> x0, blocking collectives: 58.9 us -> none  [shards(): first_sums = lax.psum(coarse_sums + fine_sums, ('lat', 'chan'))[:, :, 0]]
    all_to_all x13 -> x23, starting transfers between devices: 65.6 us -> 113 us  [swap(): lax.all_to_all(values, 'lat', split_axis=0, concat_axis=0, tiled=True)]
    unnamed x82 -> x91, local copies, waits for them, and re-layouts: 107 us -> 65.8 us
    pallas_call x14 -> x20, Pallas kernels: 532 us -> 573 us  [the longest x3 311 us: pixels(): call(body, 'feed_forward', 2 * count * points * (6 * C * hidden + 2 * tab...]
    concatenate x0 -> x5, local copies, waits for them, and re-layouts: none -> 30.7 us  [the longest x1 23 us: add_dense(): jnp.concatenate(wide, axis=0)]
  transfers between devices with their start and end apart: 20 -> 44, of which waited for: 15 -> 32; matrix products, arithmetic and copies ran while one was open for 9% -> 13% of each run, Pallas kernels for 19% -> 25%
where the time goes in v2:
time: 2530 us; the launch traced here: 2520 us
  waiting for transfers between devices  1290 us (51%)
  Pallas kernels  662 us (26%)
  local copies, waits for them, and re-layouts  245 us (10%)
  starting transfers between devices  135 us (5%)
  other arithmetic  111 us (4%)
  blocking collectives  77.4 us (3%)
    all_to_all x23, waiting for transfers between devices, swap(): lax.all_to_all(values, 'lat', split_axis=0, concat_axis=0, tiled=True)  724 us
    pallas_call x3, Pallas kernels, pixels(): call(body, 'feed_forward', 2 * count * points * (6 * C * hidden + 2 * tab...  311 us
    ppermute x5, waiting for transfers between devices, add_dense(): lax.ppermute(jnp.where(upper, low, high), axis, partners(sizes[axis], ste...  247 us
    ppermute x5, waiting for transfers between devices, add_dense(): other = lax.ppermute(held, axis, partners(sizes[axis], step)[0])  170 us
    ppermute x6, waiting for transfers between devices, share_slots(): return lax.ppermute(block, 'chan', route) if step else block  137 us
    all_to_all x23, starting transfers between devices, swap(): lax.all_to_all(values, 'lat', split_axis=0, concat_axis=0, tiled=True)  113 us
    pallas_call x8, Pallas kernels, lane_call(): call(functools.partial(body, len(inputs), len(outs)), name, flops, moved,...  101 us
    pallas_call x4, Pallas kernels, mix(): call(body, 'mix_back' if backward else 'mix', 2 * count * n_lat * subs *...  80.5 us
  transfers between devices with their start and end apart: 44, of which 32 were waited for; matrix products, arithmetic and copies ran while one was open for 13% of the time, Pallas kernels for 25%

profile of v2, /device:TPU:0, one launch (start us, length us, event | category | flops | bytes accessed | tf_op | source)
XLA Modules:
  0.0 2519.0 jit_solution(5202207849228708110)
XLA Ops:
  6.8 17.5 norm_and_dft.3
  24.3 7.2 all-to-all-start
  31.5 16.2 norm_and_dft.4
  47.8 126.2 %all-to-all-done.refs_0_ = bf16[8,12,24,1408]{3,2,1,0:T(8,128)(2,1)} async-done(((bf16[8,12,24,1408]{3,2,1,0:T(8,128)(2,1)}), bf16[8,12,24,1408]{3,2,1,0:T(8,128)(2,1)}, u32[]{:S(2)}, u32[]{:S(2)}) %all-to-all-start) | async-done | bytes 6488096 | tf_op jit(solution)/shard_map/all_to_all | solution.py:690
  179.5 20.7 reduce
  200.2 7.2 reshape_squeeze.9
  207.3 7.5 copy.118
  214.9 8.1 broadcast_in_dim.150.state
  226.2 9.8 norm_and_dft.5
  235.9 72.7 %all-to-all-done.1.refs_1_ = bf16[8,11,24,1408]{3,2,1,0:T(8,128)(2,1)} async-done(((bf16[8,11,24,1408]{3,2,1,0:T(8,128)(2,1)}), bf16[8,11,24,1408]{3,2,1,0:T(8,128)(2,1)}, u32[]{:S(2)}, u32[]{:S(2)}) %all-to-all-start.1) | async-done | bytes 5947424 | tf_op jit(solution)/shard_map/all_to_all | solution.py:690
  316.6 13.2 legendre_tables.2
  358.9 16.3 rows_to_degrees.4
  375.3 10.2 all-to-all-done.2.chunk
  403.5 9.1 rows_to_degrees.5
  412.6 51.2 %all-to-all-done.3.fine = bf16[8,6,24,1408]{3,2,1,0:T(8,128)(2,1)} async-done(((bf16[8,6,24,1408]{3,2,1,0:T(8,128)(2,1)}), bf16[8,6,24,1408]{3,2,1,0:T(8,128)(2,1)}, u32[]{:S(2)}, u32[]{:S(2)}) %all-to-all-start.3) | async-done | bytes 3244064 | tf_op jit(solution)/shard_map/all_to_all | solution.py:690
  463.9 77.4 %all_to_all.120.coarse.refs_2_ = bf16[8,6,24,1408]{3,2,1,0:T(8,128)(2,1)} all-to-all(bf16[8,6,24,1408]{3,2,1,0:T(8,128)(2,1)} %rows_to_degrees.5), channel_id=1, replica_groups=mesh['lat'=8,'chan'=4] {'lat'}, dimensions={0} | all-to-all | bytes 6488064 | tf_op jit(solution)/shard_map/all_to_all | solution.py:690
  546.1 32.3 %copy.180 = bf16[24,2,649,641]{2,3,1,0:T(8,128)(2,1)} copy(bf16[24,2,649,641]{2,1,3,0:T(2,128)(2,1)} %param.27) | data formatting | bytes 79873728 | tf_op args[9]
  578.4 20.1 mix.2
  598.6 18.5 all-to-all-done.5.refs_1_
  623.3 20.1 mix.3
  643.4 52.1 %all-to-all-done.6.refs_0_ = bf16[8,6,24,1408]{3,2,1,0:T(8,128)(2,1)} async-done(((bf16[8,6,24,1408]{3,2,1,0:T(8,128)(2,1)}), bf16[8,6,24,1408]{3,2,1,0:T(8,128)(2,1)}, u32[]{:S(2)}, u32[]{:S(2)}) %all-to-all-start.6) | async-done | bytes 3244064 | tf_op jit(solution)/shard_map/all_to_all | solution.py:690
  718.1 54.0 %all-to-all-done.7.chunk = bf16[8,6,24,1408]{3,2,1,0:T(8,128)(2,1)S(1)} async-done(((bf16[8,6,24,1408]{3,2,1,0:T(8,128)(2,1)}), bf16[8,6,24,1408]{3,2,1,0:T(8,128)(2,1)S(1)}, u32[]{:S(2)}, u32[]{:S(2)}) %all-to-all-start.7) | async-done | bytes 3244064 | tf_op jit(solution)/shard_map/all_to_all | solution.py:690
  786.0 9.1 degrees_to_rows.4
  795.1 58.4 %collective-permute-done.refs_2_ = bf16[6,8,24,1408]{3,2,1,0:T(8,128)(2,1)} collective-permute-done((bf16[6,8,24,1408]{3,2,1,0:T(8,128)(2,1)}, bf16[6,8,24,1408]{3,2,1,0:T(8,128)(2,1)}, u32[]{:S(2)}, u32[]{:S(2)}) %collective-permute-start) | collective-permute-done | bytes 3244064 | tf_op jit(solution)/shard_map/ppermute | solution.py:723
  870.6 16.0 degrees_to_rows.5
  886.6 49.3 %collective-permute-done.2.refs_3_ = bf16[6,8,24,1408]{3,2,1,0:T(8,128)(2,1)} collective-permute-done((bf16[6,8,24,1408]{3,2,1,0:T(8,128)(2,1)}, bf16[6,8,24,1408]{3,2,1,0:T(8,128)(2,1)}, u32[]{:S(2)}, u32[]{:S(2)}) %collective-permute-start.2) | collective-permute-done | bytes 3244064 | tf_op jit(solution)/shard_map/ppermute | solution.py:723
  952.1 20.7 reduce.1
  979.9 7.5 copy.131
  987.4 8.2 broadcast_in_dim.156.cotangent
  996.4 68.3 %feed_forward.3 = (f32[6,641,1,360]{3,2,1,0:T(1,128)}, f32[6,641,360]{2,1,0:T(8,128)}, bf16[8,6,24,1408]{3,2,1,0:T(8,128)(2,1)}, f32[641,1282]{1,0:T(8,128)}, f3...) custom-call(bf16[8,6,24,1408]{3,2,1,0:T(8,128)(2,1)} %all-to-all-done.9.synth, ...), custom_call_target="tpu_custom_call" | custom-call | flops 23848110080 | bytes 28641024 | tf_op jit(solution)/shard_map/feed_forward/pallas_call | solution.py:528
  1064.7 20.1 all-to-all-done.10.synth
  1090.9 8.2 part_rows.2
  1099.1 126.2 %feed_forward.4 = (f32[23,641,1,360]{3,2,1,0:T(1,128)}, f32[12,641,360]{2,1,0:T(8,128)}, bf16[8,12,24,1408]{3,2,1,0:T(8,128)(2,1)}, f32[641,1282]{1,0:T(8,128)},...) custom-call(bf16[8,12,24,1408]{3,2,1,0:T(8,128)(2,1)} %all-to-all-done.10.synth, ...), custom_call_target="tpu_custom_call" | custom-call | flops 47696220160 | bytes 57282048 | tf_op jit(solution)/shard_map/feed_forward/pallas_call | solution.py:528
  1231.6 116.8 %feed_forward.5 = (f32[23,641,1,360]{3,2,1,0:T(1,128)}, f32[11,641,360]{2,1,0:T(8,128)}, bf16[8,11,24,1408]{3,2,1,0:T(8,128)(2,1)}, f32[641,1282]{1,0:T(8,128)},...) custom-call(bf16[8,11,24,1408]{3,2,1,0:T(8,128)(2,1)} %all-to-all-done.11.r, ...), custom_call_target="tpu_custom_call", output_to_operand_aliasing={{0}: (12, {})} | custom-call | flops 43721535488 | bytes 52508544 | tf_op jit(solution)/shard_map/feed_forward/pallas_call | solution.py:528
  1348.4 24.4 all-to-all-done.12.refs_0_
  1391.7 23.0 concatenate.88
  1421.8 86.2 %all-to-all-done.13.refs_1_ = bf16[8,11,24,1408]{3,2,1,0:T(8,128)(2,1)} async-done(((bf16[8,11,24,1408]{3,2,1,0:T(8,128)(2,1)}), bf16[8,11,24,1408]{3,2,1,0:T(8,128)(2,1)}, u32[]{:S(2)}, u32[]{:S(2)}) %all-to-all-start.13) | async-done | bytes 5947424 | tf_op jit(solution)/shard_map/all_to_all | solution.py:690
  1523.2 7.2 collective-permute-done.3
  1536.0 7.4 select_add_fusion
  1543.5 16.3 rows_to_degrees.6
  1559.8 24.8 all-to-all-done.14.chunk
  1595.1 44.2 %collective-permute-done.4 = f32[384,1282]{0,1:T(8,128)} collective-permute-done((f32[384,1282]{0,1:T(8,128)}, f32[384,1282]{0,1:T(8,128)}, u32[]{:S(2)}, u32[]{:S(2)}) %collective-permute-start.4) | collective-permute-done | bytes 1969184 | tf_op jit(solution)/shard_map/ppermute | solution.py:752
  1645.4 9.1 rows_to_degrees.7
  1654.6 8.5 all-to-all-done.15.fine
  1670.6 56.5 %collective-permute-done.5 = f32[192,1282]{1,0:T(8,128)S(1)} collective-permute-done((f32[192,1282]{1,0:T(8,128)S(1)}, f32[192,1282]{1,0:T(8,128)S(1)}, u32[]{:S(2)}, u32[]{:S(2)}) %collective-permute-start.5) | collective-permute-done | bytes 984608 | tf_op jit(solution)/shard_map/ppermute | solution.py:752
  1728.3 11.4 all-to-all-done.16.coarse.refs_2_
  1749.6 60.7 %collective-permute-done.6 = f32[96,1282]{1,0:T(8,128)S(1)} collective-permute-done((f32[96,1282]{1,0:T(8,128)S(1)}, f32[96,1282]{1,0:T(8,128)S(1)}, u32[]{:S(2)}, u32[]{:S(2)}) %collective-permute-start.6) | collective-permute-done | bytes 492320 | tf_op jit(solution)/shard_map/ppermute | solution.py:752
  1812.4 20.1 mix_back.2
  1842.6 78.7 %collective-permute-done.7 = f32[48,1282]{1,0:T(8,128)S(1)} collective-permute-done((f32[48,1282]{1,0:T(8,128)S(1)}, f32[48,1282]{1,0:T(8,128)S(1)}, u32[]{:S(2)}, u32[]{:S(2)}) %collective-permute-start.7) | collective-permute-done | bytes 246176 | tf_op jit(solution)/shard_map/ppermute | solution.py:752
  1922.4 20.1 mix_back.3
  1964.5 62.1 %collective-permute-done.8 = bf16[48,1282]{1,0:T(8,128)(2,1)S(1)} collective-permute-done((bf16[48,1282]{1,0:T(8,128)(2,1)S(1)}, bf16[48,1282]{1,0:T(8,128)(2,1)S(1)}, u32[]{:S(2)}, u32[]{:S(2)}) %collective-permute-start.8) | collective-permute-done | bytes 123104 | tf_op jit(solution)/shard_map/ppermute | solution.py:761
  2037.9 52.8 %collective-permute-done.9 = bf16[96,1282]{1,0:T(8,128)(2,1)} collective-permute-done((bf16[96,1282]{1,0:T(8,128)(2,1)}, bf16[96,1282]{1,0:T(8,128)(2,1)}, u32[]{:S(2)}, u32[]{:S(2)}) %collective-permute-start.9) | collective-permute-done | bytes 246176 | tf_op jit(solution)/shard_map/ppermute | solution.py:761
  2092.6 9.1 degrees_to_rows.6
  2121.9 34.3 %collective-permute-done.12 = bf16[192,1282]{1,0:T(8,128)(2,1)S(1)} collective-permute-done((bf16[192,1282]{1,0:T(8,128)(2,1)S(1)}, bf16[192,1282]{1,0:T(8,128)(2,1)S(1)}, u32[]{:S(2)}, u32[]{:S(2)}) %collective-permute-start.12) | collective-permute-done | bytes 492320 | tf_op jit(solution)/shard_map/ppermute | solution.py:761
  2156.4 16.1 degrees_to_rows.7
  2172.4 18.0 collective-permute-done.13.refs_7_
  2196.4 14.3 first_norm_back.3
  2210.7 27.4 %mix_gradient.1 = f32[6,641,2,649]{3,2,1,0:T(2,128)} custom-call(bf16[6,8,24,1408]{3,2,1,0:T(8,128)(2,1)} %get-tuple-element.262.refs_0_, bf16[6,8,24,1408]{3,2,1,0:T(8,128)(2,1)} %collective-permute-done.1.refs_1_, bf16[6,8,24,1408]{3,2,1,0:T(8,128)(2,1)} %collective-permute-done.refs_2_, bf16[6,8,24,1408]{3,2,1,0:T(8,128)(2,1)} %collective-permute-done.2.refs_3_, ...), custom_call_target="tpu_custom_call" | custom-call | flops 15335755776 | bytes 45920688 | tf_op jit(solution)/shard_map/mix_gradient/pallas_call | solution.py:449
  2238.1 99.8 %all-to-all-done.22.wave = bf16[8,12,24,1408]{3,2,1,0:T(8,128)(2,1)} async-done(((bf16[8,12,24,1408]{3,2,1,0:T(8,128)(2,1)}), bf16[8,12,24,1408]{3,2,1,0:T(8,128)(2,1)}, u32[]{:S(2)}, u32[]{:S(2)}) %all-to-all-start.22) | async-done | bytes 6488096 | tf_op jit(solution)/shard_map/all_to_all | solution.py:690
  2346.5 21.1 collective-permute-done.14
  2371.3 8.2 part_rows.3
  2379.5 25.5 %first_norm_back.4 = (f32[23,641,1,360]{3,2,1,0:T(1,128)}, f32[2,641,1]{2,1,0:T(8,128)}) custom-call(bf16[8,12,24,1408]{3,2,1,0:T(8,128)(2,1)} %all-to-all-done.22.wave, f32[23,641,1,360]{3,2,1,0:T(1,128)} %bitcast.80, f32[12,641,360]{2,1,0:T(8,128)} %get-tuple-element.186.middle_grad, bf16[384,360]{1,0:T(8,128)(2,1)} %pad_maximum_fusion.5.table.refs_3_, ...), custom_call_target="tpu_custom_call" | custom-call | flops 2548039680 | bytes 39717504 | tf_op jit(solution)/shard_map/first_norm_back/pallas_call | solution.py:595
  2409.1 63.7 %all-to-all-done.23.refs_0_ = bf16[8,11,24,1408]{3,2,1,0:T(8,128)(2,1)} async-done(((bf16[8,11,24,1408]{3,2,1,0:T(8,128)(2,1)}), bf16[8,11,24,1408]{3,2,1,0:T(8,128)(2,1)}, u32[]{:S(2)}, u32[]{:S(2)}) %all-to-all-start.23) | async-done | bytes 5947424 | tf_op jit(solution)/shard_map/all_to_all | solution.py:690
  2472.9 23.8 first_norm_back.5
  (297 shorter events, 365.5 us)
Async XLA Ops:
  24.3 149.7 %all-to-all-start = ((bf16[8,12,24,1408]{3,2,1,0:T(8,128)(2,1)}), bf16[8,12,24,1408]{3,2,1,0:T(8,128)(2,1)}, u32[]{:S(2)}, u32[]{:S(2)}) async-start(bf16[8,12,24,1408]{3,2,1,0:T(8,128)(2,1)} %norm_and_dft.3), calls=%async_computation | async-start | bytes 12976128 | tf_op jit(solution)/shard_map/all_to_all | solution.py:690
  47.7 131.0 %copy-start.34 = (s32[1,12,180,8]{2,3,1,0:T(8,128)S(1)}, s32[1,12,180,8]{2,3,1,0:T(8,128)}, u32[]{:S(2)}) copy-start(s32[1,12,180,8]{2,3,1,0:T(8,128)} %param.20) | copy-start | bytes 207364
  174.0 134.7 %all-to-all-start.1 = ((bf16[8,11,24,1408]{3,2,1,0:T(8,128)(2,1)}), bf16[8,11,24,1408]{3,2,1,0:T(8,128)(2,1)}, u32[]{:S(2)}, u32[]{:S(2)}) async-start(bf16[8,11,24,1408]{3,2,1,0:T(8,128)(2,1)} %norm_and_dft.4), calls=%async_computation.1 | async-start | bytes 11894784 | tf_op jit(solution)/shard_map/all_to_all | solution.py:690
  235.9 76.6 %copy-start.40 = (s32[184]{0:T(256)S(1)}, s32[184]{0:T(256)}, u32[]{:S(2)}) copy-start(s32[184]{0:T(256)} %param.23) | copy-start | bytes 2212
  308.7 76.8 %all-to-all-start.2 = ((bf16[8,6,24,1408]{3,2,1,0:T(8,128)(2,1)}), bf16[8,6,24,1408]{3,2,1,0:T(8,128)(2,1)S(1)}, u32[]{:S(2)}, u32[]{:S(2)}) async-start(bf16[8,6,24,1408]{3,2,1,0:T(8,128)(2,1)} %norm_and_dft.5), calls=%async_computation.2 | async-start | bytes 6488064 | tf_op jit(solution)/shard_map/all_to_all | solution.py:690
  385.4 6.2 copy-start.41
  387.1 76.8 %all-to-all-start.3 = ((bf16[8,6,24,1408]{3,2,1,0:T(8,128)(2,1)}), bf16[8,6,24,1408]{3,2,1,0:T(8,128)(2,1)}, u32[]{:S(2)}, u32[]{:S(2)}) async-start(bf16[8,6,24,1408]{3,2,1,0:T(8,128)(2,1)} %get-tuple-element.145), calls=%async_computation.3 | async-start | bytes 6488064 | tf_op jit(solution)/shard_map/all_to_all | solution.py:690
  541.3 75.8 %all-to-all-start.5 = ((bf16[8,6,24,1408]{3,2,1,0:T(8,128)(2,1)}), bf16[8,6,24,1408]{3,2,1,0:T(8,128)(2,1)S(1)}, u32[]{:S(2)}, u32[]{:S(2)}) async-start(bf16[8,6,24,1408]{3,2,1,0:T(8,128)(2,1)} %get-tuple-element.147), calls=%async_computation.5 | async-start | bytes 6488064 | tf_op jit(solution)/shard_map/all_to_all | solution.py:690
  618.8 76.8 %all-to-all-start.6 = ((bf16[8,6,24,1408]{3,2,1,0:T(8,128)(2,1)}), bf16[8,6,24,1408]{3,2,1,0:T(8,128)(2,1)}, u32[]{:S(2)}, u32[]{:S(2)}) async-start(bf16[8,6,24,1408]{3,2,1,0:T(8,128)(2,1)} %get-tuple-element.158), calls=%async_computation.6 | async-start | bytes 6488064 | tf_op jit(solution)/shard_map/all_to_all | solution.py:690
  695.5 76.6 %all-to-all-start.7 = ((bf16[8,6,24,1408]{3,2,1,0:T(8,128)(2,1)}), bf16[8,6,24,1408]{3,2,1,0:T(8,128)(2,1)S(1)}, u32[]{:S(2)}, u32[]{:S(2)}) async-start(bf16[8,6,24,1408]{3,2,1,0:T(8,128)(2,1)} %get-tuple-element.159), calls=%async_computation.7 | async-start | bytes 6488064 | tf_op jit(solution)/shard_map/all_to_all | solution.py:690
  712.2 5.9 collective-permute-start.1
  773.8 79.7 %all-to-all-start.8 = ((bf16[8,6,24,1408]{3,2,1,0:T(8,128)(2,1)}), bf16[8,6,24,1408]{3,2,1,0:T(8,128)(2,1)S(1)}, u32[]{:S(2)}, u32[]{:S(2)}) async-start(bf16[8,6,24,1408]{3,2,1,0:T(8,128)(2,1)} %get-tuple-element.163), calls=%async_computation.8 | async-start | bytes 6488064 | tf_op jit(solution)/shard_map/all_to_all | solution.py:690
  781.4 72.1 %collective-permute-start = (bf16[6,8,24,1408]{3,2,1,0:T(8,128)(2,1)}, bf16[6,8,24,1408]{3,2,1,0:T(8,128)(2,1)}, u32[]{:S(2)}, u32[]{:S(2)}) collective-permute-start(bf16[6,8,24,1408]{3,2,1,0:T(8,128)(2,1)} %constant_dynamic-slice_fusion.7), channel_id=1, source_target_pairs={{0,2},{1,3},{2,0},{3,1},{4,6},{5,7},{6,4},{7,5},{8,10},{9,11},{10,... | collective-permute-start | bytes 9732104 | tf_op jit(solution)/shard_map/ppermute | solution.py:723
  785.1 10.0 copy-start.21
  853.6 82.4 %all-to-all-start.9 = ((bf16[8,6,24,1408]{3,2,1,0:T(8,128)(2,1)}), bf16[8,6,24,1408]{3,2,1,0:T(8,128)(2,1)}, u32[]{:S(2)}, u32[]{:S(2)}) async-start(bf16[8,6,24,1408]{3,2,1,0:T(8,128)(2,1)} %degrees_to_rows.4), calls=%async_computation.9 | async-start | bytes 6488064 | tf_op jit(solution)/shard_map/all_to_all | solution.py:690
  863.2 72.8 %collective-permute-start.2 = (bf16[6,8,24,1408]{3,2,1,0:T(8,128)(2,1)}, bf16[6,8,24,1408]{3,2,1,0:T(8,128)(2,1)}, u32[]{:S(2)}, u32[]{:S(2)}) collective-permute-start(bf16[6,8,24,1408]{3,2,1,0:T(8,128)(2,1)} %constant_dynamic-slice_fusion.4), channel_id=1, source_target_pairs={{0,3},{1,2},{2,1},{3,0},{4,7},{5,6},{6,5},{7,4},{8,11},{9,10},{10,... | collective-permute-start | bytes 9732104 | tf_op jit(solution)/shard_map/ppermute | solution.py:723
  869.1 17.5 copy-start.11
  936.0 6.1 copy-start.36
  936.0 7.0 copy-start.37
  936.0 7.9 copy-start.38
  936.0 8.8 copy-start.35
  936.0 148.8 %all-to-all-start.10 = ((bf16[8,12,24,1408]{3,2,1,0:T(8,128)(2,1)}), bf16[8,12,24,1408]{3,2,1,0:T(8,128)(2,1)}, u32[]{:S(2)}, u32[]{:S(2)}) async-start(bf16[8,12,24,1408]{3,2,1,0:T(8,128)(2,1)} %get-tuple-element.172), calls=%async_computation.10 | async-start | bytes 12976128 | tf_op jit(solution)/shard_map/all_to_all | solution.py:690
  942.1 7.5 copy-start.23
  987.4 8.2 copy-start.32
  987.4 8.2 copy-start.33
  1084.8 140.5 %all-to-all-start.11 = ((bf16[8,11,24,1408]{3,2,1,0:T(8,128)(2,1)}), bf16[8,11,24,1408]{3,2,1,0:T(8,128)(2,1)}, u32[]{:S(2)}, u32[]{:S(2)}) async-start(bf16[8,11,24,1408]{3,2,1,0:T(8,128)(2,1)} %get-tuple-element.180), calls=%async_computation.11 | async-start | bytes 11894784 | tf_op jit(solution)/shard_map/all_to_all | solution.py:690
  1225.3 147.5 %all-to-all-start.12 = ((bf16[8,12,24,1408]{3,2,1,0:T(8,128)(2,1)}), bf16[8,12,24,1408]{3,2,1,0:T(8,128)(2,1)}, u32[]{:S(2)}, u32[]{:S(2)}) async-start(bf16[8,12,24,1408]{3,2,1,0:T(8,128)(2,1)} %get-tuple-element.191), calls=%async_computation.12 | async-start | bytes 12976128 | tf_op jit(solution)/shard_map/all_to_all | solution.py:690
  1372.8 135.2 %all-to-all-start.13 = ((bf16[8,11,24,1408]{3,2,1,0:T(8,128)(2,1)}), bf16[8,11,24,1408]{3,2,1,0:T(8,128)(2,1)}, u32[]{:S(2)}, u32[]{:S(2)}) async-start(bf16[8,11,24,1408]{3,2,1,0:T(8,128)(2,1)} %get-tuple-element.198), calls=%async_computation.13 | async-start | bytes 11894784 | tf_op jit(solution)/shard_map/all_to_all | solution.py:690
  1380.5 6.7 copy-start.14
  1380.5 7.5 copy-start.15
  1380.5 8.7 copy-start.16
  1508.0 76.6 %all-to-all-start.14 = ((bf16[8,6,24,1408]{3,2,1,0:T(8,128)(2,1)}), bf16[8,6,24,1408]{3,2,1,0:T(8,128)(2,1)S(1)}, u32[]{:S(2)}, u32[]{:S(2)}) async-start(bf16[8,6,24,1408]{3,2,1,0:T(8,128)(2,1)} %get-tuple-element.205), calls=%async_computation.14 | async-start | bytes 6488064 | tf_op jit(solution)/shard_map/all_to_all | solution.py:690
  1523.2 7.2 collective-permute-start.3
  1586.3 76.8 %all-to-all-start.15 = ((bf16[8,6,24,1408]{3,2,1,0:T(8,128)(2,1)}), bf16[8,6,24,1408]{3,2,1,0:T(8,128)(2,1)}, u32[]{:S(2)}, u32[]{:S(2)}) async-start(bf16[8,6,24,1408]{3,2,1,0:T(8,128)(2,1)} %get-tuple-element.209), calls=%async_computation.15 | async-start | bytes 6488064 | tf_op jit(solution)/shard_map/all_to_all | solution.py:690
  1595.1 44.2 %collective-permute-start.4 = (f32[384,1282]{0,1:T(8,128)}, f32[384,1282]{0,1:T(8,128)}, u32[]{:S(2)}, u32[]{:S(2)}) collective-permute-start(f32[384,1282]{0,1:T(8,128)} %copy.155), channel_id=1, source_target_pairs={{0,2},{1,3},{2,0},{3,1},{4,6},{5,7},{6,4},{7,5},{8,10},{9,11},{10,... | collective-permute-start | bytes 5907464 | tf_op jit(solution)/shard_map/ppermute | solution.py:752
  1663.0 76.6 %all-to-all-start.16 = ((bf16[8,6,24,1408]{3,2,1,0:T(8,128)(2,1)}), bf16[8,6,24,1408]{3,2,1,0:T(8,128)(2,1)S(1)}, u32[]{:S(2)}, u32[]{:S(2)}) async-start(bf16[8,6,24,1408]{3,2,1,0:T(8,128)(2,1)} %rows_to_degrees.7), calls=%async_computation.16 | async-start | bytes 6488064 | tf_op jit(solution)/shard_map/all_to_all | solution.py:690
  1666.7 60.4 %copy-start.3 = (f32[384,1282]{1,0:T(8,128)S(1)}, f32[384,1282]{1,0:T(8,128)}, u32[]{:S(2)}) copy-start(f32[384,1282]{1,0:T(8,128)} %select_add_fusion.1) | copy-start | bytes 5907460
  1668.5 58.6 %collective-permute-start.5 = (f32[192,1282]{1,0:T(8,128)S(1)}, f32[192,1282]{1,0:T(8,128)S(1)}, u32[]{:S(2)}, u32[]{:S(2)}) collective-permute-start(f32[192,1282]{1,0:T(8,128)S(1)} %slice_select_fusion.2), channel_id=1, source_target_pairs={{0,4},{4,0},{8,12},{12,8},{16,20},{20,16},{24,28},{28,24},{1,5},{5... | collective-permute-start | bytes 2953736 | tf_op jit(solution)/shard_map/ppermute | solution.py:752
  1741.3 91.2 %all-to-all-start.17 = ((bf16[8,6,24,1408]{3,2,1,0:T(8,128)(2,1)}), bf16[8,6,24,1408]{3,2,1,0:T(8,128)(2,1)}, u32[]{:S(2)}, u32[]{:S(2)}) async-start(bf16[8,6,24,1408]{3,2,1,0:T(8,128)(2,1)} %get-tuple-element.211), calls=%async_computation.17 | async-start | bytes 6488064 | tf_op jit(solution)/shard_map/all_to_all | solution.py:690
  1747.5 62.8 %collective-permute-start.6 = (f32[96,1282]{1,0:T(8,128)S(1)}, f32[96,1282]{1,0:T(8,128)S(1)}, u32[]{:S(2)}, u32[]{:S(2)}) collective-permute-start(f32[96,1282]{1,0:T(8,128)S(1)} %slice_select_fusion.3), channel_id=1, source_target_pairs={{0,8},{4,12},{8,0},{12,4},{16,24},{20,28},{24,16},{28,20},{1,9},{5... | collective-permute-start | bytes 1476872 | tf_op jit(solution)/shard_map/ppermute | solution.py:752
  1832.6 110.0 %all-to-all-start.18 = ((bf16[8,6,24,1408]{3,2,1,0:T(8,128)(2,1)}), bf16[8,6,24,1408]{3,2,1,0:T(8,128)(2,1)S(1)}, u32[]{:S(2)}, u32[]{:S(2)}) async-start(bf16[8,6,24,1408]{3,2,1,0:T(8,128)(2,1)} %get-tuple-element.224), calls=%async_computation.18 | async-start | bytes 6488064 | tf_op jit(solution)/shard_map/all_to_all | solution.py:690
  1839.7 81.6 %collective-permute-start.7 = (f32[48,1282]{1,0:T(8,128)S(1)}, f32[48,1282]{1,0:T(8,128)S(1)}, u32[]{:S(2)}, u32[]{:S(2)}) collective-permute-start(f32[48,1282]{1,0:T(8,128)S(1)} %slice_select_fusion.4), channel_id=1, source_target_pairs={{0,16},{4,20},{8,24},{12,28},{16,0},{20,4},{24,8},{28,12},{1,17},{... | collective-permute-start | bytes 738440 | tf_op jit(solution)/shard_map/ppermute | solution.py:752
  1944.2 83.2 %all-to-all-start.19 = ((bf16[8,6,24,1408]{3,2,1,0:T(8,128)(2,1)}), bf16[8,6,24,1408]{3,2,1,0:T(8,128)(2,1)}, u32[]{:S(2)}, u32[]{:S(2)}) async-start(bf16[8,6,24,1408]{3,2,1,0:T(8,128)(2,1)} %get-tuple-element.225), calls=%async_computation.19 | async-start | bytes 6488064 | tf_op jit(solution)/shard_map/all_to_all | solution.py:690
  1961.7 65.7 %collective-permute-start.11 = (bf16[6,8,24,1408]{3,2,1,0:T(8,128)(2,1)S(1)}, bf16[6,8,24,1408]{3,2,1,0:T(8,128)(2,1)}, u32[]{:S(2)}, u32[]{:S(2)}) collective-permute-start(bf16[6,8,24,1408]{3,2,1,0:T(8,128)(2,1)S(1)} %get-tuple-element.259), channel_id=1, source_target_pairs={{0,1},{1,0},{2,3},{3,2},{4,5},{5,4},{6,7},{7,6},{8,9},{9,8},{10,11... | collective-permute-start | bytes 9732104 | tf_op jit(solution)/shard_map/ppermute | solution.py:723
  1961.7 64.9 %collective-permute-start.8 = (bf16[48,1282]{1,0:T(8,128)(2,1)S(1)}, bf16[48,1282]{1,0:T(8,128)(2,1)S(1)}, u32[]{:S(2)}, u32[]{:S(2)}) collective-permute-start(bf16[48,1282]{1,0:T(8,128)(2,1)S(1)} %select_add_fusion.4), channel_id=1, source_target_pairs={{0,16},{4,20},{8,24},{12,28},{16,0},{20,4},{24,8},{28,12},{1,17},{... | collective-permute-start | bytes 369224 | tf_op jit(solution)/shard_map/ppermute | solution.py:761
  2027.4 79.7 %all-to-all-start.20 = ((bf16[8,6,24,1408]{3,2,1,0:T(8,128)(2,1)}), bf16[8,6,24,1408]{3,2,1,0:T(8,128)(2,1)S(1)}, u32[]{:S(2)}, u32[]{:S(2)}) async-start(bf16[8,6,24,1408]{3,2,1,0:T(8,128)(2,1)} %get-tuple-element.231), calls=%async_computation.20 | async-start | bytes 6488064 | tf_op jit(solution)/shard_map/all_to_all | solution.py:690
  2031.1 5.9 copy-start.20
  2035.0 72.1 %collective-permute-start.10 = (bf16[6,8,24,1408]{3,2,1,0:T(8,128)(2,1)}, bf16[6,8,24,1408]{3,2,1,0:T(8,128)(2,1)}, u32[]{:S(2)}, u32[]{:S(2)}) collective-permute-start(bf16[6,8,24,1408]{3,2,1,0:T(8,128)(2,1)} %constant_dynamic-slice_fusion.3), channel_id=1, source_target_pairs={{0,2},{1,3},{2,0},{3,1},{4,6},{5,7},{6,4},{7,5},{8,10},{9,11},{10,... | collective-permute-start | bytes 9732104 | tf_op jit(solution)/shard_map/ppermute | solution.py:723
  2035.0 55.6 %collective-permute-start.9 = (bf16[96,1282]{1,0:T(8,128)(2,1)}, bf16[96,1282]{1,0:T(8,128)(2,1)}, u32[]{:S(2)}, u32[]{:S(2)}) collective-permute-start(bf16[96,1282]{1,0:T(8,128)(2,1)} %pad_maximum_fusion.9), channel_id=1, source_target_pairs={{0,8},{4,12},{8,0},{12,4},{16,24},{20,28},{24,16},{28,20},{1,9},{5... | collective-permute-start | bytes 738440 | tf_op jit(solution)/shard_map/ppermute | solution.py:761
  2108.9 81.6 %all-to-all-start.21 = ((bf16[8,6,24,1408]{3,2,1,0:T(8,128)(2,1)}), bf16[8,6,24,1408]{3,2,1,0:T(8,128)(2,1)}, u32[]{:S(2)}, u32[]{:S(2)}) async-start(bf16[8,6,24,1408]{3,2,1,0:T(8,128)(2,1)} %degrees_to_rows.6), calls=%async_computation.21 | async-start | bytes 6488064 | tf_op jit(solution)/shard_map/all_to_all | solution.py:690
  2114.8 6.0 copy-start.12
  2118.8 71.7 %collective-permute-start.13 = (bf16[6,8,24,1408]{3,2,1,0:T(8,128)(2,1)}, bf16[6,8,24,1408]{3,2,1,0:T(8,128)(2,1)}, u32[]{:S(2)}, u32[]{:S(2)}) collective-permute-start(bf16[6,8,24,1408]{3,2,1,0:T(8,128)(2,1)} %constant_dynamic-slice_fusion), channel_id=1, source_target_pairs={{0,3},{1,2},{2,1},{3,0},{4,7},{5,6},{6,5},{7,4},{8,11},{9,10},{10,... | collective-permute-start | bytes 9732104 | tf_op jit(solution)/shard_map/ppermute | solution.py:723
  2118.8 37.4 %collective-permute-start.12 = (bf16[192,1282]{1,0:T(8,128)(2,1)S(1)}, bf16[192,1282]{1,0:T(8,128)(2,1)S(1)}, u32[]{:S(2)}, u32[]{:S(2)}) collective-permute-start(bf16[192,1282]{1,0:T(8,128)(2,1)S(1)} %copy-done.22), channel_id=1, source_target_pairs={{0,4},{4,0},{8,12},{12,8},{16,20},{20,16},{24,28},{28,24},{1,5},{5... | collective-permute-start | bytes 1476872 | tf_op jit(solution)/shard_map/ppermute | solution.py:761
  2190.4 147.5 %all-to-all-start.22 = ((bf16[8,12,24,1408]{3,2,1,0:T(8,128)(2,1)}), bf16[8,12,24,1408]{3,2,1,0:T(8,128)(2,1)}, u32[]{:S(2)}, u32[]{:S(2)}) async-start(bf16[8,12,24,1408]{3,2,1,0:T(8,128)(2,1)} %get-tuple-element.241), calls=%async_computation.22 | async-start | bytes 12976128 | tf_op jit(solution)/shard_map/all_to_all | solution.py:690
  2338.0 134.9 %all-to-all-start.23 = ((bf16[8,11,24,1408]{3,2,1,0:T(8,128)(2,1)}), bf16[8,11,24,1408]{3,2,1,0:T(8,128)(2,1)}, u32[]{:S(2)}, u32[]{:S(2)}) async-start(bf16[8,11,24,1408]{3,2,1,0:T(8,128)(2,1)} %get-tuple-element.248), calls=%async_computation.23 | async-start | bytes 11894784 | tf_op jit(solution)/shard_map/all_to_all | solution.py:690
  2344.1 23.5 collective-permute-start.14
  2371.3 33.7 %collective-permute-start.15 = (bf16[768,1282]{0,1:T(8,128)(2,1)}, bf16[768,1282]{0,1:T(8,128)(2,1)}, u32[]{:S(2)}, u32[]{:S(2)}) collective-permute-start(bf16[768,1282]{0,1:T(8,128)(2,1)} %copy.164), channel_id=1, source_target_pairs={{0,1},{1,0},{2,3},{3,2},{4,5},{5,4},{6,7},{7,6},{8,9},{9,8},{10,11... | collective-permute-start | bytes 5907464 | tf_op jit(solution)/shard_map/ppermute | solution.py:761
  2472.9 23.8 copy-start.28
  2472.9 23.8 copy-start.29
  2498.0 2.1 collective-permute-start.16
  2500.1 6.2 collective-permute-start.17
  2506.3 3.7 collective-permute-start.18
  2510.0 3.6 collective-permute-start.19
  2513.7 4.5 collective-permute-start.20
  (22 other events, 79.5 us)

commit v3 on v2

--- a/solution.py
+++ b/solution.py
@@ -17,7 +17,8 @@
 TILE = 128
 MAIN = C // TILE * TILE
 HALF = TILE // 2
-LANES = 2 * MAIN + TILE
+WHOLE = 2 * MAIN
+LANES = WHOLE + TILE
 PADDED = MAIN + TILE
 
 epsilon = 1e-05
@@ -28,10 +29,10 @@
 
 
 def call(body, name, flops, moved, **options):
-    scratch = options.pop("scratch_shapes", [])
+    if "grid_spec" not in options:
+        options.setdefault("scratch_shapes", [])
     return pl.pallas_call(
         body,
-        scratch_shapes=scratch,
         compiler_params=pltpu.CompilerParams(vmem_limit_bytes=VMEM_LIMIT),
         cost_estimate=pl.CostEstimate(flops=int(flops), bytes_accessed=int(moved), transcendentals=0),
         name=name,
@@ -39,14 +40,16 @@
     )
 
 
-def filled(body, into, position, output=0):
+def filled(body, into, position, *outputs):
     if into is None:
         return body, [], {}
+    count = len(outputs)
 
     def skipping(*refs):
-        body(*refs[:position], *refs[position + 1 :])
-
-    return skipping, [pl.BlockSpec(memory_space=pl.ANY)], {position: output}
+        body(*refs[:position], *refs[position + count :])
+
+    alias = {position + k: output for k, output in enumerate(outputs)}
+    return skipping, [pl.BlockSpec(memory_space=pl.ANY)] * count, alias
 
 
 def dot(left, right, left_dim, right_dim):
@@ -77,6 +80,37 @@
     return real, imag
 
 
+def packing(rows, width):
+    share = HALF // width
+    return share, -(-rows // share)
+
+
+def eights(rows, subs):
+    return rows * (subs // 8) + 1
+
+
+def packed_group(tail, group, subs):
+    count = subs // 8
+    tiles = [tail[:, :, (group * count + k) * TILE :][:, :, :TILE] for k in range(count)]
+    return jnp.stack(tiles, axis=1).reshape(-1, TILE)
+
+
+def unpacked(group_tile, place, width):
+    turned = pltpu.roll(group_tile, (TILE - place * width) % TILE, 1)
+    lane = lax.broadcasted_iota(jnp.int32, turned.shape, 1)
+    return jnp.where(lane % HALF < width, turned, 0.0)
+
+
+def last_eight(groups, n_lat, subs):
+    count = subs // 8
+    tiles = []
+    for group in groups:
+        split = group.reshape(n_lat, count, 8, TILE)
+        tiles += [split[:, k] for k in range(count)]
+    blank = jnp.zeros((n_lat, 8, TILE), f32)
+    return jnp.concatenate(tiles + [blank] * (WHOLE // TILE - len(tiles)), axis=2)
+
+
 def flat(block):
     return block.astype(f32).reshape(-1, block.shape[-1])
 
@@ -92,40 +126,58 @@
     return centered * scale, scale
 
 
-def spread_body(state, noise, gain, bias, table, out, held):
-    @pl.when(pl.program_id(0) == 0)
+def spread_body(state, noise, gain, bias, table, out, held, tails):
+    step, last = pl.program_id(0), pl.num_programs(0) - 1
+    n_lat, count, unused, lanes = out.shape
+    width = WIDE - MAIN
+    share = HALF // width
+
+    @pl.when(step == 0)
     def _():
         held[...] = jnp.zeros_like(held)
-
-    xhat, unused = norm_stats(state[0][:, 0, :])
-    held[:C] = xhat * gain[...] + bias[...]
-    held[C:WIDE] = ((noise[0].astype(f32) + 0.5) * noise_scale - 0.5) * math.sqrt(12.0)
-    result = dot(table[...], held[...].astype(bf16), 1, 1)
-    rows = result.shape[0] // 2
-    joined = join_parts(result[:rows], result[rows:], WIDE)
-    out[:, 0] = joined.reshape(out.shape[0], out.shape[2], LANES).astype(bf16)
+        tails[...] = jnp.zeros_like(tails)
+
+    @pl.when(step < last)
+    def _():
+        xhat, unused = norm_stats(state[0][:, 0, :])
+        held[:C] = xhat * gain[...] + bias[...]
+        held[C:WIDE] = ((noise[0].astype(f32) + 0.5) * noise_scale - 0.5) * math.sqrt(12.0)
+        result = dot(table[...], held[...].astype(bf16), 1, 1)
+        rows = result.shape[0] // 2
+        joined = join_parts(result[:rows], result[rows:], WIDE)
+        out[...] = joined[:, :WHOLE].reshape(out.shape).astype(bf16)
+        tails[step // share] += pltpu.roll(joined[:, WHOLE:], step % share * width, 1)
+
+    @pl.when(step == last)
+    def _():
+        groups = [tails[k] for k in range(tails.shape[0])]
+        out[:, 0] = last_eight(groups, n_lat, 8 * count).astype(bf16)
 
 
 def spread(state, noise, gain, bias, table, n_lat, first, count):
     points = state.shape[3]
     subs = table.shape[0] // (2 * n_lat)
     const = lambda r: (0, 0)
+    row = lambda r: jnp.minimum(r, count - 1) + first
     return call(
         spread_body,
         "norm_and_dft",
         2 * count * table.shape[0] * points * PADDED,
         count * (C * points * 4 + n_lat * subs * LANES * 2),
-        grid=(count,),
+        grid=(count + 1,),
         in_specs=[
-            pl.BlockSpec((1, C, 1, points), lambda r: (r + first, 0, 0, 0)),
-            pl.BlockSpec((1, NOISE, points), lambda r: (r + first, 0, 0)),
+            pl.BlockSpec((1, C, 1, points), lambda r: (row(r), 0, 0, 0)),
+            pl.BlockSpec((1, NOISE, points), lambda r: (row(r), 0, 0)),
             pl.BlockSpec((C, 1), const),
             pl.BlockSpec((C, 1), const),
             pl.BlockSpec(table.shape, const),
         ],
-        out_specs=pl.BlockSpec((n_lat, 1, subs, LANES), lambda r: (0, r, 0, 0)),
-        out_shape=jax.ShapeDtypeStruct((n_lat, count, subs, LANES), bf16),
-        scratch_shapes=[pltpu.VMEM((PADDED, points), f32)],
+        out_specs=pl.BlockSpec((n_lat, subs // 8, 8, WHOLE), lambda r: (0, r, 0, 0)),
+        out_shape=jax.ShapeDtypeStruct((n_lat, eights(count, subs), 8, WHOLE), bf16),
+        scratch_shapes=[
+            pltpu.VMEM((PADDED, points), f32),
+            pltpu.VMEM((packing(count, WIDE - MAIN)[1], n_lat * subs, TILE), f32),
+        ],
     )(state, noise, gain, bias, table)
 
 
@@ -234,16 +286,9 @@
     return moved.reshape(pair_dev, n_lat * pair_dev, table.shape[2]).astype(bf16)
 
 
-def to_degrees_fine_body(pair_dev, n_in, n_out, *refs):
-    chunks, (table_a, table_b), rest = refs[:n_in], refs[n_in : n_in + 2], refs[n_in + 2 :]
-    outs, held, results = rest[:n_out], rest[n_out : n_out + n_in], rest[n_out + n_in :]
-    n_lat, unused, subs, lanes = outs[0].shape
-    half = n_lat * pair_dev // 2
-    for chunk, keep in zip(chunks, held):
-        keep[...] = flat(chunk[...])
-    if subs != 2 * pair_dev:
-        for result in results:
-            result[...] = jnp.zeros_like(result)
+def to_degrees_fine(pair_dev, subs, tables, held, results):
+    table_a, table_b = tables
+    half = sum(result.shape[0] for result in results) // (2 * subs)
 
     def order_rows(sub):
         parts = [keep[pl.ds(sub, keep.shape[0] // subs, stride=subs), :] for keep in held]
@@ -262,37 +307,10 @@
                 begin += count
                 result[pl.ds(start + (1 - odd) * pair_dev, count, stride=2 * subs), :] = first[rows]
                 result[pl.ds(start + odd * pair_dev, count, stride=2 * subs), :] = second[rows]
-    for out, result in zip(outs, results):
-        out[...] = result[...].reshape(out.shape).astype(bf16)
-
-
-def to_degrees_coarse_body(pair_dev, n_in, n_out, chunk, table, out, held, result):
-    n_lat, unused, subs, lanes = out.shape
-    held[...] = flat(chunk[...])
-    if subs != 2 * pair_dev:
-        result[...] = jnp.zeros_like(result)
-    rows, half = held.shape[0] // subs, result.shape[0] // subs
-    for index in range(pair_dev):
-        taken = joined_rows(
-            [held[pl.ds(odd * pair_dev + index, rows, stride=subs), :] for odd in range(2)]
-        ).astype(bf16)
-        made = dot(table[index], taken, 1, 0)
-        for odd in range(2):
-            result[pl.ds(odd * pair_dev + index, half, stride=subs), :] = made[
-                odd * half : (odd + 1) * half
-            ]
-    out[...] = result[...].reshape(out.shape).astype(bf16)
-
-
-def to_orders_fine_body(pair_dev, n_in, n_out, *refs):
-    chunks, (table_a, table_b), rest = refs[:n_in], refs[n_in : n_in + 2], refs[n_in + 2 :]
-    outs, held, results = rest[:n_out], rest[n_out : n_out + n_in], rest[n_out + n_in :]
-    n_lat, unused, subs, lanes = chunks[0].shape
-    for chunk, keep in zip(chunks, held):
-        keep[...] = flat(chunk[...])
-    if subs != 2 * pair_dev:
-        for result in results:
-            result[...] = jnp.zeros_like(result)
+
+
+def to_orders_fine(pair_dev, subs, tables, held, results):
+    table_a, table_b = tables
     for index in range(pair_dev):
         first, second = [], []
         for odd in range(2):
@@ -312,57 +330,123 @@
                     begin : begin + rows
                 ]
                 begin += rows
-    for out, result in zip(outs, results):
-        out[...] = result[...].reshape(out.shape).astype(bf16)
-
-
-def to_orders_coarse_body(pair_dev, n_in, n_out, chunk, table, out, held, result):
-    n_lat, unused, subs, lanes = out.shape
-    held[...] = flat(chunk[...])
-    if subs != 2 * pair_dev:
-        result[...] = jnp.zeros_like(result)
-    rows, half = result.shape[0] // subs, held.shape[0] // subs
+
+
+def coarse_either_way(pair_dev, subs, tables, held, results):
+    (keep,), (result,), (table,) = held, results, tables
+    before, after = keep.shape[0] // subs, result.shape[0] // subs
     for index in range(pair_dev):
         taken = joined_rows(
-            [held[pl.ds(odd * pair_dev + index, half, stride=subs), :] for odd in range(2)]
+            [keep[pl.ds(odd * pair_dev + index, before, stride=subs), :] for odd in range(2)]
         ).astype(bf16)
         made = dot(table[index], taken, 1, 0)
         for odd in range(2):
-            result[pl.ds(odd * pair_dev + index, rows, stride=subs), :] = made[
-                odd * rows : (odd + 1) * rows
+            result[pl.ds(odd * pair_dev + index, after, stride=subs), :] = made[
+                odd * after : (odd + 1) * after
             ]
-    out[...] = result[...].reshape(out.shape).astype(bf16)
-
-
-def lane_call(body, name, inputs, tables, outs):
-    tiled = lambda shape: pl.BlockSpec(tuple(shape[:3]) + (TILE,), lambda t: (0, 0, 0, t))
+
+
+def lane_body(work, subs, width, n_in, n_tables, n_out, *refs):
+    cuts = [n_in, n_in, n_tables, n_out, n_in, n_out, n_out]
+    mains, tails, tables, outs, held, results, packed = [
+        refs[sum(cuts[:k]) : sum(cuts[: k + 1])] for k in range(len(cuts))
+    ]
+    step = pl.program_id(0)
+    n_lat, per = mains[0].shape[0], subs // 8
+
+    @pl.when(step == 0)
+    def _():
+        for tail, keep in zip(tails, held):
+            rows = keep.shape[0] // (n_lat * subs)
+            share, groups = packing(rows, width)
+            whole = tail[:, 0].astype(f32)
+            for group in range(groups):
+                tile = packed_group(whole, group, subs)
+                for row in range(group * share, min(rows, (group + 1) * share)):
+                    own = unpacked(tile, row % share, width)
+                    for device in range(n_lat):
+                        keep[pl.ds((device * rows + row) * subs, subs), :] = own[
+                            device * subs : (device + 1) * subs
+                        ]
+        for result in results:
+            result[...] = jnp.zeros_like(result)
+
+    @pl.when(step > 0)
+    def _():
+        for main, keep in zip(mains, held):
+            keep[...] = flat(main[:, : main.shape[1] - 1])
+
+    work(subs, tables, held, results)
+
+    @pl.when(step == 0)
+    def _():
+        for result, pack in zip(results, packed):
+            rows = result.shape[0] // (n_lat * subs)
+            share, groups = packing(rows, width)
+            pack[...] = jnp.zeros_like(pack)
+            made = result[...].reshape(n_lat, rows, subs, TILE)
+            for group in range(groups):
+                total = jnp.zeros((n_lat * subs, TILE), f32)
+                for row in range(group * share, min(rows, (group + 1) * share)):
+                    own = made[:, row].reshape(n_lat * subs, TILE)
+                    total = total + pltpu.roll(own, row % share * width, 1)
+                split = total.reshape(n_lat, per, 8, TILE)
+                for k in range(per):
+                    pack[group * per + k] = split[:, k]
+
+    @pl.when(step > 0)
+    def _():
+        for out, result, pack in zip(outs, results, packed):
+            count = out.shape[1] - 1
+            out[:, :count] = result[...].reshape(n_lat, count, 8, TILE).astype(bf16)
+            out[:, count] = pack[step - 1].astype(bf16)
+
+
+def lane_call(work, name, inputs, tables, rows_out, subs, width):
+    n_lat = inputs[0].shape[0]
+    outs = [(n_lat, eights(rows, subs), 8, WHOLE) for rows in rows_out]
+    rows_in = [(a.shape[1] - 1) * 8 // subs for a in inputs]
+    tiled = lambda shape: pl.BlockSpec(
+        tuple(shape[:3]) + (TILE,), lambda t: (0, 0, 0, jnp.maximum(t - 1, 0))
+    )
+    tail = lambda shape: pl.BlockSpec(
+        (shape[0], 1, 8, WHOLE), lambda t, last=shape[1] - 1: (0, last, 0, 0)
+    )
     whole = lambda shape: pl.BlockSpec(shape, lambda t: (0, 0, 0))
-    held = lambda shape: pltpu.VMEM((shape[0] * shape[1] * shape[2], TILE), f32)
+    held = lambda rows: pltpu.VMEM((n_lat * rows * subs, TILE), f32)
     moved = sum(2 * math.prod(s) for s in [a.shape for a in inputs] + outs)
     flops = sum(2 * math.prod(t.shape) for t in tables) * LANES
-    made = call(
-        functools.partial(body, len(inputs), len(outs)),
+    return call(
+        functools.partial(lane_body, work, subs, width, len(inputs), len(tables), len(outs)),
         name,
         flops,
         moved,
-        grid=(LANES // TILE,),
-        in_specs=[tiled(a.shape) for a in inputs] + [whole(t.shape) for t in tables],
+        grid=(WHOLE // TILE + 1,),
+        in_specs=[tiled(a.shape) for a in inputs]
+        + [tail(a.shape) for a in inputs]
+        + [whole(t.shape) for t in tables],
         out_specs=[tiled(shape) for shape in outs],
-        out_shape=[jax.ShapeDtypeStruct(tuple(shape), bf16) for shape in outs],
-        scratch_shapes=[held(a.shape) for a in inputs] + [held(shape) for shape in outs],
-    )(*inputs, *tables)
-    return made
-
-
-def mix_body(pair_dev, first, backward, pairs, fine, coarse, weight, fine_out, coarse_out, members):
-    n_lat, unused, subs, lanes = fine.shape
+        out_shape=[jax.ShapeDtypeStruct(shape, bf16) for shape in outs],
+        scratch_shapes=[held(rows) for rows in rows_in]
+        + [held(rows) for rows in rows_out]
+        + [pltpu.VMEM((WHOLE // TILE, n_lat, 8, TILE), f32) for unused in outs],
+    )(*inputs, *inputs, *tables)
+
+
+def mix_body(
+    pair_dev, subs, first, ends, backward, pairs, fine, fine_tail, coarse, coarse_tail, weight,
+    carried, fine_out, coarse_out, members, carry, fine_held, coarse_held,
+):
+    step, last = pl.program_id(0), pl.num_programs(0) - 1
+    n_lat, per = fine.shape[0], subs // 8
     rows = n_lat * subs
-    row = lax.broadcasted_iota(jnp.int32, (rows, 1), 0)
-    sub = row % subs
-    group = sub // pair_dev
-    order_class = row // subs * pair_dev + sub % pair_dev
-    coarse_rows = flat(coarse[:, 0])
+    width = (C if backward else WIDE) - MAIN
     count = C if backward else WIDE
+
+    @pl.when(step == 0)
+    def _():
+        fine_held[...] = jnp.zeros_like(fine_held)
+        coarse_held[...] = carried[...]
 
     def apply(values, slot):
         real, imag = split_parts(values, count)
@@ -377,32 +461,76 @@
             out_imag = by_imag[:rows] + by_real[rows:]
         return join_narrow(out_real[:, :C], out_imag[:, :C])
 
-    coarse_made = jnp.zeros((rows, lanes), f32)
-    for odd in range(2):
-        pair = pairs[2 * (pl.program_id(0) + first) + odd]
-        own = group == odd
-        low = order_class <= pair
-        fine_rows = flat(fine[:, odd])
-        lower = jnp.where(own, coarse_rows, jnp.where(low, fine_rows, 0.0))
-        upper = jnp.where(own | ~low, fine_rows, 0.0)
-        members[2 * odd] = lower.reshape(n_lat, subs, lanes).astype(bf16)
-        members[2 * odd + 1] = upper.reshape(n_lat, subs, lanes).astype(bf16)
-        from_lower = apply(lower, 2 * odd)
-        from_upper = apply(upper, 2 * odd + 1)
-        made = jnp.where(own, from_upper, from_lower + from_upper)
-        fine_out[:, odd] = made.reshape(n_lat, subs, lanes).astype(bf16)
-        coarse_made = jnp.where(own, from_lower, coarse_made)
-    coarse_out[:, 0] = coarse_made.reshape(n_lat, subs, lanes).astype(bf16)
-
-
-def mix(fine, coarse, weight, local_pairs, first, backward, into):
-    n_lat, count, subs, lanes = fine.shape
+    @pl.when(step < last)
+    def _():
+        row = lax.broadcasted_iota(jnp.int32, (rows, 1), 0)
+        sub = row % subs
+        group = sub // pair_dev
+        order_class = row // subs * pair_dev + sub % pair_dev
+        share = HALF // width
+
+        def packed_at(tail, place):
+            whole = tail[:, 0].astype(f32)
+            groups = packing(WHOLE // TILE // per * share, width)[1]
+            tile = packed_group(whole, 0, subs)
+            for index in range(1, groups):
+                tile = jnp.where(place // share == index, packed_group(whole, index, subs), tile)
+            return unpacked(tile, place % share, width)
+
+        coarse_rows = jnp.concatenate(
+            [flat(coarse[...]), packed_at(coarse_tail, step + first)], axis=1
+        )
+        coarse_made = jnp.zeros((rows, LANES), f32)
+        for odd in range(2):
+            pair = pairs[2 * (step + first) + odd]
+            own = group == odd
+            low = order_class <= pair
+            fine_rows = jnp.concatenate(
+                [
+                    flat(fine[:, odd * per : (odd + 1) * per]),
+                    packed_at(fine_tail, 2 * step + odd),
+                ],
+                axis=1,
+            )
+            lower = jnp.where(own, coarse_rows, jnp.where(low, fine_rows, 0.0))
+            upper = jnp.where(own | ~low, fine_rows, 0.0)
+            members[2 * odd] = lower.reshape(n_lat, subs, LANES).astype(bf16)
+            members[2 * odd + 1] = upper.reshape(n_lat, subs, LANES).astype(bf16)
+            from_lower = apply(lower, 2 * odd)
+            from_upper = apply(upper, 2 * odd + 1)
+            made = jnp.where(own, from_upper, from_lower + from_upper)
+            fine_out[:, odd * per : (odd + 1) * per] = (
+                made[:, :WHOLE].reshape(n_lat, per, 8, WHOLE).astype(bf16)
+            )
+            fine_held[...] += pltpu.roll(made[:, WHOLE:], 2 * step + odd, 1)
+            coarse_made = jnp.where(own, from_lower, coarse_made)
+        coarse_out[...] = coarse_made[:, :WHOLE].reshape(coarse_out.shape).astype(bf16)
+        coarse_held[...] += pltpu.roll(coarse_made[:, WHOLE:], step + first, 1)
+
+    @pl.when(step == last)
+    def _():
+        fine_out[:, 0] = last_eight([fine_held[...]], n_lat, subs).astype(bf16)
+        carry[...] = coarse_held[...]
+        if ends:
+            coarse_out[:, 0] = last_eight([coarse_held[...]], n_lat, subs).astype(bf16)
+
+
+def mix(fine, coarse, weight, local_pairs, subs, first, ends, backward, into, carried):
+    n_lat, per = fine.shape[0], subs // 8
+    count = (fine.shape[1] - 1) // per
     pair_dev = weight.shape[0] // 2
-    fine_spec = pl.BlockSpec((n_lat, 2, subs, lanes), lambda k, pairs: (0, k, 0, 0))
-    coarse_spec = pl.BlockSpec((n_lat, 1, subs, lanes), lambda k, pairs: (0, k + first, 0, 0))
+    turns = count // 2
+    inside = lambda k: jnp.minimum(k, turns - 1)
+    rows = lambda height, place: pl.BlockSpec(
+        (n_lat, height, 8, WHOLE), lambda k, pairs: (0, place(k), 0, 0)
+    )
+    tail = lambda array: rows(1, lambda k: array.shape[1] - 1)
+    whole = pl.BlockSpec((n_lat * subs, TILE), lambda k, pairs: (0, 0))
     body, extra, alias = filled(
-        functools.partial(mix_body, pair_dev, first, backward), into, 4, 1
-    )
+        functools.partial(mix_body, pair_dev, subs, first, ends, backward), into, 7, 1
+    )
+    coarse_place = (lambda k: k + first) if ends else (lambda k: inside(k) + first)
+    wave = lambda array: jax.ShapeDtypeStruct(array.shape, bf16)
     return call(
         body,
         "mix_back" if backward else "mix",
@@ -410,26 +538,34 @@
         2 * weight.size * count // pair_dev + 12 * fine.size,
         grid_spec=pltpu.PrefetchScalarGridSpec(
             num_scalar_prefetch=1,
-            grid=(count // 2,),
+            grid=(turns + 1,),
             in_specs=[
-                fine_spec,
-                coarse_spec,
-                pl.BlockSpec((4,) + weight.shape[1:], lambda k, pairs: (k + first, 0, 0, 0)),
+                rows(2 * per, inside),
+                tail(fine),
+                rows(per, lambda k: inside(k) + first),
+                tail(coarse),
+                pl.BlockSpec(
+                    (4,) + weight.shape[1:], lambda k, pairs: (inside(k) + first, 0, 0, 0)
+                ),
+                whole,
             ]
             + extra,
             out_specs=[
-                fine_spec,
-                coarse_spec,
-                pl.BlockSpec((4, n_lat, subs, lanes), lambda k, pairs: (k, 0, 0, 0)),
+                rows(2 * per, lambda k: k),
+                rows(per, coarse_place),
+                pl.BlockSpec((4, n_lat, subs, LANES), lambda k, pairs: (inside(k), 0, 0, 0)),
+                whole,
             ],
+            scratch_shapes=[pltpu.VMEM((n_lat * subs, TILE), f32)] * 2,
         ),
         out_shape=[
-            jax.ShapeDtypeStruct(fine.shape, bf16),
-            jax.ShapeDtypeStruct(coarse.shape, bf16),
-            jax.ShapeDtypeStruct((2 * count, n_lat, subs, lanes), bf16),
+            wave(fine),
+            wave(coarse),
+            jax.ShapeDtypeStruct((2 * count, n_lat, subs, LANES), bf16),
+            jax.ShapeDtypeStruct((n_lat * subs, TILE), f32),
         ],
         input_output_aliases=alias,
-    )(local_pairs, fine, coarse, weight, *([] if into is None else [into]))
+    )(local_pairs, fine, fine, coarse, coarse, weight, carried, *([] if into is None else [into]))
 
 
 def mix_grad_body(n_parts, *refs):
@@ -459,11 +595,13 @@
 
 
 def pixel_body(
-    synth, state, cotangent, table, gain, bias, up, up_turned, up_bias, down, down_turned,
+    synth, tail, state, cotangent, table, gain, bias, up, up_turned, up_bias, down, down_turned,
     down_bias, out, middle_grad, synth_grad, up_grad, down_grad, wide_sums, narrow_sums, held,
-    wide_held, narrow_held,
+    wide_held, narrow_held, tails,
 ):
-    step = pl.program_id(0)
+    step, last = pl.program_id(0), pl.num_programs(0) - 1
+    n_lat, per = synth.shape[:2]
+    subs = 8 * per
 
     @pl.when(step == 0)
     def _():
@@ -472,71 +610,80 @@
         down_grad[...] = jnp.zeros_like(down_grad)
         wide_held[...] = jnp.zeros_like(wide_held)
         narrow_held[...] = jnp.zeros_like(narrow_held)
-
-    real, imag = split_parts(flat(synth[:, 0]), C)
-    stacked = jnp.concatenate([real, imag], axis=0).astype(bf16)
-    middle = state[0][:, 0, :] + dot(stacked, table[...], 0, 0)
-    xhat, scale = norm_stats(middle)
-    normed_low = (xhat * gain[...] + bias[...]).astype(bf16)
-    pre_act = dot(up_turned[...], normed_low, 1, 0) + up_bias[...]
-    share = 0.5 * (1.0 + lax.erf(pre_act * math.sqrt(0.5)))
-    density = jnp.exp(-0.5 * pre_act * pre_act) * (1.0 / math.sqrt(2.0 * math.pi))
-    hidden_low = (pre_act * share).astype(bf16)
-    slope = share + pre_act * density
-    out[0] = (middle + dot(down_turned[...], hidden_low, 1, 0) + down_bias[...])[:, None, :]
-    grad = cotangent[0][:, 0, :]
-    grad_low = grad.astype(bf16)
-    pre_grad = dot(down[...], grad_low, 1, 0) * slope
-    pre_low = pre_grad.astype(bf16)
-    wide_held[...] += pre_grad
-    down_grad[...] += dot(grad_low, hidden_low, 1, 1)
-    up_grad[...] += dot(normed_low, pre_low, 1, 1)
-    normed_grad = dot(up[...], pre_low, 1, 0)
-    narrow_held[0] += normed_grad * xhat
-    narrow_held[1] += normed_grad
-    narrow_held[2] += grad
-    scaled = normed_grad * gain[...]
-    total = grad + scale * (
-        scaled
-        - jnp.mean(scaled, axis=0, keepdims=True)
-        - xhat * jnp.mean(scaled * xhat, axis=0, keepdims=True)
-    )
-    middle_grad[0] = total
-    held[:C] = total
-    result = dot(table[...], held[...].astype(bf16), 1, 1)
-    rows = result.shape[0] // 2
-    joined = join_parts(result[:rows], result[rows:], C)
-    synth_grad[:, 0] = joined.reshape(synth_grad.shape[0], synth_grad.shape[2], LANES).astype(bf16)
-
-    @pl.when(step == pl.num_programs(0) - 1)
-    def _():
+        tails[...] = jnp.zeros_like(tails)
+
+    @pl.when(step < last)
+    def _():
+        own = unpacked(packed_group(tail[:, 0].astype(f32), 0, subs), step, C - MAIN)
+        real, imag = split_parts(jnp.concatenate([flat(synth[...]), own], axis=1), C)
+        stacked = jnp.concatenate([real, imag], axis=0).astype(bf16)
+        middle = state[0][:, 0, :] + dot(stacked, table[...], 0, 0)
+        xhat, scale = norm_stats(middle)
+        normed_low = (xhat * gain[...] + bias[...]).astype(bf16)
+        pre_act = dot(up_turned[...], normed_low, 1, 0) + up_bias[...]
+        share = 0.5 * (1.0 + lax.erf(pre_act * math.sqrt(0.5)))
+        density = jnp.exp(-0.5 * pre_act * pre_act) * (1.0 / math.sqrt(2.0 * math.pi))
+        hidden_low = (pre_act * share).astype(bf16)
+        slope = share + pre_act * density
+        out[0] = (middle + dot(down_turned[...], hidden_low, 1, 0) + down_bias[...])[:, None, :]
+        grad = cotangent[0][:, 0, :]
+        grad_low = grad.astype(bf16)
+        pre_grad = dot(down[...], grad_low, 1, 0) * slope
+        pre_low = pre_grad.astype(bf16)
+        wide_held[...] += pre_grad
+        down_grad[...] += dot(grad_low, hidden_low, 1, 1)
+        up_grad[...] += dot(normed_low, pre_low, 1, 1)
+        normed_grad = dot(up[...], pre_low, 1, 0)
+        narrow_held[0] += normed_grad * xhat
+        narrow_held[1] += normed_grad
+        narrow_held[2] += grad
+        scaled = normed_grad * gain[...]
+        total = grad + scale * (
+            scaled
+            - jnp.mean(scaled, axis=0, keepdims=True)
+            - xhat * jnp.mean(scaled * xhat, axis=0, keepdims=True)
+        )
+        middle_grad[0] = total
+        held[:C] = total
+        result = dot(table[...], held[...].astype(bf16), 1, 1)
+        rows = result.shape[0] // 2
+        joined = join_parts(result[:rows], result[rows:], C)
+        synth_grad[...] = joined[:, :WHOLE].reshape(synth_grad.shape).astype(bf16)
+        tails[...] += pltpu.roll(joined[:, WHOLE:], step, 1)
+
+    @pl.when(step == last)
+    def _():
+        synth_grad[:, 0] = last_eight([tails[...]], n_lat, subs).astype(bf16)
         wide_sums[...] = jnp.sum(wide_held[...], axis=1, keepdims=True)
         narrow_sums[...] = jnp.sum(narrow_held[...], axis=2, keepdims=True)
 
 
 def pixels(synth, state, cotangent, table, params, first, into):
-    n_lat, count, subs, lanes = synth.shape
+    n_lat, subs = synth.shape[0], table.shape[0] // (2 * synth.shape[0])
+    per = subs // 8
+    count = (synth.shape[1] - 1) // per
+    row = lambda r: jnp.minimum(r, count - 1)
     points = state.shape[3]
     hidden = params[2].shape[1]
-    row_spec = pl.BlockSpec((1, C, 1, points), lambda r: (r + first, 0, 0, 0))
+    row_spec = pl.BlockSpec((1, C, 1, points), lambda r: (row(r) + first, 0, 0, 0))
     const = lambda array: pl.BlockSpec(array.shape, lambda r: (0,) * array.ndim)
-    row_out = lambda shape: pl.BlockSpec((1,) + shape, lambda r: (r,) + (0,) * len(shape))
-    wave = pl.BlockSpec((n_lat, 1, subs, lanes), lambda r: (0, r, 0, 0))
+    wave = lambda place: pl.BlockSpec((n_lat, per, 8, WHOLE), lambda r: (0, place(r), 0, 0))
+    tail = pl.BlockSpec((n_lat, 1, 8, WHOLE), lambda r: (0, count * per, 0, 0))
     whole = lambda shape: pl.BlockSpec(shape, lambda r: (0,) * len(shape))
     shaped = lambda shape, kind=f32: jax.ShapeDtypeStruct(shape, kind)
-    body, extra, alias = filled(pixel_body, into, 4 + len(params))
+    body, extra, alias = filled(pixel_body, into, 5 + len(params), 0, 1)
     return call(
         body,
         "feed_forward",
         2 * count * points * (6 * C * hidden + 2 * table.shape[0] * PADDED),
-        count * (4 * C * points * 4 + 4 * n_lat * subs * lanes),
-        grid=(count,),
-        in_specs=[wave, row_spec, row_spec, const(table)] + [const(p) for p in params] + extra,
+        count * (4 * C * points * 4 + 4 * n_lat * subs * LANES),
+        grid=(count + 1,),
+        in_specs=[wave(row), tail, row_spec, row_spec, const(table)] + [const(p) for p in params] + extra,
         input_output_aliases=alias,
         out_specs=[
             row_spec,
-            row_out((C, points)),
-            wave,
+            pl.BlockSpec((1, C, points), lambda r: (row(r) + first, 0, 0)),
+            wave(lambda r: r),
             whole((C, hidden)),
             whole((C, hidden)),
             whole((hidden, 1)),
@@ -544,7 +691,7 @@
         ],
         out_shape=[
             shaped(state.shape),
-            shaped((count, C, points)),
+            shaped((state.shape[0], C, points)),
             shaped(synth.shape, bf16),
             shaped((C, hidden)),
             shaped((C, hidden)),
@@ -555,18 +702,20 @@
             pltpu.VMEM((PADDED, points), f32),
             pltpu.VMEM((hidden, points), f32),
             pltpu.VMEM((3, C, points), f32),
+            pltpu.VMEM((n_lat * subs, TILE), f32),
         ],
-    )(synth, state, cotangent, table, *params, *([] if into is None else [into]))
-
-
-def final_body(wave, state, middle_grad, table, gain, out, sums, held):
+    )(synth, synth, state, cotangent, table, *params, *([] if into is None else into))
+
+
+def final_body(wave, tail, state, middle_grad, table, gain, out, sums, held):
     step = pl.program_id(0)
 
     @pl.when(step == 0)
     def _():
         held[...] = jnp.zeros_like(held)
 
-    real, imag = split_parts(flat(wave[:, 0]), C)
+    own = unpacked(packed_group(tail[:, 0].astype(f32), 0, 8 * wave.shape[1]), step, C - MAIN)
+    real, imag = split_parts(jnp.concatenate([flat(wave[...]), own], axis=1), C)
     stacked = jnp.concatenate([real, imag], axis=0).astype(bf16)
     spread_grad = dot(stacked, table[...], 0, 0)
     xhat, scale = norm_stats(state[0][:, 0, :])
@@ -589,19 +738,22 @@
 
 
 def finish(wave, state, middle_grad, table, gain, first, into):
-    n_lat, count, subs, lanes = wave.shape
+    n_lat, subs = wave.shape[0], table.shape[0] // (2 * wave.shape[0])
+    per = subs // 8
+    count = (wave.shape[1] - 1) // per
     points = state.shape[3]
-    body, extra, alias = filled(final_body, into, 5)
+    body, extra, alias = filled(final_body, into, 6, 0)
     return call(
         body,
         "first_norm_back",
         2 * count * points * table.shape[0] * PADDED,
-        count * (3 * C * points * 4 + 2 * n_lat * subs * lanes),
+        count * (3 * C * points * 4 + 2 * n_lat * subs * LANES),
         grid=(count,),
         in_specs=[
-            pl.BlockSpec((n_lat, 1, subs, lanes), lambda r: (0, r, 0, 0)),
+            pl.BlockSpec((n_lat, per, 8, WHOLE), lambda r: (0, r, 0, 0)),
+            pl.BlockSpec((n_lat, 1, 8, WHOLE), lambda r: (0, count * per, 0, 0)),
             pl.BlockSpec((1, C, 1, points), lambda r: (r + first, 0, 0, 0)),
-            pl.BlockSpec((1, C, points), lambda r: (r, 0, 0)),
+            pl.BlockSpec((1, C, points), lambda r: (r + first, 0, 0)),
             pl.BlockSpec(table.shape, lambda r: (0, 0)),
             pl.BlockSpec((C, 1), lambda r: (0, 0)),
         ]
@@ -616,7 +768,7 @@
             jax.ShapeDtypeStruct((2, C, 1), f32),
         ],
         scratch_shapes=[pltpu.VMEM((2, C, points), f32)],
-    )(wave, state, middle_grad, table, gain, *([] if into is None else [into]))
+    )(wave, wave, state, middle_grad, table, gain, *([] if into is None else [into]))
 
 
 def part_rows_body(paired, out):
@@ -799,6 +951,8 @@
     line = Line()
     row_cuts = [(fine_dev + 1) // 2, fine_dev // 2] if fine_dev >= 8 else [fine_dev]
     row_starts = [sum(row_cuts[:k]) for k in range(len(row_cuts))]
+    outer_cuts = [fine_dev // 4 + 1, fine_dev - fine_dev // 4 - 1] if fine_dev >= 8 else [fine_dev]
+    outer_starts = [sum(outer_cuts[:k]) for k in range(len(outer_cuts))]
     n_chunks = 2 if pair_dev % 4 == 0 else 1
     chunk_pairs = pair_dev // n_chunks
     chunk_range = range(n_chunks)
@@ -808,7 +962,7 @@
     fine_forward, fine_inverse = fine_fourier(n_lat, pair_dev, subs, fine_points)
     gain_one, bias_one = column(first_gain), column(first_bias)
     fine_four = []
-    for start, count in zip(row_starts, row_cuts):
+    for start, count in zip(outer_starts, outer_cuts):
         made = spread(fine_x, fine_noise_in, gain_one, bias_one, fine_forward, n_lat, start, count)
         fine_four.append(line.swap(line.keep(made)))
     coarse_x = coarse_in(coarse_state)
@@ -823,10 +977,15 @@
     classes = jnp.where(jnp.arange(wide) < pair_dev, classes, LB).astype(jnp.int32)
     coarse_order = coarse_rows.reshape(-1, 2).T.reshape(-1)
     by_device = fine_rows.reshape(n_lat, fine_dev)
-    fine_order = jnp.concatenate(
-        [by_device[:, a : a + c].reshape(-1) for a, c in zip(row_starts, row_cuts)]
-    )
-    fine_plain, fine_quad = legendre_tables(fine_order, pair_slots, classes, LB, True)
+    in_order = lambda starts, cuts: jnp.concatenate(
+        [by_device[:, a : a + c].reshape(-1) for a, c in zip(starts, cuts)]
+    )
+    unused, fine_quad = legendre_tables(
+        in_order(outer_starts, outer_cuts), pair_slots, classes, LB, True
+    )
+    fine_plain, unused = legendre_tables(
+        in_order(row_starts, row_cuts), pair_slots, classes, LB, True
+    )
     coarse_plain, coarse_quad = legendre_tables(coarse_order, pair_slots, classes, LA, False)
     turn = lambda table, chunks=n_chunks: by_class(table, n_lat, pair_dev, chunks)
 
@@ -844,24 +1003,25 @@
     local_pairs = lax.dynamic_slice_in_dim(pair_slots, lat_rank * pair_dev, pair_dev)
     weight = mix_weight.transpose(0, 1, 3, 2)
 
-    fine_degrees = [[n_lat, chunk_pairs, subs, LANES]] * n_chunks
-    coarse_degrees = [[n_lat, pair_dev // 2, subs, LANES]]
-    fine_waves = [[n_lat, count, subs, LANES] for count in row_cuts]
-    coarse_waves = [[n_lat, coarse_two, subs, LANES]]
-
-    def spectral(coarse_chunk, fine_chunks, in_tables, out_tables, backward, aside):
+    fine_work = functools.partial(to_degrees_fine, pair_dev)
+    fine_back_work = functools.partial(to_orders_fine, pair_dev)
+    coarse_work = functools.partial(coarse_either_way, pair_dev)
+
+    def spectral(coarse_chunk, fine_chunks, in_tables, out_tables, cuts, backward, aside):
+        wide = (C if backward else WIDE) - MAIN
         fine_made = lane_call(
-            functools.partial(to_degrees_fine_body, pair_dev), "rows_to_degrees",
-            line.hold(fine_chunks), in_tables[1], fine_degrees,
+            fine_work, "rows_to_degrees", line.hold(fine_chunks), in_tables[1],
+            [chunk_pairs] * n_chunks, subs, wide,
         )
         line.keep(fine_made)
         arrived, mixed, shared = [], [], []
 
         def mix_chunk(k):
             fine, coarse = line.hold((arrived[k], arrived_coarse))
+            carried = mixed[-1][3] if mixed else jnp.zeros((n_lat * subs, TILE), f32)
             made = mix(
-                fine, coarse, weight, local_pairs, k * chunk_pairs // 2, backward,
-                mixed[-1][1] if mixed else None,
+                fine, coarse, weight, local_pairs, subs, k * chunk_pairs // 2, k == n_chunks - 1,
+                backward, mixed[-1][1] if mixed else None, carried,
             )
             mixed.append(line.keep(made))
 
@@ -872,8 +1032,8 @@
 
         arrived.append(line.swap(fine_made[0]))
         coarse_made = lane_call(
-            functools.partial(to_degrees_coarse_body, pair_dev), "rows_to_degrees",
-            [line.hold(coarse_chunk)], [in_tables[0]], coarse_degrees,
+            coarse_work, "rows_to_degrees", [line.hold(coarse_chunk)], [in_tables[0]],
+            [pair_dev // 2], subs, wide,
         )[0]
         arrived_coarse = line.swap(line.keep(coarse_made))
         for k in range(1, n_chunks):
@@ -890,19 +1050,22 @@
         fine_back.append(line.swap(mixed[-1][0]))
         share_next()
         coarse_made = lane_call(
-            functools.partial(to_orders_coarse_body, pair_dev), "degrees_to_rows",
-            [line.hold(arrived_coarse)], [out_tables[0]], coarse_waves,
+            coarse_work, "degrees_to_rows", [line.hold(arrived_coarse)], [out_tables[0]],
+            [coarse_two], subs, C - MAIN,
         )[0]
         coarse_end = line.swap(line.keep(coarse_made))
         share_next(n_chan)
         fine_made = lane_call(
-            functools.partial(to_orders_fine_body, pair_dev), "degrees_to_rows",
-            line.hold(fine_back), out_tables[1], fine_waves,
+            fine_back_work, "degrees_to_rows", line.hold(fine_back), out_tables[1],
+            cuts, subs, C - MAIN,
         )
         line.keep(fine_made)
-        fine_end = []
-        for k, made in enumerate(fine_made):
-            fine_end.append(line.swap(made))
+        fine_end = [None] * len(cuts)
+        order = list(range(len(cuts)))
+        if backward:
+            order.reverse()
+        for k, place in enumerate(order):
+            fine_end[place] = line.swap(fine_made[place])
             aside(k, coarse_end, fine_end, shared)
         return fine_end, shared
 
@@ -914,7 +1077,7 @@
     coarse_made, fine_made = [], []
 
     def fine_pixels(k, synth):
-        into = fine_made[-1][0] if fine_made else None
+        into = fine_made[-1][:2] if fine_made else None
         made = pixels(
             line.hold(synth), fine_x, fine_g, fine_inverse, params, row_starts[k], into
         )
@@ -933,7 +1096,7 @@
 
     fine_synth, values = spectral(
         coarse_four, fine_four, (coarse_quad_in, fine_quad_in), (coarse_plain_out, fine_plain_out),
-        False, forward_aside,
+        row_cuts, False, forward_aside,
     )
     if len(row_cuts) == 1:
         fine_pixels(0, fine_synth[0])
@@ -957,6 +1120,12 @@
         coarse_made[0] = coarse_back(coarse_made[0])
     ends, mix_grads = [], []
 
+    def finish_fine(place, wave):
+        into = ends[-1][0] if len(ends) > 1 else None
+        return finish(
+            wave, fine_x, fine_made[-1][1], fine_forward, gain_one, outer_starts[place], into
+        )
+
     def backward_aside(k, coarse_end, fine_end, shared):
         if k == 0:
             mix_grads.append(line.keep(mix_gradient(values, line.hold(shared))))
@@ -966,16 +1135,12 @@
         else:
             if k == 1:
                 ends[0][0] = line.keep(coarse_back(line.hold(ends[0][0])))
-            into = ends[-1][0] if k > 1 else None
-            made = finish(
-                line.hold(fine_end[k - 1]), fine_x, fine_made[k - 1][1], fine_forward, gain_one,
-                row_starts[k - 1], into,
-            )
+            made = finish_fine(len(outer_cuts) - k, line.hold(fine_end[-k]))
         ends.append(list(line.keep(made)))
 
     fine_fgrad, grads = spectral(
         coarse_sgrad, fine_sgrad, (coarse_plain_in, fine_plain_in), (coarse_quad_out, fine_quad_out),
-        True, backward_aside,
+        outer_cuts, True, backward_aside,
     )
     for unused in line.aside:
         pass
@@ -984,13 +1149,8 @@
     narrow_sums = narrow[hidden : hidden + 3 * C].reshape(3, C)
     if len(row_cuts) == 1:
         ends[0][0] = coarse_back(ends[0][0])
-    into = ends[-1][0] if len(row_cuts) > 1 else None
-    last_wave = lax.optimization_barrier((fine_fgrad[-1], line.work + line.later))[0]
-    ends.append(
-        finish(
-            last_wave, fine_x, fine_made[-1][1], fine_forward, gain_one, row_starts[-1], into
-        )
-    )
+    last_wave = lax.optimization_barrier((fine_fgrad[0], line.work + line.later))[0]
+    ends.append(finish_fine(0, last_wave))
     mix_grad = mix_grads[0].transpose(0, 2, 3, 1)
     sums = sum(end[1] for end in ends)
     first_sums = sum_over(sums[:, :, 0], axes)

time: 2530 us -> 2440 us (0.964)
  waiting for transfers between devices: 1290 us -> 1150 us
  Pallas kernels: 662 us -> 690 us
    all_to_all x23, waiting for transfers between devices: 724 us -> 620 us  [swap(): lax.all_to_all(values, 'lat', split_axis=0, concat_axis=0, tiled=True)]
    unnamed x91 -> x85, local copies, waits for them, and re-layouts: 65.8 us -> 70.1 us
  transfers between devices with their start and end apart: 44 -> 44, of which waited for: 32 -> 31; matrix products, arithmetic and copies ran while one was open for 13% -> 14% of each run, Pallas kernels for 25% -> 27%
where the time goes in v3:
time: 2440 us; the launch traced here: 2430 us
  waiting for transfers between devices  1150 us (47%)
  Pallas kernels  690 us (28%)
  local copies, waits for them, and re-layouts  254 us (10%)
  starting transfers between devices  138 us (6%)
  other arithmetic  121 us (5%)
  blocking collectives  74.1 us (3%)
    all_to_all x23, waiting for transfers between devices, swap(): lax.all_to_all(values, 'lat', split_axis=0, concat_axis=0, tiled=True)  620 us
    pallas_call x3, Pallas kernels, pixels(): call(body, 'feed_forward', 2 * count * points * (6 * C * hidden + 2 * tab...  321 us
    ppermute x5, waiting for transfers between devices, add_dense(): lax.ppermute(jnp.where(upper, low, high), axis, partners(sizes[axis], ste...  241 us
    ppermute x5, waiting for transfers between devices, add_dense(): other = lax.ppermute(held, axis, partners(sizes[axis], step)[0])  167 us
    ppermute x6, waiting for transfers between devices, share_slots(): return lax.ppermute(block, 'chan', route) if step else block  115 us
    all_to_all x23, starting transfers between devices, swap(): lax.all_to_all(values, 'lat', split_axis=0, concat_axis=0, tiled=True)  111 us
    pallas_call x8, Pallas kernels, lane_call(): call(functools.partial(lane_body, work, subs, width, len(inputs), len(tab...  106 us
    pallas_call x4, Pallas kernels, mix(): call(body, 'mix_back' if backward else 'mix', 2 * count * n_lat * subs *...  81.1 us
  transfers between devices with their start and end apart: 44, of which 31 were waited for; matrix products, arithmetic and copies ran while one was open for 14% of the time, Pallas kernels for 27%

profile of v3, /device:TPU:0, one launch (start us, length us, event | category | flops | bytes accessed | tf_op | source)
XLA Modules:
  0.0 2427.3 jit_solution(7863570359474462250)
XLA Ops:
  6.8 10.0 norm_and_dft.3
  16.8 7.2 all-to-all-start
  24.1 24.3 %norm_and_dft.4 = bf16[8,52,8,1280]{3,2,1,0:T(8,128)(2,1)} custom-call(f32[23,641,1,360]{3,2,1,0:T(1,128)} %bitcast.78, s32[23,8,360]{2,1,0:T(8,128)} %bitcast.116, f32[641,1]{1,0:T(8,128)} %broadcast_in_dim.201.gain.refs_5_, f32[641,1]{1,0:T(8,128)} %broadcast_in_dim.202.bias, bf16[384,360]{1,0:T(8,128)(2,1)} %pad_maximum_fusion.5.table.refs_4_), custom_call_target="tpu_custom_call" | custom-call | flops 3609722880 | bytes 24883104 | tf_op jit(solution)/shard_map/norm_and_dft/pallas_call | solution.py:162
  48.4 45.7 %all-to-all-done.refs_0_.refs_2_ = bf16[8,19,8,1280]{3,2,1,0:T(8,128)(2,1)S(1)} async-done(((bf16[8,19,8,1280]{3,2,1,0:T(8,128)(2,1)}), bf16[8,19,8,1280]{3,2,1,0:T(8,128)(2,1)S(1)}, u32[]{:S(2)}, u32[]{:S(2)}) %all-to-all-start) | async-done | bytes 3112992 | tf_op jit(solution)/shard_map/all_to_all | solution.py:842
  101.5 20.7 reduce
  122.2 7.2 reshape_squeeze.9
  129.3 7.5 copy.119
  136.8 8.1 broadcast_in_dim.105.state
  148.1 10.0 norm_and_dft.5
  158.1 127.6 %all-to-all-done.1.refs_1_.refs_3_ = bf16[8,52,8,1280]{3,2,1,0:T(8,128)(2,1)} async-done(((bf16[8,52,8,1280]{3,2,1,0:T(8,128)(2,1)}), bf16[8,52,8,1280]{3,2,1,0:T(8,128)(2,1)}, u32[]{:S(2)}, u32[]{:S(2)}) %all-to-all-start.1) | async-done | bytes 8519712 | tf_op jit(solution)/shard_map/all_to_all | solution.py:842
  294.2 13.2 legendre_tables.3
  336.1 17.0 rows_to_degrees.4
  377.2 9.5 rows_to_degrees.5
  386.7 48.8 %all-to-all-done.3.fine.fine_tail = bf16[8,19,8,1280]{3,2,1,0:T(8,128)(2,1)S(1)} async-done(((bf16[8,19,8,1280]{3,2,1,0:T(8,128)(2,1)}), bf16[8,19,8,1280]{3,2,1,0:T(8,128)(2,1)S(1)}, u32[]{:S(2)}, u32[]{:S(2)}) %all-to-all-start.3) | async-done | bytes 3112992 | tf_op jit(solution)/shard_map/all_to_all | solution.py:842
  435.5 74.1 %all_to_all.120.coarse.coarse_tail.refs_3_.refs_4_ = bf16[8,19,8,1280]{3,2,1,0:T(8,128)(2,1)} all-to-all(bf16[8,19,8,1280]{3,2,1,0:T(8,128)(2,1)} %rows_to_degrees.5), channel_id=1, replica_groups=mesh['lat'=8,'chan'=4] {'lat'}, dimensions={0} | all-to-all | bytes 6225920 | tf_op jit(solution)/shard_map/all_to_all | solution.py:842
  514.9 31.7 %copy.181 = bf16[24,2,649,641]{2,3,1,0:T(8,128)(2,1)} copy(bf16[24,2,649,641]{2,1,3,0:T(2,128)(2,1)} %param.27) | data formatting | bytes 79873728 | tf_op args[9]
  547.2 20.4 mix.2
  567.6 15.4 all-to-all-done.5.refs_1_.refs_2_
  586.6 20.3 mix.3
  606.9 49.8 %all-to-all-done.6.refs_0_.refs_2_ = bf16[8,19,8,1280]{3,2,1,0:T(8,128)(2,1)S(1)} async-done(((bf16[8,19,8,1280]{3,2,1,0:T(8,128)(2,1)}), bf16[8,19,8,1280]{3,2,1,0:T(8,128)(2,1)S(1)}, u32[]{:S(2)}, u32[]{:S(2)}) %all-to-all-start.6) | async-done | bytes 3112992 | tf_op jit(solution)/shard_map/all_to_all | solution.py:842
  681.0 51.2 %all-to-all-done.7.refs_0_.refs_1_ = bf16[8,19,8,1280]{3,2,1,0:T(8,128)(2,1)S(1)} async-done(((bf16[8,19,8,1280]{3,2,1,0:T(8,128)(2,1)}), bf16[8,19,8,1280]{3,2,1,0:T(8,128)(2,1)S(1)}, u32[]{:S(2)}, u32[]{:S(2)}) %all-to-all-start.7) | async-done | bytes 3112992 | tf_op jit(solution)/shard_map/all_to_all | solution.py:842
  745.4 9.5 degrees_to_rows.4
  754.9 57.1 %collective-permute-done.refs_2_ = bf16[6,8,24,1408]{3,2,1,0:T(8,128)(2,1)} collective-permute-done((bf16[6,8,24,1408]{3,2,1,0:T(8,128)(2,1)S(1)}, bf16[6,8,24,1408]{3,2,1,0:T(8,128)(2,1)}, u32[]{:S(2)}, u32[]{:S(2)}) %collective-permute-start) | collective-permute-done | bytes 3244064 | tf_op jit(solution)/shard_map/ppermute | solution.py:875
  822.2 13.2 legendre_tables.5
  845.8 16.9 degrees_to_rows.5
  862.7 31.7 %collective-permute-done.2.refs_3_ = bf16[6,8,24,1408]{3,2,1,0:T(8,128)(2,1)} collective-permute-done((bf16[6,8,24,1408]{3,2,1,0:T(8,128)(2,1)}, bf16[6,8,24,1408]{3,2,1,0:T(8,128)(2,1)}, u32[]{:S(2)}, u32[]{:S(2)}) %collective-permute-start.2) | collective-permute-done | bytes 3244064 | tf_op jit(solution)/shard_map/ppermute | solution.py:875
  910.6 20.7 reduce.1
  931.3 7.2 reshape_squeeze.11
  938.5 7.5 copy.132
  946.0 8.2 broadcast_in_dim.193.cotangent
  954.9 70.5 %feed_forward.3 = (f32[6,641,1,360]{3,2,1,0:T(1,128)}, f32[6,641,360]{2,1,0:T(8,128)}, bf16[8,19,8,1280]{3,2,1,0:T(8,128)(2,1)}, f32[641,1282]{1,0:T(8,128)}, f3...) custom-call(bf16[8,19,8,1280]{3,2,1,0:T(8,128)(2,1)} %all-to-all-done.9.synth.tail, ...), custom_call_target="tpu_custom_call" | custom-call | flops 23848110080 | bytes 28641024 | tf_op jit(solution)/shard_map/feed_forward/pallas_call | solution.py:675
  1025.5 8.6 all-to-all-done.10.synth.tail
  1039.9 8.2 part_rows.2
  1048.1 130.1 %feed_forward.4 = (f32[23,641,1,360]{3,2,1,0:T(1,128)}, f32[23,641,360]{2,1,0:T(8,128)}, bf16[8,37,8,1280]{3,2,1,0:T(8,128)(2,1)}, f32[641,1282]{1,0:T(8,128)}, ...) custom-call(bf16[8,37,8,1280]{3,2,1,0:T(8,128)(2,1)} %all-to-all-done.10.synth.tail, ...), custom_call_target="tpu_custom_call" | custom-call | flops 47696220160 | bytes 57282048 | tf_op jit(solution)/shard_map/feed_forward/pallas_call | solution.py:675
  1184.6 120.2 %feed_forward.5 = (f32[23,641,1,360]{3,2,1,0:T(1,128)}, f32[23,641,360]{2,1,0:T(8,128)}, bf16[8,34,8,1280]{3,2,1,0:T(8,128)(2,1)}, f32[641,1282]{1,0:T(8,128)}, ...) custom-call(bf16[8,34,8,1280]{3,2,1,0:T(8,128)(2,1)} %all-to-all-don, ...), custom_call_target="tpu_custom_call", output_to_operand_aliasing={{0}: (13, {}), {1}: (14, {})} | custom-call | flops 43721535488 | bytes 52508544 | tf_op jit(solution)/shard_map/feed_forward/pallas_call | solution.py:675
  1304.7 11.9 all-to-all-done.12.refs_0_.refs_2_
  1335.7 23.0 concatenate.109
  1358.7 7.1 pad.9
  1365.8 78.1 %all-to-all-done.13.refs_1_.refs_3_ = bf16[8,34,8,1280]{3,2,1,0:T(8,128)(2,1)} async-done(((bf16[8,34,8,1280]{3,2,1,0:T(8,128)(2,1)}), bf16[8,34,8,1280]{3,2,1,0:T(8,128)(2,1)}, u32[]{:S(2)}, u32[]{:S(2)}) %all-to-all-start.13) | async-done | bytes 5570592 | tf_op jit(solution)/shard_map/all_to_all | solution.py:842
  1459.2 7.2 collective-permute-done.3
  1472.0 7.4 select_add_fusion
  1479.4 17.0 rows_to_degrees.6
  1496.4 21.4 all-to-all-done.14.refs_0_.refs_1_
  1529.8 45.0 %collective-permute-done.4 = f32[384,1282]{0,1:T(8,128)} collective-permute-done((f32[384,1282]{0,1:T(8,128)}, f32[384,1282]{0,1:T(8,128)}, u32[]{:S(2)}, u32[]{:S(2)}) %collective-permute-start.4) | collective-permute-done | bytes 1969184 | tf_op jit(solution)/shard_map/ppermute | solution.py:904
  1582.4 9.5 rows_to_degrees.7
  1603.1 54.4 %collective-permute-done.5 = f32[192,1282]{1,0:T(8,128)S(1)} collective-permute-done((f32[192,1282]{1,0:T(8,128)S(1)}, f32[192,1282]{1,0:T(8,128)S(1)}, u32[]{:S(2)}, u32[]{:S(2)}) %collective-permute-start.5) | collective-permute-done | bytes 984608 | tf_op jit(solution)/shard_map/ppermute | solution.py:904
  1658.7 10.0 all-to-all-done.16.coarse.coarse_tail.refs_3_.refs_4_
  1676.7 58.7 %collective-permute-done.6 = f32[96,1282]{1,0:T(8,128)S(1)} collective-permute-done((f32[96,1282]{1,0:T(8,128)S(1)}, f32[96,1282]{1,0:T(8,128)S(1)}, u32[]{:S(2)}, u32[]{:S(2)}) %collective-permute-start.6) | collective-permute-done | bytes 492320 | tf_op jit(solution)/shard_map/ppermute | solution.py:904
  1737.5 20.2 mix_back.2
  1767.8 75.9 %collective-permute-done.7 = f32[48,1282]{1,0:T(8,128)S(1)} collective-permute-done((f32[48,1282]{1,0:T(8,128)S(1)}, f32[48,1282]{1,0:T(8,128)S(1)}, u32[]{:S(2)}, u32[]{:S(2)}) %collective-permute-start.7) | collective-permute-done | bytes 246176 | tf_op jit(solution)/shard_map/ppermute | solution.py:904
  1844.8 20.3 mix_back.3
  1886.3 60.0 %collective-permute-done.8 = bf16[48,1282]{1,0:T(8,128)(2,1)S(1)} collective-permute-done((bf16[48,1282]{1,0:T(8,128)(2,1)S(1)}, bf16[48,1282]{1,0:T(8,128)(2,1)S(1)}, u32[]{:S(2)}, u32[]{:S(2)}) %collective-permute-start.8) | collective-permute-done | bytes 123104 | tf_op jit(solution)/shard_map/ppermute | solution.py:913
  1958.6 51.1 %collective-permute-done.9 = bf16[96,1282]{1,0:T(8,128)(2,1)} collective-permute-done((bf16[96,1282]{1,0:T(8,128)(2,1)}, bf16[96,1282]{1,0:T(8,128)(2,1)}, u32[]{:S(2)}, u32[]{:S(2)}) %collective-permute-start.9) | collective-permute-done | bytes 246176 | tf_op jit(solution)/shard_map/ppermute | solution.py:913
  2011.6 9.5 degrees_to_rows.6
  2040.6 34.2 %collective-permute-done.12 = bf16[192,1282]{1,0:T(8,128)(2,1)} collective-permute-done((bf16[192,1282]{1,0:T(8,128)(2,1)}, bf16[192,1282]{1,0:T(8,128)(2,1)}, u32[]{:S(2)}, u32[]{:S(2)}) %collective-permute-start.12) | collective-permute-done | bytes 492320 | tf_op jit(solution)/shard_map/ppermute | solution.py:913
  2077.2 16.9 degrees_to_rows.7
  2094.1 14.0 collective-permute-done.13.refs_7_
  2115.8 14.2 first_norm_back.3
  2130.0 27.4 %mix_gradient.1 = f32[6,641,2,649]{3,2,1,0:T(2,128)} custom-call(bf16[6,8,24,1408]{3,2,1,0:T(8,128)(2,1)} %get-tuple-element.272.refs_0_, bf16[6,8,24,1408]{3,2,1,0:T(8,128)(2,1)} %collective-permute-done.1.refs_1_, bf16[6,8,24,1408]{3,2,1,0:T(8,128)(2,1)} %collective-permute-done.refs_2_, bf16[6,8,24,1408]{3,2,1,0:T(8,128)(2,1)} %collective-permute-done.2.refs_3_, ...), custom_call_target="tpu_custom_call" | custom-call | flops 15335755776 | bytes 45920688 | tf_op jit(solution)/shard_map/mix_gradient/pallas_call | solution.py:585
  2157.4 143.5 %all-to-all-done.22.wave.tail = bf16[8,52,8,1280]{3,2,1,0:T(8,128)(2,1)} async-done(((bf16[8,52,8,1280]{3,2,1,0:T(8,128)(2,1)}), bf16[8,52,8,1280]{3,2,1,0:T(8,128)(2,1)}, u32[]{:S(2)}, u32[]{:S(2)}) %all-to-all-start.22) | async-done | bytes 8519712 | tf_op jit(solution)/shard_map/all_to_all | solution.py:842
  2309.5 22.1 collective-permute-done.14
  2341.2 8.2 part_rows.3
  2349.4 34.6 %first_norm_back.4 = (f32[23,641,1,360]{3,2,1,0:T(1,128)}, f32[2,641,1]{2,1,0:T(8,128)}) custom-call(bf16[8,52,8,1280]{3,2,1,0:T(8,128)(2,1)} %all-to-all-done.22.wave.tail, bf16[8,52,8,1280]{3,2,1,0:T(8,128)(2,1)} %all-to-all-done.22.wave.tail, f32[23,641,1,360]{3,2,1,0:T(1,128)} %bitcast.81, f32[23,641,360]{2,1,0:T(8,128)} %get-tuple-element.202.middle_grad.refs_3_, ...), custom_call_target="tpu_custom_call" | custom-call | flops 3609722880 | bytes 56266464 | tf_op jit(solution)/shard_map/first_norm_back/pallas_call | solution.py:746
  2389.8 14.2 first_norm_back.5
  (299 shorter events, 379.1 us)
Async XLA Ops:
  16.8 77.3 %all-to-all-start = ((bf16[8,19,8,1280]{3,2,1,0:T(8,128)(2,1)}), bf16[8,19,8,1280]{3,2,1,0:T(8,128)(2,1)S(1)}, u32[]{:S(2)}, u32[]{:S(2)}) async-start(bf16[8,19,8,1280]{3,2,1,0:T(8,128)(2,1)} %norm_and_dft.3), calls=%async_computation | async-start | bytes 6225920 | tf_op jit(solution)/shard_map/all_to_all | solution.py:842
  48.4 52.3 %copy-start.31 = (s32[1,12,180,8]{2,3,1,0:T(8,128)S(1)}, s32[1,12,180,8]{2,3,1,0:T(8,128)}, u32[]{:S(2)}) copy-start(s32[1,12,180,8]{2,3,1,0:T(8,128)} %param.20) | copy-start | bytes 207364
  95.7 190.0 %all-to-all-start.1 = ((bf16[8,52,8,1280]{3,2,1,0:T(8,128)(2,1)}), bf16[8,52,8,1280]{3,2,1,0:T(8,128)(2,1)}, u32[]{:S(2)}, u32[]{:S(2)}) async-start(bf16[8,52,8,1280]{3,2,1,0:T(8,128)(2,1)} %norm_and_dft.4), calls=%async_computation.1 | async-start | bytes 17039360 | tf_op jit(solution)/shard_map/all_to_all | solution.py:842
  158.1 131.7 %copy-start.37 = (s32[184]{0:T(256)S(1)}, s32[184]{0:T(256)}, u32[]{:S(2)}) copy-start(s32[184]{0:T(256)} %param.23) | copy-start | bytes 2212
  285.7 74.3 %all-to-all-start.2 = ((bf16[8,19,8,1280]{3,2,1,0:T(8,128)(2,1)}), bf16[8,19,8,1280]{3,2,1,0:T(8,128)(2,1)S(1)}, u32[]{:S(2)}, u32[]{:S(2)}) async-start(bf16[8,19,8,1280]{3,2,1,0:T(8,128)(2,1)} %norm_and_dft.5), calls=%async_computation.2 | async-start | bytes 6225920 | tf_op jit(solution)/shard_map/all_to_all | solution.py:842
  361.6 73.8 %all-to-all-start.3 = ((bf16[8,19,8,1280]{3,2,1,0:T(8,128)(2,1)}), bf16[8,19,8,1280]{3,2,1,0:T(8,128)(2,1)S(1)}, u32[]{:S(2)}, u32[]{:S(2)}) async-start(bf16[8,19,8,1280]{3,2,1,0:T(8,128)(2,1)} %get-tuple-element.150), calls=%async_computation.3 | async-start | bytes 6225920 | tf_op jit(solution)/shard_map/all_to_all | solution.py:842
  435.5 74.1 %copy-start.4 = (bf16[8,19,8,1280]{3,2,1,0:T(8,128)(2,1)}, bf16[8,19,8,1280]{3,2,1,0:T(8,128)(2,1)S(1)}, u32[]{:S(2)}) copy-start(bf16[8,19,8,1280]{3,2,1,0:T(8,128)(2,1)S(1)} %all-to-all-done.3.fine.fine_tail) | copy-start | bytes 9338884
  509.5 73.4 %all-to-all-start.5 = ((bf16[8,19,8,1280]{3,2,1,0:T(8,128)(2,1)}), bf16[8,19,8,1280]{3,2,1,0:T(8,128)(2,1)}, u32[]{:S(2)}, u32[]{:S(2)}) async-start(bf16[8,19,8,1280]{3,2,1,0:T(8,128)(2,1)} %get-tuple-element.152), calls=%async_computation.5 | async-start | bytes 6225920 | tf_op jit(solution)/shard_map/all_to_all | solution.py:842
  583.0 73.8 %all-to-all-start.6 = ((bf16[8,19,8,1280]{3,2,1,0:T(8,128)(2,1)}), bf16[8,19,8,1280]{3,2,1,0:T(8,128)(2,1)S(1)}, u32[]{:S(2)}, u32[]{:S(2)}) async-start(bf16[8,19,8,1280]{3,2,1,0:T(8,128)(2,1)} %get-tuple-element.164), calls=%async_computation.6 | async-start | bytes 6225920 | tf_op jit(solution)/shard_map/all_to_all | solution.py:842
  658.4 73.8 %all-to-all-start.7 = ((bf16[8,19,8,1280]{3,2,1,0:T(8,128)(2,1)}), bf16[8,19,8,1280]{3,2,1,0:T(8,128)(2,1)S(1)}, u32[]{:S(2)}, u32[]{:S(2)}) async-start(bf16[8,19,8,1280]{3,2,1,0:T(8,128)(2,1)} %get-tuple-element.165), calls=%async_computation.7 | async-start | bytes 6225920 | tf_op jit(solution)/shard_map/all_to_all | solution.py:842
  669.2 5.9 copy-start.1
  675.1 5.9 collective-permute-start.1
  733.9 78.2 %all-to-all-start.8 = ((bf16[8,19,8,1280]{3,2,1,0:T(8,128)(2,1)}), bf16[8,19,8,1280]{3,2,1,0:T(8,128)(2,1)}, u32[]{:S(2)}, u32[]{:S(2)}) async-start(bf16[8,19,8,1280]{3,2,1,0:T(8,128)(2,1)} %get-tuple-element.169), calls=%async_computation.8 | async-start | bytes 6225920 | tf_op jit(solution)/shard_map/all_to_all | solution.py:842
  740.8 71.2 %collective-permute-start = (bf16[6,8,24,1408]{3,2,1,0:T(8,128)(2,1)S(1)}, bf16[6,8,24,1408]{3,2,1,0:T(8,128)(2,1)}, u32[]{:S(2)}, u32[]{:S(2)}) collective-permute-start(bf16[6,8,24,1408]{3,2,1,0:T(8,128)(2,1)S(1)} %constant_dynamic-slice_fusion.7), channel_id=1, source_target_pairs={{0,2},{1,3},{2,0},{3,1},{4,6},{5,7},{6,4},{7,5},{8,10},{9,11},{10,... | collective-permute-start | bytes 9732104 | tf_op jit(solution)/shard_map/ppermute | solution.py:875
  744.5 10.4 copy-start.21
  812.0 82.3 %all-to-all-start.9 = ((bf16[8,19,8,1280]{3,2,1,0:T(8,128)(2,1)}), bf16[8,19,8,1280]{3,2,1,0:T(8,128)(2,1)}, u32[]{:S(2)}, u32[]{:S(2)}) async-start(bf16[8,19,8,1280]{3,2,1,0:T(8,128)(2,1)} %degrees_to_rows.4), calls=%async_computation.9 | async-start | bytes 6225920 | tf_op jit(solution)/shard_map/all_to_all | solution.py:842
  821.6 72.8 %collective-permute-start.2 = (bf16[6,8,24,1408]{3,2,1,0:T(8,128)(2,1)}, bf16[6,8,24,1408]{3,2,1,0:T(8,128)(2,1)}, u32[]{:S(2)}, u32[]{:S(2)}) collective-permute-start(bf16[6,8,24,1408]{3,2,1,0:T(8,128)(2,1)} %constant_dynamic-slice_fusion.4), channel_id=1, source_target_pairs={{0,3},{1,2},{2,1},{3,0},{4,7},{5,6},{6,5},{7,4},{8,11},{9,10},{10,... | collective-permute-start | bytes 9732104 | tf_op jit(solution)/shard_map/ppermute | solution.py:875
  844.3 18.4 copy-start.15
  894.4 6.2 copy-start.34
  894.4 7.1 copy-start.35
  894.4 8.0 copy-start.36
  894.4 8.9 copy-start.32
  894.4 139.7 %all-to-all-start.10 = ((bf16[8,37,8,1280]{3,2,1,0:T(8,128)(2,1)}), bf16[8,37,8,1280]{3,2,1,0:T(8,128)(2,1)}, u32[]{:S(2)}, u32[]{:S(2)}) async-start(bf16[8,37,8,1280]{3,2,1,0:T(8,128)(2,1)} %get-tuple-element.181), calls=%async_computation.10 | async-start | bytes 12124160 | tf_op jit(solution)/shard_map/all_to_all | solution.py:842
  900.5 7.6 copy-start.22
  946.0 8.2 copy-start.29
  946.0 8.2 copy-start.30
  1034.1 144.1 %all-to-all-start.11 = ((bf16[8,34,8,1280]{3,2,1,0:T(8,128)(2,1)}), bf16[8,34,8,1280]{3,2,1,0:T(8,128)(2,1)}, u32[]{:S(2)}, u32[]{:S(2)}) async-start(bf16[8,34,8,1280]{3,2,1,0:T(8,128)(2,1)} %get-tuple-element.189), calls=%async_computation.11 | async-start | bytes 11141120 | tf_op jit(solution)/shard_map/all_to_all | solution.py:842
  1178.3 138.4 %all-to-all-start.12 = ((bf16[8,37,8,1280]{3,2,1,0:T(8,128)(2,1)}), bf16[8,37,8,1280]{3,2,1,0:T(8,128)(2,1)}, u32[]{:S(2)}, u32[]{:S(2)}) async-start(bf16[8,37,8,1280]{3,2,1,0:T(8,128)(2,1)} %get-tuple-element.200), calls=%async_computation.12 | async-start | bytes 12124160 | tf_op jit(solution)/shard_map/all_to_all | solution.py:842
  1316.7 5.4 copy-start.25
  1316.7 5.4 copy-start.26
  1316.7 127.3 %all-to-all-start.13 = ((bf16[8,34,8,1280]{3,2,1,0:T(8,128)(2,1)}), bf16[8,34,8,1280]{3,2,1,0:T(8,128)(2,1)}, u32[]{:S(2)}, u32[]{:S(2)}) async-start(bf16[8,34,8,1280]{3,2,1,0:T(8,128)(2,1)} %get-tuple-element.207), calls=%async_computation.13 | async-start | bytes 11141120 | tf_op jit(solution)/shard_map/all_to_all | solution.py:842
  1324.5 6.7 copy-start.17
  1324.5 7.5 copy-start.18
  1324.5 8.7 copy-start.19
  1443.9 73.8 %all-to-all-start.14 = ((bf16[8,19,8,1280]{3,2,1,0:T(8,128)(2,1)}), bf16[8,19,8,1280]{3,2,1,0:T(8,128)(2,1)S(1)}, u32[]{:S(2)}, u32[]{:S(2)}) async-start(bf16[8,19,8,1280]{3,2,1,0:T(8,128)(2,1)} %get-tuple-element.214), calls=%async_computation.14 | async-start | bytes 6225920 | tf_op jit(solution)/shard_map/all_to_all | solution.py:842
  1459.2 7.2 collective-permute-start.3
  1519.4 73.8 %all-to-all-start.15 = ((bf16[8,19,8,1280]{3,2,1,0:T(8,128)(2,1)}), bf16[8,19,8,1280]{3,2,1,0:T(8,128)(2,1)S(1)}, u32[]{:S(2)}, u32[]{:S(2)}) async-start(bf16[8,19,8,1280]{3,2,1,0:T(8,128)(2,1)} %get-tuple-element.218), calls=%async_computation.15 | async-start | bytes 6225920 | tf_op jit(solution)/shard_map/all_to_all | solution.py:842
  1529.8 45.0 %collective-permute-start.4 = (f32[384,1282]{0,1:T(8,128)}, f32[384,1282]{0,1:T(8,128)}, u32[]{:S(2)}, u32[]{:S(2)}) collective-permute-start(f32[384,1282]{0,1:T(8,128)} %copy.156), channel_id=1, source_target_pairs={{0,2},{1,3},{2,0},{3,1},{4,6},{5,7},{6,4},{7,5},{8,10},{9,11},{10,... | collective-permute-start | bytes 5907464 | tf_op jit(solution)/shard_map/ppermute | solution.py:904
  1594.9 73.8 %all-to-all-start.16 = ((bf16[8,19,8,1280]{3,2,1,0:T(8,128)(2,1)}), bf16[8,19,8,1280]{3,2,1,0:T(8,128)(2,1)S(1)}, u32[]{:S(2)}, u32[]{:S(2)}) async-start(bf16[8,19,8,1280]{3,2,1,0:T(8,128)(2,1)} %rows_to_degrees.7), calls=%async_computation.16 | async-start | bytes 6225920 | tf_op jit(solution)/shard_map/all_to_all | solution.py:842
  1599.2 58.4 %copy-start.14 = (f32[384,1282]{1,0:T(8,128)S(1)}, f32[384,1282]{1,0:T(8,128)}, u32[]{:S(2)}) copy-start(f32[384,1282]{1,0:T(8,128)} %select_add_fusion.1) | copy-start | bytes 5907460
  1601.1 56.5 %collective-permute-start.5 = (f32[192,1282]{1,0:T(8,128)S(1)}, f32[192,1282]{1,0:T(8,128)S(1)}, u32[]{:S(2)}, u32[]{:S(2)}) collective-permute-start(f32[192,1282]{1,0:T(8,128)S(1)} %slice_select_fusion.2), channel_id=1, source_target_pairs={{0,4},{4,0},{8,12},{12,8},{16,20},{20,16},{24,28},{28,24},{1,5},{5... | collective-permute-start | bytes 2953736 | tf_op jit(solution)/shard_map/ppermute | solution.py:904
  1668.7 89.0 %all-to-all-start.17 = ((bf16[8,19,8,1280]{3,2,1,0:T(8,128)(2,1)}), bf16[8,19,8,1280]{3,2,1,0:T(8,128)(2,1)}, u32[]{:S(2)}, u32[]{:S(2)}) async-start(bf16[8,19,8,1280]{3,2,1,0:T(8,128)(2,1)} %get-tuple-element.220), calls=%async_computation.17 | async-start | bytes 6225920 | tf_op jit(solution)/shard_map/all_to_all | solution.py:842
  1674.7 60.7 %collective-permute-start.6 = (f32[96,1282]{1,0:T(8,128)S(1)}, f32[96,1282]{1,0:T(8,128)S(1)}, u32[]{:S(2)}, u32[]{:S(2)}) collective-permute-start(f32[96,1282]{1,0:T(8,128)S(1)} %slice_select_fusion.3), channel_id=1, source_target_pairs={{0,8},{4,12},{8,0},{12,4},{16,24},{20,28},{24,16},{28,20},{1,9},{5... | collective-permute-start | bytes 1476872 | tf_op jit(solution)/shard_map/ppermute | solution.py:904
  1757.7 107.3 %all-to-all-start.18 = ((bf16[8,19,8,1280]{3,2,1,0:T(8,128)(2,1)}), bf16[8,19,8,1280]{3,2,1,0:T(8,128)(2,1)S(1)}, u32[]{:S(2)}, u32[]{:S(2)}) async-start(bf16[8,19,8,1280]{3,2,1,0:T(8,128)(2,1)} %get-tuple-element.234), calls=%async_computation.18 | async-start | bytes 6225920 | tf_op jit(solution)/shard_map/all_to_all | solution.py:842
  1764.8 78.9 %collective-permute-start.7 = (f32[48,1282]{1,0:T(8,128)S(1)}, f32[48,1282]{1,0:T(8,128)S(1)}, u32[]{:S(2)}, u32[]{:S(2)}) collective-permute-start(f32[48,1282]{1,0:T(8,128)S(1)} %slice_select_fusion.4), channel_id=1, source_target_pairs={{0,16},{4,20},{8,24},{12,28},{16,0},{20,4},{24,8},{28,12},{1,17},{... | collective-permute-start | bytes 738440 | tf_op jit(solution)/shard_map/ppermute | solution.py:904
  1866.7 80.4 %all-to-all-start.19 = ((bf16[8,19,8,1280]{3,2,1,0:T(8,128)(2,1)}), bf16[8,19,8,1280]{3,2,1,0:T(8,128)(2,1)S(1)}, u32[]{:S(2)}, u32[]{:S(2)}) async-start(bf16[8,19,8,1280]{3,2,1,0:T(8,128)(2,1)} %get-tuple-element.235), calls=%async_computation.19 | async-start | bytes 6225920 | tf_op jit(solution)/shard_map/all_to_all | solution.py:842
  1877.5 5.9 copy-start.2
  1883.4 63.7 %collective-permute-start.11 = (bf16[6,8,24,1408]{3,2,1,0:T(8,128)(2,1)S(1)}, bf16[6,8,24,1408]{3,2,1,0:T(8,128)(2,1)}, u32[]{:S(2)}, u32[]{:S(2)}) collective-permute-start(bf16[6,8,24,1408]{3,2,1,0:T(8,128)(2,1)S(1)} %get-tuple-element.269), channel_id=1, source_target_pairs={{0,1},{1,0},{2,3},{3,2},{4,5},{5,4},{6,7},{7,6},{8,9},{9,8},{10,11... | collective-permute-start | bytes 9732104 | tf_op jit(solution)/shard_map/ppermute | solution.py:875
  1883.4 62.9 %collective-permute-start.8 = (bf16[48,1282]{1,0:T(8,128)(2,1)S(1)}, bf16[48,1282]{1,0:T(8,128)(2,1)S(1)}, u32[]{:S(2)}, u32[]{:S(2)}) collective-permute-start(bf16[48,1282]{1,0:T(8,128)(2,1)S(1)} %select_add_fusion.4), channel_id=1, source_target_pairs={{0,16},{4,20},{8,24},{12,28},{16,0},{20,4},{24,8},{28,12},{1,17},{... | collective-permute-start | bytes 369224 | tf_op jit(solution)/shard_map/ppermute | solution.py:913
  1948.7 78.2 %all-to-all-start.20 = ((bf16[8,19,8,1280]{3,2,1,0:T(8,128)(2,1)}), bf16[8,19,8,1280]{3,2,1,0:T(8,128)(2,1)}, u32[]{:S(2)}, u32[]{:S(2)}) async-start(bf16[8,19,8,1280]{3,2,1,0:T(8,128)(2,1)} %get-tuple-element.241), calls=%async_computation.20 | async-start | bytes 6225920 | tf_op jit(solution)/shard_map/all_to_all | solution.py:842
  1955.6 71.3 %collective-permute-start.10 = (bf16[6,8,24,1408]{3,2,1,0:T(8,128)(2,1)S(1)}, bf16[6,8,24,1408]{3,2,1,0:T(8,128)(2,1)}, u32[]{:S(2)}, u32[]{:S(2)}) collective-permute-start(bf16[6,8,24,1408]{3,2,1,0:T(8,128)(2,1)S(1)} %constant_dynamic-slice_fusion.3), channel_id=1, source_target_pairs={{0,2},{1,3},{2,0},{3,1},{4,6},{5,7},{6,4},{7,5},{8,10},{9,11},{10,... | collective-permute-start | bytes 9732104 | tf_op jit(solution)/shard_map/ppermute | solution.py:875
  1955.7 54.0 %collective-permute-start.9 = (bf16[96,1282]{1,0:T(8,128)(2,1)}, bf16[96,1282]{1,0:T(8,128)(2,1)}, u32[]{:S(2)}, u32[]{:S(2)}) collective-permute-start(bf16[96,1282]{1,0:T(8,128)(2,1)} %pad_maximum_fusion.9), channel_id=1, source_target_pairs={{0,8},{4,12},{8,0},{12,4},{16,24},{20,28},{24,16},{28,20},{1,9},{5... | collective-permute-start | bytes 738440 | tf_op jit(solution)/shard_map/ppermute | solution.py:913
  2026.9 81.2 %all-to-all-start.21 = ((bf16[8,19,8,1280]{3,2,1,0:T(8,128)(2,1)}), bf16[8,19,8,1280]{3,2,1,0:T(8,128)(2,1)S(1)}, u32[]{:S(2)}, u32[]{:S(2)}) async-start(bf16[8,19,8,1280]{3,2,1,0:T(8,128)(2,1)} %degrees_to_rows.6), calls=%async_computation.21 | async-start | bytes 6225920 | tf_op jit(solution)/shard_map/all_to_all | solution.py:842
  2036.5 71.7 %collective-permute-start.13 = (bf16[6,8,24,1408]{3,2,1,0:T(8,128)(2,1)}, bf16[6,8,24,1408]{3,2,1,0:T(8,128)(2,1)}, u32[]{:S(2)}, u32[]{:S(2)}) collective-permute-start(bf16[6,8,24,1408]{3,2,1,0:T(8,128)(2,1)} %constant_dynamic-slice_fusion), channel_id=1, source_target_pairs={{0,3},{1,2},{2,1},{3,0},{4,7},{5,6},{6,5},{7,4},{8,11},{9,10},{10,... | collective-permute-start | bytes 9732104 | tf_op jit(solution)/shard_map/ppermute | solution.py:875
  2036.5 38.3 %collective-permute-start.12 = (bf16[192,1282]{1,0:T(8,128)(2,1)}, bf16[192,1282]{1,0:T(8,128)(2,1)}, u32[]{:S(2)}, u32[]{:S(2)}) collective-permute-start(bf16[192,1282]{1,0:T(8,128)(2,1)} %pad_maximum_fusion.4), channel_id=1, source_target_pairs={{0,4},{4,0},{8,12},{12,8},{16,20},{20,16},{24,28},{28,24},{1,5},{5... | collective-permute-start | bytes 1476872 | tf_op jit(solution)/shard_map/ppermute | solution.py:913
  2109.8 191.1 %all-to-all-start.22 = ((bf16[8,52,8,1280]{3,2,1,0:T(8,128)(2,1)}), bf16[8,52,8,1280]{3,2,1,0:T(8,128)(2,1)}, u32[]{:S(2)}, u32[]{:S(2)}) async-start(bf16[8,52,8,1280]{3,2,1,0:T(8,128)(2,1)} %get-tuple-element.251), calls=%async_computation.22 | async-start | bytes 17039360 | tf_op jit(solution)/shard_map/all_to_all | solution.py:842
  2300.9 87.2 %all-to-all-start.23 = ((bf16[8,19,8,1280]{3,2,1,0:T(8,128)(2,1)}), bf16[8,19,8,1280]{3,2,1,0:T(8,128)(2,1)S(1)}, u32[]{:S(2)}, u32[]{:S(2)}) async-start(bf16[8,19,8,1280]{3,2,1,0:T(8,128)(2,1)} %get-tuple-element.258), calls=%async_computation.23 | async-start | bytes 6225920 | tf_op jit(solution)/shard_map/all_to_all | solution.py:842
  2307.1 24.4 %collective-permute-start.14 = (bf16[384,1282]{0,1:T(8,128)(2,1)}, bf16[384,1282]{0,1:T(8,128)(2,1)}, u32[]{:S(2)}, u32[]{:S(2)}) collective-permute-start(bf16[384,1282]{0,1:T(8,128)(2,1)} %copy.161), channel_id=1, source_target_pairs={{0,2},{1,3},{2,0},{3,1},{4,6},{5,7},{6,4},{7,5},{8,10},{9,11},{10,... | collective-permute-start | bytes 2953736 | tf_op jit(solution)/shard_map/ppermute | solution.py:913
  2341.2 42.8 %collective-permute-start.15 = (bf16[768,1282]{0,1:T(8,128)(2,1)}, bf16[768,1282]{0,1:T(8,128)(2,1)}, u32[]{:S(2)}, u32[]{:S(2)}) collective-permute-start(bf16[768,1282]{0,1:T(8,128)(2,1)} %copy.165), channel_id=1, source_target_pairs={{0,1},{1,0},{2,3},{3,2},{4,5},{5,4},{6,7},{7,6},{8,9},{9,8},{10,11... | collective-permute-start | bytes 5907464 | tf_op jit(solution)/shard_map/ppermute | solution.py:913
  2405.7 3.2 collective-permute-start.16
  2409.0 5.3 collective-permute-start.17
  2414.3 3.7 collective-permute-start.18
  2418.0 3.6 collective-permute-start.19
  2421.7 4.5 collective-permute-start.20
  (19 other events, 56.9 us)

commit v4 on v3

--- a/solution.py
+++ b/solution.py
@@ -596,7 +596,7 @@
 
 def pixel_body(
     synth, tail, state, cotangent, table, gain, bias, up, up_turned, up_bias, down, down_turned,
-    down_bias, out, middle_grad, synth_grad, up_grad, down_grad, wide_sums, narrow_sums, held,
+    down_bias, out, middle_grad, synth_grad, dense, wide_sums, narrow_sums, held,
     wide_held, narrow_held, tails,
 ):
     step, last = pl.program_id(0), pl.num_programs(0) - 1
@@ -606,8 +606,7 @@
     @pl.when(step == 0)
     def _():
         held[...] = jnp.zeros_like(held)
-        up_grad[...] = jnp.zeros_like(up_grad)
-        down_grad[...] = jnp.zeros_like(down_grad)
+        dense[...] = jnp.zeros_like(dense)
         wide_held[...] = jnp.zeros_like(wide_held)
         narrow_held[...] = jnp.zeros_like(narrow_held)
         tails[...] = jnp.zeros_like(tails)
@@ -631,8 +630,8 @@
         pre_grad = dot(down[...], grad_low, 1, 0) * slope
         pre_low = pre_grad.astype(bf16)
         wide_held[...] += pre_grad
-        down_grad[...] += dot(grad_low, hidden_low, 1, 1)
-        up_grad[...] += dot(normed_low, pre_low, 1, 1)
+        dense[1, :C] += dot(grad_low, hidden_low, 1, 1)
+        dense[0, :C] += dot(normed_low, pre_low, 1, 1)
         normed_grad = dot(up[...], pre_low, 1, 0)
         narrow_held[0] += normed_grad * xhat
         narrow_held[1] += normed_grad
@@ -658,7 +657,7 @@
         narrow_sums[...] = jnp.sum(narrow_held[...], axis=2, keepdims=True)
 
 
-def pixels(synth, state, cotangent, table, params, first, into):
+def pixels(synth, state, cotangent, table, params, first, into, dense_rows):
     n_lat, subs = synth.shape[0], table.shape[0] // (2 * synth.shape[0])
     per = subs // 8
     count = (synth.shape[1] - 1) // per
@@ -684,8 +683,7 @@
             row_spec,
             pl.BlockSpec((1, C, points), lambda r: (row(r) + first, 0, 0)),
             wave(lambda r: r),
-            whole((C, hidden)),
-            whole((C, hidden)),
+            whole((2, dense_rows, hidden)),
             whole((hidden, 1)),
             whole((3, C, 1)),
         ],
@@ -693,8 +691,7 @@
             shaped(state.shape),
             shaped((state.shape[0], C, points)),
             shaped(synth.shape, bf16),
-            shaped((C, hidden)),
-            shaped((C, hidden)),
+            shaped((2, dense_rows, hidden)),
             shaped((hidden, 1)),
             shaped((3, C, 1)),
         ],
@@ -835,13 +832,13 @@
         self.aside = None
 
     def swap(self, values):
+        self.step_aside()
         waits = self.work + ([] if self.last is None else [self.last])
         if waits:
             values = lax.optimization_barrier((values, waits))[0]
         self.before = self.last
         self.last = lax.all_to_all(values, "lat", split_axis=0, concat_axis=0, tiled=True)
         self.work, self.later = self.later, []
-        self.step_aside()
         return self.last
 
     def step_aside(self):
@@ -852,6 +849,9 @@
         if self.before is None:
             return values
         return lax.optimization_barrier((values, self.before))[0]
+
+    def after_work(self, values):
+        return lax.optimization_barrier((values, self.work))[0] if self.work else values
 
     def keep(self, values):
         self.work.append(values)
@@ -887,39 +887,58 @@
     return values
 
 
-def add_dense(arrays, axes, line, result):
-    columns = max(array.shape[1] for array in arrays)
-    heights = [array.shape[0] for array in arrays]
-    steps = [
-        (axis, 2**k) for axis, size in axes for k in range(size.bit_length() - 1)
-    ]
-    rows = -(-sum(heights) // (8 * 2 ** len(steps))) * 8 * 2 ** len(steps)
-    wide = [jnp.pad(a, ((0, 0), (0, columns - a.shape[1]))) for a in arrays]
-    held = jnp.pad(jnp.concatenate(wide, axis=0), ((0, rows - sum(heights)), (0, 0)))
-    sizes = dict(axes)
+def add_dense(array, n_lat, n_chan, line, result):
+    shape, columns = array.shape, array.shape[2]
+    sizes = {"chan": n_chan, "lat": n_lat}
+    pairs = [("chan", 2**k) for k in range(n_chan.bit_length() - 1)] + [("lat", 1)]
+    others = n_lat // 2
+    held = array.reshape(-1, columns)
     odd = lambda axis, step: (lax.axis_index(axis) // step) % 2 == 1
-    for axis, step in steps:
+    group = lax.axis_index("lat") // 2
+
+    def halve(held, axis, step):
         low, high = jnp.split(line.hold(held), 2, axis=0)
         upper = odd(axis, step)
         other = lax.ppermute(jnp.where(upper, low, high), axis, partners(sizes[axis], step)[0])
-        held = line.keep_later(jnp.where(upper, high, low) + other)
-        yield
-    held = held.astype(bf16)
-    for axis, step in reversed(steps):
-        if (axis, step) == steps[1]:
-            yield
-        held = line.hold(held)
+        return line.keep(jnp.where(upper, high, low) + other)
+
+    def double(held, axis, step):
         upper = odd(axis, step)
-        other = lax.ppermute(held, axis, partners(sizes[axis], step)[0])
-        held = jnp.concatenate(
-            [jnp.where(upper, other, held), jnp.where(upper, held, other)], axis=0
+        other = lax.ppermute(line.hold(held), axis, partners(sizes[axis], step)[0])
+        return line.keep_later(
+            jnp.concatenate([jnp.where(upper, other, held), jnp.where(upper, held, other)], axis=0)
         )
-        line.keep_later(held)
-        yield
-    begin = 0
-    for array, height in zip(arrays, heights):
-        result.append(held[begin : begin + height, : array.shape[1]].astype(f32))
-        begin += height
+
+    for axis, step in pairs[:-1]:
+        held = halve(held, axis, step)
+    yield
+    yield
+    held = halve(held, *pairs[-1])
+    yield
+    pieces = line.hold(held).reshape(others, -1, columns)
+    own = lax.dynamic_index_in_dim(pieces, group, 0, False)
+    for step in range(1, others):
+        block = lax.dynamic_index_in_dim(pieces, jnp.bitwise_xor(group, step), 0, False)
+        block = lax.ppermute(block.astype(bf16), "lat", partners(n_lat, 2 * step)[0])
+        own = own + block.astype(f32)
+    own = line.keep_later(own).astype(bf16)
+    yield
+    yield
+    yield
+    own = line.hold(own)
+    held = jnp.zeros((others,) + own.shape, bf16)
+    for step in range(others):
+        block = lax.ppermute(own, "lat", partners(n_lat, 2 * step)[0]) if step else own
+        held = lax.dynamic_update_index_in_dim(held, block, jnp.bitwise_xor(group, step), 0)
+    held = line.keep_later(held).reshape(-1, columns)
+    yield
+    yield
+    yield
+    for axis, step in reversed(pairs[1:]):
+        held = double(held, axis, step)
+    yield
+    held = double(held, *pairs[0])
+    result.append(held.astype(f32).reshape(shape))
 
 
 def shards(
@@ -949,6 +968,8 @@
         return part_rows(values).transpose(2, 0, 1, 3)
 
     line = Line()
+    dense_unit = 4 * n_lat * n_chan
+    dense_rows = -(-(C + 3) // dense_unit) * dense_unit
     row_cuts = [(fine_dev + 1) // 2, fine_dev // 2] if fine_dev >= 8 else [fine_dev]
     row_starts = [sum(row_cuts[:k]) for k in range(len(row_cuts))]
     outer_cuts = [fine_dev // 4 + 1, fine_dev - fine_dev // 4 - 1] if fine_dev >= 8 else [fine_dev]
@@ -1028,7 +1049,7 @@
         def share_next(count=1):
             members = joined_rows([made[2] for made in mixed])
             for step in range(len(shared), min(len(shared) + count, n_chan)):
-                shared.append(line.keep(share_slots(line.hold(members), n_chan, step)))
+                shared.append(line.keep_later(share_slots(line.hold(members), n_chan, step)))
 
         arrived.append(line.swap(fine_made[0]))
         coarse_made = lane_call(
@@ -1079,14 +1100,16 @@
     def fine_pixels(k, synth):
         into = fine_made[-1][:2] if fine_made else None
         made = pixels(
-            line.hold(synth), fine_x, fine_g, fine_inverse, params, row_starts[k], into
+            line.hold(synth), fine_x, fine_g, fine_inverse, params, row_starts[k], into,
+            dense_rows,
         )
         fine_made.append(line.keep(made))
 
     def forward_aside(k, coarse_end, fine_end, shared):
         if k == 0:
             made = pixels(
-                line.hold(coarse_end), coarse_x, coarse_g, coarse_inverse, params, 0, None
+                line.hold(coarse_end), coarse_x, coarse_g, coarse_inverse, params, 0, None,
+                dense_rows,
             )
             coarse_made.extend(line.keep(made))
         else:
@@ -1110,10 +1133,11 @@
     total = coarse_made[3:]
     for made in fine_made:
         total = [x + y for x, y in zip(total, made[3:])]
-    narrow = jnp.concatenate([total[2][:, 0], total[3].reshape(-1)])
-    narrow = jnp.pad(narrow, (0, -narrow.shape[0] % hidden)).reshape(-1, hidden)
+    narrow = jnp.concatenate([total[1][:, 0], total[2].reshape(-1)])
+    narrow = jnp.pad(narrow, (0, 3 * hidden - narrow.shape[0])).reshape(1, 3, hidden)
+    stacked = lax.dynamic_update_slice(total[0], narrow, (0, C, 0))
     dense = []
-    line.aside = add_dense([line.hold(total[0]), total[1], narrow], axes, line, dense)
+    line.aside = add_dense(line.hold(stacked), n_lat, n_chan, line, dense)
     line.step_aside()
     coarse_sgrad = line.swap(coarse_made[2])
     if len(row_cuts) == 1:
@@ -1144,8 +1168,8 @@
     )
     for unused in line.aside:
         pass
-    up_grad, down_grad, narrow = dense
-    narrow = narrow.reshape(-1)
+    up_grad, down_grad = dense[0][0, :C], dense[0][1, :C]
+    narrow = dense[0][0, C : C + 3].reshape(-1)
     narrow_sums = narrow[hidden : hidden + 3 * C].reshape(3, C)
     if len(row_cuts) == 1:
         ends[0][0] = coarse_back(ends[0][0])

time: 2440 us -> 2380 us (0.975)
  waiting for transfers between devices: 1150 us -> 1050 us
  blocking collectives: 74.1 us -> 148 us
    all_to_all x1 -> x2, blocking collectives: 74.1 us -> 148 us  [swap(): lax.all_to_all(values, 'lat', split_axis=0, concat_axis=0, tiled=True)]
    ppermute x10 -> x12, waiting for transfers between devices: 409 us -> 338 us  [the longest x3 101 us: double(): other = lax.ppermute(line.hold(held), axis, partners(sizes[axis], step)[0])]
    ppermute x6, waiting for transfers between devices: 115 us -> 80.4 us  [share_slots(): return lax.ppermute(block, 'chan', route) if step else block]
    all_to_all x23 -> x22, starting transfers between devices: 111 us -> 100 us  [swap(): lax.all_to_all(values, 'lat', split_axis=0, concat_axis=0, tiled=True)]
    all_to_all x23 -> x22, waiting for transfers between devices: 620 us -> 629 us  [swap(): lax.all_to_all(values, 'lat', split_axis=0, concat_axis=0, tiled=True)]
    unnamed x85 -> x87, local copies, waits for them, and re-layouts: 70.1 us -> 69.8 us
  transfers between devices with their start and end apart: 44 -> 45, of which waited for: 31 -> 33; matrix products, arithmetic and copies ran while one was open for 14% -> 13% of each run, Pallas kernels for 27% -> 28%
where the time goes in v4:
time: 2380 us; the launch traced here: 2360 us
  waiting for transfers between devices  1050 us (44%)
  Pallas kernels  692 us (29%)
  local copies, waits for them, and re-layouts  237 us (10%)
  blocking collectives  148 us (6%)
  starting transfers between devices  119 us (5%)
  other arithmetic  112 us (5%)
    all_to_all x22, waiting for transfers between devices, swap(): lax.all_to_all(values, 'lat', split_axis=0, concat_axis=0, tiled=True)  629 us
    pallas_call x3, Pallas kernels, pixels(): call(body, 'feed_forward', 2 * count * points * (6 * C * hidden + 2 * tab...  322 us
    all_to_all x2, blocking collectives, swap(): lax.all_to_all(values, 'lat', split_axis=0, concat_axis=0, tiled=True)  148 us
    pallas_call x8, Pallas kernels, lane_call(): call(functools.partial(lane_body, work, subs, width, len(inputs), len(tab...  106 us
    ppermute x3, waiting for transfers between devices, double(): other = lax.ppermute(line.hold(held), axis, partners(sizes[axis], step)[0])  101 us
    all_to_all x22, starting transfers between devices, swap(): lax.all_to_all(values, 'lat', split_axis=0, concat_axis=0, tiled=True)  100 us
    ppermute x3, waiting for transfers between devices, halve(): lax.ppermute(jnp.where(upper, low, high), axis, partners(sizes[axis], ste...  89.6 us
    pallas_call x4, Pallas kernels, mix(): call(body, 'mix_back' if backward else 'mix', 2 * count * n_lat * subs *...  81.1 us
  transfers between devices with their start and end apart: 45, of which 33 were waited for; matrix products, arithmetic and copies ran while one was open for 13% of the time, Pallas kernels for 28%

profile of v4, /device:TPU:0, one launch (start us, length us, event | category | flops | bytes accessed | tf_op | source)
XLA Modules:
  0.0 2363.2 jit_solution(6203998585393168585)
XLA Ops:
  6.8 10.0 norm_and_dft.3
  16.8 7.2 all-to-all-start
  24.0 24.3 %norm_and_dft.4 = bf16[8,52,8,1280]{3,2,1,0:T(8,128)(2,1)} custom-call(f32[23,641,1,360]{3,2,1,0:T(1,128)} %bitcast.109, s32[23,8,360]{2,1,0:T(8,128)} %bitcast.153, f32[641,1]{1,0:T(8,128)} %broadcast_in_dim.222.gain.refs_5_, f32[641,1]{1,0:T(8,128)} %broadcast_in_dim.223.bias, bf16[384,360]{1,0:T(8,128)(2,1)} %pad_maximum_fusion.4.table.refs_4_), custom_call_target="tpu_custom_call" | custom-call | flops 3609722880 | bytes 24883104 | tf_op jit(solution)/shard_map/norm_and_dft/pallas_call | solution.py:162
  48.4 45.7 %all-to-all-done.refs_0_.refs_2_ = bf16[8,19,8,1280]{3,2,1,0:T(8,128)(2,1)S(1)} async-done(((bf16[8,19,8,1280]{3,2,1,0:T(8,128)(2,1)}), bf16[8,19,8,1280]{3,2,1,0:T(8,128)(2,1)S(1)}, u32[]{:S(2)}, u32[]{:S(2)}) %all-to-all-start) | async-done | bytes 3112992 | tf_op jit(solution)/shard_map/all_to_all | solution.py:840
  100.7 20.7 reduce
  121.4 7.2 reshape_squeeze.12
  128.5 7.5 copy.180
  136.0 8.2 broadcast_in_dim.203.state
  148.2 10.0 norm_and_dft.5
  158.2 127.5 %all-to-all-done.1.refs_1_.refs_3_ = bf16[8,52,8,1280]{3,2,1,0:T(8,128)(2,1)} async-done(((bf16[8,52,8,1280]{3,2,1,0:T(8,128)(2,1)}), bf16[8,52,8,1280]{3,2,1,0:T(8,128)(2,1)}, u32[]{:S(2)}, u32[]{:S(2)}) %all-to-all-start.1) | async-done | bytes 8519712 | tf_op jit(solution)/shard_map/all_to_all | solution.py:840
  294.0 13.2 legendre_tables.3
  335.9 17.0 rows_to_degrees.4
  377.9 9.5 rows_to_degrees.5
  387.4 47.8 %all-to-all-done.3.fine.fine_tail = bf16[8,19,8,1280]{3,2,1,0:T(8,128)(2,1)S(1)} async-done(((bf16[8,19,8,1280]{3,2,1,0:T(8,128)(2,1)}), bf16[8,19,8,1280]{3,2,1,0:T(8,128)(2,1)S(1)}, u32[]{:S(2)}, u32[]{:S(2)}) %all-to-all-start.3) | async-done | bytes 3112992 | tf_op jit(solution)/shard_map/all_to_all | solution.py:840
  435.2 74.1 %all_to_all.120.coarse.coarse_tail.refs_3_.refs_4_ = bf16[8,19,8,1280]{3,2,1,0:T(8,128)(2,1)} all-to-all(bf16[8,19,8,1280]{3,2,1,0:T(8,128)(2,1)} %rows_to_degrees.5), channel_id=1, replica_groups=mesh['lat'=8,'chan'=4] {'lat'}, dimensions={0} | all-to-all | bytes 6225920 | tf_op jit(solution)/shard_map/all_to_all | solution.py:840
  514.9 31.7 %copy.242 = bf16[24,2,649,641]{2,3,1,0:T(8,128)(2,1)} copy(bf16[24,2,649,641]{2,1,3,0:T(2,128)(2,1)} %param.27) | data formatting | bytes 79873728 | tf_op args[9]
  547.2 20.4 mix.2
  567.6 15.4 all-to-all-done.5.refs_1_.refs_2_
  586.6 20.3 mix.3
  606.9 49.8 %all-to-all-done.6.refs_0_.refs_2_ = bf16[8,19,8,1280]{3,2,1,0:T(8,128)(2,1)S(1)} async-done(((bf16[8,19,8,1280]{3,2,1,0:T(8,128)(2,1)}), bf16[8,19,8,1280]{3,2,1,0:T(8,128)(2,1)S(1)}, u32[]{:S(2)}, u32[]{:S(2)}) %all-to-all-start.6) | async-done | bytes 3112992 | tf_op jit(solution)/shard_map/all_to_all | solution.py:840
  656.7 74.1 %all_to_all.121.refs_0_.refs_1_ = bf16[8,19,8,1280]{3,2,1,0:T(8,128)(2,1)} all-to-all(bf16[8,19,8,1280]{3,2,1,0:T(8,128)(2,1)} %get-tuple-element.160), channel_id=1, replica_groups=mesh['lat'=8,'chan'=4] {'lat'}, dimensions={0} | all-to-all | bytes 6225920 | tf_op jit(solution)/shard_map/all_to_all | solution.py:840
  751.6 9.5 degrees_to_rows.4
  761.1 42.8 %all-to-all-done.8.refs_1_.refs_3_ = bf16[8,19,8,1280]{3,2,1,0:T(8,128)(2,1)S(1)} async-done(((bf16[8,19,8,1280]{3,2,1,0:T(8,128)(2,1)}), bf16[8,19,8,1280]{3,2,1,0:T(8,128)(2,1)S(1)}, u32[]{:S(2)}, u32[]{:S(2)}) %all-to-all-start.8) | async-done | bytes 3112992 | tf_op jit(solution)/shard_map/all_to_all | solution.py:840
  816.0 13.2 legendre_tables.5
  839.6 17.0 degrees_to_rows.5
  856.6 28.6 %collective-permute-done.1.refs_2_ = bf16[6,8,24,1408]{3,2,1,0:T(8,128)(2,1)} collective-permute-done((bf16[6,8,24,1408]{3,2,1,0:T(8,128)(2,1)}, bf16[6,8,24,1408]{3,2,1,0:T(8,128)(2,1)}, u32[]{:S(2)}, u32[]{:S(2)}) %collective-permute-start.1) | collective-permute-done | bytes 3244064 | tf_op jit(solution)/shard_map/ppermute | solution.py:875
  904.9 20.7 reduce.1
  932.7 7.5 copy.193
  940.2 8.2 broadcast_in_dim.209.cotangent
  949.2 70.8 %feed_forward.3 = (f32[6,641,1,360]{3,2,1,0:T(1,128)}, f32[6,641,360]{2,1,0:T(8,128)}, bf16[8,19,8,1280]{3,2,1,0:T(8,128)(2,1)}, f32[2,768,1282]{2,1,0:T(8,128)}...) custom-call(bf16[8,19,8,1280]{3,2,1,0:T(8,128)(2,1)} %all-to-all-done.9.synth.tail, ...), custom_call_target="tpu_custom_call" | custom-call | flops 23848110080 | bytes 28641024 | tf_op jit(solution)/shard_map/feed_forward/pallas_call | solution.py:674
  1028.4 8.2 part_rows.2
  1036.6 130.7 %feed_forward.4 = (f32[23,641,1,360]{3,2,1,0:T(1,128)}, f32[23,641,360]{2,1,0:T(8,128)}, bf16[8,37,8,1280]{3,2,1,0:T(8,128)(2,1)}, f32[2,768,1282]{2,1,0:T(8,128...) custom-call(bf16[8,37,8,1280]{3,2,1,0:T(8,128)(2,1)} %all-to-all-done.10.synth.tail, ...), custom_call_target="tpu_custom_call" | custom-call | flops 47696220160 | bytes 57282048 | tf_op jit(solution)/shard_map/feed_forward/pallas_call | solution.py:674
  1173.6 120.8 %feed_forward.5 = (f32[23,641,1,360]{3,2,1,0:T(1,128)}, f32[23,641,360]{2,1,0:T(8,128)}, bf16[8,34,8,1280]{3,2,1,0:T(8,128)(2,1)}, f32[2,768,1282]{2,1,0:T(8,128...) custom-call(bf16[8,34,8,1280]{3,2,1,0:T(8,128)(2,1)} %all-to-all-done.11.refs_0_.refs_, ...), custom_call_target="tpu_custom_call", output_to_operand_aliasing={{0}: (13, {}), {1}: (14, {})} | custom-call | flops 43721535488 | bytes 52508544 | tf_op jit(solution)/shard_map/feed_forward/pallas_call | solution.py:674
  1294.4 12.4 all-to-all-done.12.refs_0_.refs_2_
  1312.0 12.8 add_add_fusion
  1339.9 7.2 collective-permute-done.3
  1362.7 44.9 %collective-permute-done.4 = f32[384,1282]{0,1:T(8,128)} collective-permute-done((f32[384,1282]{0,1:T(8,128)}, f32[384,1282]{0,1:T(8,128)}, u32[]{:S(2)}, u32[]{:S(2)}) %collective-permute-start.4) | collective-permute-done | bytes 1969184 | tf_op jit(solution)/shard_map/ppermute | solution.py:902
  1413.8 20.1 all-to-all-done.13.refs_1_.refs_3_
  1442.2 17.0 rows_to_degrees.6
  1459.1 37.5 %collective-permute-done.5 = f32[192,1282]{1,0:T(8,128)} collective-permute-done((f32[192,1282]{1,0:T(8,128)}, f32[192,1282]{1,0:T(8,128)}, u32[]{:S(2)}, u32[]{:S(2)}) %collective-permute-start.5) | collective-permute-done | bytes 984608 | tf_op jit(solution)/shard_map/ppermute | solution.py:902
  1499.6 8.0 all-to-all-done.14.refs_0_.refs_1_
  1513.0 9.5 rows_to_degrees.7
  1522.5 60.7 %all-to-all-done.15.fine.fine_tail = bf16[8,19,8,1280]{3,2,1,0:T(8,128)(2,1)S(1)} async-done(((bf16[8,19,8,1280]{3,2,1,0:T(8,128)(2,1)}), bf16[8,19,8,1280]{3,2,1,0:T(8,128)(2,1)S(1)}, u32[]{:S(2)}, u32[]{:S(2)}) %all-to-all-start.15) | async-done | bytes 3112992 | tf_op jit(solution)/shard_map/all_to_all | solution.py:840
  1594.8 49.2 %collective-permute-done.6 = bf16[48,1282]{1,0:T(8,128)(2,1)S(1)} collective-permute-done((bf16[48,1282]{1,0:T(8,128)(2,1)}, bf16[48,1282]{1,0:T(8,128)(2,1)S(1)}, u32[]{:S(2)}, u32[]{:S(2)}) %collective-permute-start.6) | collective-permute-done | bytes 123104 | tf_op jit(solution)/shard_map/ppermute | solution.py:922
  1644.0 24.6 %collective-permute-done.7 = bf16[48,1282]{1,0:T(8,128)(2,1)S(1)} collective-permute-done((bf16[48,1282]{1,0:T(8,128)(2,1)}, bf16[48,1282]{1,0:T(8,128)(2,1)S(1)}, u32[]{:S(2)}, u32[]{:S(2)}) %collective-permute-start.7) | collective-permute-done | bytes 123104 | tf_op jit(solution)/shard_map/ppermute | solution.py:922
  1674.5 20.2 mix_back.2
  1694.7 50.9 %all-to-all-done.17.refs_1_.refs_2_ = bf16[8,19,8,1280]{3,2,1,0:T(8,128)(2,1)} async-done(((bf16[8,19,8,1280]{3,2,1,0:T(8,128)(2,1)}), bf16[8,19,8,1280]{3,2,1,0:T(8,128)(2,1)}, u32[]{:S(2)}, u32[]{:S(2)}) %all-to-all-start.17) | async-done | bytes 3112992 | tf_op jit(solution)/shard_map/all_to_all | solution.py:840
  1749.2 20.3 mix_back.3
  1769.5 49.6 %all-to-all-done.18.refs_0_.refs_2_ = bf16[8,19,8,1280]{3,2,1,0:T(8,128)(2,1)S(1)} async-done(((bf16[8,19,8,1280]{3,2,1,0:T(8,128)(2,1)}), bf16[8,19,8,1280]{3,2,1,0:T(8,128)(2,1)S(1)}, u32[]{:S(2)}, u32[]{:S(2)}) %all-to-all-start.18) | async-done | bytes 3112992 | tf_op jit(solution)/shard_map/all_to_all | solution.py:840
  1830.4 49.4 %collective-permute-done.10 = bf16[48,1282]{1,0:T(8,128)(2,1)S(1)} collective-permute-done((bf16[48,1282]{1,0:T(8,128)(2,1)S(1)}, bf16[48,1282]{1,0:T(8,128)(2,1)S(1)}, u32[]{:S(2)}, u32[]{:S(2)}) %collective-permute-start.10) | collective-permute-done | bytes 123104 | tf_op jit(solution)/shard_map/ppermute | solution.py:931
  1880.5 24.0 %collective-permute-done.11 = bf16[48,1282]{1,0:T(8,128)(2,1)S(1)} collective-permute-done((bf16[48,1282]{1,0:T(8,128)(2,1)S(1)}, bf16[48,1282]{1,0:T(8,128)(2,1)S(1)}, u32[]{:S(2)}, u32[]{:S(2)}) %collective-permute-start.11) | collective-permute-done | bytes 123104 | tf_op jit(solution)/shard_map/ppermute | solution.py:931
  1924.2 9.5 degrees_to_rows.6
  1933.8 47.1 %all-to-all-done.20.refs_1_.refs_3_ = bf16[8,19,8,1280]{3,2,1,0:T(8,128)(2,1)} async-done(((bf16[8,19,8,1280]{3,2,1,0:T(8,128)(2,1)}), bf16[8,19,8,1280]{3,2,1,0:T(8,128)(2,1)}, u32[]{:S(2)}, u32[]{:S(2)}) %all-to-all-start.20) | async-done | bytes 3112992 | tf_op jit(solution)/shard_map/all_to_all | solution.py:840
  1991.2 16.9 degrees_to_rows.7
  2008.2 51.7 %collective-permute-done.13.refs_6_ = bf16[6,8,24,1408]{3,2,1,0:T(8,128)(2,1)} collective-permute-done((bf16[6,8,24,1408]{3,2,1,0:T(8,128)(2,1)}, bf16[6,8,24,1408]{3,2,1,0:T(8,128)(2,1)}, u32[]{:S(2)}, u32[]{:S(2)}) %collective-permute-start.13) | collective-permute-done | bytes 3244064 | tf_op jit(solution)/shard_map/ppermute | solution.py:875
  2073.1 74.6 %collective-permute-done.15 = bf16[192,1282]{1,0:T(8,128)(2,1)S(1)} collective-permute-done((bf16[192,1282]{1,0:T(8,128)(2,1)}, bf16[192,1282]{1,0:T(8,128)(2,1)S(1)}, u32[]{:S(2)}, u32[]{:S(2)}) %collective-permute-start.15) | collective-permute-done | bytes 492320 | tf_op jit(solution)/shard_map/ppermute | solution.py:907
  2150.7 22.2 collective-permute-done.16
  2177.5 14.2 first_norm_back.3
  2191.7 27.4 %mix_gradient.1 = f32[6,641,2,649]{3,2,1,0:T(2,128)} custom-call(bf16[6,8,24,1408]{3,2,1,0:T(8,128)(2,1)} %get-tuple-element.262.refs_0_, bf16[6,8,24,1408]{3,2,1,0:T(8,128)(2,1)} %collective-permute-done.refs_1_, bf16[6,8,24,1408]{3,2,1,0:T(8,128)(2,1)} %collective-permute-done.1.refs_2_, bf16[6,8,24,1408]{3,2,1,0:T(8,128)(2,1)} %collective-permute-done.2.refs_3_, ...), custom_call_target="tpu_custom_call" | custom-call | flops 15335755776 | bytes 45920688 | tf_op jit(solution)/shard_map/mix_gradient/pallas_call | solution.py:585
  2219.1 32.0 %all-to-all-done.22.wave.tail = bf16[8,52,8,1280]{3,2,1,0:T(8,128)(2,1)} async-done(((bf16[8,52,8,1280]{3,2,1,0:T(8,128)(2,1)}), bf16[8,52,8,1280]{3,2,1,0:T(8,128)(2,1)}, u32[]{:S(2)}, u32[]{:S(2)}) %all-to-all-start.22) | async-done | bytes 8519712 | tf_op jit(solution)/shard_map/all_to_all | solution.py:840
  2273.0 8.2 part_rows.3
  2281.2 34.6 %first_norm_back.4 = (f32[23,641,1,360]{3,2,1,0:T(1,128)}, f32[2,641,1]{2,1,0:T(8,128)}) custom-call(bf16[8,52,8,1280]{3,2,1,0:T(8,128)(2,1)} %all-to-all-done.22.wave.tail, bf16[8,52,8,1280]{3,2,1,0:T(8,128)(2,1)} %all-to-all-done.22.wave.tail, f32[23,641,1,360]{3,2,1,0:T(1,128)} %bitcast.112, f32[23,641,360]{2,1,0:T(8,128)} %get-tuple-element.195.middle_grad.refs_3_, ...), custom_call_target="tpu_custom_call" | custom-call | flops 3609722880 | bytes 56266464 | tf_op jit(solution)/shard_map/first_norm_back/pallas_call | solution.py:743
  2315.7 9.4 all-to-all-done.23.refs_0_.refs_1_
  2326.8 14.2 first_norm_back.5
  (303 shorter events, 361.4 us)
Async XLA Ops:
  16.8 77.3 %all-to-all-start = ((bf16[8,19,8,1280]{3,2,1,0:T(8,128)(2,1)}), bf16[8,19,8,1280]{3,2,1,0:T(8,128)(2,1)S(1)}, u32[]{:S(2)}, u32[]{:S(2)}) async-start(bf16[8,19,8,1280]{3,2,1,0:T(8,128)(2,1)} %norm_and_dft.3), calls=%async_computation | async-start | bytes 6225920 | tf_op jit(solution)/shard_map/all_to_all | solution.py:840
  95.7 190.0 %all-to-all-start.1 = ((bf16[8,52,8,1280]{3,2,1,0:T(8,128)(2,1)}), bf16[8,52,8,1280]{3,2,1,0:T(8,128)(2,1)}, u32[]{:S(2)}, u32[]{:S(2)}) async-start(bf16[8,52,8,1280]{3,2,1,0:T(8,128)(2,1)} %norm_and_dft.4), calls=%async_computation.1 | async-start | bytes 17039360 | tf_op jit(solution)/shard_map/all_to_all | solution.py:840
  136.0 8.2 copy-start.32
  158.2 131.4 %copy-start.38 = (s32[184]{0:T(256)S(1)}, s32[184]{0:T(256)}, u32[]{:S(2)}) copy-start(s32[184]{0:T(256)} %param.23) | copy-start | bytes 2212
  285.7 74.0 %all-to-all-start.2 = ((bf16[8,19,8,1280]{3,2,1,0:T(8,128)(2,1)}), bf16[8,19,8,1280]{3,2,1,0:T(8,128)(2,1)S(1)}, u32[]{:S(2)}, u32[]{:S(2)}) async-start(bf16[8,19,8,1280]{3,2,1,0:T(8,128)(2,1)} %norm_and_dft.5), calls=%async_computation.2 | async-start | bytes 6225920 | tf_op jit(solution)/shard_map/all_to_all | solution.py:840
  361.4 73.8 %all-to-all-start.3 = ((bf16[8,19,8,1280]{3,2,1,0:T(8,128)(2,1)}), bf16[8,19,8,1280]{3,2,1,0:T(8,128)(2,1)S(1)}, u32[]{:S(2)}, u32[]{:S(2)}) async-start(bf16[8,19,8,1280]{3,2,1,0:T(8,128)(2,1)} %get-tuple-element.145), calls=%async_computation.3 | async-start | bytes 6225920 | tf_op jit(solution)/shard_map/all_to_all | solution.py:840
  435.2 74.1 %copy-start.6 = (bf16[8,19,8,1280]{3,2,1,0:T(8,128)(2,1)}, bf16[8,19,8,1280]{3,2,1,0:T(8,128)(2,1)S(1)}, u32[]{:S(2)}) copy-start(bf16[8,19,8,1280]{3,2,1,0:T(8,128)(2,1)S(1)} %all-to-all-done.3.fine.fine_tail) | copy-start | bytes 9338884
  509.3 73.7 %all-to-all-start.5 = ((bf16[8,19,8,1280]{3,2,1,0:T(8,128)(2,1)}), bf16[8,19,8,1280]{3,2,1,0:T(8,128)(2,1)}, u32[]{:S(2)}, u32[]{:S(2)}) async-start(bf16[8,19,8,1280]{3,2,1,0:T(8,128)(2,1)} %get-tuple-element.147), calls=%async_computation.5 | async-start | bytes 6225920 | tf_op jit(solution)/shard_map/all_to_all | solution.py:840
  582.9 73.8 %all-to-all-start.6 = ((bf16[8,19,8,1280]{3,2,1,0:T(8,128)(2,1)}), bf16[8,19,8,1280]{3,2,1,0:T(8,128)(2,1)S(1)}, u32[]{:S(2)}, u32[]{:S(2)}) async-start(bf16[8,19,8,1280]{3,2,1,0:T(8,128)(2,1)} %get-tuple-element.159), calls=%async_computation.6 | async-start | bytes 6225920 | tf_op jit(solution)/shard_map/all_to_all | solution.py:840
  656.7 74.1 %copy-start.12 = (bf16[8,19,8,1280]{3,2,1,0:T(8,128)(2,1)}, bf16[8,19,8,1280]{3,2,1,0:T(8,128)(2,1)S(1)}, u32[]{:S(2)}) copy-start(bf16[8,19,8,1280]{3,2,1,0:T(8,128)(2,1)S(1)} %all-to-all-done.6.refs_0_.refs_2_) | copy-start | bytes 9338884
  730.8 73.2 %all-to-all-start.8 = ((bf16[8,19,8,1280]{3,2,1,0:T(8,128)(2,1)}), bf16[8,19,8,1280]{3,2,1,0:T(8,128)(2,1)S(1)}, u32[]{:S(2)}, u32[]{:S(2)}) async-start(bf16[8,19,8,1280]{3,2,1,0:T(8,128)(2,1)} %get-tuple-element.163), calls=%async_computation.8 | async-start | bytes 6225920 | tf_op jit(solution)/shard_map/all_to_all | solution.py:840
  741.7 6.9 copy-start.3
  748.6 12.5 collective-permute-start
  750.7 10.4 copy-start.21
  805.6 79.7 %all-to-all-start.9 = ((bf16[8,19,8,1280]{3,2,1,0:T(8,128)(2,1)}), bf16[8,19,8,1280]{3,2,1,0:T(8,128)(2,1)}, u32[]{:S(2)}, u32[]{:S(2)}) async-start(bf16[8,19,8,1280]{3,2,1,0:T(8,128)(2,1)} %degrees_to_rows.4), calls=%async_computation.9 | async-start | bytes 6225920 | tf_op jit(solution)/shard_map/all_to_all | solution.py:840
  813.9 71.3 %collective-permute-start.1 = (bf16[6,8,24,1408]{3,2,1,0:T(8,128)(2,1)}, bf16[6,8,24,1408]{3,2,1,0:T(8,128)(2,1)}, u32[]{:S(2)}, u32[]{:S(2)}) collective-permute-start(bf16[6,8,24,1408]{3,2,1,0:T(8,128)(2,1)} %constant_dynamic-slice_fusion.5), channel_id=1, source_target_pairs={{0,2},{1,3},{2,0},{3,1},{4,6},{5,7},{6,4},{7,5},{8,10},{9,11},{10,... | collective-permute-start | bytes 9732104 | tf_op jit(solution)/shard_map/ppermute | solution.py:875
  838.6 18.1 copy-start.19
  885.2 137.4 %all-to-all-start.10 = ((bf16[8,37,8,1280]{3,2,1,0:T(8,128)(2,1)}), bf16[8,37,8,1280]{3,2,1,0:T(8,128)(2,1)}, u32[]{:S(2)}, u32[]{:S(2)}) async-start(bf16[8,37,8,1280]{3,2,1,0:T(8,128)(2,1)} %get-tuple-element.175), calls=%async_computation.10 | async-start | bytes 12124160 | tf_op jit(solution)/shard_map/all_to_all | solution.py:840
  893.6 7.6 copy-start.33
  893.6 126.4 %collective-permute-start.2 = (bf16[6,8,24,1408]{3,2,1,0:T(8,128)(2,1)S(1)}, bf16[6,8,24,1408]{3,2,1,0:T(8,128)(2,1)}, u32[]{:S(2)}, u32[]{:S(2)}) collective-permute-start(bf16[6,8,24,1408]{3,2,1,0:T(8,128)(2,1)S(1)} %constant_dynamic-slice_fusion.4), channel_id=1, source_target_pairs={{0,3},{1,2},{2,1},{3,0},{4,7},{5,6},{6,5},{7,4},{8,11},{9,10},{10,... | collective-permute-start | bytes 9732104 | tf_op jit(solution)/shard_map/ppermute | solution.py:875
  897.4 5.8 copy-start.36
  897.4 6.6 copy-start.37
  940.2 8.2 copy-start.30
  940.2 8.2 copy-start.31
  1022.6 144.7 %all-to-all-start.11 = ((bf16[8,34,8,1280]{3,2,1,0:T(8,128)(2,1)}), bf16[8,34,8,1280]{3,2,1,0:T(8,128)(2,1)}, u32[]{:S(2)}, u32[]{:S(2)}) async-start(bf16[8,34,8,1280]{3,2,1,0:T(8,128)(2,1)} %get-tuple-element.183), calls=%async_computation.11 | async-start | bytes 11141120 | tf_op jit(solution)/shard_map/all_to_all | solution.py:840
  1167.3 139.5 %all-to-all-start.12 = ((bf16[8,37,8,1280]{3,2,1,0:T(8,128)(2,1)}), bf16[8,37,8,1280]{3,2,1,0:T(8,128)(2,1)}, u32[]{:S(2)}, u32[]{:S(2)}) async-start(bf16[8,37,8,1280]{3,2,1,0:T(8,128)(2,1)} %get-tuple-element.193), calls=%async_computation.12 | async-start | bytes 12124160 | tf_op jit(solution)/shard_map/all_to_all | solution.py:840
  1306.8 127.0 %all-to-all-start.13 = ((bf16[8,34,8,1280]{3,2,1,0:T(8,128)(2,1)}), bf16[8,34,8,1280]{3,2,1,0:T(8,128)(2,1)}, u32[]{:S(2)}, u32[]{:S(2)}) async-start(bf16[8,34,8,1280]{3,2,1,0:T(8,128)(2,1)} %get-tuple-element.199), calls=%async_computation.13 | async-start | bytes 11141120 | tf_op jit(solution)/shard_map/all_to_all | solution.py:840
  1311.9 12.9 copy-start.22
  1311.9 12.9 copy-start.23
  1312.0 12.9 copy-start.24
  1339.9 7.2 collective-permute-start.3
  1362.2 45.4 %collective-permute-start.4 = (f32[384,1282]{0,1:T(8,128)}, f32[384,1282]{0,1:T(8,128)}, u32[]{:S(2)}, u32[]{:S(2)}) collective-permute-start(f32[384,1282]{0,1:T(8,128)} %copy.217), channel_id=1, source_target_pairs={{0,2},{1,3},{2,0},{3,1},{4,6},{5,7},{6,4},{7,5},{8,10},{9,11},{10,... | collective-permute-start | bytes 5907464 | tf_op jit(solution)/shard_map/ppermute | solution.py:902
  1433.9 73.8 %all-to-all-start.14 = ((bf16[8,19,8,1280]{3,2,1,0:T(8,128)(2,1)}), bf16[8,19,8,1280]{3,2,1,0:T(8,128)(2,1)S(1)}, u32[]{:S(2)}, u32[]{:S(2)}) async-start(bf16[8,19,8,1280]{3,2,1,0:T(8,128)(2,1)} %get-tuple-element.207), calls=%async_computation.14 | async-start | bytes 6225920 | tf_op jit(solution)/shard_map/all_to_all | solution.py:840
  1440.2 56.4 %collective-permute-start.5 = (f32[192,1282]{1,0:T(8,128)}, f32[192,1282]{1,0:T(8,128)}, u32[]{:S(2)}, u32[]{:S(2)}) collective-permute-start(f32[192,1282]{1,0:T(8,128)} %slice_select_fusion.2), channel_id=1, source_target_pairs={{0,4},{4,0},{8,12},{12,8},{16,20},{20,16},{24,28},{28,24},{1,5},{5... | collective-permute-start | bytes 2953736 | tf_op jit(solution)/shard_map/ppermute | solution.py:902
  1509.3 73.9 %all-to-all-start.15 = ((bf16[8,19,8,1280]{3,2,1,0:T(8,128)(2,1)}), bf16[8,19,8,1280]{3,2,1,0:T(8,128)(2,1)S(1)}, u32[]{:S(2)}, u32[]{:S(2)}) async-start(bf16[8,19,8,1280]{3,2,1,0:T(8,128)(2,1)} %get-tuple-element.211), calls=%async_computation.15 | async-start | bytes 6225920 | tf_op jit(solution)/shard_map/all_to_all | solution.py:840
  1584.8 84.8 %all-to-all-start.16 = ((bf16[8,19,8,1280]{3,2,1,0:T(8,128)(2,1)}), bf16[8,19,8,1280]{3,2,1,0:T(8,128)(2,1)S(1)}, u32[]{:S(2)}, u32[]{:S(2)}) async-start(bf16[8,19,8,1280]{3,2,1,0:T(8,128)(2,1)} %rows_to_degrees.7), calls=%async_computation.16 | async-start | bytes 6225920 | tf_op jit(solution)/shard_map/all_to_all | solution.py:840
  1590.4 53.6 %collective-permute-start.6 = (bf16[48,1282]{1,0:T(8,128)(2,1)}, bf16[48,1282]{1,0:T(8,128)(2,1)S(1)}, u32[]{:S(2)}, u32[]{:S(2)}) collective-permute-start(bf16[48,1282]{1,0:T(8,128)(2,1)} %get-tuple-element.273), channel_id=1, source_target_pairs={{0,8},{4,12},{8,0},{12,4},{16,24},{20,28},{24,16},{28,20},{1,9},{5... | collective-permute-start | bytes 369224 | tf_op jit(solution)/shard_map/ppermute | solution.py:922
  1592.3 76.2 %collective-permute-start.7 = (bf16[48,1282]{1,0:T(8,128)(2,1)}, bf16[48,1282]{1,0:T(8,128)(2,1)S(1)}, u32[]{:S(2)}, u32[]{:S(2)}) collective-permute-start(bf16[48,1282]{1,0:T(8,128)(2,1)} %get-tuple-element.275), channel_id=1, source_target_pairs={{0,16},{4,20},{8,24},{12,28},{16,0},{20,4},{24,8},{28,12},{1,17},{... | collective-permute-start | bytes 369224 | tf_op jit(solution)/shard_map/ppermute | solution.py:922
  1594.7 73.9 %collective-permute-start.8 = (bf16[48,1282]{1,0:T(8,128)(2,1)S(1)}, bf16[48,1282]{1,0:T(8,128)(2,1)}, u32[]{:S(2)}, u32[]{:S(2)}) collective-permute-start(bf16[48,1282]{1,0:T(8,128)(2,1)S(1)} %get-tuple-element.274), channel_id=1, source_target_pairs={{0,24},{4,28},{8,16},{12,20},{16,8},{20,12},{24,0},{28,4},{1,25},{... | collective-permute-start | bytes 369224 | tf_op jit(solution)/shard_map/ppermute | solution.py:922
  1669.7 75.9 %all-to-all-start.17 = ((bf16[8,19,8,1280]{3,2,1,0:T(8,128)(2,1)}), bf16[8,19,8,1280]{3,2,1,0:T(8,128)(2,1)}, u32[]{:S(2)}, u32[]{:S(2)}) async-start(bf16[8,19,8,1280]{3,2,1,0:T(8,128)(2,1)} %get-tuple-element.213), calls=%async_computation.17 | async-start | bytes 6225920 | tf_op jit(solution)/shard_map/all_to_all | solution.py:840
  1745.6 73.5 %all-to-all-start.18 = ((bf16[8,19,8,1280]{3,2,1,0:T(8,128)(2,1)}), bf16[8,19,8,1280]{3,2,1,0:T(8,128)(2,1)S(1)}, u32[]{:S(2)}, u32[]{:S(2)}) async-start(bf16[8,19,8,1280]{3,2,1,0:T(8,128)(2,1)} %get-tuple-element.225), calls=%async_computation.18 | async-start | bytes 6225920 | tf_op jit(solution)/shard_map/all_to_all | solution.py:840
  1820.8 85.0 %all-to-all-start.19 = ((bf16[8,19,8,1280]{3,2,1,0:T(8,128)(2,1)}), bf16[8,19,8,1280]{3,2,1,0:T(8,128)(2,1)S(1)}, u32[]{:S(2)}, u32[]{:S(2)}) async-start(bf16[8,19,8,1280]{3,2,1,0:T(8,128)(2,1)} %get-tuple-element.226), calls=%async_computation.19 | async-start | bytes 6225920 | tf_op jit(solution)/shard_map/all_to_all | solution.py:840
  1824.5 55.4 %collective-permute-start.10 = (bf16[48,1282]{1,0:T(8,128)(2,1)S(1)}, bf16[48,1282]{1,0:T(8,128)(2,1)S(1)}, u32[]{:S(2)}, u32[]{:S(2)}) collective-permute-start(bf16[48,1282]{1,0:T(8,128)(2,1)S(1)} %fusion.11), channel_id=1, source_target_pairs={{0,8},{4,12},{8,0},{12,4},{16,24},{20,28},{24,16},{28,20},{1,9},{5... | collective-permute-start | bytes 369224 | tf_op jit(solution)/shard_map/ppermute | solution.py:931
  1826.5 78.1 %collective-permute-start.11 = (bf16[48,1282]{1,0:T(8,128)(2,1)S(1)}, bf16[48,1282]{1,0:T(8,128)(2,1)S(1)}, u32[]{:S(2)}, u32[]{:S(2)}) collective-permute-start(bf16[48,1282]{1,0:T(8,128)(2,1)S(1)} %fusion.11), channel_id=1, source_target_pairs={{0,16},{4,20},{8,24},{12,28},{16,0},{20,4},{24,8},{28,12},{1,17},{... | collective-permute-start | bytes 369224 | tf_op jit(solution)/shard_map/ppermute | solution.py:931
  1828.8 76.4 %collective-permute-start.12 = (bf16[48,1282]{1,0:T(8,128)(2,1)S(1)}, bf16[48,1282]{1,0:T(8,128)(2,1)S(1)}, u32[]{:S(2)}, u32[]{:S(2)}) collective-permute-start(bf16[48,1282]{1,0:T(8,128)(2,1)S(1)} %fusion.11), channel_id=1, source_target_pairs={{0,24},{4,28},{8,16},{12,20},{16,8},{20,12},{24,0},{28,4},{1,25},{... | collective-permute-start | bytes 369224 | tf_op jit(solution)/shard_map/ppermute | solution.py:931
  1905.9 7.8 copy-start.10
  1905.9 75.0 %all-to-all-start.20 = ((bf16[8,19,8,1280]{3,2,1,0:T(8,128)(2,1)}), bf16[8,19,8,1280]{3,2,1,0:T(8,128)(2,1)}, u32[]{:S(2)}, u32[]{:S(2)}) async-start(bf16[8,19,8,1280]{3,2,1,0:T(8,128)(2,1)} %get-tuple-element.230), calls=%async_computation.20 | async-start | bytes 6225920 | tf_op jit(solution)/shard_map/all_to_all | solution.py:840
  1917.5 5.9 copy-start.4
  1917.5 5.9 copy-start.20
  1923.4 10.4 collective-permute-start.9
  1980.8 79.1 %all-to-all-start.21 = ((bf16[8,19,8,1280]{3,2,1,0:T(8,128)(2,1)}), bf16[8,19,8,1280]{3,2,1,0:T(8,128)(2,1)S(1)}, u32[]{:S(2)}, u32[]{:S(2)}) async-start(bf16[8,19,8,1280]{3,2,1,0:T(8,128)(2,1)} %degrees_to_rows.6), calls=%async_computation.21 | async-start | bytes 6225920 | tf_op jit(solution)/shard_map/all_to_all | solution.py:840
  1988.6 71.3 %collective-permute-start.13 = (bf16[6,8,24,1408]{3,2,1,0:T(8,128)(2,1)}, bf16[6,8,24,1408]{3,2,1,0:T(8,128)(2,1)}, u32[]{:S(2)}, u32[]{:S(2)}) collective-permute-start(bf16[6,8,24,1408]{3,2,1,0:T(8,128)(2,1)} %constant_dynamic-slice_fusion.1), channel_id=1, source_target_pairs={{0,2},{1,3},{2,0},{3,1},{4,6},{5,7},{6,4},{7,5},{8,10},{9,11},{10,... | collective-permute-start | bytes 9732104 | tf_op jit(solution)/shard_map/ppermute | solution.py:875
  2061.6 189.5 %all-to-all-start.22 = ((bf16[8,52,8,1280]{3,2,1,0:T(8,128)(2,1)}), bf16[8,52,8,1280]{3,2,1,0:T(8,128)(2,1)}, u32[]{:S(2)}, u32[]{:S(2)}) async-start(bf16[8,52,8,1280]{3,2,1,0:T(8,128)(2,1)} %get-tuple-element.239), calls=%async_computation.22 | async-start | bytes 17039360 | tf_op jit(solution)/shard_map/all_to_all | solution.py:840
  2071.1 106.4 %collective-permute-start.14 = (bf16[6,8,24,1408]{3,2,1,0:T(8,128)(2,1)}, bf16[6,8,24,1408]{3,2,1,0:T(8,128)(2,1)}, u32[]{:S(2)}, u32[]{:S(2)}) collective-permute-start(bf16[6,8,24,1408]{3,2,1,0:T(8,128)(2,1)} %constant_dynamic-slice_fusion), channel_id=1, source_target_pairs={{0,3},{1,2},{2,1},{3,0},{4,7},{5,6},{6,5},{7,4},{8,11},{9,10},{10,... | collective-permute-start | bytes 9732104 | tf_op jit(solution)/shard_map/ppermute | solution.py:875
  2071.1 76.6 %collective-permute-start.15 = (bf16[192,1282]{1,0:T(8,128)(2,1)}, bf16[192,1282]{1,0:T(8,128)(2,1)S(1)}, u32[]{:S(2)}, u32[]{:S(2)}) collective-permute-start(bf16[192,1282]{1,0:T(8,128)(2,1)} %bitcast.50), channel_id=1, source_target_pairs={{0,4},{4,0},{8,12},{12,8},{16,20},{20,16},{24,28},{28,24},{1,5},{5... | collective-permute-start | bytes 1476872 | tf_op jit(solution)/shard_map/ppermute | solution.py:907
  2150.1 22.7 collective-permute-start.16
  2251.1 74.1 %all-to-all-start.23 = ((bf16[8,19,8,1280]{3,2,1,0:T(8,128)(2,1)}), bf16[8,19,8,1280]{3,2,1,0:T(8,128)(2,1)S(1)}, u32[]{:S(2)}, u32[]{:S(2)}) async-start(bf16[8,19,8,1280]{3,2,1,0:T(8,128)(2,1)} %get-tuple-element.249), calls=%async_computation.23 | async-start | bytes 6225920 | tf_op jit(solution)/shard_map/all_to_all | solution.py:840
  2259.1 4.3 collective-permute-start.17
  2342.8 1.2 collective-permute-start.18
  2344.0 3.6 collective-permute-start.19
  2347.3 5.8 copy-start.2
  2347.7 6.3 collective-permute-start.20
  2354.0 3.7 collective-permute-start.21
  2357.7 4.5 collective-permute-start.22
  (21 other events, 55.7 us)

commit v5 on v4

--- a/solution.py
+++ b/solution.py
@@ -1057,6 +1057,7 @@
             [pair_dev // 2], subs, wide,
         )[0]
         arrived_coarse = line.swap(line.keep(coarse_made))
+        line.keep(out_tables)
         for k in range(1, n_chunks):
             arrived.append(line.swap(fine_made[k]))
             mix_chunk(k - 1)
@@ -1113,8 +1114,6 @@
             )
             coarse_made.extend(line.keep(made))
         else:
-            if k == 1:
-                coarse_made[0] = line.keep(coarse_back(line.hold(coarse_made[0])))
             fine_pixels(k - 1, fine_end[k - 1])
 
     fine_synth, values = spectral(
@@ -1140,8 +1139,7 @@
     line.aside = add_dense(line.hold(stacked), n_lat, n_chan, line, dense)
     line.step_aside()
     coarse_sgrad = line.swap(coarse_made[2])
-    if len(row_cuts) == 1:
-        coarse_made[0] = coarse_back(coarse_made[0])
+    coarse_made[0] = line.keep(coarse_back(line.hold(coarse_made[0])))
     ends, mix_grads = [], []
 
     def finish_fine(place, wave):
@@ -1156,9 +1154,8 @@
             made = finish(
                 line.hold(coarse_end), coarse_x, coarse_made[1], coarse_forward, gain_one, 0, None
             )
+            made = [coarse_back(made[0]), made[1]]
         else:
-            if k == 1:
-                ends[0][0] = line.keep(coarse_back(line.hold(ends[0][0])))
             made = finish_fine(len(outer_cuts) - k, line.hold(fine_end[-k]))
         ends.append(list(line.keep(made)))
 
@@ -1168,11 +1165,9 @@
     )
     for unused in line.aside:
         pass
-    up_grad, down_grad = dense[0][0, :C], dense[0][1, :C]
+    up_grad, down_grad = line.keep((dense[0][0, :C], dense[0][1, :C]))
     narrow = dense[0][0, C : C + 3].reshape(-1)
     narrow_sums = narrow[hidden : hidden + 3 * C].reshape(3, C)
-    if len(row_cuts) == 1:
-        ends[0][0] = coarse_back(ends[0][0])
     last_wave = lax.optimization_barrier((fine_fgrad[0], line.work + line.later))[0]
     ends.append(finish_fine(0, last_wave))
     mix_grad = mix_grads[0].transpose(0, 2, 3, 1)

time: 2380 us -> 2370 us (level)
  blocking collectives: 148 us -> 74.1 us
  waiting for transfers between devices: 1050 us -> 1100 us
    all_to_all x2 -> x1, blocking collectives: 148 us -> 74.1 us  [swap(): lax.all_to_all(values, 'lat', split_axis=0, concat_axis=0, tiled=True)]
    all_to_all x22 -> x23, waiting for transfers between devices: 629 us -> 655 us  [swap(): lax.all_to_all(values, 'lat', split_axis=0, concat_axis=0, tiled=True)]
    all_to_all x22 -> x23, starting transfers between devices: 100 us -> 103 us  [swap(): lax.all_to_all(values, 'lat', split_axis=0, concat_axis=0, tiled=True)]
  transfers between devices with their start and end apart: 45 -> 46, of which waited for: 33 -> 35; matrix products, arithmetic and copies ran while one was open for 13% -> 14% of each run, Pallas kernels for 28% -> 28%
where the time goes in v5:
time: 2370 us; the launch traced here: 2360 us
  waiting for transfers between devices  1100 us (46%)
  Pallas kernels  692 us (29%)
  local copies, waits for them, and re-layouts  260 us (11%)
  starting transfers between devices  122 us (5%)
  other arithmetic  109 us (5%)
  blocking collectives  74.1 us (3%)
    all_to_all x23, waiting for transfers between devices, swap(): lax.all_to_all(values, 'lat', split_axis=0, concat_axis=0, tiled=True)  655 us
    pallas_call x3, Pallas kernels, pixels(): call(body, 'feed_forward', 2 * count * points * (6 * C * hidden + 2 * tab...  323 us
    pallas_call x8, Pallas kernels, lane_call(): call(functools.partial(lane_body, work, subs, width, len(inputs), len(tab...  106 us
    ppermute x6, waiting for transfers between devices, share_slots(): return lax.ppermute(block, 'chan', route) if step else block  104 us
    all_to_all x23, starting transfers between devices, swap(): lax.all_to_all(values, 'lat', split_axis=0, concat_axis=0, tiled=True)  103 us
    ppermute x3, waiting for transfers between devices, double(): other = lax.ppermute(line.hold(held), axis, partners(sizes[axis], step)[0])  101 us
    unnamed x87, local copies, waits for them, and re-layouts  81.6 us
    ppermute x3, waiting for transfers between devices, halve(): lax.ppermute(jnp.where(upper, low, high), axis, partners(sizes[axis], ste...  81.4 us
  transfers between devices with their start and end apart: 46, of which 35 were waited for; matrix products, arithmetic and copies ran while one was open for 14% of the time, Pallas kernels for 28%

profile of v5, /device:TPU:0, one launch (start us, length us, event | category | flops | bytes accessed | tf_op | source)
XLA Modules:
  0.0 2356.2 jit_solution(3228873516701433967)
XLA Ops:
  6.8 10.0 norm_and_dft.3
  16.8 7.3 all-to-all-start
  24.1 24.3 %norm_and_dft.4 = bf16[8,52,8,1280]{3,2,1,0:T(8,128)(2,1)} custom-call(f32[23,641,1,360]{3,2,1,0:T(1,128)} %bitcast.109, s32[23,8,360]{2,1,0:T(8,128)} %bitcast.152, f32[641,1]{1,0:T(8,128)} %broadcast_in_dim.222.gain.refs_5_, f32[641,1]{1,0:T(8,128)} %broadcast_in_dim.223.bias, bf16[384,360]{1,0:T(8,128)(2,1)} %pad_maximum_fusion.4.table.refs_4_), custom_call_target="tpu_custom_call" | custom-call | flops 3609722880 | bytes 24883104 | tf_op jit(solution)/shard_map/norm_and_dft/pallas_call | solution.py:162
  48.4 45.7 %all-to-all-done.refs_0_.refs_2_ = bf16[8,19,8,1280]{3,2,1,0:T(8,128)(2,1)S(1)} async-done(((bf16[8,19,8,1280]{3,2,1,0:T(8,128)(2,1)}), bf16[8,19,8,1280]{3,2,1,0:T(8,128)(2,1)S(1)}, u32[]{:S(2)}, u32[]{:S(2)}) %all-to-all-start) | async-done | bytes 3112992 | tf_op jit(solution)/shard_map/all_to_all | solution.py:840
  100.7 20.7 reduce
  121.4 7.2 reshape_squeeze.12
  128.5 7.5 copy.189
  136.1 8.2 broadcast_in_dim.209.state
  148.2 10.0 norm_and_dft.5
  158.2 127.5 %all-to-all-done.1.refs_1_.refs_3_ = bf16[8,52,8,1280]{3,2,1,0:T(8,128)(2,1)} async-done(((bf16[8,52,8,1280]{3,2,1,0:T(8,128)(2,1)}), bf16[8,52,8,1280]{3,2,1,0:T(8,128)(2,1)}, u32[]{:S(2)}, u32[]{:S(2)}) %all-to-all-start.1) | async-done | bytes 8519712 | tf_op jit(solution)/shard_map/all_to_all | solution.py:840
  294.3 13.2 legendre_tables.3
  336.1 17.0 rows_to_degrees.4
  378.2 9.5 rows_to_degrees.5
  387.7 47.8 %all-to-all-done.3.fine.fine_tail = bf16[8,19,8,1280]{3,2,1,0:T(8,128)(2,1)S(1)} async-done(((bf16[8,19,8,1280]{3,2,1,0:T(8,128)(2,1)}), bf16[8,19,8,1280]{3,2,1,0:T(8,128)(2,1)S(1)}, u32[]{:S(2)}, u32[]{:S(2)}) %all-to-all-start.3) | async-done | bytes 3112992 | tf_op jit(solution)/shard_map/all_to_all | solution.py:840
  441.6 13.2 legendre_tables.5
  482.6 28.5 %all-to-all-done.4.coarse.coarse_tail.refs_3_.refs_4_ = bf16[8,19,8,1280]{3,2,1,0:T(8,128)(2,1)S(1)} async-done(((bf16[8,19,8,1280]{3,2,1,0:T(8,128)(2,1)}), bf16[8,19,8,1280]{3,2,1,0:T(8,128)(2,1)S(1)}, u32[]{:S(2)}, u32[]{:S(2)}) %all-to-all-start.4) | async-done | bytes 3112992 | tf_op jit(solution)/shard_map/all_to_all | solution.py:840
  517.8 31.7 %copy.242 = bf16[24,2,649,641]{2,3,1,0:T(8,128)(2,1)} copy(bf16[24,2,649,641]{2,1,3,0:T(2,128)(2,1)} %param.27) | data formatting | bytes 79873728 | tf_op args[9]
  550.2 20.3 mix.2
  570.5 16.3 all-to-all-done.5.refs_1_.refs_2_
  590.6 20.3 mix.3
  610.9 49.8 %all-to-all-done.6.refs_0_.refs_2_ = bf16[8,19,8,1280]{3,2,1,0:T(8,128)(2,1)S(1)} async-done(((bf16[8,19,8,1280]{3,2,1,0:T(8,128)(2,1)}), bf16[8,19,8,1280]{3,2,1,0:T(8,128)(2,1)S(1)}, u32[]{:S(2)}, u32[]{:S(2)}) %all-to-all-start.6) | async-done | bytes 3112992 | tf_op jit(solution)/shard_map/all_to_all | solution.py:840
  660.7 74.1 %all_to_all.120.refs_0_.refs_1_ = bf16[8,19,8,1280]{3,2,1,0:T(8,128)(2,1)} all-to-all(bf16[8,19,8,1280]{3,2,1,0:T(8,128)(2,1)} %get-tuple-element.162), channel_id=1, replica_groups=mesh['lat'=8,'chan'=4] {'lat'}, dimensions={0} | all-to-all | bytes 6225920 | tf_op jit(solution)/shard_map/all_to_all | solution.py:840
  752.5 9.5 degrees_to_rows.4
  762.0 45.8 %all-to-all-done.8.refs_1_.refs_3_ = bf16[8,19,8,1280]{3,2,1,0:T(8,128)(2,1)S(1)} async-done(((bf16[8,19,8,1280]{3,2,1,0:T(8,128)(2,1)}), bf16[8,19,8,1280]{3,2,1,0:T(8,128)(2,1)S(1)}, u32[]{:S(2)}, u32[]{:S(2)}) %all-to-all-start.8) | async-done | bytes 3112992 | tf_op jit(solution)/shard_map/all_to_all | solution.py:840
  820.1 17.0 degrees_to_rows.5
  837.1 50.2 %collective-permute-done.2.refs_2_ = bf16[6,8,24,1408]{3,2,1,0:T(8,128)(2,1)} collective-permute-done((bf16[6,8,24,1408]{3,2,1,0:T(8,128)(2,1)S(1)}, bf16[6,8,24,1408]{3,2,1,0:T(8,128)(2,1)}, u32[]{:S(2)}, u32[]{:S(2)}) %collective-permute-start.2) | collective-permute-done | bytes 3244064 | tf_op jit(solution)/shard_map/ppermute | solution.py:875
  906.5 20.7 reduce.1
  934.3 7.5 copy.197
  941.8 8.2 broadcast_in_dim.210.cotangent
  950.7 71.1 %feed_forward.3 = (f32[6,641,1,360]{3,2,1,0:T(1,128)}, f32[6,641,360]{2,1,0:T(8,128)}, bf16[8,19,8,1280]{3,2,1,0:T(8,128)(2,1)}, f32[2,768,1282]{2,1,0:T(8,128)}...) custom-call(bf16[8,19,8,1280]{3,2,1,0:T(8,128)(2,1)} %all-to-all-done.9.synth.tail, ...), custom_call_target="tpu_custom_call" | custom-call | flops 23848110080 | bytes 28641024 | tf_op jit(solution)/shard_map/feed_forward/pallas_call | solution.py:674
  1030.1 130.7 %feed_forward.4 = (f32[23,641,1,360]{3,2,1,0:T(1,128)}, f32[23,641,360]{2,1,0:T(8,128)}, bf16[8,37,8,1280]{3,2,1,0:T(8,128)(2,1)}, f32[2,768,1282]{2,1,0:T(8,128...) custom-call(bf16[8,37,8,1280]{3,2,1,0:T(8,128)(2,1)} %all-to-all-done.10.synth.tail, ...), custom_call_target="tpu_custom_call" | custom-call | flops 47696220160 | bytes 57282048 | tf_op jit(solution)/shard_map/feed_forward/pallas_call | solution.py:674
  1167.1 120.8 %feed_forward.5 = (f32[23,641,1,360]{3,2,1,0:T(1,128)}, f32[23,641,360]{2,1,0:T(8,128)}, bf16[8,34,8,1280]{3,2,1,0:T(8,128)(2,1)}, f32[2,768,1282]{2,1,0:T(8,128...) custom-call(bf16[8,34,8,1280]{3,2,1,0:T(8,128)(2,1)} %all-to-all-done.11.refs_0_.refs_, ...), custom_call_target="tpu_custom_call", output_to_operand_aliasing={{0}: (13, {}), {1}: (14, {})} | custom-call | flops 43721535488 | bytes 52508544 | tf_op jit(solution)/shard_map/feed_forward/pallas_call | solution.py:674
  1288.0 12.6 all-to-all-done.12.refs_0_.refs_2_
  1305.7 12.8 add_add_fusion
  1333.7 7.2 collective-permute-done.3
  1356.5 44.9 %collective-permute-done.4 = f32[384,1282]{0,1:T(8,128)} collective-permute-done((f32[384,1282]{0,1:T(8,128)}, f32[384,1282]{0,1:T(8,128)}, u32[]{:S(2)}, u32[]{:S(2)}) %collective-permute-start.4) | collective-permute-done | bytes 1969184 | tf_op jit(solution)/shard_map/ppermute | solution.py:902
  1407.6 20.2 all-to-all-done.13.refs_1_.refs_3_
  1436.1 8.2 part_rows.2
  1444.3 17.0 rows_to_degrees.6
  1461.3 29.3 %collective-permute-done.5 = f32[192,1282]{1,0:T(8,128)} collective-permute-done((f32[192,1282]{1,0:T(8,128)}, f32[192,1282]{1,0:T(8,128)}, u32[]{:S(2)}, u32[]{:S(2)}) %collective-permute-start.5) | collective-permute-done | bytes 984608 | tf_op jit(solution)/shard_map/ppermute | solution.py:902
  1493.6 8.0 all-to-all-done.14.refs_0_.refs_1_
  1506.9 9.5 rows_to_degrees.7
  1516.4 60.7 %all-to-all-done.15.fine.fine_tail = bf16[8,19,8,1280]{3,2,1,0:T(8,128)(2,1)S(1)} async-done(((bf16[8,19,8,1280]{3,2,1,0:T(8,128)(2,1)}), bf16[8,19,8,1280]{3,2,1,0:T(8,128)(2,1)S(1)}, u32[]{:S(2)}, u32[]{:S(2)}) %all-to-all-start.15) | async-done | bytes 3112992 | tf_op jit(solution)/shard_map/all_to_all | solution.py:840
  1591.7 46.2 %collective-permute-done.6 = bf16[48,1282]{1,0:T(8,128)(2,1)S(1)} collective-permute-done((bf16[48,1282]{1,0:T(8,128)(2,1)}, bf16[48,1282]{1,0:T(8,128)(2,1)S(1)}, u32[]{:S(2)}, u32[]{:S(2)}) %collective-permute-start.6) | collective-permute-done | bytes 123104 | tf_op jit(solution)/shard_map/ppermute | solution.py:922
  1637.9 24.7 %collective-permute-done.7 = bf16[48,1282]{1,0:T(8,128)(2,1)} collective-permute-done((bf16[48,1282]{1,0:T(8,128)(2,1)}, bf16[48,1282]{1,0:T(8,128)(2,1)}, u32[]{:S(2)}, u32[]{:S(2)}) %collective-permute-start.7) | collective-permute-done | bytes 123104 | tf_op jit(solution)/shard_map/ppermute | solution.py:922
  1670.0 20.3 mix_back.2
  1690.3 50.9 %all-to-all-done.17.refs_1_.refs_2_ = bf16[8,19,8,1280]{3,2,1,0:T(8,128)(2,1)} async-done(((bf16[8,19,8,1280]{3,2,1,0:T(8,128)(2,1)}), bf16[8,19,8,1280]{3,2,1,0:T(8,128)(2,1)}, u32[]{:S(2)}, u32[]{:S(2)}) %all-to-all-start.17) | async-done | bytes 3112992 | tf_op jit(solution)/shard_map/all_to_all | solution.py:840
  1744.9 20.3 mix_back.3
  1765.1 49.6 %all-to-all-done.18.refs_0_.refs_2_ = bf16[8,19,8,1280]{3,2,1,0:T(8,128)(2,1)S(1)} async-done(((bf16[8,19,8,1280]{3,2,1,0:T(8,128)(2,1)}), bf16[8,19,8,1280]{3,2,1,0:T(8,128)(2,1)S(1)}, u32[]{:S(2)}, u32[]{:S(2)}) %all-to-all-start.18) | async-done | bytes 3112992 | tf_op jit(solution)/shard_map/all_to_all | solution.py:840
  1826.0 49.4 %collective-permute-done.10 = bf16[48,1282]{1,0:T(8,128)(2,1)S(1)} collective-permute-done((bf16[48,1282]{1,0:T(8,128)(2,1)S(1)}, bf16[48,1282]{1,0:T(8,128)(2,1)S(1)}, u32[]{:S(2)}, u32[]{:S(2)}) %collective-permute-start.10) | collective-permute-done | bytes 123104 | tf_op jit(solution)/shard_map/ppermute | solution.py:931
  1876.1 24.0 %collective-permute-done.11 = bf16[48,1282]{1,0:T(8,128)(2,1)S(1)} collective-permute-done((bf16[48,1282]{1,0:T(8,128)(2,1)S(1)}, bf16[48,1282]{1,0:T(8,128)(2,1)S(1)}, u32[]{:S(2)}, u32[]{:S(2)}) %collective-permute-start.11) | collective-permute-done | bytes 123104 | tf_op jit(solution)/shard_map/ppermute | solution.py:931
  1919.0 9.5 degrees_to_rows.6
  1928.5 47.9 %all-to-all-done.20.refs_1_.refs_3_ = bf16[8,19,8,1280]{3,2,1,0:T(8,128)(2,1)} async-done(((bf16[8,19,8,1280]{3,2,1,0:T(8,128)(2,1)}), bf16[8,19,8,1280]{3,2,1,0:T(8,128)(2,1)}, u32[]{:S(2)}, u32[]{:S(2)}) %all-to-all-start.20) | async-done | bytes 3112992 | tf_op jit(solution)/shard_map/all_to_all | solution.py:840
  1984.5 17.0 degrees_to_rows.7
  2001.5 53.9 %collective-permute-done.16.refs_6_ = bf16[6,8,24,1408]{3,2,1,0:T(8,128)(2,1)} collective-permute-done((bf16[6,8,24,1408]{3,2,1,0:T(8,128)(2,1)}, bf16[6,8,24,1408]{3,2,1,0:T(8,128)(2,1)}, u32[]{:S(2)}, u32[]{:S(2)}) %collective-permute-start.16) | collective-permute-done | bytes 3244064 | tf_op jit(solution)/shard_map/ppermute | solution.py:875
  2068.7 74.6 %collective-permute-done.14 = bf16[192,1282]{1,0:T(8,128)(2,1)S(1)} collective-permute-done((bf16[192,1282]{1,0:T(8,128)(2,1)}, bf16[192,1282]{1,0:T(8,128)(2,1)S(1)}, u32[]{:S(2)}, u32[]{:S(2)}) %collective-permute-start.14) | collective-permute-done | bytes 492320 | tf_op jit(solution)/shard_map/ppermute | solution.py:907
  2146.1 22.3 collective-permute-done.15
  2173.0 14.2 first_norm_back.3
  2187.2 8.2 part_rows.3
  2195.5 27.4 %mix_gradient.1 = f32[6,641,2,649]{3,2,1,0:T(2,128)} custom-call(bf16[6,8,24,1408]{3,2,1,0:T(8,128)(2,1)} %get-tuple-element.260.refs_0_, bf16[6,8,24,1408]{3,2,1,0:T(8,128)(2,1)} %collective-permute-done.refs_1_, bf16[6,8,24,1408]{3,2,1,0:T(8,128)(2,1)} %collective-permute-done.2.refs_2_, bf16[6,8,24,1408]{3,2,1,0:T(8,128)(2,1)} %collective-permute-done.1.refs_3_, ...), custom_call_target="tpu_custom_call" | custom-call | flops 15335755776 | bytes 45920688 | tf_op jit(solution)/shard_map/mix_gradient/pallas_call | solution.py:585
  2222.9 23.7 %all-to-all-done.22.wave.tail = bf16[8,52,8,1280]{3,2,1,0:T(8,128)(2,1)} async-done(((bf16[8,52,8,1280]{3,2,1,0:T(8,128)(2,1)}), bf16[8,52,8,1280]{3,2,1,0:T(8,128)(2,1)}, u32[]{:S(2)}, u32[]{:S(2)}) %all-to-all-start.22) | async-done | bytes 8519712 | tf_op jit(solution)/shard_map/all_to_all | solution.py:840
  2275.3 34.6 %first_norm_back.4 = (f32[23,641,1,360]{3,2,1,0:T(1,128)}, f32[2,641,1]{2,1,0:T(8,128)}) custom-call(bf16[8,52,8,1280]{3,2,1,0:T(8,128)(2,1)} %all-to-all-done.22.wave.tail, bf16[8,52,8,1280]{3,2,1,0:T(8,128)(2,1)} %all-to-all-done.22.wave.tail, f32[23,641,1,360]{3,2,1,0:T(1,128)} %bitcast.112, f32[23,641,360]{2,1,0:T(8,128)} %get-tuple-element.188.middle_grad.refs_3_, ...), custom_call_target="tpu_custom_call" | custom-call | flops 3609722880 | bytes 56266464 | tf_op jit(solution)/shard_map/first_norm_back/pallas_call | solution.py:743
  2309.9 10.8 all-to-all-done.23.refs_0_.refs_1_
  2322.4 14.2 first_norm_back.5
  (304 shorter events, 388.4 us)
Async XLA Ops:
  16.8 77.3 %all-to-all-start = ((bf16[8,19,8,1280]{3,2,1,0:T(8,128)(2,1)}), bf16[8,19,8,1280]{3,2,1,0:T(8,128)(2,1)S(1)}, u32[]{:S(2)}, u32[]{:S(2)}) async-start(bf16[8,19,8,1280]{3,2,1,0:T(8,128)(2,1)} %norm_and_dft.3), calls=%async_computation | async-start | bytes 6225920 | tf_op jit(solution)/shard_map/all_to_all | solution.py:840
  95.7 190.0 %all-to-all-start.1 = ((bf16[8,52,8,1280]{3,2,1,0:T(8,128)(2,1)}), bf16[8,52,8,1280]{3,2,1,0:T(8,128)(2,1)}, u32[]{:S(2)}, u32[]{:S(2)}) async-start(bf16[8,52,8,1280]{3,2,1,0:T(8,128)(2,1)} %norm_and_dft.4), calls=%async_computation.1 | async-start | bytes 17039360 | tf_op jit(solution)/shard_map/all_to_all | solution.py:840
  136.1 8.2 copy-start.32
  158.2 131.6 %copy-start.38 = (s32[184]{0:T(256)S(1)}, s32[184]{0:T(256)}, u32[]{:S(2)}) copy-start(s32[184]{0:T(256)} %param.23) | copy-start | bytes 2212
  285.7 74.3 %all-to-all-start.2 = ((bf16[8,19,8,1280]{3,2,1,0:T(8,128)(2,1)}), bf16[8,19,8,1280]{3,2,1,0:T(8,128)(2,1)S(1)}, u32[]{:S(2)}, u32[]{:S(2)}) async-start(bf16[8,19,8,1280]{3,2,1,0:T(8,128)(2,1)} %norm_and_dft.5), calls=%async_computation.2 | async-start | bytes 6225920 | tf_op jit(solution)/shard_map/all_to_all | solution.py:840
  360.0 5.3 copy-start.39
  361.7 73.8 %all-to-all-start.3 = ((bf16[8,19,8,1280]{3,2,1,0:T(8,128)(2,1)}), bf16[8,19,8,1280]{3,2,1,0:T(8,128)(2,1)S(1)}, u32[]{:S(2)}, u32[]{:S(2)}) async-start(bf16[8,19,8,1280]{3,2,1,0:T(8,128)(2,1)} %get-tuple-element.147), calls=%async_computation.3 | async-start | bytes 6225920 | tf_op jit(solution)/shard_map/all_to_all | solution.py:840
  437.1 74.0 %all-to-all-start.4 = ((bf16[8,19,8,1280]{3,2,1,0:T(8,128)(2,1)}), bf16[8,19,8,1280]{3,2,1,0:T(8,128)(2,1)S(1)}, u32[]{:S(2)}, u32[]{:S(2)}) async-start(bf16[8,19,8,1280]{3,2,1,0:T(8,128)(2,1)} %rows_to_degrees.5), calls=%async_computation.4 | async-start | bytes 6225920 | tf_op jit(solution)/shard_map/all_to_all | solution.py:840
  477.9 33.3 %copy-start.21 = (bf16[12,96,96]{2,1,0:T(8,128)(2,1)}, bf16[12,96,96]{2,1,0:T(8,128)(2,1)S(1)}, u32[]{:S(2)}) copy-start(bf16[12,96,96]{2,1,0:T(8,128)(2,1)S(1)} %convert_element_type.218.refs_2_) | copy-start | bytes 663556
  511.1 6.1 copy-start.34
  512.8 73.9 %all-to-all-start.5 = ((bf16[8,19,8,1280]{3,2,1,0:T(8,128)(2,1)}), bf16[8,19,8,1280]{3,2,1,0:T(8,128)(2,1)}, u32[]{:S(2)}, u32[]{:S(2)}) async-start(bf16[8,19,8,1280]{3,2,1,0:T(8,128)(2,1)} %get-tuple-element.149), calls=%async_computation.5 | async-start | bytes 6225920 | tf_op jit(solution)/shard_map/all_to_all | solution.py:840
  586.7 74.0 %all-to-all-start.6 = ((bf16[8,19,8,1280]{3,2,1,0:T(8,128)(2,1)}), bf16[8,19,8,1280]{3,2,1,0:T(8,128)(2,1)S(1)}, u32[]{:S(2)}, u32[]{:S(2)}) async-start(bf16[8,19,8,1280]{3,2,1,0:T(8,128)(2,1)} %get-tuple-element.161), calls=%async_computation.6 | async-start | bytes 6225920 | tf_op jit(solution)/shard_map/all_to_all | solution.py:840
  660.7 74.1 %copy-start.14 = (bf16[8,19,8,1280]{3,2,1,0:T(8,128)(2,1)}, bf16[8,19,8,1280]{3,2,1,0:T(8,128)(2,1)S(1)}, u32[]{:S(2)}) copy-start(bf16[8,19,8,1280]{3,2,1,0:T(8,128)(2,1)S(1)} %all-to-all-done.6.refs_0_.refs_2_) | copy-start | bytes 9338884
  734.8 73.0 %all-to-all-start.8 = ((bf16[8,19,8,1280]{3,2,1,0:T(8,128)(2,1)}), bf16[8,19,8,1280]{3,2,1,0:T(8,128)(2,1)S(1)}, u32[]{:S(2)}, u32[]{:S(2)}) async-start(bf16[8,19,8,1280]{3,2,1,0:T(8,128)(2,1)} %get-tuple-element.165), calls=%async_computation.8 | async-start | bytes 6225920 | tf_op jit(solution)/shard_map/all_to_all | solution.py:840
  745.6 6.9 copy-start.4
  752.5 9.5 collective-permute-start
  809.5 77.8 %all-to-all-start.9 = ((bf16[8,19,8,1280]{3,2,1,0:T(8,128)(2,1)}), bf16[8,19,8,1280]{3,2,1,0:T(8,128)(2,1)}, u32[]{:S(2)}, u32[]{:S(2)}) async-start(bf16[8,19,8,1280]{3,2,1,0:T(8,128)(2,1)} %degrees_to_rows.4), calls=%async_computation.9 | async-start | bytes 6225920 | tf_op jit(solution)/shard_map/all_to_all | solution.py:840
  816.1 71.2 %collective-permute-start.2 = (bf16[6,8,24,1408]{3,2,1,0:T(8,128)(2,1)S(1)}, bf16[6,8,24,1408]{3,2,1,0:T(8,128)(2,1)}, u32[]{:S(2)}, u32[]{:S(2)}) collective-permute-start(bf16[6,8,24,1408]{3,2,1,0:T(8,128)(2,1)S(1)} %constant_dynamic-slice_fusion.4), channel_id=1, source_target_pairs={{0,2},{1,3},{2,0},{3,1},{4,6},{5,7},{6,4},{7,5},{8,10},{9,11},{10,... | collective-permute-start | bytes 9732104 | tf_op jit(solution)/shard_map/ppermute | solution.py:875
  887.3 137.0 %all-to-all-start.10 = ((bf16[8,37,8,1280]{3,2,1,0:T(8,128)(2,1)}), bf16[8,37,8,1280]{3,2,1,0:T(8,128)(2,1)}, u32[]{:S(2)}, u32[]{:S(2)}) async-start(bf16[8,37,8,1280]{3,2,1,0:T(8,128)(2,1)} %get-tuple-element.180), calls=%async_computation.10 | async-start | bytes 12124160 | tf_op jit(solution)/shard_map/all_to_all | solution.py:840
  895.1 7.6 copy-start.33
  895.2 126.7 %collective-permute-start.1 = (bf16[6,8,24,1408]{3,2,1,0:T(8,128)(2,1)S(1)}, bf16[6,8,24,1408]{3,2,1,0:T(8,128)(2,1)}, u32[]{:S(2)}, u32[]{:S(2)}) collective-permute-start(bf16[6,8,24,1408]{3,2,1,0:T(8,128)(2,1)S(1)} %constant_dynamic-slice_fusion.5), channel_id=1, source_target_pairs={{0,3},{1,2},{2,1},{3,0},{4,7},{5,6},{6,5},{7,4},{8,11},{9,10},{10,... | collective-permute-start | bytes 9732104 | tf_op jit(solution)/shard_map/ppermute | solution.py:875
  899.0 5.7 copy-start.36
  899.0 6.6 copy-start.37
  941.8 8.2 copy-start.30
  941.8 8.2 copy-start.31
  1024.3 136.6 %all-to-all-start.11 = ((bf16[8,34,8,1280]{3,2,1,0:T(8,128)(2,1)}), bf16[8,34,8,1280]{3,2,1,0:T(8,128)(2,1)}, u32[]{:S(2)}, u32[]{:S(2)}) async-start(bf16[8,34,8,1280]{3,2,1,0:T(8,128)(2,1)} %get-tuple-element.181), calls=%async_computation.11 | async-start | bytes 11141120 | tf_op jit(solution)/shard_map/all_to_all | solution.py:840
  1160.8 139.8 %all-to-all-start.12 = ((bf16[8,37,8,1280]{3,2,1,0:T(8,128)(2,1)}), bf16[8,37,8,1280]{3,2,1,0:T(8,128)(2,1)}, u32[]{:S(2)}, u32[]{:S(2)}) async-start(bf16[8,37,8,1280]{3,2,1,0:T(8,128)(2,1)} %get-tuple-element.196), calls=%async_computation.12 | async-start | bytes 12124160 | tf_op jit(solution)/shard_map/all_to_all | solution.py:840
  1300.6 127.2 %all-to-all-start.13 = ((bf16[8,34,8,1280]{3,2,1,0:T(8,128)(2,1)}), bf16[8,34,8,1280]{3,2,1,0:T(8,128)(2,1)}, u32[]{:S(2)}, u32[]{:S(2)}) async-start(bf16[8,34,8,1280]{3,2,1,0:T(8,128)(2,1)} %get-tuple-element.197), calls=%async_computation.13 | async-start | bytes 11141120 | tf_op jit(solution)/shard_map/all_to_all | solution.py:840
  1305.7 12.9 copy-start.22
  1305.7 12.9 copy-start.23
  1305.7 12.9 copy-start.24
  1333.7 7.2 collective-permute-start.3
  1356.0 45.4 %collective-permute-start.4 = (f32[384,1282]{0,1:T(8,128)}, f32[384,1282]{0,1:T(8,128)}, u32[]{:S(2)}, u32[]{:S(2)}) collective-permute-start(f32[384,1282]{0,1:T(8,128)} %copy.217), channel_id=1, source_target_pairs={{0,2},{1,3},{2,0},{3,1},{4,6},{5,7},{6,4},{7,5},{8,10},{9,11},{10,... | collective-permute-start | bytes 5907464 | tf_op jit(solution)/shard_map/ppermute | solution.py:902
  1427.8 73.8 %all-to-all-start.14 = ((bf16[8,19,8,1280]{3,2,1,0:T(8,128)(2,1)}), bf16[8,19,8,1280]{3,2,1,0:T(8,128)(2,1)S(1)}, u32[]{:S(2)}, u32[]{:S(2)}) async-start(bf16[8,19,8,1280]{3,2,1,0:T(8,128)(2,1)} %get-tuple-element.206), calls=%async_computation.14 | async-start | bytes 6225920 | tf_op jit(solution)/shard_map/all_to_all | solution.py:840
  1434.1 56.5 %collective-permute-start.5 = (f32[192,1282]{1,0:T(8,128)}, f32[192,1282]{1,0:T(8,128)}, u32[]{:S(2)}, u32[]{:S(2)}) collective-permute-start(f32[192,1282]{1,0:T(8,128)} %slice_select_fusion.2), channel_id=1, source_target_pairs={{0,4},{4,0},{8,12},{12,8},{16,20},{20,16},{24,28},{28,24},{1,5},{5... | collective-permute-start | bytes 2953736 | tf_op jit(solution)/shard_map/ppermute | solution.py:902
  1503.3 73.9 %all-to-all-start.15 = ((bf16[8,19,8,1280]{3,2,1,0:T(8,128)(2,1)}), bf16[8,19,8,1280]{3,2,1,0:T(8,128)(2,1)S(1)}, u32[]{:S(2)}, u32[]{:S(2)}) async-start(bf16[8,19,8,1280]{3,2,1,0:T(8,128)(2,1)} %get-tuple-element.210), calls=%async_computation.15 | async-start | bytes 6225920 | tf_op jit(solution)/shard_map/all_to_all | solution.py:840
  1516.4 74.4 %copy-start.20 = (bf16[12,96,96]{2,1,0:T(8,128)(2,1)S(1)}, bf16[12,96,96]{2,1,0:T(8,128)(2,1)}, u32[]{:S(2)}) copy-start(bf16[12,96,96]{2,1,0:T(8,128)(2,1)} %convert_element_type.225.refs_2_) | copy-start | bytes 663556
  1578.7 85.0 %all-to-all-start.16 = ((bf16[8,19,8,1280]{3,2,1,0:T(8,128)(2,1)}), bf16[8,19,8,1280]{3,2,1,0:T(8,128)(2,1)S(1)}, u32[]{:S(2)}, u32[]{:S(2)}) async-start(bf16[8,19,8,1280]{3,2,1,0:T(8,128)(2,1)} %rows_to_degrees.7), calls=%async_computation.16 | async-start | bytes 6225920 | tf_op jit(solution)/shard_map/all_to_all | solution.py:840
  1584.3 53.6 %collective-permute-start.6 = (bf16[48,1282]{1,0:T(8,128)(2,1)}, bf16[48,1282]{1,0:T(8,128)(2,1)S(1)}, u32[]{:S(2)}, u32[]{:S(2)}) collective-permute-start(bf16[48,1282]{1,0:T(8,128)(2,1)} %get-tuple-element.271), channel_id=1, source_target_pairs={{0,8},{4,12},{8,0},{12,4},{16,24},{20,28},{24,16},{28,20},{1,9},{5... | collective-permute-start | bytes 369224 | tf_op jit(solution)/shard_map/ppermute | solution.py:922
  1586.3 76.3 %collective-permute-start.7 = (bf16[48,1282]{1,0:T(8,128)(2,1)}, bf16[48,1282]{1,0:T(8,128)(2,1)}, u32[]{:S(2)}, u32[]{:S(2)}) collective-permute-start(bf16[48,1282]{1,0:T(8,128)(2,1)} %get-tuple-element.273), channel_id=1, source_target_pairs={{0,16},{4,20},{8,24},{12,28},{16,0},{20,4},{24,8},{28,12},{1,17},{... | collective-permute-start | bytes 369224 | tf_op jit(solution)/shard_map/ppermute | solution.py:922
  1588.6 73.9 %collective-permute-start.8 = (bf16[48,1282]{1,0:T(8,128)(2,1)}, bf16[48,1282]{1,0:T(8,128)(2,1)}, u32[]{:S(2)}, u32[]{:S(2)}) collective-permute-start(bf16[48,1282]{1,0:T(8,128)(2,1)} %get-tuple-element.272), channel_id=1, source_target_pairs={{0,24},{4,28},{8,16},{12,20},{16,8},{20,12},{24,0},{28,4},{1,25},{... | collective-permute-start | bytes 369224 | tf_op jit(solution)/shard_map/ppermute | solution.py:922
  1665.4 75.8 %all-to-all-start.17 = ((bf16[8,19,8,1280]{3,2,1,0:T(8,128)(2,1)}), bf16[8,19,8,1280]{3,2,1,0:T(8,128)(2,1)}, u32[]{:S(2)}, u32[]{:S(2)}) async-start(bf16[8,19,8,1280]{3,2,1,0:T(8,128)(2,1)} %get-tuple-element.212), calls=%async_computation.17 | async-start | bytes 6225920 | tf_op jit(solution)/shard_map/all_to_all | solution.py:840
  1741.2 73.5 %all-to-all-start.18 = ((bf16[8,19,8,1280]{3,2,1,0:T(8,128)(2,1)}), bf16[8,19,8,1280]{3,2,1,0:T(8,128)(2,1)S(1)}, u32[]{:S(2)}, u32[]{:S(2)}) async-start(bf16[8,19,8,1280]{3,2,1,0:T(8,128)(2,1)} %get-tuple-element.224), calls=%async_computation.18 | async-start | bytes 6225920 | tf_op jit(solution)/shard_map/all_to_all | solution.py:840
  1816.4 85.0 %all-to-all-start.19 = ((bf16[8,19,8,1280]{3,2,1,0:T(8,128)(2,1)}), bf16[8,19,8,1280]{3,2,1,0:T(8,128)(2,1)S(1)}, u32[]{:S(2)}, u32[]{:S(2)}) async-start(bf16[8,19,8,1280]{3,2,1,0:T(8,128)(2,1)} %get-tuple-element.225), calls=%async_computation.19 | async-start | bytes 6225920 | tf_op jit(solution)/shard_map/all_to_all | solution.py:840
  1820.1 55.4 %collective-permute-start.10 = (bf16[48,1282]{1,0:T(8,128)(2,1)S(1)}, bf16[48,1282]{1,0:T(8,128)(2,1)S(1)}, u32[]{:S(2)}, u32[]{:S(2)}) collective-permute-start(bf16[48,1282]{1,0:T(8,128)(2,1)S(1)} %fusion.11), channel_id=1, source_target_pairs={{0,8},{4,12},{8,0},{12,4},{16,24},{20,28},{24,16},{28,20},{1,9},{5... | collective-permute-start | bytes 369224 | tf_op jit(solution)/shard_map/ppermute | solution.py:931
  1822.1 78.1 %collective-permute-start.11 = (bf16[48,1282]{1,0:T(8,128)(2,1)S(1)}, bf16[48,1282]{1,0:T(8,128)(2,1)S(1)}, u32[]{:S(2)}, u32[]{:S(2)}) collective-permute-start(bf16[48,1282]{1,0:T(8,128)(2,1)S(1)} %fusion.11), channel_id=1, source_target_pairs={{0,16},{4,20},{8,24},{12,28},{16,0},{20,4},{24,8},{28,12},{1,17},{... | collective-permute-start | bytes 369224 | tf_op jit(solution)/shard_map/ppermute | solution.py:931
  1824.4 76.4 %collective-permute-start.12 = (bf16[48,1282]{1,0:T(8,128)(2,1)S(1)}, bf16[48,1282]{1,0:T(8,128)(2,1)S(1)}, u32[]{:S(2)}, u32[]{:S(2)}) collective-permute-start(bf16[48,1282]{1,0:T(8,128)(2,1)S(1)} %fusion.11), channel_id=1, source_target_pairs={{0,24},{4,28},{8,16},{12,20},{16,8},{20,12},{24,0},{28,4},{1,25},{... | collective-permute-start | bytes 369224 | tf_op jit(solution)/shard_map/ppermute | solution.py:931
  1901.5 7.8 copy-start.11
  1901.5 75.0 %all-to-all-start.20 = ((bf16[8,19,8,1280]{3,2,1,0:T(8,128)(2,1)}), bf16[8,19,8,1280]{3,2,1,0:T(8,128)(2,1)}, u32[]{:S(2)}, u32[]{:S(2)}) async-start(bf16[8,19,8,1280]{3,2,1,0:T(8,128)(2,1)} %get-tuple-element.229), calls=%async_computation.20 | async-start | bytes 6225920 | tf_op jit(solution)/shard_map/all_to_all | solution.py:840
  1913.1 5.9 copy-start.5
  1919.0 9.5 collective-permute-start.9
  1976.4 79.0 %all-to-all-start.21 = ((bf16[8,19,8,1280]{3,2,1,0:T(8,128)(2,1)}), bf16[8,19,8,1280]{3,2,1,0:T(8,128)(2,1)S(1)}, u32[]{:S(2)}, u32[]{:S(2)}) async-start(bf16[8,19,8,1280]{3,2,1,0:T(8,128)(2,1)} %degrees_to_rows.6), calls=%async_computation.21 | async-start | bytes 6225920 | tf_op jit(solution)/shard_map/all_to_all | solution.py:840
  1984.2 71.3 %collective-permute-start.16 = (bf16[6,8,24,1408]{3,2,1,0:T(8,128)(2,1)}, bf16[6,8,24,1408]{3,2,1,0:T(8,128)(2,1)}, u32[]{:S(2)}, u32[]{:S(2)}) collective-permute-start(bf16[6,8,24,1408]{3,2,1,0:T(8,128)(2,1)} %constant_dynamic-slice_fusion), channel_id=1, source_target_pairs={{0,2},{1,3},{2,0},{3,1},{4,6},{5,7},{6,4},{7,5},{8,10},{9,11},{10,... | collective-permute-start | bytes 9732104 | tf_op jit(solution)/shard_map/ppermute | solution.py:875
  2057.1 189.5 %all-to-all-start.22 = ((bf16[8,52,8,1280]{3,2,1,0:T(8,128)(2,1)}), bf16[8,52,8,1280]{3,2,1,0:T(8,128)(2,1)}, u32[]{:S(2)}, u32[]{:S(2)}) async-start(bf16[8,52,8,1280]{3,2,1,0:T(8,128)(2,1)} %get-tuple-element.246), calls=%async_computation.22 | async-start | bytes 17039360 | tf_op jit(solution)/shard_map/all_to_all | solution.py:840
  2066.7 106.3 %collective-permute-start.13 = (bf16[6,8,24,1408]{3,2,1,0:T(8,128)(2,1)}, bf16[6,8,24,1408]{3,2,1,0:T(8,128)(2,1)}, u32[]{:S(2)}, u32[]{:S(2)}) collective-permute-start(bf16[6,8,24,1408]{3,2,1,0:T(8,128)(2,1)} %constant_dynamic-slice_fusion.1), channel_id=1, source_target_pairs={{0,3},{1,2},{2,1},{3,0},{4,7},{5,6},{6,5},{7,4},{8,11},{9,10},{10,... | collective-permute-start | bytes 9732104 | tf_op jit(solution)/shard_map/ppermute | solution.py:875
  2066.7 76.6 %collective-permute-start.14 = (bf16[192,1282]{1,0:T(8,128)(2,1)}, bf16[192,1282]{1,0:T(8,128)(2,1)S(1)}, u32[]{:S(2)}, u32[]{:S(2)}) collective-permute-start(bf16[192,1282]{1,0:T(8,128)(2,1)} %bitcast.50), channel_id=1, source_target_pairs={{0,4},{4,0},{8,12},{12,8},{16,20},{20,16},{24,28},{28,24},{1,5},{5... | collective-permute-start | bytes 1476872 | tf_op jit(solution)/shard_map/ppermute | solution.py:907
  2145.7 22.7 collective-permute-start.15
  2246.6 74.1 %all-to-all-start.23 = ((bf16[8,19,8,1280]{3,2,1,0:T(8,128)(2,1)}), bf16[8,19,8,1280]{3,2,1,0:T(8,128)(2,1)S(1)}, u32[]{:S(2)}, u32[]{:S(2)}) async-start(bf16[8,19,8,1280]{3,2,1,0:T(8,128)(2,1)} %get-tuple-element.247), calls=%async_computation.23 | async-start | bytes 6225920 | tf_op jit(solution)/shard_map/all_to_all | solution.py:840
  2254.6 4.3 collective-permute-start.17
  2338.4 1.2 collective-permute-start.18
  2339.7 3.6 collective-permute-start.19
  2343.3 3.6 collective-permute-start.20
  2346.9 3.6 collective-permute-start.21
  2350.6 4.5 collective-permute-start.22
  (22 other events, 48.1 us)

commit v6 on v5

--- a/solution.py
+++ b/solution.py
@@ -25,7 +25,7 @@
 noise_scale = 1.0 / 262144.0
 bf16 = jnp.bfloat16
 f32 = jnp.float32
-VMEM_LIMIT = 60 * 2**20
+VMEM_LIMIT = 62 * 2**20
 
 
 def call(body, name, flops, moved, **options):

time: 2370 us -> 2360 us (level)
  local copies, waits for them, and re-layouts: 260 us -> 216 us
  waiting for transfers between devices: 1100 us -> 1130 us
    all_to_all x23, waiting for transfers between devices: 655 us -> 683 us  [swap(): lax.all_to_all(values, 'lat', split_axis=0, concat_axis=0, tiled=True)]
    unnamed x87 -> x81, local copies, waits for them, and re-layouts: 81.6 us -> 61.8 us
  transfers between devices with their start and end apart: 46 -> 46, of which waited for: 35 -> 35; matrix products, arithmetic and copies ran while one was open for 14% -> 13% of each run, Pallas kernels for 28% -> 28%
where the time goes in v6:
time: 2360 us; the launch traced here: 2350 us
  waiting for transfers between devices  1130 us (48%)
  Pallas kernels  692 us (29%)
  local copies, waits for them, and re-layouts  216 us (9%)
  starting transfers between devices  129 us (5%)
  other arithmetic  104 us (4%)
  blocking collectives  74 us (3%)
    all_to_all x23, waiting for transfers between devices, swap(): lax.all_to_all(values, 'lat', split_axis=0, concat_axis=0, tiled=True)  683 us
    pallas_call x3, Pallas kernels, pixels(): call(body, 'feed_forward', 2 * count * points * (6 * C * hidden + 2 * tab...  323 us
    all_to_all x23, starting transfers between devices, swap(): lax.all_to_all(values, 'lat', split_axis=0, concat_axis=0, tiled=True)  111 us
    pallas_call x8, Pallas kernels, lane_call(): call(functools.partial(lane_body, work, subs, width, len(inputs), len(tab...  106 us
    ppermute x6, waiting for transfers between devices, share_slots(): return lax.ppermute(block, 'chan', route) if step else block  106 us
    ppermute x3, waiting for transfers between devices, double(): other = lax.ppermute(line.hold(held), axis, partners(sizes[axis], step)[0])  101 us
    ppermute x3, waiting for transfers between devices, halve(): lax.ppermute(jnp.where(upper, low, high), axis, partners(sizes[axis], ste...  82.1 us
    pallas_call x4, Pallas kernels, mix(): call(body, 'mix_back' if backward else 'mix', 2 * count * n_lat * subs *...  81.2 us
  transfers between devices with their start and end apart: 46, of which 35 were waited for; matrix products, arithmetic and copies ran while one was open for 13% of the time, Pallas kernels for 28%

profile of v6, /device:TPU:0, one launch (start us, length us, event | category | flops | bytes accessed | tf_op | source)
XLA Modules:
  0.0 2345.4 jit_solution(4538251806246856229)
XLA Ops:
  6.8 10.0 norm_and_dft.3
  16.8 7.3 all-to-all-start
  24.1 24.3 %norm_and_dft.4 = bf16[8,52,8,1280]{3,2,1,0:T(8,128)(2,1)} custom-call(f32[23,641,1,360]{3,2,1,0:T(1,128)} %bitcast.109, s32[23,8,360]{2,1,0:T(8,128)} %bitcast.153, f32[641,1]{1,0:T(8,128)} %broadcast_in_dim.222.gain.refs_5_, f32[641,1]{1,0:T(8,128)} %broadcast_in_dim.223.bias, bf16[384,360]{1,0:T(8,128)(2,1)} %pad_maximum_fusion.4.table.refs_4_), custom_call_target="tpu_custom_call" | custom-call | flops 3609722880 | bytes 24883104 | tf_op jit(solution)/shard_map/norm_and_dft/pallas_call | solution.py:162
  48.4 45.8 %all-to-all-done.refs_0_.refs_2_ = bf16[8,19,8,1280]{3,2,1,0:T(8,128)(2,1)} async-done(((bf16[8,19,8,1280]{3,2,1,0:T(8,128)(2,1)}), bf16[8,19,8,1280]{3,2,1,0:T(8,128)(2,1)}, u32[]{:S(2)}, u32[]{:S(2)}) %all-to-all-start) | async-done | bytes 3112992 | tf_op jit(solution)/shard_map/all_to_all | solution.py:840
  99.1 20.7 reduce
  127.0 7.5 copy.189
  134.5 8.2 broadcast_in_dim.209.state
  146.6 10.0 norm_and_dft.5
  156.6 127.5 %all-to-all-done.1.refs_1_.refs_3_ = bf16[8,52,8,1280]{3,2,1,0:T(8,128)(2,1)} async-done(((bf16[8,52,8,1280]{3,2,1,0:T(8,128)(2,1)}), bf16[8,52,8,1280]{3,2,1,0:T(8,128)(2,1)}, u32[]{:S(2)}, u32[]{:S(2)}) %all-to-all-start.1) | async-done | bytes 8519712 | tf_op jit(solution)/shard_map/all_to_all | solution.py:840
  293.5 13.2 legendre_tables.3
  321.3 17.0 rows_to_degrees.4
  338.3 20.2 all-to-all-done.2.refs_0_.refs_1_
  375.1 9.5 rows_to_degrees.5
  384.5 48.1 %all-to-all-done.3.fine.fine_tail = bf16[8,19,8,1280]{3,2,1,0:T(8,128)(2,1)} async-done(((bf16[8,19,8,1280]{3,2,1,0:T(8,128)(2,1)}), bf16[8,19,8,1280]{3,2,1,0:T(8,128)(2,1)}, u32[]{:S(2)}, u32[]{:S(2)}) %all-to-all-start.3) | async-done | bytes 3112992 | tf_op jit(solution)/shard_map/all_to_all | solution.py:840
  437.9 13.2 legendre_tables.5
  462.0 44.7 %all-to-all-done.4.coarse.coarse_tail.refs_3_.refs_4_ = bf16[8,19,8,1280]{3,2,1,0:T(8,128)(2,1)} async-done(((bf16[8,19,8,1280]{3,2,1,0:T(8,128)(2,1)}), bf16[8,19,8,1280]{3,2,1,0:T(8,128)(2,1)}, u32[]{:S(2)}, u32[]{:S(2)}) %all-to-all-start.4) | async-done | bytes 3112992 | tf_op jit(solution)/shard_map/all_to_all | solution.py:840
  511.9 31.7 %copy.242 = bf16[24,2,649,641]{2,3,1,0:T(8,128)(2,1)} copy(bf16[24,2,649,641]{2,1,3,0:T(2,128)(2,1)} %param.27) | data formatting | bytes 79873728 | tf_op args[9]
  544.3 20.3 mix.2
  564.6 16.2 all-to-all-done.5.refs_1_.refs_2_
  585.5 20.3 mix.3
  605.8 49.2 %all-to-all-done.6.refs_0_.refs_2_ = bf16[8,19,8,1280]{3,2,1,0:T(8,128)(2,1)} async-done(((bf16[8,19,8,1280]{3,2,1,0:T(8,128)(2,1)}), bf16[8,19,8,1280]{3,2,1,0:T(8,128)(2,1)}, u32[]{:S(2)}, u32[]{:S(2)}) %all-to-all-start.6) | async-done | bytes 3112992 | tf_op jit(solution)/shard_map/all_to_all | solution.py:840
  654.9 74.0 %all_to_all.120.refs_0_.refs_1_ = bf16[8,19,8,1280]{3,2,1,0:T(8,128)(2,1)} all-to-all(bf16[8,19,8,1280]{3,2,1,0:T(8,128)(2,1)} %get-tuple-element.162), channel_id=1, replica_groups=mesh['lat'=8,'chan'=4] {'lat'}, dimensions={0} | all-to-all | bytes 6225920 | tf_op jit(solution)/shard_map/all_to_all | solution.py:840
  747.4 9.5 degrees_to_rows.4
  756.9 45.2 %all-to-all-done.8.refs_1_.refs_3_ = bf16[8,19,8,1280]{3,2,1,0:T(8,128)(2,1)} async-done(((bf16[8,19,8,1280]{3,2,1,0:T(8,128)(2,1)}), bf16[8,19,8,1280]{3,2,1,0:T(8,128)(2,1)}, u32[]{:S(2)}, u32[]{:S(2)}) %all-to-all-start.8) | async-done | bytes 3112992 | tf_op jit(solution)/shard_map/all_to_all | solution.py:840
  813.4 16.9 degrees_to_rows.5
  830.3 51.4 %collective-permute-done.2.refs_2_ = bf16[6,8,24,1408]{3,2,1,0:T(8,128)(2,1)} collective-permute-done((bf16[6,8,24,1408]{3,2,1,0:T(8,128)(2,1)}, bf16[6,8,24,1408]{3,2,1,0:T(8,128)(2,1)}, u32[]{:S(2)}, u32[]{:S(2)}) %collective-permute-start.2) | collective-permute-done | bytes 3244064 | tf_op jit(solution)/shard_map/ppermute | solution.py:875
  901.5 20.7 reduce.1
  929.4 7.5 copy.197
  936.9 8.2 broadcast_in_dim.210.cotangent
  945.8 71.1 %feed_forward.3 = (f32[6,641,1,360]{3,2,1,0:T(1,128)}, f32[6,641,360]{2,1,0:T(8,128)}, bf16[8,19,8,1280]{3,2,1,0:T(8,128)(2,1)}, f32[2,768,1282]{2,1,0:T(8,128)}...) custom-call(bf16[8,19,8,1280]{3,2,1,0:T(8,128)(2,1)} %all-to-all-done.9.synth.tail, ...), custom_call_target="tpu_custom_call" | custom-call | flops 23848110080 | bytes 28641024 | tf_op jit(solution)/shard_map/feed_forward/pallas_call | solution.py:674
  1024.4 130.7 %feed_forward.4 = (f32[23,641,1,360]{3,2,1,0:T(1,128)}, f32[23,641,360]{2,1,0:T(8,128)}, bf16[8,37,8,1280]{3,2,1,0:T(8,128)(2,1)}, f32[2,768,1282]{2,1,0:T(8,128...) custom-call(bf16[8,37,8,1280]{3,2,1,0:T(8,128)(2,1)} %all-to-all-done.10.synth.tail, ...), custom_call_target="tpu_custom_call" | custom-call | flops 47696220160 | bytes 57282048 | tf_op jit(solution)/shard_map/feed_forward/pallas_call | solution.py:674
  1161.4 120.8 %feed_forward.5 = (f32[23,641,1,360]{3,2,1,0:T(1,128)}, f32[23,641,360]{2,1,0:T(8,128)}, bf16[8,34,8,1280]{3,2,1,0:T(8,128)(2,1)}, f32[2,768,1282]{2,1,0:T(8,128...) custom-call(bf16[8,34,8,1280]{3,2,1,0:T(8,128)(2,1)} %all-to-all-done.11.refs_0_.refs_, ...), custom_call_target="tpu_custom_call", output_to_operand_aliasing={{0}: (13, {}), {1}: (14, {})} | custom-call | flops 43721535488 | bytes 52508544 | tf_op jit(solution)/shard_map/feed_forward/pallas_call | solution.py:674
  1282.3 13.3 all-to-all-done.12.refs_0_.refs_2_
  1300.7 12.8 add_add_fusion
  1328.6 7.2 collective-permute-done.3
  1351.4 44.8 %collective-permute-done.4 = f32[384,1282]{0,1:T(8,128)S(1)} collective-permute-done((f32[384,1282]{0,1:T(8,128)}, f32[384,1282]{0,1:T(8,128)S(1)}, u32[]{:S(2)}, u32[]{:S(2)}) %collective-permute-start.4) | collective-permute-done | bytes 1969184 | tf_op jit(solution)/shard_map/ppermute | solution.py:902
  1401.5 22.0 all-to-all-done.13.refs_1_.refs_3_
  1430.9 8.2 part_rows.2
  1439.2 17.0 rows_to_degrees.6
  1456.1 30.1 %collective-permute-done.5 = f32[192,1282]{1,0:T(8,128)S(1)} collective-permute-done((f32[192,1282]{1,0:T(8,128)}, f32[192,1282]{1,0:T(8,128)S(1)}, u32[]{:S(2)}, u32[]{:S(2)}) %collective-permute-start.5) | collective-permute-done | bytes 984608 | tf_op jit(solution)/shard_map/ppermute | solution.py:902
  1488.9 8.6 all-to-all-done.14.refs_0_.refs_1_
  1501.9 9.5 rows_to_degrees.7
  1511.4 60.0 %all-to-all-done.15.fine.fine_tail = bf16[8,19,8,1280]{3,2,1,0:T(8,128)(2,1)} async-done(((bf16[8,19,8,1280]{3,2,1,0:T(8,128)(2,1)}), bf16[8,19,8,1280]{3,2,1,0:T(8,128)(2,1)}, u32[]{:S(2)}, u32[]{:S(2)}) %all-to-all-start.15) | async-done | bytes 3112992 | tf_op jit(solution)/shard_map/all_to_all | solution.py:840
  1584.4 46.2 %collective-permute-done.6 = bf16[48,1282]{1,0:T(8,128)(2,1)S(1)} collective-permute-done((bf16[48,1282]{1,0:T(8,128)(2,1)}, bf16[48,1282]{1,0:T(8,128)(2,1)S(1)}, u32[]{:S(2)}, u32[]{:S(2)}) %collective-permute-start.6) | collective-permute-done | bytes 123104 | tf_op jit(solution)/shard_map/ppermute | solution.py:922
  1630.6 24.7 %collective-permute-done.7 = bf16[48,1282]{1,0:T(8,128)(2,1)} collective-permute-done((bf16[48,1282]{1,0:T(8,128)(2,1)}, bf16[48,1282]{1,0:T(8,128)(2,1)}, u32[]{:S(2)}, u32[]{:S(2)}) %collective-permute-start.7) | collective-permute-done | bytes 123104 | tf_op jit(solution)/shard_map/ppermute | solution.py:922
  1662.7 20.3 mix_back.2
  1683.0 50.9 %all-to-all-done.17.refs_1_.refs_2_ = bf16[8,19,8,1280]{3,2,1,0:T(8,128)(2,1)} async-done(((bf16[8,19,8,1280]{3,2,1,0:T(8,128)(2,1)}), bf16[8,19,8,1280]{3,2,1,0:T(8,128)(2,1)}, u32[]{:S(2)}, u32[]{:S(2)}) %all-to-all-start.17) | async-done | bytes 3112992 | tf_op jit(solution)/shard_map/all_to_all | solution.py:840
  1738.3 20.3 mix_back.3
  1758.6 49.7 %all-to-all-done.18.refs_0_.refs_2_ = bf16[8,19,8,1280]{3,2,1,0:T(8,128)(2,1)} async-done(((bf16[8,19,8,1280]{3,2,1,0:T(8,128)(2,1)}), bf16[8,19,8,1280]{3,2,1,0:T(8,128)(2,1)}, u32[]{:S(2)}, u32[]{:S(2)}) %all-to-all-start.18) | async-done | bytes 3112992 | tf_op jit(solution)/shard_map/all_to_all | solution.py:840
  1817.8 49.4 %collective-permute-done.10 = bf16[48,1282]{1,0:T(8,128)(2,1)S(1)} collective-permute-done((bf16[48,1282]{1,0:T(8,128)(2,1)S(1)}, bf16[48,1282]{1,0:T(8,128)(2,1)S(1)}, u32[]{:S(2)}, u32[]{:S(2)}) %collective-permute-start.10) | collective-permute-done | bytes 123104 | tf_op jit(solution)/shard_map/ppermute | solution.py:931
  1867.9 24.0 %collective-permute-done.11 = bf16[48,1282]{1,0:T(8,128)(2,1)S(1)} collective-permute-done((bf16[48,1282]{1,0:T(8,128)(2,1)S(1)}, bf16[48,1282]{1,0:T(8,128)(2,1)S(1)}, u32[]{:S(2)}, u32[]{:S(2)}) %collective-permute-start.11) | collective-permute-done | bytes 123104 | tf_op jit(solution)/shard_map/ppermute | solution.py:931
  1911.8 9.5 degrees_to_rows.6
  1921.2 47.0 %all-to-all-done.20.refs_1_.refs_3_ = bf16[8,19,8,1280]{3,2,1,0:T(8,128)(2,1)} async-done(((bf16[8,19,8,1280]{3,2,1,0:T(8,128)(2,1)}), bf16[8,19,8,1280]{3,2,1,0:T(8,128)(2,1)}, u32[]{:S(2)}, u32[]{:S(2)}) %all-to-all-start.20) | async-done | bytes 3112992 | tf_op jit(solution)/shard_map/all_to_all | solution.py:840
  1976.8 17.0 degrees_to_rows.7
  1993.8 54.3 %collective-permute-done.16.refs_6_ = bf16[6,8,24,1408]{3,2,1,0:T(8,128)(2,1)} collective-permute-done((bf16[6,8,24,1408]{3,2,1,0:T(8,128)(2,1)}, bf16[6,8,24,1408]{3,2,1,0:T(8,128)(2,1)}, u32[]{:S(2)}, u32[]{:S(2)}) %collective-permute-start.16) | collective-permute-done | bytes 3244064 | tf_op jit(solution)/shard_map/ppermute | solution.py:875
  2059.7 74.6 %collective-permute-done.14 = bf16[192,1282]{1,0:T(8,128)(2,1)S(1)} collective-permute-done((bf16[192,1282]{1,0:T(8,128)(2,1)}, bf16[192,1282]{1,0:T(8,128)(2,1)S(1)}, u32[]{:S(2)}, u32[]{:S(2)}) %collective-permute-start.14) | collective-permute-done | bytes 492320 | tf_op jit(solution)/shard_map/ppermute | solution.py:907
  2137.2 22.1 collective-permute-done.15
  2165.2 14.3 first_norm_back.3
  2179.5 8.2 part_rows.3
  2187.7 27.4 %mix_gradient.1 = f32[6,641,2,649]{3,2,1,0:T(2,128)} custom-call(bf16[6,8,24,1408]{3,2,1,0:T(8,128)(2,1)} %get-tuple-element.260.refs_0_, bf16[6,8,24,1408]{3,2,1,0:T(8,128)(2,1)} %collective-permute-done.refs_1_, bf16[6,8,24,1408]{3,2,1,0:T(8,128)(2,1)} %collective-permute-done.2.refs_2_, bf16[6,8,24,1408]{3,2,1,0:T(8,128)(2,1)} %collective-permute-done.1.refs_3_, ...), custom_call_target="tpu_custom_call" | custom-call | flops 15335755776 | bytes 45920688 | tf_op jit(solution)/shard_map/mix_gradient/pallas_call | solution.py:585
  2215.1 22.6 all-to-all-done.22.wave.tail
  2266.7 34.6 %first_norm_back.4 = (f32[23,641,1,360]{3,2,1,0:T(1,128)}, f32[2,641,1]{2,1,0:T(8,128)}) custom-call(bf16[8,52,8,1280]{3,2,1,0:T(8,128)(2,1)} %all-to-all-done.22.wave.tail, bf16[8,52,8,1280]{3,2,1,0:T(8,128)(2,1)} %all-to-all-done.22.wave.tail, f32[23,641,1,360]{3,2,1,0:T(1,128)} %bitcast.112, f32[23,641,360]{2,1,0:T(8,128)} %get-tuple-element.188.middle_grad.refs_3_, ...), custom_call_target="tpu_custom_call" | custom-call | flops 3609722880 | bytes 56266464 | tf_op jit(solution)/shard_map/first_norm_back/pallas_call | solution.py:743
  2301.3 10.6 all-to-all-done.23.refs_0_.refs_1_
  2311.9 14.3 first_norm_back.5
  (298 shorter events, 346.9 us)
Async XLA Ops:
  16.8 77.4 %all-to-all-start = ((bf16[8,19,8,1280]{3,2,1,0:T(8,128)(2,1)}), bf16[8,19,8,1280]{3,2,1,0:T(8,128)(2,1)}, u32[]{:S(2)}, u32[]{:S(2)}) async-start(bf16[8,19,8,1280]{3,2,1,0:T(8,128)(2,1)} %norm_and_dft.3), calls=%async_computation | async-start | bytes 6225920 | tf_op jit(solution)/shard_map/all_to_all | solution.py:840
  94.2 190.0 %all-to-all-start.1 = ((bf16[8,52,8,1280]{3,2,1,0:T(8,128)(2,1)}), bf16[8,52,8,1280]{3,2,1,0:T(8,128)(2,1)}, u32[]{:S(2)}, u32[]{:S(2)}) async-start(bf16[8,52,8,1280]{3,2,1,0:T(8,128)(2,1)} %norm_and_dft.4), calls=%async_computation.1 | async-start | bytes 17039360 | tf_op jit(solution)/shard_map/all_to_all | solution.py:840
  134.5 8.2 copy-start.29
  156.6 132.5 %copy-start.35 = (s32[184]{0:T(256)S(1)}, s32[184]{0:T(256)}, u32[]{:S(2)}) copy-start(s32[184]{0:T(256)} %param.23) | copy-start | bytes 2212
  284.1 74.4 %all-to-all-start.2 = ((bf16[8,19,8,1280]{3,2,1,0:T(8,128)(2,1)}), bf16[8,19,8,1280]{3,2,1,0:T(8,128)(2,1)}, u32[]{:S(2)}, u32[]{:S(2)}) async-start(bf16[8,19,8,1280]{3,2,1,0:T(8,128)(2,1)} %norm_and_dft.5), calls=%async_computation.2 | async-start | bytes 6225920 | tf_op jit(solution)/shard_map/all_to_all | solution.py:840
  358.6 74.1 %all-to-all-start.3 = ((bf16[8,19,8,1280]{3,2,1,0:T(8,128)(2,1)}), bf16[8,19,8,1280]{3,2,1,0:T(8,128)(2,1)}, u32[]{:S(2)}, u32[]{:S(2)}) async-start(bf16[8,19,8,1280]{3,2,1,0:T(8,128)(2,1)} %get-tuple-element.147), calls=%async_computation.3 | async-start | bytes 6225920 | tf_op jit(solution)/shard_map/all_to_all | solution.py:840
  432.6 74.1 %all-to-all-start.4 = ((bf16[8,19,8,1280]{3,2,1,0:T(8,128)(2,1)}), bf16[8,19,8,1280]{3,2,1,0:T(8,128)(2,1)}, u32[]{:S(2)}, u32[]{:S(2)}) async-start(bf16[8,19,8,1280]{3,2,1,0:T(8,128)(2,1)} %rows_to_degrees.5), calls=%async_computation.4 | async-start | bytes 6225920 | tf_op jit(solution)/shard_map/all_to_all | solution.py:840
  461.0 45.7 %copy-start.13 = (bf16[12,96,96]{2,1,0:T(8,128)(2,1)}, bf16[12,96,96]{2,1,0:T(8,128)(2,1)S(1)}, u32[]{:S(2)}) copy-start(bf16[12,96,96]{2,1,0:T(8,128)(2,1)S(1)} %convert_element_type.218.refs_2_) | copy-start | bytes 663556
  462.0 350.0 %copy-start.10 = (bf16[12,192,184]{2,1,0:T(8,128)(2,1)}, bf16[12,192,184]{2,1,0:T(8,128)(2,1)S(1)}, u32[]{:S(2)}) copy-start(bf16[12,192,184]{2,1,0:T(8,128)(2,1)S(1)} %constant_dynamic-update-slice_fusion.refs_4_) | copy-start | bytes 2543620
  506.7 74.1 %all-to-all-start.5 = ((bf16[8,19,8,1280]{3,2,1,0:T(8,128)(2,1)}), bf16[8,19,8,1280]{3,2,1,0:T(8,128)(2,1)}, u32[]{:S(2)}, u32[]{:S(2)}) async-start(bf16[8,19,8,1280]{3,2,1,0:T(8,128)(2,1)} %get-tuple-element.149), calls=%async_computation.5 | async-start | bytes 6225920 | tf_op jit(solution)/shard_map/all_to_all | solution.py:840
  580.8 74.1 %all-to-all-start.6 = ((bf16[8,19,8,1280]{3,2,1,0:T(8,128)(2,1)}), bf16[8,19,8,1280]{3,2,1,0:T(8,128)(2,1)}, u32[]{:S(2)}, u32[]{:S(2)}) async-start(bf16[8,19,8,1280]{3,2,1,0:T(8,128)(2,1)} %get-tuple-element.161), calls=%async_computation.6 | async-start | bytes 6225920 | tf_op jit(solution)/shard_map/all_to_all | solution.py:840
  729.0 73.1 %all-to-all-start.8 = ((bf16[8,19,8,1280]{3,2,1,0:T(8,128)(2,1)}), bf16[8,19,8,1280]{3,2,1,0:T(8,128)(2,1)}, u32[]{:S(2)}, u32[]{:S(2)}) async-start(bf16[8,19,8,1280]{3,2,1,0:T(8,128)(2,1)} %get-tuple-element.165), calls=%async_computation.8 | async-start | bytes 6225920 | tf_op jit(solution)/shard_map/all_to_all | solution.py:840
  740.6 6.9 copy-start.3
  747.4 9.5 collective-permute-start
  802.1 79.6 %all-to-all-start.9 = ((bf16[8,19,8,1280]{3,2,1,0:T(8,128)(2,1)}), bf16[8,19,8,1280]{3,2,1,0:T(8,128)(2,1)}, u32[]{:S(2)}, u32[]{:S(2)}) async-start(bf16[8,19,8,1280]{3,2,1,0:T(8,128)(2,1)} %degrees_to_rows.4), calls=%async_computation.9 | async-start | bytes 6225920 | tf_op jit(solution)/shard_map/all_to_all | solution.py:840
  810.4 71.3 %collective-permute-start.2 = (bf16[6,8,24,1408]{3,2,1,0:T(8,128)(2,1)}, bf16[6,8,24,1408]{3,2,1,0:T(8,128)(2,1)}, u32[]{:S(2)}, u32[]{:S(2)}) collective-permute-start(bf16[6,8,24,1408]{3,2,1,0:T(8,128)(2,1)} %constant_dynamic-slice_fusion.4), channel_id=1, source_target_pairs={{0,2},{1,3},{2,0},{3,1},{4,6},{5,7},{6,4},{7,5},{8,10},{9,11},{10,... | collective-permute-start | bytes 9732104 | tf_op jit(solution)/shard_map/ppermute | solution.py:875
  881.7 136.9 %all-to-all-start.10 = ((bf16[8,37,8,1280]{3,2,1,0:T(8,128)(2,1)}), bf16[8,37,8,1280]{3,2,1,0:T(8,128)(2,1)}, u32[]{:S(2)}, u32[]{:S(2)}) async-start(bf16[8,37,8,1280]{3,2,1,0:T(8,128)(2,1)} %get-tuple-element.180), calls=%async_computation.10 | async-start | bytes 12124160 | tf_op jit(solution)/shard_map/all_to_all | solution.py:840
  891.4 6.4 copy-start.30
  891.4 125.5 %collective-permute-start.1 = (bf16[6,8,24,1408]{3,2,1,0:T(8,128)(2,1)}, bf16[6,8,24,1408]{3,2,1,0:T(8,128)(2,1)}, u32[]{:S(2)}, u32[]{:S(2)}) collective-permute-start(bf16[6,8,24,1408]{3,2,1,0:T(8,128)(2,1)} %constant_dynamic-slice_fusion.5), channel_id=1, source_target_pairs={{0,3},{1,2},{2,1},{3,0},{4,7},{5,6},{6,5},{7,4},{8,11},{9,10},{10,... | collective-permute-start | bytes 9732104 | tf_op jit(solution)/shard_map/ppermute | solution.py:875
  894.0 6.7 copy-start.34
  936.9 8.2 copy-start.28
  1018.6 136.5 %all-to-all-start.11 = ((bf16[8,34,8,1280]{3,2,1,0:T(8,128)(2,1)}), bf16[8,34,8,1280]{3,2,1,0:T(8,128)(2,1)}, u32[]{:S(2)}, u32[]{:S(2)}) async-start(bf16[8,34,8,1280]{3,2,1,0:T(8,128)(2,1)} %get-tuple-element.181), calls=%async_computation.11 | async-start | bytes 11141120 | tf_op jit(solution)/shard_map/all_to_all | solution.py:840
  1155.1 140.4 %all-to-all-start.12 = ((bf16[8,37,8,1280]{3,2,1,0:T(8,128)(2,1)}), bf16[8,37,8,1280]{3,2,1,0:T(8,128)(2,1)}, u32[]{:S(2)}, u32[]{:S(2)}) async-start(bf16[8,37,8,1280]{3,2,1,0:T(8,128)(2,1)} %get-tuple-element.196), calls=%async_computation.12 | async-start | bytes 12124160 | tf_op jit(solution)/shard_map/all_to_all | solution.py:840
  1295.6 127.9 %all-to-all-start.13 = ((bf16[8,34,8,1280]{3,2,1,0:T(8,128)(2,1)}), bf16[8,34,8,1280]{3,2,1,0:T(8,128)(2,1)}, u32[]{:S(2)}, u32[]{:S(2)}) async-start(bf16[8,34,8,1280]{3,2,1,0:T(8,128)(2,1)} %get-tuple-element.197), calls=%async_computation.13 | async-start | bytes 11141120 | tf_op jit(solution)/shard_map/all_to_all | solution.py:840
  1300.7 12.9 copy-start.18
  1300.7 12.9 copy-start.19
  1300.7 12.9 copy-start.20
  1328.6 7.2 collective-permute-start.3
  1350.9 45.3 %collective-permute-start.4 = (f32[384,1282]{0,1:T(8,128)}, f32[384,1282]{0,1:T(8,128)S(1)}, u32[]{:S(2)}, u32[]{:S(2)}) collective-permute-start(f32[384,1282]{0,1:T(8,128)} %copy.217), channel_id=1, source_target_pairs={{0,2},{1,3},{2,0},{3,1},{4,6},{5,7},{6,4},{7,5},{8,10},{9,11},{10,... | collective-permute-start | bytes 5907464 | tf_op jit(solution)/shard_map/ppermute | solution.py:902
  1401.5 26.5 %copy-start.6 = (f32[384,1282]{1,0:T(8,128)}, f32[384,1282]{1,0:T(8,128)S(1)}, u32[]{:S(2)}) copy-start(f32[384,1282]{1,0:T(8,128)S(1)} %select_add_fusion.1) | copy-start | bytes 5907460
  1423.5 73.9 %all-to-all-start.14 = ((bf16[8,19,8,1280]{3,2,1,0:T(8,128)(2,1)}), bf16[8,19,8,1280]{3,2,1,0:T(8,128)(2,1)}, u32[]{:S(2)}, u32[]{:S(2)}) async-start(bf16[8,19,8,1280]{3,2,1,0:T(8,128)(2,1)} %get-tuple-element.206), calls=%async_computation.14 | async-start | bytes 6225920 | tf_op jit(solution)/shard_map/all_to_all | solution.py:840
  1429.1 57.1 %collective-permute-start.5 = (f32[192,1282]{1,0:T(8,128)}, f32[192,1282]{1,0:T(8,128)S(1)}, u32[]{:S(2)}, u32[]{:S(2)}) collective-permute-start(f32[192,1282]{1,0:T(8,128)} %slice_select_fusion.2), channel_id=1, source_target_pairs={{0,4},{4,0},{8,12},{12,8},{16,20},{20,16},{24,28},{28,24},{1,5},{5... | collective-permute-start | bytes 2953736 | tf_op jit(solution)/shard_map/ppermute | solution.py:902
  1497.4 74.0 %all-to-all-start.15 = ((bf16[8,19,8,1280]{3,2,1,0:T(8,128)(2,1)}), bf16[8,19,8,1280]{3,2,1,0:T(8,128)(2,1)}, u32[]{:S(2)}, u32[]{:S(2)}) async-start(bf16[8,19,8,1280]{3,2,1,0:T(8,128)(2,1)} %get-tuple-element.210), calls=%async_computation.15 | async-start | bytes 6225920 | tf_op jit(solution)/shard_map/all_to_all | solution.py:840
  1511.4 72.1 %copy-start.12 = (bf16[12,96,96]{2,1,0:T(8,128)(2,1)S(1)}, bf16[12,96,96]{2,1,0:T(8,128)(2,1)}, u32[]{:S(2)}) copy-start(bf16[12,96,96]{2,1,0:T(8,128)(2,1)} %convert_element_type.225.refs_2_) | copy-start | bytes 663556
  1571.4 85.0 %all-to-all-start.16 = ((bf16[8,19,8,1280]{3,2,1,0:T(8,128)(2,1)}), bf16[8,19,8,1280]{3,2,1,0:T(8,128)(2,1)S(1)}, u32[]{:S(2)}, u32[]{:S(2)}) async-start(bf16[8,19,8,1280]{3,2,1,0:T(8,128)(2,1)} %rows_to_degrees.7), calls=%async_computation.16 | async-start | bytes 6225920 | tf_op jit(solution)/shard_map/all_to_all | solution.py:840
  1577.0 53.6 %collective-permute-start.6 = (bf16[48,1282]{1,0:T(8,128)(2,1)}, bf16[48,1282]{1,0:T(8,128)(2,1)S(1)}, u32[]{:S(2)}, u32[]{:S(2)}) collective-permute-start(bf16[48,1282]{1,0:T(8,128)(2,1)} %get-tuple-element.271), channel_id=1, source_target_pairs={{0,8},{4,12},{8,0},{12,4},{16,24},{20,28},{24,16},{28,20},{1,9},{5... | collective-permute-start | bytes 369224 | tf_op jit(solution)/shard_map/ppermute | solution.py:922
  1578.9 76.3 %collective-permute-start.7 = (bf16[48,1282]{1,0:T(8,128)(2,1)}, bf16[48,1282]{1,0:T(8,128)(2,1)}, u32[]{:S(2)}, u32[]{:S(2)}) collective-permute-start(bf16[48,1282]{1,0:T(8,128)(2,1)} %get-tuple-element.273), channel_id=1, source_target_pairs={{0,16},{4,20},{8,24},{12,28},{16,0},{20,4},{24,8},{28,12},{1,17},{... | collective-permute-start | bytes 369224 | tf_op jit(solution)/shard_map/ppermute | solution.py:922
  1581.3 73.9 %collective-permute-start.8 = (bf16[48,1282]{1,0:T(8,128)(2,1)}, bf16[48,1282]{1,0:T(8,128)(2,1)}, u32[]{:S(2)}, u32[]{:S(2)}) collective-permute-start(bf16[48,1282]{1,0:T(8,128)(2,1)} %get-tuple-element.272), channel_id=1, source_target_pairs={{0,24},{4,28},{8,16},{12,20},{16,8},{20,12},{24,0},{28,4},{1,25},{... | collective-permute-start | bytes 369224 | tf_op jit(solution)/shard_map/ppermute | solution.py:922
  1658.1 75.8 %all-to-all-start.17 = ((bf16[8,19,8,1280]{3,2,1,0:T(8,128)(2,1)}), bf16[8,19,8,1280]{3,2,1,0:T(8,128)(2,1)}, u32[]{:S(2)}, u32[]{:S(2)}) async-start(bf16[8,19,8,1280]{3,2,1,0:T(8,128)(2,1)} %get-tuple-element.212), calls=%async_computation.17 | async-start | bytes 6225920 | tf_op jit(solution)/shard_map/all_to_all | solution.py:840
  1733.8 74.4 %all-to-all-start.18 = ((bf16[8,19,8,1280]{3,2,1,0:T(8,128)(2,1)}), bf16[8,19,8,1280]{3,2,1,0:T(8,128)(2,1)}, u32[]{:S(2)}, u32[]{:S(2)}) async-start(bf16[8,19,8,1280]{3,2,1,0:T(8,128)(2,1)} %get-tuple-element.224), calls=%async_computation.18 | async-start | bytes 6225920 | tf_op jit(solution)/shard_map/all_to_all | solution.py:840
  1808.2 85.0 %all-to-all-start.19 = ((bf16[8,19,8,1280]{3,2,1,0:T(8,128)(2,1)}), bf16[8,19,8,1280]{3,2,1,0:T(8,128)(2,1)S(1)}, u32[]{:S(2)}, u32[]{:S(2)}) async-start(bf16[8,19,8,1280]{3,2,1,0:T(8,128)(2,1)} %get-tuple-element.225), calls=%async_computation.19 | async-start | bytes 6225920 | tf_op jit(solution)/shard_map/all_to_all | solution.py:840
  1811.9 55.4 %collective-permute-start.10 = (bf16[48,1282]{1,0:T(8,128)(2,1)S(1)}, bf16[48,1282]{1,0:T(8,128)(2,1)S(1)}, u32[]{:S(2)}, u32[]{:S(2)}) collective-permute-start(bf16[48,1282]{1,0:T(8,128)(2,1)S(1)} %fusion.11), channel_id=1, source_target_pairs={{0,8},{4,12},{8,0},{12,4},{16,24},{20,28},{24,16},{28,20},{1,9},{5... | collective-permute-start | bytes 369224 | tf_op jit(solution)/shard_map/ppermute | solution.py:931
  1813.9 78.1 %collective-permute-start.11 = (bf16[48,1282]{1,0:T(8,128)(2,1)S(1)}, bf16[48,1282]{1,0:T(8,128)(2,1)S(1)}, u32[]{:S(2)}, u32[]{:S(2)}) collective-permute-start(bf16[48,1282]{1,0:T(8,128)(2,1)S(1)} %fusion.11), channel_id=1, source_target_pairs={{0,16},{4,20},{8,24},{12,28},{16,0},{20,4},{24,8},{28,12},{1,17},{... | collective-permute-start | bytes 369224 | tf_op jit(solution)/shard_map/ppermute | solution.py:931
  1816.2 76.4 %collective-permute-start.12 = (bf16[48,1282]{1,0:T(8,128)(2,1)S(1)}, bf16[48,1282]{1,0:T(8,128)(2,1)S(1)}, u32[]{:S(2)}, u32[]{:S(2)}) collective-permute-start(bf16[48,1282]{1,0:T(8,128)(2,1)S(1)} %fusion.11), channel_id=1, source_target_pairs={{0,24},{4,28},{8,16},{12,20},{16,8},{20,12},{24,0},{28,4},{1,25},{... | collective-permute-start | bytes 369224 | tf_op jit(solution)/shard_map/ppermute | solution.py:931
  1893.3 7.8 copy-start.5
  1893.3 75.0 %all-to-all-start.20 = ((bf16[8,19,8,1280]{3,2,1,0:T(8,128)(2,1)}), bf16[8,19,8,1280]{3,2,1,0:T(8,128)(2,1)}, u32[]{:S(2)}, u32[]{:S(2)}) async-start(bf16[8,19,8,1280]{3,2,1,0:T(8,128)(2,1)} %get-tuple-element.229), calls=%async_computation.20 | async-start | bytes 6225920 | tf_op jit(solution)/shard_map/all_to_all | solution.py:840
  1904.9 6.9 copy-start.4
  1911.8 9.5 collective-permute-start.9
  1968.3 79.9 %all-to-all-start.21 = ((bf16[8,19,8,1280]{3,2,1,0:T(8,128)(2,1)}), bf16[8,19,8,1280]{3,2,1,0:T(8,128)(2,1)}, u32[]{:S(2)}, u32[]{:S(2)}) async-start(bf16[8,19,8,1280]{3,2,1,0:T(8,128)(2,1)} %degrees_to_rows.6), calls=%async_computation.21 | async-start | bytes 6225920 | tf_op jit(solution)/shard_map/all_to_all | solution.py:840
  1976.8 71.3 %collective-permute-start.16 = (bf16[6,8,24,1408]{3,2,1,0:T(8,128)(2,1)}, bf16[6,8,24,1408]{3,2,1,0:T(8,128)(2,1)}, u32[]{:S(2)}, u32[]{:S(2)}) collective-permute-start(bf16[6,8,24,1408]{3,2,1,0:T(8,128)(2,1)} %constant_dynamic-slice_fusion), channel_id=1, source_target_pairs={{0,2},{1,3},{2,0},{3,1},{4,6},{5,7},{6,4},{7,5},{8,10},{9,11},{10,... | collective-permute-start | bytes 9732104 | tf_op jit(solution)/shard_map/ppermute | solution.py:875
  2048.1 189.5 %all-to-all-start.22 = ((bf16[8,52,8,1280]{3,2,1,0:T(8,128)(2,1)}), bf16[8,52,8,1280]{3,2,1,0:T(8,128)(2,1)}, u32[]{:S(2)}, u32[]{:S(2)}) async-start(bf16[8,52,8,1280]{3,2,1,0:T(8,128)(2,1)} %get-tuple-element.246), calls=%async_computation.22 | async-start | bytes 17039360 | tf_op jit(solution)/shard_map/all_to_all | solution.py:840
  2057.7 107.5 %collective-permute-start.13 = (bf16[6,8,24,1408]{3,2,1,0:T(8,128)(2,1)}, bf16[6,8,24,1408]{3,2,1,0:T(8,128)(2,1)}, u32[]{:S(2)}, u32[]{:S(2)}) collective-permute-start(bf16[6,8,24,1408]{3,2,1,0:T(8,128)(2,1)} %constant_dynamic-slice_fusion.1), channel_id=1, source_target_pairs={{0,3},{1,2},{2,1},{3,0},{4,7},{5,6},{6,5},{7,4},{8,11},{9,10},{10,... | collective-permute-start | bytes 9732104 | tf_op jit(solution)/shard_map/ppermute | solution.py:875
  2057.7 76.6 %collective-permute-start.14 = (bf16[192,1282]{1,0:T(8,128)(2,1)}, bf16[192,1282]{1,0:T(8,128)(2,1)S(1)}, u32[]{:S(2)}, u32[]{:S(2)}) collective-permute-start(bf16[192,1282]{1,0:T(8,128)(2,1)} %bitcast.50), channel_id=1, source_target_pairs={{0,4},{4,0},{8,12},{12,8},{16,20},{20,16},{24,28},{28,24},{1,5},{5... | collective-permute-start | bytes 1476872 | tf_op jit(solution)/shard_map/ppermute | solution.py:907
  2136.7 22.6 collective-permute-start.15
  2237.7 74.2 %all-to-all-start.23 = ((bf16[8,19,8,1280]{3,2,1,0:T(8,128)(2,1)}), bf16[8,19,8,1280]{3,2,1,0:T(8,128)(2,1)}, u32[]{:S(2)}, u32[]{:S(2)}) async-start(bf16[8,19,8,1280]{3,2,1,0:T(8,128)(2,1)} %get-tuple-element.247), calls=%async_computation.23 | async-start | bytes 6225920 | tf_op jit(solution)/shard_map/all_to_all | solution.py:840
  2242.4 12.5 copy-start.9
  2246.5 4.3 collective-permute-start.17
  2311.9 14.3 copy-start.21
  2311.9 14.3 copy-start.22
  2327.6 1.2 collective-permute-start.18
  2328.9 3.6 collective-permute-start.19
  2332.5 3.6 collective-permute-start.20
  2336.1 3.6 collective-permute-start.21
  2339.8 4.5 collective-permute-start.22
  (19 other events, 58.1 us)

commit v7 on v6

--- a/solution.py
+++ b/solution.py
@@ -868,10 +868,14 @@
     return [(k, (k + step) % count) for k in range(count)], lambda rank: (rank + step) % count
 
 
-def share_slots(members, n_chan, step):
+def share_slots(members, n_chan, step, half):
     share = members.shape[0] // n_chan
     route, find = partners(n_chan, step)
-    block = lax.dynamic_slice_in_dim(members, find(lax.axis_index("chan")) * share, share)
+    begin = find(lax.axis_index("chan")) * share
+    if half is not None:
+        share //= 2
+        begin = begin + half * share
+    block = lax.dynamic_slice_in_dim(members, begin, share)
     return lax.ppermute(block, "chan", route) if step else block
 
 
@@ -1046,10 +1050,14 @@
             )
             mixed.append(line.keep(made))
 
-        def share_next(count=1):
+        def share_next(wanted, keep):
             members = joined_rows([made[2] for made in mixed])
-            for step in range(len(shared), min(len(shared) + count, n_chan)):
-                shared.append(line.keep_later(share_slots(line.hold(members), n_chan, step)))
+            for step, half in wanted:
+                block = share_slots(line.hold(members), n_chan, step, half)
+                shared.append(((step, half), keep(block)))
+
+        final = n_chan - 1
+        whole_share = 2 * pair_dev // n_chan % 2 or final < 2
 
         arrived.append(line.swap(fine_made[0]))
         coarse_made = lane_call(
@@ -1068,15 +1076,22 @@
             fine_back.append(line.swap(mixed[k][0]))
             mix_chunk(k + 1)
         arrived_coarse = line.swap(mixed[-1][1])
-        share_next(2)
+        share_next([(k, None) for k in range(min(2, n_chan))], line.keep_later)
+        if not whole_share:
+            share_next([(final, 0)], line.keep)
         fine_back.append(line.swap(mixed[-1][0]))
-        share_next()
+        share_next([(k, None) for k in range(2, final)], line.keep_later)
         coarse_made = lane_call(
             coarse_work, "degrees_to_rows", [line.hold(arrived_coarse)], [out_tables[0]],
             [coarse_two], subs, C - MAIN,
         )[0]
         coarse_end = line.swap(line.keep(coarse_made))
-        share_next(n_chan)
+        if final >= 2:
+            share_next([(final, None if whole_share else 1)], line.keep_later)
+        shared = [
+            joined_rows([block for (place, half), block in shared if place == step])
+            for step in range(n_chan)
+        ]
         fine_made = lane_call(
             fine_back_work, "degrees_to_rows", line.hold(fine_back), out_tables[1],
             cuts, subs, C - MAIN,

time: 2360 us -> 2370 us (level)
  blocking collectives: 74 us -> 0 us
  waiting for transfers between devices: 1130 us -> 1200 us
    all_to_all x1 -> x0, blocking collectives: 74 us -> none  [swap(): lax.all_to_all(values, 'lat', split_axis=0, concat_axis=0, tiled=True)]
    ppermute x6 -> x8, waiting for transfers between devices: 106 us -> 168 us  [share_slots(): return lax.ppermute(block, 'chan', route) if step else block]
    all_to_all x23 -> x24, waiting for transfers between devices: 683 us -> 700 us  [swap(): lax.all_to_all(values, 'lat', split_axis=0, concat_axis=0, tiled=True)]
    all_to_all x23 -> x24, starting transfers between devices: 111 us -> 118 us  [swap(): lax.all_to_all(values, 'lat', split_axis=0, concat_axis=0, tiled=True)]
    unnamed x81 -> x89, local copies, waits for them, and re-layouts: 61.8 us -> 66.8 us
  transfers between devices with their start and end apart: 46 -> 49, of which waited for: 35 -> 37; matrix products, arithmetic and copies ran while one was open for 13% -> 13% of each run, Pallas kernels for 28% -> 28%
where the time goes in v7:
time: 2370 us; the launch traced here: 2360 us
  waiting for transfers between devices  1200 us (51%)
  Pallas kernels  692 us (29%)
  local copies, waits for them, and re-layouts  220 us (9%)
  starting transfers between devices  138 us (6%)
  other arithmetic  110 us (5%)
    all_to_all x24, waiting for transfers between devices, swap(): lax.all_to_all(values, 'lat', split_axis=0, concat_axis=0, tiled=True)  700 us
    pallas_call x3, Pallas kernels, pixels(): call(body, 'feed_forward', 2 * count * points * (6 * C * hidden + 2 * tab...  323 us
    ppermute x8, waiting for transfers between devices, share_slots(): return lax.ppermute(block, 'chan', route) if step else block  168 us
    all_to_all x24, starting transfers between devices, swap(): lax.all_to_all(values, 'lat', split_axis=0, concat_axis=0, tiled=True)  118 us
    pallas_call x8, Pallas kernels, lane_call(): call(functools.partial(lane_body, work, subs, width, len(inputs), len(tab...  106 us
    ppermute x3, waiting for transfers between devices, double(): other = lax.ppermute(line.hold(held), axis, partners(sizes[axis], step)[0])  101 us
    ppermute x3, waiting for transfers between devices, halve(): lax.ppermute(jnp.where(upper, low, high), axis, partners(sizes[axis], ste...  82.1 us
    pallas_call x4, Pallas kernels, mix(): call(body, 'mix_back' if backward else 'mix', 2 * count * n_lat * subs *...  81.2 us
  transfers between devices with their start and end apart: 49, of which 37 were waited for; matrix products, arithmetic and copies ran while one was open for 13% of the time, Pallas kernels for 28%

profile of v7, /device:TPU:0, one launch (start us, length us, event | category | flops | bytes accessed | tf_op | source)
XLA Modules:
  0.0 2358.1 jit_solution(4912792228541683180)
XLA Ops:
  6.8 10.0 norm_and_dft.3
  24.1 24.3 %norm_and_dft.4 = bf16[8,52,8,1280]{3,2,1,0:T(8,128)(2,1)} custom-call(f32[23,641,1,360]{3,2,1,0:T(1,128)} %bitcast.109, s32[23,8,360]{2,1,0:T(8,128)} %bitcast.154, f32[641,1]{1,0:T(8,128)} %broadcast_in_dim.222.gain.refs_5_, f32[641,1]{1,0:T(8,128)} %broadcast_in_dim.223.bias, bf16[384,360]{1,0:T(8,128)(2,1)} %pad_maximum_fusion.6.table.refs_4_), custom_call_target="tpu_custom_call" | custom-call | flops 3609722880 | bytes 24883104 | tf_op jit(solution)/shard_map/norm_and_dft/pallas_call | solution.py:162
  48.4 45.8 %all-to-all-done.refs_0_.refs_2_ = bf16[8,19,8,1280]{3,2,1,0:T(8,128)(2,1)} async-done(((bf16[8,19,8,1280]{3,2,1,0:T(8,128)(2,1)}), bf16[8,19,8,1280]{3,2,1,0:T(8,128)(2,1)}, u32[]{:S(2)}, u32[]{:S(2)}) %all-to-all-start) | async-done | bytes 3112992 | tf_op jit(solution)/shard_map/all_to_all | solution.py:840
  99.2 20.7 reduce
  127.0 7.5 copy.189
  134.5 8.2 broadcast_in_dim.209.state
  146.6 10.0 norm_and_dft.5
  156.6 127.6 %all-to-all-done.1.refs_1_.refs_3_ = bf16[8,52,8,1280]{3,2,1,0:T(8,128)(2,1)} async-done(((bf16[8,52,8,1280]{3,2,1,0:T(8,128)(2,1)}), bf16[8,52,8,1280]{3,2,1,0:T(8,128)(2,1)}, u32[]{:S(2)}, u32[]{:S(2)}) %all-to-all-start.1) | async-done | bytes 8519712 | tf_op jit(solution)/shard_map/all_to_all | solution.py:840
  293.5 13.2 legendre_tables.3
  321.4 17.0 rows_to_degrees.4
  338.3 20.3 all-to-all-done.2.refs_0_.refs_1_
  374.3 9.5 rows_to_degrees.5
  383.8 48.8 %all-to-all-done.3.fine.fine_tail = bf16[8,19,8,1280]{3,2,1,0:T(8,128)(2,1)} async-done(((bf16[8,19,8,1280]{3,2,1,0:T(8,128)(2,1)}), bf16[8,19,8,1280]{3,2,1,0:T(8,128)(2,1)}, u32[]{:S(2)}, u32[]{:S(2)}) %all-to-all-start.3) | async-done | bytes 3112992 | tf_op jit(solution)/shard_map/all_to_all | solution.py:840
  437.9 13.2 legendre_tables.5
  462.0 44.8 %all-to-all-done.4.coarse.coarse_tail.refs_3_.refs_4_ = bf16[8,19,8,1280]{3,2,1,0:T(8,128)(2,1)} async-done(((bf16[8,19,8,1280]{3,2,1,0:T(8,128)(2,1)}), bf16[8,19,8,1280]{3,2,1,0:T(8,128)(2,1)}, u32[]{:S(2)}, u32[]{:S(2)}) %all-to-all-start.4) | async-done | bytes 3112992 | tf_op jit(solution)/shard_map/all_to_all | solution.py:840
  511.9 31.7 %copy.242 = bf16[24,2,649,641]{2,3,1,0:T(8,128)(2,1)} copy(bf16[24,2,649,641]{2,1,3,0:T(2,128)(2,1)} %param.27) | data formatting | bytes 79873728 | tf_op args[9]
  544.3 20.3 mix.2
  564.6 16.2 all-to-all-done.5.refs_1_.refs_2_
  585.5 20.3 mix.3
  605.8 49.1 %all-to-all-done.6.refs_0_.refs_2_ = bf16[8,19,8,1280]{3,2,1,0:T(8,128)(2,1)} async-done(((bf16[8,19,8,1280]{3,2,1,0:T(8,128)(2,1)}), bf16[8,19,8,1280]{3,2,1,0:T(8,128)(2,1)}, u32[]{:S(2)}, u32[]{:S(2)}) %all-to-all-start.6) | async-done | bytes 3112992 | tf_op jit(solution)/shard_map/all_to_all | solution.py:840
  671.7 37.0 %collective-permute-done.1 = bf16[3,8,24,1408]{3,2,1,0:T(8,128)(2,1)} collective-permute-done((bf16[3,8,24,1408]{3,2,1,0:T(8,128)(2,1)S(1)}, bf16[3,8,24,1408]{3,2,1,0:T(8,128)(2,1)}, u32[]{:S(2)}, u32[]{:S(2)}) %collective-permute-start.1) | collective-permute-done | bytes 1622048 | tf_op jit(solution)/shard_map/ppermute | solution.py:879
  708.7 20.1 all-to-all-done.7.refs_0_.refs_1_
  739.4 9.5 degrees_to_rows.4
  748.9 53.8 %all-to-all-done.8.refs_1_.refs_3_ = bf16[8,19,8,1280]{3,2,1,0:T(8,128)(2,1)} async-done(((bf16[8,19,8,1280]{3,2,1,0:T(8,128)(2,1)}), bf16[8,19,8,1280]{3,2,1,0:T(8,128)(2,1)}, u32[]{:S(2)}, u32[]{:S(2)}) %all-to-all-start.8) | async-done | bytes 3112992 | tf_op jit(solution)/shard_map/all_to_all | solution.py:840
  814.1 17.0 degrees_to_rows.5
  831.1 51.4 %collective-permute-done.3.refs_2_ = bf16[6,8,24,1408]{3,2,1,0:T(8,128)(2,1)} collective-permute-done((bf16[6,8,24,1408]{3,2,1,0:T(8,128)(2,1)}, bf16[6,8,24,1408]{3,2,1,0:T(8,128)(2,1)}, u32[]{:S(2)}, u32[]{:S(2)}) %collective-permute-start.3) | collective-permute-done | bytes 3244064 | tf_op jit(solution)/shard_map/ppermute | solution.py:879
  898.4 20.7 reduce.1
  926.2 7.5 copy.197
  933.8 8.2 broadcast_in_dim.210.cotangent
  945.4 71.1 %feed_forward.3 = (f32[6,641,1,360]{3,2,1,0:T(1,128)}, f32[6,641,360]{2,1,0:T(8,128)}, bf16[8,19,8,1280]{3,2,1,0:T(8,128)(2,1)}, f32[2,768,1282]{2,1,0:T(8,128)}...) custom-call(bf16[8,19,8,1280]{3,2,1,0:T(8,128)(2,1)} %all-to-all-done.9.synth.tail, ...), custom_call_target="tpu_custom_call" | custom-call | flops 23848110080 | bytes 28641024 | tf_op jit(solution)/shard_map/feed_forward/pallas_call | solution.py:674
  1025.4 130.8 %feed_forward.4 = (f32[23,641,1,360]{3,2,1,0:T(1,128)}, f32[23,641,360]{2,1,0:T(8,128)}, bf16[8,37,8,1280]{3,2,1,0:T(8,128)(2,1)}, f32[2,768,1282]{2,1,0:T(8,128...) custom-call(bf16[8,37,8,1280]{3,2,1,0:T(8,128)(2,1)} %all-to-all-done.10.synth.tail, ...), custom_call_target="tpu_custom_call" | custom-call | flops 47696220160 | bytes 57282048 | tf_op jit(solution)/shard_map/feed_forward/pallas_call | solution.py:674
  1162.4 120.8 %feed_forward.5 = (f32[23,641,1,360]{3,2,1,0:T(1,128)}, f32[23,641,360]{2,1,0:T(8,128)}, bf16[8,34,8,1280]{3,2,1,0:T(8,128)(2,1)}, f32[2,768,1282]{2,1,0:T(8,128...) custom-call(bf16[8,34,8,1280]{3,2,1,0:T(8,128)(2,1)} %all-to-all-done.11.refs_0_.refs_, ...), custom_call_target="tpu_custom_call", output_to_operand_aliasing={{0}: (13, {}), {1}: (14, {})} | custom-call | flops 43721535488 | bytes 52508544 | tf_op jit(solution)/shard_map/feed_forward/pallas_call | solution.py:674
  1283.3 12.9 all-to-all-done.12.refs_0_.refs_2_
  1301.3 12.8 add_add_fusion
  1352.1 44.8 %collective-permute-done.5 = f32[384,1282]{0,1:T(8,128)S(1)} collective-permute-done((f32[384,1282]{0,1:T(8,128)}, f32[384,1282]{0,1:T(8,128)S(1)}, u32[]{:S(2)}, u32[]{:S(2)}) %collective-permute-start.5) | collective-permute-done | bytes 1969184 | tf_op jit(solution)/shard_map/ppermute | solution.py:906
  1402.2 21.5 all-to-all-done.13.refs_1_.refs_3_
  1431.1 8.2 part_rows.2
  1439.3 17.0 rows_to_degrees.6
  1456.3 30.1 %collective-permute-done.6 = f32[192,1282]{1,0:T(8,128)S(1)} collective-permute-done((f32[192,1282]{1,0:T(8,128)}, f32[192,1282]{1,0:T(8,128)S(1)}, u32[]{:S(2)}, u32[]{:S(2)}) %collective-permute-start.6) | collective-permute-done | bytes 984608 | tf_op jit(solution)/shard_map/ppermute | solution.py:906
  1489.1 8.5 all-to-all-done.14.refs_0_.refs_1_
  1502.0 9.5 rows_to_degrees.7
  1511.5 60.0 %all-to-all-done.15.fine.fine_tail = bf16[8,19,8,1280]{3,2,1,0:T(8,128)(2,1)} async-done(((bf16[8,19,8,1280]{3,2,1,0:T(8,128)(2,1)}), bf16[8,19,8,1280]{3,2,1,0:T(8,128)(2,1)}, u32[]{:S(2)}, u32[]{:S(2)}) %all-to-all-start.15) | async-done | bytes 3112992 | tf_op jit(solution)/shard_map/all_to_all | solution.py:840
  1584.5 46.2 %collective-permute-done.7 = bf16[48,1282]{1,0:T(8,128)(2,1)S(1)} collective-permute-done((bf16[48,1282]{1,0:T(8,128)(2,1)}, bf16[48,1282]{1,0:T(8,128)(2,1)S(1)}, u32[]{:S(2)}, u32[]{:S(2)}) %collective-permute-start.7) | collective-permute-done | bytes 123104 | tf_op jit(solution)/shard_map/ppermute | solution.py:926
  1630.7 24.7 %collective-permute-done.8 = bf16[48,1282]{1,0:T(8,128)(2,1)} collective-permute-done((bf16[48,1282]{1,0:T(8,128)(2,1)}, bf16[48,1282]{1,0:T(8,128)(2,1)}, u32[]{:S(2)}, u32[]{:S(2)}) %collective-permute-start.8) | collective-permute-done | bytes 123104 | tf_op jit(solution)/shard_map/ppermute | solution.py:926
  1662.9 20.3 mix_back.2
  1683.2 50.8 %all-to-all-done.17.refs_1_.refs_2_ = bf16[8,19,8,1280]{3,2,1,0:T(8,128)(2,1)} async-done(((bf16[8,19,8,1280]{3,2,1,0:T(8,128)(2,1)}), bf16[8,19,8,1280]{3,2,1,0:T(8,128)(2,1)}, u32[]{:S(2)}, u32[]{:S(2)}) %all-to-all-start.17) | async-done | bytes 3112992 | tf_op jit(solution)/shard_map/all_to_all | solution.py:840
  1738.4 20.3 mix_back.3
  1758.7 49.7 %all-to-all-done.18.refs_0_.refs_2_ = bf16[8,19,8,1280]{3,2,1,0:T(8,128)(2,1)} async-done(((bf16[8,19,8,1280]{3,2,1,0:T(8,128)(2,1)}), bf16[8,19,8,1280]{3,2,1,0:T(8,128)(2,1)}, u32[]{:S(2)}, u32[]{:S(2)}) %all-to-all-start.18) | async-done | bytes 3112992 | tf_op jit(solution)/shard_map/all_to_all | solution.py:840
  1828.9 38.5 %collective-permute-done.11 = bf16[48,1282]{1,0:T(8,128)(2,1)S(1)} collective-permute-done((bf16[48,1282]{1,0:T(8,128)(2,1)S(1)}, bf16[48,1282]{1,0:T(8,128)(2,1)S(1)}, u32[]{:S(2)}, u32[]{:S(2)}) %collective-permute-start.11) | collective-permute-done | bytes 123104 | tf_op jit(solution)/shard_map/ppermute | solution.py:935
  1867.4 24.7 %collective-permute-done.12 = bf16[48,1282]{1,0:T(8,128)(2,1)S(1)} collective-permute-done((bf16[48,1282]{1,0:T(8,128)(2,1)S(1)}, bf16[48,1282]{1,0:T(8,128)(2,1)S(1)}, u32[]{:S(2)}, u32[]{:S(2)}) %collective-permute-start.12) | collective-permute-done | bytes 123104 | tf_op jit(solution)/shard_map/ppermute | solution.py:935
  1903.6 9.5 degrees_to_rows.6
  1913.1 55.5 %all-to-all-done.20.refs_1_.refs_3_ = bf16[8,19,8,1280]{3,2,1,0:T(8,128)(2,1)} async-done(((bf16[8,19,8,1280]{3,2,1,0:T(8,128)(2,1)}), bf16[8,19,8,1280]{3,2,1,0:T(8,128)(2,1)}, u32[]{:S(2)}, u32[]{:S(2)}) %all-to-all-start.20) | async-done | bytes 3112992 | tf_op jit(solution)/shard_map/all_to_all | solution.py:840
  1977.2 17.0 degrees_to_rows.7
  1994.1 54.9 %collective-permute-done.18.refs_6_ = bf16[6,8,24,1408]{3,2,1,0:T(8,128)(2,1)} collective-permute-done((bf16[6,8,24,1408]{3,2,1,0:T(8,128)(2,1)}, bf16[6,8,24,1408]{3,2,1,0:T(8,128)(2,1)}, u32[]{:S(2)}, u32[]{:S(2)}) %collective-permute-start.18) | collective-permute-done | bytes 3244064 | tf_op jit(solution)/shard_map/ppermute | solution.py:879
  2056.9 78.7 %collective-permute-done.16 = bf16[192,1282]{1,0:T(8,128)(2,1)S(1)} collective-permute-done((bf16[192,1282]{1,0:T(8,128)(2,1)S(1)}, bf16[192,1282]{1,0:T(8,128)(2,1)S(1)}, u32[]{:S(2)}, u32[]{:S(2)}) %collective-permute-start.16) | collective-permute-done | bytes 492320 | tf_op jit(solution)/shard_map/ppermute | solution.py:911
  2143.5 18.3 collective-permute-done.17
  2167.7 24.6 %collective-permute-done.15 = bf16[3,8,24,1408]{3,2,1,0:T(8,128)(2,1)} collective-permute-done((bf16[3,8,24,1408]{3,2,1,0:T(8,128)(2,1)}, bf16[3,8,24,1408]{3,2,1,0:T(8,128)(2,1)}, u32[]{:S(2)}, u32[]{:S(2)}) %collective-permute-start.15) | collective-permute-done | bytes 1622048 | tf_op jit(solution)/shard_map/ppermute | solution.py:879
  2196.2 14.2 first_norm_back.3
  2210.4 8.2 part_rows.3
  2218.7 27.4 %mix_gradient.1 = f32[6,641,2,649]{3,2,1,0:T(2,128)} custom-call(bf16[6,8,24,1408]{3,2,1,0:T(8,128)(2,1)} %get-tuple-element.260.refs_0_, bf16[6,8,24,1408]{3,2,1,0:T(8,128)(2,1)} %collective-permute-done.refs_1_, bf16[6,8,24,1408]{3,2,1,0:T(8,128)(2,1)} %collective-permute-done.3.refs_2_, bf16[6,8,24,1408]{3,2,1,0:T(8,128)(2,1)} %pad_maximum_fusion.1.refs_3_, ...), custom_call_target="tpu_custom_call" | custom-call | flops 15335755776 | bytes 45920688 | tf_op jit(solution)/shard_map/mix_gradient/pallas_call | solution.py:585
  2246.1 7.4 all-to-all-start.23
  2278.0 34.6 %first_norm_back.4 = (f32[23,641,1,360]{3,2,1,0:T(1,128)}, f32[2,641,1]{2,1,0:T(8,128)}) custom-call(bf16[8,52,8,1280]{3,2,1,0:T(8,128)(2,1)} %all-to-all-done.22.wave.tail, bf16[8,52,8,1280]{3,2,1,0:T(8,128)(2,1)} %all-to-all-done.22.wave.tail, f32[23,641,1,360]{3,2,1,0:T(1,128)} %bitcast.112, f32[23,641,360]{2,1,0:T(8,128)} %get-tuple-element.188.middle_grad.refs_3_, ...), custom_call_target="tpu_custom_call" | custom-call | flops 3609722880 | bytes 56266464 | tf_op jit(solution)/shard_map/first_norm_back/pallas_call | solution.py:743
  2312.6 12.0 all-to-all-done.23.refs_0_.refs_1_
  2324.6 14.4 first_norm_back.5
  (315 shorter events, 372.8 us)
Async XLA Ops:
  16.8 77.4 %all-to-all-start = ((bf16[8,19,8,1280]{3,2,1,0:T(8,128)(2,1)}), bf16[8,19,8,1280]{3,2,1,0:T(8,128)(2,1)}, u32[]{:S(2)}, u32[]{:S(2)}) async-start(bf16[8,19,8,1280]{3,2,1,0:T(8,128)(2,1)} %norm_and_dft.3), calls=%async_computation | async-start | bytes 6225920 | tf_op jit(solution)/shard_map/all_to_all | solution.py:840
  94.2 190.0 %all-to-all-start.1 = ((bf16[8,52,8,1280]{3,2,1,0:T(8,128)(2,1)}), bf16[8,52,8,1280]{3,2,1,0:T(8,128)(2,1)}, u32[]{:S(2)}, u32[]{:S(2)}) async-start(bf16[8,52,8,1280]{3,2,1,0:T(8,128)(2,1)} %norm_and_dft.4), calls=%async_computation.1 | async-start | bytes 17039360 | tf_op jit(solution)/shard_map/all_to_all | solution.py:840
  134.5 8.2 copy-start.33
  156.6 132.5 %copy-start.39 = (s32[184]{0:T(256)S(1)}, s32[184]{0:T(256)}, u32[]{:S(2)}) copy-start(s32[184]{0:T(256)} %param.23) | copy-start | bytes 2212
  284.2 74.4 %all-to-all-start.2 = ((bf16[8,19,8,1280]{3,2,1,0:T(8,128)(2,1)}), bf16[8,19,8,1280]{3,2,1,0:T(8,128)(2,1)}, u32[]{:S(2)}, u32[]{:S(2)}) async-start(bf16[8,19,8,1280]{3,2,1,0:T(8,128)(2,1)} %norm_and_dft.5), calls=%async_computation.2 | async-start | bytes 6225920 | tf_op jit(solution)/shard_map/all_to_all | solution.py:840
  358.6 74.1 %all-to-all-start.3 = ((bf16[8,19,8,1280]{3,2,1,0:T(8,128)(2,1)}), bf16[8,19,8,1280]{3,2,1,0:T(8,128)(2,1)}, u32[]{:S(2)}, u32[]{:S(2)}) async-start(bf16[8,19,8,1280]{3,2,1,0:T(8,128)(2,1)} %get-tuple-element.147), calls=%async_computation.3 | async-start | bytes 6225920 | tf_op jit(solution)/shard_map/all_to_all | solution.py:840
  432.6 74.1 %all-to-all-start.4 = ((bf16[8,19,8,1280]{3,2,1,0:T(8,128)(2,1)}), bf16[8,19,8,1280]{3,2,1,0:T(8,128)(2,1)}, u32[]{:S(2)}, u32[]{:S(2)}) async-start(bf16[8,19,8,1280]{3,2,1,0:T(8,128)(2,1)} %rows_to_degrees.5), calls=%async_computation.4 | async-start | bytes 6225920 | tf_op jit(solution)/shard_map/all_to_all | solution.py:840
  462.0 44.8 %copy-start.11 = (bf16[12,192,184]{2,1,0:T(8,128)(2,1)}, bf16[12,192,184]{2,1,0:T(8,128)(2,1)S(1)}, u32[]{:S(2)}) copy-start(bf16[12,192,184]{2,1,0:T(8,128)(2,1)S(1)} %constant_dynamic-update-slice_fusion.refs_4_) | copy-start | bytes 2543620
  506.8 74.1 %all-to-all-start.5 = ((bf16[8,19,8,1280]{3,2,1,0:T(8,128)(2,1)}), bf16[8,19,8,1280]{3,2,1,0:T(8,128)(2,1)}, u32[]{:S(2)}, u32[]{:S(2)}) async-start(bf16[8,19,8,1280]{3,2,1,0:T(8,128)(2,1)} %get-tuple-element.149), calls=%async_computation.5 | async-start | bytes 6225920 | tf_op jit(solution)/shard_map/all_to_all | solution.py:840
  580.8 74.1 %all-to-all-start.6 = ((bf16[8,19,8,1280]{3,2,1,0:T(8,128)(2,1)}), bf16[8,19,8,1280]{3,2,1,0:T(8,128)(2,1)}, u32[]{:S(2)}, u32[]{:S(2)}) async-start(bf16[8,19,8,1280]{3,2,1,0:T(8,128)(2,1)} %get-tuple-element.161), calls=%async_computation.6 | async-start | bytes 6225920 | tf_op jit(solution)/shard_map/all_to_all | solution.py:840
  655.0 73.8 %all-to-all-start.7 = ((bf16[8,19,8,1280]{3,2,1,0:T(8,128)(2,1)}), bf16[8,19,8,1280]{3,2,1,0:T(8,128)(2,1)S(1)}, u32[]{:S(2)}, u32[]{:S(2)}) async-start(bf16[8,19,8,1280]{3,2,1,0:T(8,128)(2,1)} %get-tuple-element.162), calls=%async_computation.7 | async-start | bytes 6225920 | tf_op jit(solution)/shard_map/all_to_all | solution.py:840
  670.8 37.8 %collective-permute-start.1 = (bf16[3,8,24,1408]{3,2,1,0:T(8,128)(2,1)S(1)}, bf16[3,8,24,1408]{3,2,1,0:T(8,128)(2,1)}, u32[]{:S(2)}, u32[]{:S(2)}) collective-permute-start(bf16[3,8,24,1408]{3,2,1,0:T(8,128)(2,1)S(1)} %constant_dynamic-slice_fusion.7), channel_id=1, source_target_pairs={{0,3},{1,2},{2,1},{3,0},{4,7},{5,6},{6,5},{7,4},{8,11},{9,10},{10,... | collective-permute-start | bytes 4866056 | tf_op jit(solution)/shard_map/ppermute | solution.py:879
  728.8 73.9 %all-to-all-start.8 = ((bf16[8,19,8,1280]{3,2,1,0:T(8,128)(2,1)}), bf16[8,19,8,1280]{3,2,1,0:T(8,128)(2,1)}, u32[]{:S(2)}, u32[]{:S(2)}) async-start(bf16[8,19,8,1280]{3,2,1,0:T(8,128)(2,1)} %get-tuple-element.165), calls=%async_computation.8 | async-start | bytes 6225920 | tf_op jit(solution)/shard_map/all_to_all | solution.py:840
  739.4 9.5 collective-permute-start
  802.7 79.7 %all-to-all-start.9 = ((bf16[8,19,8,1280]{3,2,1,0:T(8,128)(2,1)}), bf16[8,19,8,1280]{3,2,1,0:T(8,128)(2,1)}, u32[]{:S(2)}, u32[]{:S(2)}) async-start(bf16[8,19,8,1280]{3,2,1,0:T(8,128)(2,1)} %degrees_to_rows.4), calls=%async_computation.9 | async-start | bytes 6225920 | tf_op jit(solution)/shard_map/all_to_all | solution.py:840
  811.1 71.3 %collective-permute-start.3 = (bf16[6,8,24,1408]{3,2,1,0:T(8,128)(2,1)}, bf16[6,8,24,1408]{3,2,1,0:T(8,128)(2,1)}, u32[]{:S(2)}, u32[]{:S(2)}) collective-permute-start(bf16[6,8,24,1408]{3,2,1,0:T(8,128)(2,1)} %constant_dynamic-slice_fusion.5), channel_id=1, source_target_pairs={{0,2},{1,3},{2,0},{3,1},{4,6},{5,7},{6,4},{7,5},{8,10},{9,11},{10,... | collective-permute-start | bytes 9732104 | tf_op jit(solution)/shard_map/ppermute | solution.py:879
  882.5 137.1 %all-to-all-start.10 = ((bf16[8,37,8,1280]{3,2,1,0:T(8,128)(2,1)}), bf16[8,37,8,1280]{3,2,1,0:T(8,128)(2,1)}, u32[]{:S(2)}, u32[]{:S(2)}) async-start(bf16[8,37,8,1280]{3,2,1,0:T(8,128)(2,1)} %get-tuple-element.180), calls=%async_computation.10 | async-start | bytes 12124160 | tf_op jit(solution)/shard_map/all_to_all | solution.py:840
  888.3 6.4 copy-start.34
  890.9 6.6 copy-start.38
  933.8 8.2 copy-start.32
  945.4 71.1 %collective-permute-start.2 = (bf16[3,8,24,1408]{3,2,1,0:T(8,128)(2,1)}, bf16[3,8,24,1408]{3,2,1,0:T(8,128)(2,1)S(1)}, u32[]{:S(2)}, u32[]{:S(2)}) collective-permute-start(bf16[3,8,24,1408]{3,2,1,0:T(8,128)(2,1)} %constant_dynamic-slice_fusion.6), channel_id=1, source_target_pairs={{0,3},{1,2},{2,1},{3,0},{4,7},{5,6},{6,5},{7,4},{8,11},{9,10},{10,... | collective-permute-start | bytes 4866056 | tf_op jit(solution)/shard_map/ppermute | solution.py:879
  1019.6 136.6 %all-to-all-start.11 = ((bf16[8,34,8,1280]{3,2,1,0:T(8,128)(2,1)}), bf16[8,34,8,1280]{3,2,1,0:T(8,128)(2,1)}, u32[]{:S(2)}, u32[]{:S(2)}) async-start(bf16[8,34,8,1280]{3,2,1,0:T(8,128)(2,1)} %get-tuple-element.181), calls=%async_computation.11 | async-start | bytes 11141120 | tf_op jit(solution)/shard_map/all_to_all | solution.py:840
  1156.2 140.0 %all-to-all-start.12 = ((bf16[8,37,8,1280]{3,2,1,0:T(8,128)(2,1)}), bf16[8,37,8,1280]{3,2,1,0:T(8,128)(2,1)}, u32[]{:S(2)}, u32[]{:S(2)}) async-start(bf16[8,37,8,1280]{3,2,1,0:T(8,128)(2,1)} %get-tuple-element.196), calls=%async_computation.12 | async-start | bytes 12124160 | tf_op jit(solution)/shard_map/all_to_all | solution.py:840
  1296.2 127.5 %all-to-all-start.13 = ((bf16[8,34,8,1280]{3,2,1,0:T(8,128)(2,1)}), bf16[8,34,8,1280]{3,2,1,0:T(8,128)(2,1)}, u32[]{:S(2)}, u32[]{:S(2)}) async-start(bf16[8,34,8,1280]{3,2,1,0:T(8,128)(2,1)} %get-tuple-element.197), calls=%async_computation.13 | async-start | bytes 11141120 | tf_op jit(solution)/shard_map/all_to_all | solution.py:840
  1301.3 12.9 copy-start.22
  1301.3 12.9 copy-start.23
  1301.3 12.9 copy-start.24
  1329.3 7.2 collective-permute-start.4
  1351.6 45.3 %collective-permute-start.5 = (f32[384,1282]{0,1:T(8,128)}, f32[384,1282]{0,1:T(8,128)S(1)}, u32[]{:S(2)}, u32[]{:S(2)}) collective-permute-start(f32[384,1282]{0,1:T(8,128)} %copy.217), channel_id=1, source_target_pairs={{0,2},{1,3},{2,0},{3,1},{4,6},{5,7},{6,4},{7,5},{8,10},{9,11},{10,... | collective-permute-start | bytes 5907464 | tf_op jit(solution)/shard_map/ppermute | solution.py:906
  1402.1 26.0 %copy-start.7 = (f32[384,1282]{1,0:T(8,128)}, f32[384,1282]{1,0:T(8,128)S(1)}, u32[]{:S(2)}) copy-start(f32[384,1282]{1,0:T(8,128)S(1)} %select_add_fusion.1) | copy-start | bytes 5907460
  1423.6 73.9 %all-to-all-start.14 = ((bf16[8,19,8,1280]{3,2,1,0:T(8,128)(2,1)}), bf16[8,19,8,1280]{3,2,1,0:T(8,128)(2,1)}, u32[]{:S(2)}, u32[]{:S(2)}) async-start(bf16[8,19,8,1280]{3,2,1,0:T(8,128)(2,1)} %get-tuple-element.206), calls=%async_computation.14 | async-start | bytes 6225920 | tf_op jit(solution)/shard_map/all_to_all | solution.py:840
  1429.2 57.1 %collective-permute-start.6 = (f32[192,1282]{1,0:T(8,128)}, f32[192,1282]{1,0:T(8,128)S(1)}, u32[]{:S(2)}, u32[]{:S(2)}) collective-permute-start(f32[192,1282]{1,0:T(8,128)} %slice_select_fusion.2), channel_id=1, source_target_pairs={{0,4},{4,0},{8,12},{12,8},{16,20},{20,16},{24,28},{28,24},{1,5},{5... | collective-permute-start | bytes 2953736 | tf_op jit(solution)/shard_map/ppermute | solution.py:906
  1497.6 74.0 %all-to-all-start.15 = ((bf16[8,19,8,1280]{3,2,1,0:T(8,128)(2,1)}), bf16[8,19,8,1280]{3,2,1,0:T(8,128)(2,1)}, u32[]{:S(2)}, u32[]{:S(2)}) async-start(bf16[8,19,8,1280]{3,2,1,0:T(8,128)(2,1)} %get-tuple-element.210), calls=%async_computation.15 | async-start | bytes 6225920 | tf_op jit(solution)/shard_map/all_to_all | solution.py:840
  1511.5 72.1 %copy-start.14 = (bf16[12,96,96]{2,1,0:T(8,128)(2,1)S(1)}, bf16[12,96,96]{2,1,0:T(8,128)(2,1)}, u32[]{:S(2)}) copy-start(bf16[12,96,96]{2,1,0:T(8,128)(2,1)} %convert_element_type.225.refs_2_) | copy-start | bytes 663556
  1571.6 85.0 %all-to-all-start.16 = ((bf16[8,19,8,1280]{3,2,1,0:T(8,128)(2,1)}), bf16[8,19,8,1280]{3,2,1,0:T(8,128)(2,1)S(1)}, u32[]{:S(2)}, u32[]{:S(2)}) async-start(bf16[8,19,8,1280]{3,2,1,0:T(8,128)(2,1)} %rows_to_degrees.7), calls=%async_computation.16 | async-start | bytes 6225920 | tf_op jit(solution)/shard_map/all_to_all | solution.py:840
  1577.1 53.6 %collective-permute-start.7 = (bf16[48,1282]{1,0:T(8,128)(2,1)}, bf16[48,1282]{1,0:T(8,128)(2,1)S(1)}, u32[]{:S(2)}, u32[]{:S(2)}) collective-permute-start(bf16[48,1282]{1,0:T(8,128)(2,1)} %get-tuple-element.271), channel_id=1, source_target_pairs={{0,8},{4,12},{8,0},{12,4},{16,24},{20,28},{24,16},{28,20},{1,9},{5... | collective-permute-start | bytes 369224 | tf_op jit(solution)/shard_map/ppermute | solution.py:926
  1579.1 76.3 %collective-permute-start.8 = (bf16[48,1282]{1,0:T(8,128)(2,1)}, bf16[48,1282]{1,0:T(8,128)(2,1)}, u32[]{:S(2)}, u32[]{:S(2)}) collective-permute-start(bf16[48,1282]{1,0:T(8,128)(2,1)} %get-tuple-element.273), channel_id=1, source_target_pairs={{0,16},{4,20},{8,24},{12,28},{16,0},{20,4},{24,8},{28,12},{1,17},{... | collective-permute-start | bytes 369224 | tf_op jit(solution)/shard_map/ppermute | solution.py:926
  1581.4 73.9 %collective-permute-start.9 = (bf16[48,1282]{1,0:T(8,128)(2,1)}, bf16[48,1282]{1,0:T(8,128)(2,1)}, u32[]{:S(2)}, u32[]{:S(2)}) collective-permute-start(bf16[48,1282]{1,0:T(8,128)(2,1)} %get-tuple-element.272), channel_id=1, source_target_pairs={{0,24},{4,28},{8,16},{12,20},{16,8},{20,12},{24,0},{28,4},{1,25},{... | collective-permute-start | bytes 369224 | tf_op jit(solution)/shard_map/ppermute | solution.py:926
  1658.2 75.8 %all-to-all-start.17 = ((bf16[8,19,8,1280]{3,2,1,0:T(8,128)(2,1)}), bf16[8,19,8,1280]{3,2,1,0:T(8,128)(2,1)}, u32[]{:S(2)}, u32[]{:S(2)}) async-start(bf16[8,19,8,1280]{3,2,1,0:T(8,128)(2,1)} %get-tuple-element.212), calls=%async_computation.17 | async-start | bytes 6225920 | tf_op jit(solution)/shard_map/all_to_all | solution.py:840
  1734.0 74.4 %all-to-all-start.18 = ((bf16[8,19,8,1280]{3,2,1,0:T(8,128)(2,1)}), bf16[8,19,8,1280]{3,2,1,0:T(8,128)(2,1)}, u32[]{:S(2)}, u32[]{:S(2)}) async-start(bf16[8,19,8,1280]{3,2,1,0:T(8,128)(2,1)} %get-tuple-element.224), calls=%async_computation.18 | async-start | bytes 6225920 | tf_op jit(solution)/shard_map/all_to_all | solution.py:840
  1808.4 84.6 %all-to-all-start.19 = ((bf16[8,19,8,1280]{3,2,1,0:T(8,128)(2,1)}), bf16[8,19,8,1280]{3,2,1,0:T(8,128)(2,1)S(1)}, u32[]{:S(2)}, u32[]{:S(2)}) async-start(bf16[8,19,8,1280]{3,2,1,0:T(8,128)(2,1)} %get-tuple-element.225), calls=%async_computation.19 | async-start | bytes 6225920 | tf_op jit(solution)/shard_map/all_to_all | solution.py:840
  1815.4 52.0 %collective-permute-start.11 = (bf16[48,1282]{1,0:T(8,128)(2,1)S(1)}, bf16[48,1282]{1,0:T(8,128)(2,1)S(1)}, u32[]{:S(2)}, u32[]{:S(2)}) collective-permute-start(bf16[48,1282]{1,0:T(8,128)(2,1)S(1)} %fusion.11), channel_id=1, source_target_pairs={{0,8},{4,12},{8,0},{12,4},{16,24},{20,28},{24,16},{28,20},{1,9},{5... | collective-permute-start | bytes 369224 | tf_op jit(solution)/shard_map/ppermute | solution.py:935
  1817.4 74.7 %collective-permute-start.12 = (bf16[48,1282]{1,0:T(8,128)(2,1)S(1)}, bf16[48,1282]{1,0:T(8,128)(2,1)S(1)}, u32[]{:S(2)}, u32[]{:S(2)}) collective-permute-start(bf16[48,1282]{1,0:T(8,128)(2,1)S(1)} %fusion.11), channel_id=1, source_target_pairs={{0,16},{4,20},{8,24},{12,28},{16,0},{20,4},{24,8},{28,12},{1,17},{... | collective-permute-start | bytes 369224 | tf_op jit(solution)/shard_map/ppermute | solution.py:935
  1819.8 72.3 %collective-permute-start.13 = (bf16[48,1282]{1,0:T(8,128)(2,1)S(1)}, bf16[48,1282]{1,0:T(8,128)(2,1)S(1)}, u32[]{:S(2)}, u32[]{:S(2)}) collective-permute-start(bf16[48,1282]{1,0:T(8,128)(2,1)S(1)} %fusion.11), channel_id=1, source_target_pairs={{0,24},{4,28},{8,16},{12,20},{16,8},{20,12},{24,0},{28,4},{1,25},{... | collective-permute-start | bytes 369224 | tf_op jit(solution)/shard_map/ppermute | solution.py:935
  1828.7 64.3 %collective-permute-start.14 = (bf16[3,8,24,1408]{3,2,1,0:T(8,128)(2,1)S(1)}, bf16[3,8,24,1408]{3,2,1,0:T(8,128)(2,1)}, u32[]{:S(2)}, u32[]{:S(2)}) collective-permute-start(bf16[3,8,24,1408]{3,2,1,0:T(8,128)(2,1)S(1)} %constant_dynamic-slice_fusion.2), channel_id=1, source_target_pairs={{0,3},{1,2},{2,1},{3,0},{4,7},{5,6},{6,5},{7,4},{8,11},{9,10},{10,... | collective-permute-start | bytes 4866056 | tf_op jit(solution)/shard_map/ppermute | solution.py:879
  1893.0 10.6 copy-start.5
  1893.0 75.6 %all-to-all-start.20 = ((bf16[8,19,8,1280]{3,2,1,0:T(8,128)(2,1)}), bf16[8,19,8,1280]{3,2,1,0:T(8,128)(2,1)}, u32[]{:S(2)}, u32[]{:S(2)}) async-start(bf16[8,19,8,1280]{3,2,1,0:T(8,128)(2,1)} %get-tuple-element.229), calls=%async_computation.20 | async-start | bytes 6225920 | tf_op jit(solution)/shard_map/all_to_all | solution.py:840
  1903.6 9.5 collective-permute-start.10
  1968.6 80.5 %all-to-all-start.21 = ((bf16[8,19,8,1280]{3,2,1,0:T(8,128)(2,1)}), bf16[8,19,8,1280]{3,2,1,0:T(8,128)(2,1)}, u32[]{:S(2)}, u32[]{:S(2)}) async-start(bf16[8,19,8,1280]{3,2,1,0:T(8,128)(2,1)} %degrees_to_rows.6), calls=%async_computation.21 | async-start | bytes 6225920 | tf_op jit(solution)/shard_map/all_to_all | solution.py:840
  1977.1 71.9 %collective-permute-start.18 = (bf16[6,8,24,1408]{3,2,1,0:T(8,128)(2,1)}, bf16[6,8,24,1408]{3,2,1,0:T(8,128)(2,1)}, u32[]{:S(2)}, u32[]{:S(2)}) collective-permute-start(bf16[6,8,24,1408]{3,2,1,0:T(8,128)(2,1)} %constant_dynamic-slice_fusion), channel_id=1, source_target_pairs={{0,2},{1,3},{2,0},{3,1},{4,6},{5,7},{6,4},{7,5},{8,10},{9,11},{10,... | collective-permute-start | bytes 9732104 | tf_op jit(solution)/shard_map/ppermute | solution.py:879
  2049.0 197.1 %all-to-all-start.22 = ((bf16[8,52,8,1280]{3,2,1,0:T(8,128)(2,1)}), bf16[8,52,8,1280]{3,2,1,0:T(8,128)(2,1)}, u32[]{:S(2)}, u32[]{:S(2)}) async-start(bf16[8,52,8,1280]{3,2,1,0:T(8,128)(2,1)} %get-tuple-element.246), calls=%async_computation.22 | async-start | bytes 17039360 | tf_op jit(solution)/shard_map/all_to_all | solution.py:840
  2054.9 80.7 %collective-permute-start.16 = (bf16[192,1282]{1,0:T(8,128)(2,1)S(1)}, bf16[192,1282]{1,0:T(8,128)(2,1)S(1)}, u32[]{:S(2)}, u32[]{:S(2)}) collective-permute-start(bf16[192,1282]{1,0:T(8,128)(2,1)S(1)} %bitcast.140), channel_id=1, source_target_pairs={{0,4},{4,0},{8,12},{12,8},{16,20},{20,16},{24,28},{28,24},{1,5},{5... | collective-permute-start | bytes 1476872 | tf_op jit(solution)/shard_map/ppermute | solution.py:911
  2136.9 24.9 %collective-permute-start.17 = (bf16[384,1282]{0,1:T(8,128)(2,1)S(1)}, bf16[384,1282]{0,1:T(8,128)(2,1)S(1)}, u32[]{:S(2)}, u32[]{:S(2)}) collective-permute-start(bf16[384,1282]{0,1:T(8,128)(2,1)S(1)} %copy.222), channel_id=1, source_target_pairs={{0,2},{1,3},{2,0},{3,1},{4,6},{5,7},{6,4},{7,5},{8,10},{9,11},{10,... | collective-permute-start | bytes 2953736 | tf_op jit(solution)/shard_map/ppermute | solution.py:911
  2140.1 52.2 %collective-permute-start.15 = (bf16[3,8,24,1408]{3,2,1,0:T(8,128)(2,1)}, bf16[3,8,24,1408]{3,2,1,0:T(8,128)(2,1)}, u32[]{:S(2)}, u32[]{:S(2)}) collective-permute-start(bf16[3,8,24,1408]{3,2,1,0:T(8,128)(2,1)} %constant_dynamic-slice_fusion.1), channel_id=1, source_target_pairs={{0,3},{1,2},{2,1},{3,0},{4,7},{5,6},{6,5},{7,4},{8,11},{9,10},{10,... | collective-permute-start | bytes 4866056 | tf_op jit(solution)/shard_map/ppermute | solution.py:879
  2246.1 78.5 %all-to-all-start.23 = ((bf16[8,19,8,1280]{3,2,1,0:T(8,128)(2,1)}), bf16[8,19,8,1280]{3,2,1,0:T(8,128)(2,1)}, u32[]{:S(2)}, u32[]{:S(2)}) async-start(bf16[8,19,8,1280]{3,2,1,0:T(8,128)(2,1)} %get-tuple-element.247), calls=%async_computation.23 | async-start | bytes 6225920 | tf_op jit(solution)/shard_map/all_to_all | solution.py:840
  2253.4 12.8 copy-start.10
  2257.6 4.6 collective-permute-start.19
  2324.6 14.4 copy-start.25
  2324.6 14.4 copy-start.26
  2340.4 1.2 collective-permute-start.20
  2341.6 3.6 collective-permute-start.21
  2345.3 3.6 collective-permute-start.22
  2348.9 3.6 collective-permute-start.23
  2352.5 4.5 collective-permute-start.24
  (26 other events, 87.3 us)
